TPU v7x, 32 devices: a whole 2x2x4 slice. The times are simulated.
32 devices in a mesh: dp: 8 (over z, y), seq: 4 (over x, core).
Axes of the slice: x: 2, y: 2, z: 4, core: 2. Of those that a mesh axis runs over, the one named last changes fastest.
Arguments:
- tokens: bfloat16 [8192, 768], P(('dp', 'seq')), may hold values from -6 to 6
- lengths: int32 [8], P('dp'), may hold values from 769 to 1024, as said below
- cotangent: bfloat16 [8192, 768], P(('dp', 'seq')), may hold values from -6 to 6
- w_gate: bfloat16 [2, 768, 1536], P(None, ('dp', 'seq')), may hold values from -0.21875 to 0.21875
- w_value: bfloat16 [2, 768, 3072], P(None, ('dp', 'seq')), may hold values from -0.21875 to 0.21875
- w_mix: bfloat16 [2, 1536, 1536], P(None, ('dp', 'seq')), may hold values from -0.15625 to 0.15625
- w_out: bfloat16 [2, 1536, 768], P(None, ('dp', 'seq')), may hold values from -0.4375 to 0.4375
- ln_gain: bfloat16 [2, 768], P(None, ('dp', 'seq')), may hold values from 0.5 to 1.5
- ln_bias: bfloat16 [2, 768], P(None, ('dp', 'seq')), may hold values from -1.5 to 1.5
- ssm_coef: float32 [2, 2, 1536, 64], P(None, None, 'seq'), may hold values from -1.5 to 1.5
- ssm_rate: float32 [2, 2, 1536, 64], P(None, None, 'seq'), may hold values from 0.00029296876 to 0.033
- ssm_skip: float32 [2, 2, 1536], P(None, None, 'seq'), may hold values from -4 to 4
Outputs:
- output: float32 [8192, 768], P(('dp', 'seq'))
- grad_tokens: float32 [8192, 768], P(('dp', 'seq'))
- grad_w_gate: float32 [2, 768, 1536], P(None, ('dp', 'seq'))
- grad_w_value: float32 [2, 768, 3072], P(None, ('dp', 'seq'))
- grad_w_mix: float32 [2, 1536, 1536], P(None, ('dp', 'seq'))
- grad_w_out: float32 [2, 1536, 768], P(None, ('dp', 'seq'))
- grad_ln_gain: float32 [2, 768], P(None, ('dp', 'seq'))
- grad_ln_bias: float32 [2, 768], P(None, ('dp', 'seq'))
- grad_ssm_coef: float32 [2, 2, 1536, 64], P(None, None, 'seq')
- grad_ssm_rate: float32 [2, 2, 1536, 64], P(None, None, 'seq')
- grad_ssm_skip: float32 [2, 2, 1536], P(None, None, 'seq')
Inputs may be any that keep to these rules, and one draw needn't show every extreme that they name: `lengths`: every sequence ends within the rows of the last device of seq; in each draw at least one slot is full.
All inputs are finite; a program needn't handle non-finite values.
Results may differ from a plain program's by a relative error of at most 0.02.
Values may be sent and summed in bfloat16 or wider, within the bound.
No kernel may reach another device: no remote copies, remote signals or barrier semaphores. Data moves between devices by JAX's collectives and lax.ppermute only.
A program may use at most 448 MiB of HBM per device.

v0:
```python
from functools import partial

import jax
import jax.numpy as jnp
from jax import lax
from jax.sharding import PartitionSpec as P

EPSILON = 1e-05
PRECISE = lax.Precision.HIGHEST
SPLIT_THREE = lax.Precision.HIGH
AS_ROWS = (((0,), (0,)), ((), ()))
AS_COLS = (((1,), (1,)), ((), ()))


def gelu_exact(values):
    return jax.nn.gelu(values, approximate=False)


def layer_norm(stream, ln_scale, ln_shift):
    centre = jnp.mean(stream, axis=-1, keepdims=True)
    centred = stream - centre
    spread = jnp.mean(centred * centred, axis=-1, keepdims=True)
    return centred * lax.rsqrt(spread + EPSILON) * ln_scale + ln_shift


def rows_product(left_op, right_op):
    return lax.dot_general(left_op, right_op, AS_ROWS, preferred_element_type=jnp.float32)


def cols_product(left_op, right_op):
    return lax.dot_general(left_op, right_op, AS_COLS, preferred_element_type=jnp.float32)


def prepare_tables(coef_rows, rate_rows, series_len):
    block_len = min(128, series_len)
    block_count = series_len // block_len
    offsets = jnp.arange(block_len, dtype=jnp.float32)
    scaled = coef_rows * rate_rows
    rate_cols = rate_rows[:, :, None]
    lag_kernel = jnp.sum(scaled[:, :, None] * jnp.exp(-rate_cols * offsets), axis=1)
    steps_index = jnp.arange(block_len, dtype=jnp.int32)
    lag_index = jnp.maximum(steps_index[:, None] - steps_index[None, :], 0)
    lower_mask = (steps_index[:, None] >= steps_index[None, :]).astype(jnp.float32)
    toeplitz = jnp.take(lag_kernel, lag_index, axis=1) * lower_mask
    tail_terms = jnp.exp(-rate_cols * (block_len - 1.0 - offsets))
    block_ids = jnp.arange(block_count, dtype=jnp.float32)
    block_gaps = block_ids[:, None] - block_ids[None, :]
    carry_mat = jnp.exp(
        -rate_rows[:, :, None, None] * (block_len * jnp.maximum(block_gaps, 0.0))
    ) * (block_gaps >= 0).astype(jnp.float32)
    head_terms = scaled[:, :, None] * jnp.exp(-rate_cols * (offsets + 1.0))
    return (toeplitz, tail_terms, carry_mat, head_terms)


def prepare_pair(ssm_coef, ssm_rate, series_len):
    return (
        prepare_tables(ssm_coef[0], ssm_rate[0], series_len),
        prepare_tables(ssm_coef[1], ssm_rate[1], series_len),
    )


def causal_mix(series, tables):
    toeplitz, tail_terms, carry_mat, head_terms = tables
    series_len, channels = series.shape
    block_len = toeplitz.shape[1]
    block_count = series_len // block_len
    pieces = series.reshape(block_count, block_len, channels)
    inside = jnp.einsum("cij,bjc->bic", toeplitz, pieces, precision=SPLIT_THREE)
    block_sums = jnp.einsum("bjc,cnj->bcn", pieces, tail_terms, precision=SPLIT_THREE)
    states = jnp.einsum("cnab,bcn->acn", carry_mat, block_sums, precision=PRECISE)
    earlier = jnp.concatenate([jnp.zeros_like(states[:1]), states[:-1]], axis=0)
    outside = jnp.einsum("bcn,cni->bic", earlier, head_terms, precision=PRECISE)
    return (inside + outside).reshape(series_len, channels)


def ssm_local(values, tables, ssm_skip):
    ahead = values[:, 0]
    behind = values[:, 1]
    forward_mix = causal_mix(ahead, tables[0]) + ssm_skip[0] * ahead
    backward_mix = jnp.flip(causal_mix(jnp.flip(behind, 0), tables[1]), 0) + ssm_skip[1] * behind
    return forward_mix * backward_mix


def run_layer(stream, keep_rows, weights, tables, ssm_skip):
    w_gate, w_value, w_mix, w_out, ln_scale, ln_shift = weights
    normed = layer_norm(stream, ln_scale.astype(jnp.float32), ln_shift.astype(jnp.float32))
    normed_low = normed.astype(jnp.bfloat16)
    gate_pre = jnp.dot(normed_low, w_gate, preferred_element_type=jnp.float32)
    value_pre = jnp.dot(normed_low, w_value, preferred_element_type=jnp.float32)
    gate_act = gelu_exact(gate_pre)
    values = (gelu_exact(value_pre) * keep_rows).astype(jnp.bfloat16)
    row_count = normed_low.shape[0]
    ssm_width = w_mix.shape[0]
    channel_major = lax.all_to_all(
        values.reshape(row_count, 2, ssm_width), "seq", split_axis=2, concat_axis=0, tiled=True
    )
    product = ssm_local(channel_major.astype(jnp.float32), tables, ssm_skip).astype(jnp.bfloat16)
    token_major = lax.all_to_all(product, "seq", split_axis=0, concat_axis=1, tiled=True)
    update = jnp.dot(token_major, w_mix, preferred_element_type=jnp.float32)
    mixed_low = (update * gate_act).astype(jnp.bfloat16)
    result = stream + jnp.dot(mixed_low, w_out, preferred_element_type=jnp.float32)
    return (
        result,
        (normed_low, gate_pre, value_pre, gate_act, channel_major, token_major, update, mixed_low),
    )


def back_layer(stream, grad_stream, keep_rows, weights, ssm_coef, ssm_rate, ssm_skip, series_len):
    w_gate, w_value, w_mix, w_out, ln_scale, ln_shift = weights
    scale_full = ln_scale.astype(jnp.float32)
    shift_full = ln_shift.astype(jnp.float32)
    tables, table_pull = jax.vjp(partial(prepare_pair, series_len=series_len), ssm_coef, ssm_rate)
    unused, saved = run_layer(stream, keep_rows, weights, tables, ssm_skip)
    normed_low, gate_pre, value_pre, gate_act, channel_major, token_major, update, mixed_low = saved
    out_low = grad_stream.astype(jnp.bfloat16)
    grad_out = rows_product(mixed_low, out_low)
    grad_mixed = cols_product(out_low, w_out)
    update_low = (grad_mixed * gate_act).astype(jnp.bfloat16)
    grad_gate = grad_mixed * update
    grad_mix = rows_product(token_major, update_low)
    product_low = cols_product(update_low, w_mix).astype(jnp.bfloat16)
    product_chan = lax.all_to_all(product_low, "seq", split_axis=1, concat_axis=0, tiled=True)
    unused_mix, ssm_pull = jax.vjp(ssm_local, channel_major.astype(jnp.float32), tables, ssm_skip)
    grad_values, grad_tables, grad_skip = ssm_pull(product_chan.astype(jnp.float32))
    grad_coef, grad_rate = table_pull(grad_tables)
    value_tokens = lax.all_to_all(
        grad_values.astype(jnp.bfloat16), "seq", split_axis=0, concat_axis=2, tiled=True
    )
    row_count = value_tokens.shape[0]
    value_flat = value_tokens.reshape(row_count, -1).astype(jnp.float32) * keep_rows
    unused_value, value_pull = jax.vjp(gelu_exact, value_pre)
    value_grad_low = value_pull(value_flat)[0].astype(jnp.bfloat16)
    unused_gate, gate_pull = jax.vjp(gelu_exact, gate_pre)
    gate_grad_low = gate_pull(grad_gate)[0].astype(jnp.bfloat16)
    grad_value = rows_product(normed_low, value_grad_low)
    grad_gate_w = rows_product(normed_low, gate_grad_low)
    grad_normed = cols_product(value_grad_low, w_value) + cols_product(gate_grad_low, w_gate)
    unused_norm, norm_pull = jax.vjp(layer_norm, stream, scale_full, shift_full)
    grad_input, grad_scale, grad_shift = norm_pull(grad_normed)
    weight_terms = (grad_gate_w, grad_value, grad_mix, grad_out)
    return (
        grad_stream + grad_input,
        weight_terms,
        (grad_scale, grad_shift),
        (grad_coef, grad_rate, grad_skip),
    )


def shards(
    tokens,
    lengths,
    cotangent,
    w_gate,
    w_value,
    w_mix,
    w_out,
    ln_gain,
    ln_bias,
    ssm_coef,
    ssm_rate,
    ssm_skip,
):
    row_count = tokens.shape[0]
    series_len = row_count * lax.axis_size("seq")
    positions = lax.axis_index("seq") * row_count + jnp.arange(row_count, dtype=jnp.int32)
    keep_rows = (positions < lengths[0]).astype(jnp.float32)[:, None]
    depth = w_gate.shape[0]
    fetched = []
    inputs = []
    stream = tokens.astype(jnp.float32)
    for layer in range(depth):
        weights = (
            lax.all_gather(w_gate[layer], ("dp", "seq"), axis=0, tiled=True),
            lax.all_gather(w_value[layer], ("dp", "seq"), axis=0, tiled=True),
            lax.all_gather(w_mix[layer], ("dp", "seq"), axis=0, tiled=True),
            lax.all_gather(w_out[layer], ("dp", "seq"), axis=0, tiled=True),
            lax.all_gather(ln_gain[layer], ("dp", "seq"), axis=0, tiled=True),
            lax.all_gather(ln_bias[layer], ("dp", "seq"), axis=0, tiled=True),
        )
        fetched.append(weights)
        inputs.append(stream)
        tables = prepare_pair(ssm_coef[layer], ssm_rate[layer], series_len)
        stream, unused = run_layer(stream, keep_rows, weights, tables, ssm_skip[layer])
    grad_stream = cotangent.astype(jnp.float32)
    reduced = [None] * depth
    gain_grads = []
    shift_grads = []
    coef_grads = []
    rate_grads = []
    skip_grads = []
    for layer in reversed(range(depth)):
        weights = (
            lax.all_gather(w_gate[layer], ("dp", "seq"), axis=0, tiled=True),
            lax.all_gather(w_value[layer], ("dp", "seq"), axis=0, tiled=True),
            lax.all_gather(w_mix[layer], ("dp", "seq"), axis=0, tiled=True),
            lax.all_gather(w_out[layer], ("dp", "seq"), axis=0, tiled=True),
            lax.all_gather(ln_gain[layer], ("dp", "seq"), axis=0, tiled=True),
            lax.all_gather(ln_bias[layer], ("dp", "seq"), axis=0, tiled=True),
        )
        grad_stream, weight_terms, norm_terms, ssm_terms = back_layer(
            inputs[layer],
            grad_stream,
            keep_rows,
            weights,
            ssm_coef[layer],
            ssm_rate[layer],
            ssm_skip[layer],
            series_len,
        )
        shares = (
            lax.psum_scatter(weight_terms[0], ("dp", "seq"), scatter_dimension=0, tiled=True),
            lax.psum_scatter(weight_terms[1], ("dp", "seq"), scatter_dimension=0, tiled=True),
            lax.psum_scatter(weight_terms[2], ("dp", "seq"), scatter_dimension=0, tiled=True),
            lax.psum_scatter(weight_terms[3], ("dp", "seq"), scatter_dimension=0, tiled=True),
        )
        reduced[layer] = shares
        gain_grads.insert(0, norm_terms[0])
        shift_grads.insert(0, norm_terms[1])
        coef_grads.insert(0, ssm_terms[0])
        rate_grads.insert(0, ssm_terms[1])
        skip_grads.insert(0, ssm_terms[2])
    summed = (
        lax.psum(jnp.stack(coef_grads).astype(jnp.bfloat16), "dp").astype(jnp.float32),
        lax.psum(jnp.stack(rate_grads).astype(jnp.bfloat16), "dp").astype(jnp.float32),
        lax.psum(jnp.stack(skip_grads).astype(jnp.bfloat16), "dp").astype(jnp.float32),
    )
    norm_sums = lax.psum((jnp.stack(gain_grads), jnp.stack(shift_grads)), ("dp", "seq"))
    share = norm_sums[0].shape[1] // lax.axis_size(("dp", "seq"))
    start = lax.axis_index(("dp", "seq")) * share
    gain_share = lax.dynamic_slice_in_dim(norm_sums[0], start, share, 1)
    shift_share = lax.dynamic_slice_in_dim(norm_sums[1], start, share, 1)
    stacked = [jnp.stack([reduced[layer][member] for layer in range(depth)]) for member in range(4)]
    return (
        stream,
        grad_stream,
        stacked[0],
        stacked[1],
        stacked[2],
        stacked[3],
        gain_share,
        shift_share,
        summed[0],
        summed[1],
        summed[2],
    )


def solution(mesh):
    in_specs = (
        P(("dp", "seq"), None),
        P("dp"),
        P(("dp", "seq"), None),
        P(None, ("dp", "seq"), None),
        P(None, ("dp", "seq"), None),
        P(None, ("dp", "seq"), None),
        P(None, ("dp", "seq"), None),
        P(None, ("dp", "seq")),
        P(None, ("dp", "seq")),
        P(None, None, "seq", None),
        P(None, None, "seq", None),
        P(None, None, "seq"),
    )
    out_specs = (
        P(("dp", "seq"), None),
        P(("dp", "seq"), None),
        P(None, ("dp", "seq"), None),
        P(None, ("dp", "seq"), None),
        P(None, ("dp", "seq"), None),
        P(None, ("dp", "seq"), None),
        P(None, ("dp", "seq")),
        P(None, ("dp", "seq")),
        P(None, None, "seq", None),
        P(None, None, "seq", None),
        P(None, None, "seq"),
    )
    return jax.shard_map(shards, mesh=mesh, in_specs=in_specs, out_specs=out_specs, check_vma=False)
```

profile of v0, /device:TPU:0, one launch (start us, length us, event | category | flops | bytes accessed | tf_op | source)
XLA Modules:
  0.0 3154.6 jit_solution(13955696929363525079)
XLA Ops:
  19.2 42.3 %all-reduce.29 = (bf16[768]{0:T(1024)(128)(2,1)S(1)}, bf16[768]{0:T(1024)(128)(2,1)S(1)}, bf16[768]{0:T(1024)(128)(2,1)}, bf16[768]{0:T(1024)(128)(2,1)}) all-reduce(bf16[768]{0:T(1024)(128)(2,1)S(1)} %dynamic-update-slice.1, bf16[768]{0:T(1024)(128)(2,1)S(1)} %dynamic-update-slice, ...), channel_id=3, replica_groups=mesh['dp'=8,'seq'=4] {'dp','seq'}, use_global_device_ids=true, to_apply=%add.25 | all-reduce | flops 3072 | bytes 12288
  78.1 63.1 %gather_fusion.1 = f32[16384,384]{1,0:T(8,128)} fusion(f32[384,128]{0,1:T(8,128)S(1)} %copy.408, s32[16384]{0:T(1024)S(1)} %broadcast_clamp_fusion), kind=kCustom, calls=%fused_computation.2.clone | custom fusion | bytes 50397184 | tf_op jit(solution)/shard_map/jit(_take)/gather | solution.py:44
  141.2 24.9 copy.554
  174.1 63.0 %gather_fusion = f32[16384,384]{1,0:T(8,128)} fusion(f32[384,128]{0,1:T(8,128)S(1)} %copy.402, s32[16384]{0:T(1024)S(1)} %broadcast_clamp_fusion), kind=kCustom, calls=%fused_computation.clone | custom fusion | bytes 50397184 | tf_op jit(solution)/shard_map/jit(_take)/gather | solution.py:44
  237.2 24.9 copy.552
  297.6 63.0 %gather_fusion.2 = f32[16384,384]{1,0:T(8,128)} fusion(f32[384,128]{0,1:T(8,128)S(1)} %copy.420, s32[16384]{0:T(1024)S(1)} %broadcast_clamp_fusion), kind=kCustom, calls=%fused_computation.3.clone | custom fusion | bytes 50397184 | tf_op jit(solution)/shard_map/jit(_take)/gather | solution.py:44
  360.6 24.8 copy.557
  395.6 12.9 rev.39
  411.6 12.5 fusion.31
  453.7 19.5 fusion.35
  473.2 24.0 bitcast_add_fusion.5
  500.3 12.8 rev.40
  515.9 17.0 fusion.1
  532.9 18.4 bitcast_add_fusion.7
  641.6 12.8 rev.41
  657.6 12.5 fusion.17
  689.2 18.9 fusion.5
  718.2 18.0 bitcast_add_fusion.4
  742.2 12.8 rev.43
  758.1 24.8 multiply_bitcast_fusion.1
  782.9 24.7 copy.575
  807.7 103.9 %scatter_custom_fusion.2 = f32[384,128]{0,1:T(8,128)S(1)} fusion(s32[16384]{0:T(1024)} %fusion.289, f32[16384,384]{1,0:T(8,128)} %bitcast.569, f32[]{:T(128)} %constant.60.clone.1), kind=kCustom, calls=%fused_computation.418 | custom fusion | flops 6291456 | bytes 197120 | tf_op jit(solution)/shard_map/transpose(jvp(jit(_take)))/scatter-add | solution.py:44
  915.2 26.1 fusion.221
  941.4 18.4 fusion.21
  959.8 43.4 %multiply_reduce_fusion.5 = (f32[384,64]{1,0:T(8,128)}, f32[384,64]{1,0:T(8,128)}, f32[384,64]{1,0:T(8,128)}, f32[384,64]{1,0:T(8,128)}, f32[384,128]{1,0:T(8,128)}) fusion(f32[384,64]{1,0:T(8,128)S(1)} %copy-done.99, f32[384,64]{1,0:T(8,128)S(1)} %copy-done.123, f32[128]{0:T(128)S(1)} %copy-done.185, f32[384,128]{1,0:T(8,128)S(1)} %copy-done.119, ...), kind=kOutput, calls=%fused_computation.41 | convolution fusion | flops 352174080 | bytes 3244544 | tf_op jit(solution)/shard_map/transpose(jvp(bcn,cni->bic))/dot_general | solution.py:72
  1004.2 63.0 %gather_fusion.3 = f32[16384,384]{1,0:T(8,128)} fusion(f32[384,128]{0,1:T(8,128)S(1)} %copy.426, s32[16384]{0:T(1024)S(1)} %copy-done.72), kind=kCustom, calls=%fused_computation.4.clone | custom fusion | bytes 50397184 | tf_op jit(solution)/shard_map/jit(_take)/gather | solution.py:44
  1067.2 24.7 copy.559
  1092.0 24.3 bitcast_add_fusion.2
  1119.3 13.1 rev.42
  1139.6 25.1 fusion.216
  1164.7 16.6 multiply_bitcast_fusion
  1211.2 14.3 add_bitcast_fusion.5
  1228.6 12.8 rev.44
  1254.0 14.5 add_bitcast_fusion.3
  1275.7 18.6 multiply_reduce_fusion.4
  1298.4 15.6 multiply_reduce_fusion.1
  1348.5 24.8 copy.576
  1373.3 103.9 %scatter_custom_fusion.3 = f32[384,128]{0,1:T(8,128)S(1)} fusion(s32[16384]{0:T(1024)} %fusion.289, f32[16384,384]{1,0:T(8,128)} %bitcast.570, f32[]{:T(128)} %constant.60.clone.1), kind=kCustom, calls=%fused_computation.416 | custom fusion | flops 6291456 | bytes 197120 | tf_op jit(solution)/shard_map/transpose(jvp(jit(_take)))/scatter-add | solution.py:44
  1478.8 23.7 fusion.184
  1509.6 16.5 multiply_bitcast_fusion.2
  1526.2 22.5 fusion.174
  1548.7 25.6 fusion.204
  1584.1 23.2 multiply_bitcast_fusion.3
  1607.3 25.6 fusion.209
  1632.9 24.7 copy.573
  1657.6 104.5 %scatter_custom_fusion = f32[384,128]{0,1:T(8,128)} fusion(s32[16384]{0:T(1024)} %fusion.289, f32[16384,384]{1,0:T(8,128)} %bitcast.571, f32[]{:T(128)} %constant.60.clone.1), kind=kCustom, calls=%fused_computation.422 | custom fusion | flops 6291456 | bytes 197120 | tf_op jit(solution)/shard_map/transpose(jvp(jit(_take)))/scatter-add | solution.py:44
  1763.9 25.1 copy.574
  1789.0 104.5 %scatter_custom_fusion.1 = f32[384,128]{0,1:T(8,128)} fusion(s32[16384]{0:T(1024)} %fusion.289, f32[16384,384]{1,0:T(8,128)} %bitcast.568, f32[]{:T(128)} %constant.60.clone.1), kind=kCustom, calls=%fused_computation.420 | custom fusion | flops 6291456 | bytes 197120 | tf_op jit(solution)/shard_map/transpose(jvp(jit(_take)))/scatter-add | solution.py:44
  1917.8 18.7 multiply_reduce_fusion.10
  1940.0 15.3 multiply_reduce_fusion.7
  1956.2 98.3 %multiply_reduce_fusion.11 = (f32[384,64]{1,0:T(8,128)S(1)}, f32[384,64]{1,0:T(8,128)S(1)}, f32[384,64]{1,0:T(8,128)S(1)}, f32[384,64]{1,0:T(8,128)S(1)}, f32[38...) fusion(f32[384,64]{1,0:T(8,128)S(1)} %copy-done.88, ...), kind=kOutput, calls=%fused_computation.47 | convolution fusion | flops 433815552 | bytes 29786624 | tf_op jit(solution)/shard_map/transpose(jvp(bcn,cni->bic))/dot_general | solution.py:72
  2109.5 14.4 add_bitcast_fusion.2
  2142.8 14.5 add_bitcast_fusion
  2164.5 23.4 all_to_all.166
  2209.3 12.5 all-to-all-done.3
  2230.2 21.3 psum.39
  2261.9 37.1 %all-reduce.28 = (f32[2,768]{1,0:T(2,128)S(1)}, f32[2,768]{1,0:T(2,128)S(1)}) all-reduce(f32[2,768]{1,0:T(2,128)S(1)} %pad_maximum_fusion.6, f32[2,768]{1,0:T(2,128)S(1)} %pad_maximum_fusion.7), channel_id=1, replica_groups=mesh['dp'=8,'seq'=4] {'dp','seq'}, use_global_device_ids=true, to_apply=%region_22.25 | all-reduce | flops 3072 | bytes 24576 | tf_op jit(solution)/shard_map/psum | solution.py:227
  2301.5 56.8 %reduce-scatter.21.cloned.1.call-done = f32[48,768]{1,0:T(8,128)} async-done(((f32[1536,768]{1,0:T(8,128)}), f32[48,768]{1,0:T(8,128)}) %reduce-scatter.21.cloned.1.call-update) | async-done | bytes 147472 | tf_op jit(solution)/shard_map/reduce_scatter | solution.py:214
  2359.9 110.7 %reduce-scatter.11.cloned.1.call-done = f32[24,1536]{1,0:T(8,128)} async-done(((f32[768,1536]{1,0:T(8,128)}), f32[24,1536]{1,0:T(8,128)}) %reduce-scatter.11.cloned.1.call-update) | async-done | bytes 147472 | tf_op jit(solution)/shard_map/reduce_scatter | solution.py:211
  2470.6 111.6 %reduce-scatter.9.cloned.1.call-done = f32[24,1536]{1,0:T(8,128)} async-done(((f32[768,1536]{1,0:T(8,128)}), f32[24,1536]{1,0:T(8,128)}) %reduce-scatter.9.cloned.1.call-update) | async-done | bytes 147472 | tf_op jit(solution)/shard_map/reduce_scatter | solution.py:211
  2583.9 139.8 %reduce-scatter.19.cloned.1.call-done = f32[48,1536]{1,0:T(8,128)} async-done(((f32[1536,1536]{1,0:T(8,128)}), f32[48,1536]{1,0:T(8,128)}) %reduce-scatter.19.cloned.1.call-update) | async-done | bytes 294928 | tf_op jit(solution)/shard_map/reduce_scatter | solution.py:213
  2723.7 140.4 %reduce-scatter.17.cloned.1.call-done = f32[48,1536]{1,0:T(8,128)} async-done(((f32[1536,1536]{1,0:T(8,128)}), f32[48,1536]{1,0:T(8,128)}) %reduce-scatter.17.cloned.1.call-update) | async-done | bytes 294928 | tf_op jit(solution)/shard_map/reduce_scatter | solution.py:213
  2866.0 139.4 %reduce-scatter.15.cloned.1.call-done = f32[24,3072]{1,0:T(8,128)} async-done(((f32[768,3072]{1,0:T(8,128)}), f32[24,3072]{1,0:T(8,128)}) %reduce-scatter.15.cloned.1.call-update) | async-done | bytes 294928 | tf_op jit(solution)/shard_map/reduce_scatter | solution.py:212
  3005.3 140.3 %reduce-scatter.13.cloned.1.call-done = f32[24,3072]{1,0:T(8,128)} async-done(((f32[768,3072]{1,0:T(8,128)}), f32[24,3072]{1,0:T(8,128)}) %reduce-scatter.13.cloned.1.call-update) | async-done | bytes 294928 | tf_op jit(solution)/shard_map/reduce_scatter | solution.py:212
  (661 shorter events, 535.8 us)
Async XLA Ops:
  7.2 56.7 %copy-start.6 = (bf16[256,768]{1,0:T(8,128)(2,1)S(1)}, bf16[256,768]{1,0:T(8,128)(2,1)}, u32[]{:S(2)}) copy-start(bf16[256,768]{1,0:T(8,128)(2,1)} %param.16) | copy-start | bytes 1179652
  7.2 58.2 %copy-start.110 = (f32[2,2,384,64]{2,3,1,0:T(8,128)S(1)}, f32[2,2,384,64]{2,3,1,0:T(8,128)}, u32[]{:S(2)}) copy-start(f32[2,2,384,64]{2,3,1,0:T(8,128)} %param.25) | copy-start | bytes 1179652
  7.2 59.0 %copy-start.111 = (f32[2,2,384,64]{2,3,1,0:T(8,128)S(1)}, f32[2,2,384,64]{2,3,1,0:T(8,128)}, u32[]{:S(2)}) copy-start(f32[2,2,384,64]{2,3,1,0:T(8,128)} %param.26) | copy-start | bytes 1179652
  7.2 258.6 %all-gather.21.cloned.1.call-start = ((), (), s32[]{:S(2)}) async-start(), calls=%async_computation.26 | async-start | bytes 4866048 | tf_op jit(solution)/shard_map/all_gather | solution.py:174
  9.1 552.0 %all-gather.25.cloned.1.call-start = ((), (), s32[]{:S(2)}) async-start(), calls=%async_computation.28 | async-start | bytes 2433024 | tf_op jit(solution)/shard_map/all_gather | solution.py:173
  10.7 566.6 %all-gather.27.cloned.1.call-start = ((), (), s32[]{:S(2)}) async-start(), calls=%async_computation.29 | async-start | bytes 2433024 | tf_op jit(solution)/shard_map/all_gather | solution.py:176
  12.4 564.9 %all-gather.23.cloned.1.call-start = ((), (), s32[]{:S(2)}) async-start(), calls=%async_computation.27 | async-start | bytes 4866048 | tf_op jit(solution)/shard_map/all_gather | solution.py:175
  14.2 570.3 %all-gather.29.cloned.1.call-start = ((), (), s32[]{:S(2)}) async-start(), calls=%async_computation.30 | async-start | bytes 4866048 | tf_op jit(solution)/shard_map/all_gather | solution.py:174
  14.8 589.5 %all-gather.33.cloned.1.call-start = ((), (), s32[]{:S(2)}) async-start(), calls=%async_computation.32 | async-start | bytes 2433024 | tf_op jit(solution)/shard_map/all_gather | solution.py:173
  15.4 596.2 %all-gather.35.cloned.1.call-start = ((), (), s32[]{:S(2)}) async-start(), calls=%async_computation.33 | async-start | bytes 2433024 | tf_op jit(solution)/shard_map/all_gather | solution.py:176
  16.1 602.6 %all-gather.31.cloned.1.call-start = ((), (), s32[]{:S(2)}) async-start(), calls=%async_computation.31 | async-start | bytes 4866048 | tf_op jit(solution)/shard_map/all_gather | solution.py:175
  16.9 280.7 %copy-start.71 = (s32[16384]{0:T(1024)}, s32[16384]{0:T(1024)S(1)}, u32[]{:S(2)}) copy-start(s32[16384]{0:T(1024)S(1)} %broadcast_clamp_fusion) | copy-start | bytes 196612
  69.2 96.9 %copy-start.93 = (f32[384,64]{1,0:T(8,128)}, f32[384,64]{1,0:T(8,128)S(1)}, u32[]{:S(2)}) copy-start(f32[384,64]{1,0:T(8,128)S(1)} %get-tuple-element.164) | copy-start | bytes 294916
  69.2 96.9 %copy-start.120 = (f32[384,64]{1,0:T(8,128)}, f32[384,64]{1,0:T(8,128)S(1)}, u32[]{:S(2)}) copy-start(f32[384,64]{1,0:T(8,128)S(1)} %get-tuple-element.163) | copy-start | bytes 294916
  237.1 25.6 copy-start.179
  237.1 26.2 copy-start.112
  237.1 26.3 copy-start.113
  237.1 26.5 copy-start.90
  237.1 28.7 copy-start.7
  237.1 28.7 copy-start.108
  237.1 28.7 copy-start.114
  237.2 28.7 copy-start.141
  237.2 28.7 copy-start.145
  285.7 103.9 %all-to-all-start = ((bf16[256,2,1536]{0,1,2:T(2,128)(2,1)}), bf16[256,2,1536]{0,1,2:T(2,128)(2,1)S(1)}, u32[]{:S(2)}, u32[]{:S(2)}) async-start(bf16[256,2,1536]{0,1,2:T(2,128)(2,1)} %copy.397), calls=%async_computation | async-start | bytes 3145728 | tf_op jit(solution)/shard_map/all_to_all | solution.py:94
  360.6 27.1 copy-start.171
  389.0 865.0 %copy-start.83 = (pred[128,128]{1,0:T(8,128)(4,1)}, pred[128,128]{1,0:T(8,128)(4,1)S(1)}, u32[]{:S(2)}) copy-start(pred[128,128]{1,0:T(8,128)(4,1)S(1)} %get-tuple-element.186) | copy-start | bytes 49156
  394.2 160.1 %copy-start = (f32[1024,2,384]{2,0,1:T(8,128)}, f32[1024,2,384]{2,0,1:T(8,128)S(1)}, u32[]{:S(2)}) copy-start(f32[1024,2,384]{2,0,1:T(8,128)S(1)} %bitcast_convert_fusion.1) | copy-start | bytes 9437188
  557.4 15.3 all-to-all-start.1
  572.7 34.1 %all-to-all-start.9 = ((bf16[4,256,384]{1,2,0:T(8,128)(2,1)}), bf16[4,256,384]{1,2,0:T(8,128)(2,1)S(1)}, u32[]{:S(2)}, u32[]{:S(2)}) async-start(bf16[4,256,384]{1,2,0:T(8,128)(2,1)} %copy.468), calls=%async_computation.9 | async-start | bytes 1572864 | tf_op jit(solution)/shard_map/all_to_all | solution.py:98
  607.7 23.8 all-to-all-start.2
  631.5 107.7 %all-to-all-start.4 = ((bf16[256,4,384]{2,0,1:T(8,128)(2,1)}), bf16[256,4,384]{2,0,1:T(8,128)(2,1)}, u32[]{:S(2)}, u32[]{:S(2)}) async-start(bf16[256,4,384]{2,0,1:T(8,128)(2,1)} %bitcast.558), calls=%async_computation.4 | async-start | bytes 1572864 | tf_op jit(solution)/shard_map/all_to_all | solution.py:122
  915.2 26.2 copy-start.81
  915.2 26.2 copy-start.99
  915.2 26.2 copy-start.123
  959.8 44.4 %copy-start.72 = (s32[16384]{0:T(1024)S(1)}, s32[16384]{0:T(1024)}, u32[]{:S(2)}) copy-start(s32[16384]{0:T(1024)} %copy-done.71) | copy-start | bytes 196612
  1139.6 114.4 %copy-start.5 = (f32[8,128,384]{1,0,2:T(8,128)}, f32[8,128,384]{1,0,2:T(8,128)S(1)}, u32[]{:S(2)}) copy-start(f32[8,128,384]{1,0,2:T(8,128)S(1)} %copy.444) | copy-start | bytes 4718596
  1139.6 25.1 copy-start.33
  1183.6 110.7 %all-to-all-start.6 = ((bf16[4,256,384]{1,2,0:T(8,128)(2,1)}), bf16[4,256,384]{1,2,0:T(8,128)(2,1)}, u32[]{:S(2)}, u32[]{:S(2)}) async-start(bf16[4,256,384]{1,2,0:T(8,128)(2,1)} %copy.450), calls=%async_computation.6 | async-start | bytes 1572864 | tf_op jit(solution)/shard_map/all_to_all | solution.py:98
  1294.3 25.6 all-to-all-start.5
  1343.3 159.2 %all-to-all-start.7 = ((bf16[256,4,384]{2,0,1:T(8,128)(2,1)}), bf16[256,4,384]{2,0,1:T(8,128)(2,1)}, u32[]{:S(2)}, u32[]{:S(2)}) async-start(bf16[256,4,384]{2,0,1:T(8,128)(2,1)} %bitcast.557), calls=%async_computation.7 | async-start | bytes 1572864 | tf_op jit(solution)/shard_map/all_to_all | solution.py:122
  1347.5 904.6 %all-reduce.33.cloned.1.call-start = ((), (), s32[]{:S(2)}) async-start(), calls=%async_computation.34 | async-start | bytes 1572864 | tf_op jit(solution)/shard_map/psum | solution.py:223
  1348.5 129.6 %copy-start.136 = (f32[384,64]{0,1:T(8,128)S(1)}, f32[384,64]{0,1:T(8,128)}, u32[]{:S(2)}) copy-start(f32[384,64]{0,1:T(8,128)} %get-tuple-element.100) | copy-start | bytes 294916
  1509.6 39.1 %copy-start.3 = (f32[8,128,384]{1,0,2:T(8,128)}, f32[8,128,384]{1,0,2:T(8,128)S(1)}, u32[]{:S(2)}) copy-start(f32[8,128,384]{1,0,2:T(8,128)S(1)} %copy.462) | copy-start | bytes 4718596
  1548.7 25.6 copy-start.18
  1956.2 98.4 %copy-start.60 = (f32[1,1,384,64]{3,2,1,0:T(8,128)S(1)}, f32[1,1,384,64]{3,2,1,0:T(8,128)}, u32[]{:S(2)}) copy-start(f32[1,1,384,64]{3,2,1,0:T(8,128)} %copy-done.59) | copy-start | bytes 294916
  1956.2 98.4 %copy-start.62 = (f32[1,1,384,64]{3,2,1,0:T(8,128)S(1)}, f32[1,1,384,64]{3,2,1,0:T(8,128)}, u32[]{:S(2)}) copy-start(f32[1,1,384,64]{3,2,1,0:T(8,128)} %copy-done.61) | copy-start | bytes 294916
  1956.2 98.4 %copy-start.105 = (f32[384,64]{1,0:T(8,128)S(1)}, f32[384,64]{1,0:T(8,128)}, u32[]{:S(2)}) copy-start(f32[384,64]{1,0:T(8,128)} %copy.481) | copy-start | bytes 294916
  1956.2 98.4 %copy-start.131 = (f32[384,64]{1,0:T(8,128)S(1)}, f32[384,64]{1,0:T(8,128)}, u32[]{:S(2)}) copy-start(f32[384,64]{1,0:T(8,128)} %multiply_reduce_fusion.10) | copy-start | bytes 294916
  1956.2 98.5 %copy-start.64 = (f32[1,1,384,64]{3,2,1,0:T(8,128)S(1)}, f32[1,1,384,64]{3,2,1,0:T(8,128)}, u32[]{:S(2)}) copy-start(f32[1,1,384,64]{3,2,1,0:T(8,128)} %copy-done.63) | copy-start | bytes 294916
  1956.2 98.5 %copy-start.66 = (f32[1,1,384,64]{3,2,1,0:T(8,128)S(1)}, f32[1,1,384,64]{3,2,1,0:T(8,128)}, u32[]{:S(2)}) copy-start(f32[1,1,384,64]{3,2,1,0:T(8,128)} %copy-done.65) | copy-start | bytes 294916
  1956.2 98.5 %copy-start.104 = (f32[384,64]{1,0:T(8,128)S(1)}, f32[384,64]{1,0:T(8,128)}, u32[]{:S(2)}) copy-start(f32[384,64]{1,0:T(8,128)} %copy.485) | copy-start | bytes 294916
  1956.2 98.5 %copy-start.130 = (f32[384,64]{1,0:T(8,128)S(1)}, f32[384,64]{1,0:T(8,128)}, u32[]{:S(2)}) copy-start(f32[384,64]{1,0:T(8,128)} %multiply_reduce_fusion.7) | copy-start | bytes 294916
  2057.7 243.7 %reduce-scatter.23.cloned.1.call-start = ((), (), s32[]{:S(2)}) async-start(), calls=%async_computation.25 | async-start | bytes 4866048 | tf_op jit(solution)/shard_map/reduce_scatter | solution.py:214
  2062.9 295.3 %reduce-scatter.21.cloned.1.call-start = ((), (), s32[]{:S(2)}) async-start(), calls=%async_computation.24 | async-start | bytes 4866048 | tf_op jit(solution)/shard_map/reduce_scatter | solution.py:214
  2069.6 401.0 %reduce-scatter.11.cloned.1.call-start = ((), (), s32[]{:S(2)}) async-start(), calls=%async_computation.19 | async-start | bytes 4866048 | tf_op jit(solution)/shard_map/reduce_scatter | solution.py:211
  2073.9 508.3 %reduce-scatter.9.cloned.1.call-start = ((), (), s32[]{:S(2)}) async-start(), calls=%async_computation.18 | async-start | bytes 4866048 | tf_op jit(solution)/shard_map/reduce_scatter | solution.py:211
  2078.4 645.3 %reduce-scatter.19.cloned.1.call-start = ((), (), s32[]{:S(2)}) async-start(), calls=%async_computation.23 | async-start | bytes 9732096 | tf_op jit(solution)/shard_map/reduce_scatter | solution.py:213
  2085.7 778.4 %reduce-scatter.17.cloned.1.call-start = ((), (), s32[]{:S(2)}) async-start(), calls=%async_computation.22 | async-start | bytes 9732096 | tf_op jit(solution)/shard_map/reduce_scatter | solution.py:213
  2092.9 912.4 %reduce-scatter.15.cloned.1.call-start = ((), (), s32[]{:S(2)}) async-start(), calls=%async_computation.21 | async-start | bytes 9732096 | tf_op jit(solution)/shard_map/reduce_scatter | solution.py:212
  2099.4 1046.3 %reduce-scatter.13.cloned.1.call-start = ((), (), s32[]{:S(2)}) async-start(), calls=%async_computation.20 | async-start | bytes 9732096 | tf_op jit(solution)/shard_map/reduce_scatter | solution.py:212
  2204.4 17.4 all-to-all-start.3
  2260.4 39.8 %copy-start.37 = (f32[256,768]{1,0:T(8,128)S(1)}, f32[256,768]{1,0:T(8,128)}, u32[]{:S(2)}) copy-start(f32[256,768]{1,0:T(8,128)} %copy-done.36) | copy-start | bytes 2359300
  2260.4 39.8 %copy-start.51 = (bf16[256,768]{1,0:T(8,128)(2,1)S(1)}, bf16[256,768]{1,0:T(8,128)(2,1)}, u32[]{:S(2)}) copy-start(bf16[256,768]{1,0:T(8,128)(2,1)} %param.18) | copy-start | bytes 1179652
  2260.4 39.8 %copy-start.167 = (f32[256]{0:T(256)S(1)}, f32[256]{0:T(256)}, u32[]{:S(2)}) copy-start(f32[256]{0:T(256)} %copy-done.166) | copy-start | bytes 3076
  (150 other events, 1250.6 us)
Sparse Core Ops, SparseCore 0:
  11.5 66.9 all-gather.20
  81.4 55.4 all-gather.24
  139.9 56.1 all-gather.26
  198.8 62.4 all-gather.22
  264.1 65.1 all-gather.28
  332.0 56.0 all-gather.32
  391.0 56.1 all-gather.34
  450.0 62.5 all-gather.30
  2057.8 76.3 all-reduce.32
  2140.5 106.0 reduce-scatter.22
  2252.1 106.0 reduce-scatter.20
  2364.4 106.1 reduce-scatter.10
  2476.1 106.0 reduce-scatter.8
  2588.9 134.7 reduce-scatter.18
  2729.4 134.6 reduce-scatter.16
  2870.8 134.4 reduce-scatter.14
  3011.1 134.5 reduce-scatter.12
where the time goes:
time: 3180 us; the launch traced here: 3150 us
  waiting for transfers between devices  861 us (27%)
  matrix products  857 us (27%)
  local copies, waits for them, and re-layouts  729 us (23%)
  other arithmetic  531 us (17%)
  blocking collectives  124 us (4%)
  starting transfers between devices  36 us (1%)
    scatter-add x4, other arithmetic, prepare_tables(): toeplitz = jnp.take(lag_kernel, lag_index, axis=1) * lower_mask  417 us
    dot_general x12, matrix products, causal_mix(): outside = jnp.einsum('bcn,cni->bic', earlier, head_terms, precision=PRECISE)  365 us
    gather x8, local copies, waits for them, and re-layouts, prepare_tables(): toeplitz = jnp.take(lag_kernel, lag_index, axis=1) * lower_mask  352 us
    reduce_scatter x2, waiting for transfers between devices, shards(): lax.psum_scatter(weight_terms[2], ('dp', 'seq'), scatter_dimension=0, til...  280 us
    reduce_scatter x2, waiting for transfers between devices, shards(): lax.psum_scatter(weight_terms[1], ('dp', 'seq'), scatter_dimension=0, til...  280 us
    dot_general x12, matrix products, causal_mix(): inside = jnp.einsum('cij,bjc->bic', toeplitz, pieces, precision=SPLIT_THREE)  223 us
    reduce_scatter x2, waiting for transfers between devices, shards(): lax.psum_scatter(weight_terms[0], ('dp', 'seq'), scatter_dimension=0, til...  222 us
    dot_general x12, matrix products, causal_mix(): jnp.einsum('bjc,cnj->bcn', pieces, tail_terms, precision=SPLIT_THREE)  145 us
  transfers between devices with their start and end apart: 26, of which 10 were waited for; matrix products, arithmetic and copies ran while one was open for 34% of the time, Pallas kernels for 0%

commit v1 on v0

v1 whole, which is shorter than its diff:
```python
import numpy as np

import jax
import jax.numpy as jnp
from jax import lax
from jax.sharding import PartitionSpec as P

EPSILON = 1e-05
BF = jnp.bfloat16
F32 = jnp.float32
LAG_BLOCK = 128


def dot(left, right, left_dim, right_dim):
    return lax.dot_general(
        left, right, (((left_dim,), (right_dim,)), ((), ())), preferred_element_type=F32
    )


def wave_table(length):
    turns = 4 * length
    step = np.arange(length, dtype=np.int64)
    phase = ((2 * step[:, None] + 1) * step[None, :]) % turns
    angle = phase * (2.0 * np.pi / turns)
    return np.concatenate([np.cos(angle), np.sin(angle)], 0).astype(jnp.bfloat16)


def seq_pairs(count, bit):
    return [(i, i ^ bit) for i in range(count)]


def seq_gather(block, count):
    blocks = {0: block}
    bit = count // 2
    while bit:
        for member in list(blocks):
            blocks[member ^ bit] = lax.ppermute(blocks[member], "seq", seq_pairs(count, bit))
        bit //= 2
    return [blocks[m] for m in range(count)]


def seq_reduce(blocks, count):
    blocks = dict(enumerate(blocks))
    bit = 1
    while bit < count:
        for member in sorted(blocks, reverse=True):
            if member & bit:
                sent = blocks.pop(member).astype(BF)
                came = lax.ppermute(sent, "seq", seq_pairs(count, bit))
                blocks[member ^ bit] = blocks[member ^ bit] + came.astype(F32)
        bit *= 2
    return blocks[0]


def gelu_parts(pre):
    share = 0.5 * (1.0 + lax.erf(pre * np.float32(np.sqrt(0.5))))
    slope = share + pre * (jnp.exp(-0.5 * pre * pre) * np.float32(1.0 / np.sqrt(2.0 * np.pi)))
    return pre * share, slope


def normalize(stream):
    centre = jnp.mean(stream, axis=-1, keepdims=True)
    centred = stream - centre
    spread = jnp.mean(centred * centred, axis=-1, keepdims=True)
    factor = lax.rsqrt(spread + EPSILON)
    return centred * factor, factor


def lag_factors(rates, length):
    block = min(LAG_BLOCK, length)
    far = jnp.exp(-rates[:, None, :] * (block * jnp.arange(length // block, dtype=F32))[None, :, None])
    near = jnp.exp(-rates[:, None, :] * jnp.arange(block, dtype=F32)[None, :, None])
    return far, near


def lag_kernels(coef, rates, length):
    far, near = lag_factors(rates, length)
    left = ((coef * rates)[:, None, :] * far).astype(BF)
    kern = lax.dot_general(
        left, near.astype(BF), (((2,), (2,)), ((0,), (0,))), preferred_element_type=F32
    )
    return kern.reshape(coef.shape[0], length)


def lag_grads(coef, rates, kern_grad, length):
    far, near = lag_factors(rates, length)
    block = near.shape[1]
    lags = jnp.arange(block, dtype=F32)[None, :, None]
    pair = jnp.concatenate([near, near * lags], axis=2).astype(BF)
    pieces = kern_grad.reshape(rates.shape[0], length // block, block).astype(BF)
    sums = lax.dot_general(pieces, pair, (((2,), (1,)), ((0,), (0,))), preferred_element_type=F32)
    states = rates.shape[1]
    plain = sums[:, :, :states]
    starts = (block * jnp.arange(length // block, dtype=F32))[None, :, None]
    total = jnp.sum(far * plain, axis=1)
    moment = jnp.sum(far * (starts * plain + sums[:, :, states:]), axis=1)
    return rates * total, coef * (total - rates * moment)


def spectrum_of(waves, series):
    both = dot(waves, series, 1, 0)
    half = both.shape[0] // 2
    return both[:half], both[half:]


def series_of(waves, cos_part, sin_part):
    half = cos_part.shape[0]
    both = jnp.concatenate([cos_part, sin_part], 0).astype(BF)
    return dot(waves, both, 0, 0) * (1.0 / half)


def run_layer(stream, keep, weights, kernel_hat, skip, waves, count):
    w_gate, w_value, w_mix, w_out, gain, bias = weights
    xhat, factor = normalize(stream)
    normed_own = (xhat * gain + bias).astype(BF)
    normed = jnp.concatenate(seq_gather(normed_own, count), 0)
    gate_act, gate_slope = gelu_parts(dot(normed, w_gate, 1, 0))
    value_act, value_slope = gelu_parts(dot(normed, w_value, 1, 0))
    values = (value_act * keep).astype(BF)
    value_slope = (value_slope * keep).astype(BF)
    x_cos, x_sin = spectrum_of(waves, values)
    k_cos, k_sin = kernel_hat
    mixes = series_of(waves, k_cos * x_cos - k_sin * x_sin, k_cos * x_sin + k_sin * x_cos)
    mixes = mixes + skip * values.astype(F32)
    width = mixes.shape[1] // 2
    product = (mixes[:, :width] * mixes[:, width:]).astype(BF)
    rows = stream.shape[0]
    products = []
    for member, came in enumerate(seq_gather(product, count)):
        pieces = came.reshape(count, rows, width)
        products.append(jnp.concatenate([pieces[m ^ member] for m in range(count)], 0))
    update = dot(products[0], w_mix[0], 1, 0)
    for member in range(1, count):
        update = update + dot(products[member], w_mix[member], 1, 0)
    mixed = (update * gate_act).astype(BF)
    partial = dot(mixed, w_out, 1, 0)
    result = stream + seq_reduce(
        [partial[m * rows : (m + 1) * rows] for m in range(count)], count
    )
    saved = (
        xhat,
        factor,
        normed,
        gate_act.astype(BF),
        (update * gate_slope).astype(BF),
        value_slope,
        values,
        (x_cos.astype(BF), x_sin.astype(BF)),
        mixes.astype(BF),
        products,
        mixed,
    )
    return result, saved


def back_layer(grad_stream, saved, weights, kernel_hat, skip, waves, count):
    w_gate, w_value, w_mix, w_out, gain, bias = weights
    xhat, factor, normed, gate_act, gate_back, value_slope, values, x_hat, mixes, products, mixed = saved
    rows = grad_stream.shape[0]
    out_low = jnp.concatenate(seq_gather(grad_stream.astype(BF), count), 0)
    grad_mixed = dot(out_low, w_out, 1, 1)
    grad_out = dot(mixed, out_low, 0, 0)
    update_low = (grad_mixed * gate_act.astype(F32)).astype(BF)
    gate_grad = (grad_mixed * gate_back.astype(F32)).astype(BF)
    width = products[0].shape[1]
    partials = []
    for member in range(count):
        part = dot(update_low, w_mix[member], 1, 1).reshape(count, rows, width)
        partials.append(jnp.concatenate([part[m ^ member] for m in range(count)], 0))
    product_low = seq_reduce(partials, count).astype(BF).astype(F32)
    grad_mix = [dot(products[member], update_low, 0, 0) for member in range(count)]
    mixes = mixes.astype(F32)
    back = jnp.concatenate([product_low * mixes[:, width:], product_low * mixes[:, :width]], 1)
    back_low = back.astype(BF)
    g_cos, g_sin = spectrum_of(waves, back_low)
    k_cos, k_sin = kernel_hat
    grad_values = series_of(waves, k_cos * g_cos + k_sin * g_sin, k_cos * g_sin - k_sin * g_cos)
    grad_values = grad_values + skip * back
    x_cos, x_sin = x_hat
    x_cos = x_cos.astype(F32)
    x_sin = x_sin.astype(F32)
    kern_hat = (g_cos * x_cos + g_sin * x_sin, g_sin * x_cos - g_cos * x_sin)
    grad_skip = jnp.sum(back * values.astype(F32), axis=0)
    value_grad = (grad_values.astype(BF).astype(F32) * value_slope.astype(F32)).astype(BF)
    grad_value = dot(normed, value_grad, 0, 0)
    grad_gate = dot(normed, gate_grad, 0, 0)
    partial = dot(value_grad, w_value, 1, 1) + dot(gate_grad, w_gate, 1, 1)
    grad_normed = seq_reduce([partial[m * rows : (m + 1) * rows] for m in range(count)], count)
    norm_terms = jnp.stack([jnp.sum(grad_normed * xhat, 0), jnp.sum(grad_normed, 0)])
    inner = grad_normed * gain
    slope = jnp.mean(inner, axis=-1, keepdims=True)
    tilt = jnp.mean(inner * xhat, axis=-1, keepdims=True)
    grad_stream = grad_stream + (inner - slope - xhat * tilt) * factor
    return grad_stream, (grad_gate, grad_value, grad_mix, grad_out), norm_terms, kern_hat, grad_skip


def shards(tokens, lengths, cotangent, w_gate, w_value, w_mix, w_out, ln_gain, ln_bias, ssm_coef, ssm_rate, ssm_skip):
    dp = lax.axis_size("dp")
    count = lax.axis_size("seq")
    me = lax.axis_index("seq")
    rows, model = tokens.shape
    length = rows * count
    depth, in_rows, gate_width = w_gate.shape
    mix_rows = w_mix.shape[1]
    width = ssm_coef.shape[2]
    states = ssm_coef.shape[3]
    share = gate_width // (dp * count)

    waves_flat = jnp.asarray(wave_table(length))
    order = me ^ jnp.arange(count, dtype=jnp.int32)
    waves = jnp.take(waves_flat.reshape(2 * length, count, rows), order, axis=1).reshape(2 * length, length)
    positions = (order[:, None] * rows + jnp.arange(rows, dtype=jnp.int32)[None, :]).reshape(length)
    keep = (positions < lengths[0]).astype(F32)[:, None]

    def by_column(weight):
        cut = weight.reshape(depth, weight.shape[1], dp, count, share)
        return cut.transpose(3, 0, 1, 2, 4).reshape(count, depth, weight.shape[1], width)

    sent_value = w_value.reshape(depth, in_rows, 2, count, width).transpose(3, 0, 2, 1, 4)
    sent_value = sent_value.reshape(count, depth, 2 * in_rows, width)
    norm_rows = jnp.stack([ln_gain, ln_bias], 1).reshape(2 * depth, in_rows)
    sent = jnp.concatenate([by_column(w_gate), sent_value, by_column(w_mix)], 2)
    sent = sent.reshape(count, depth * (3 * in_rows + mix_rows), width)
    norm_pad = jnp.pad(norm_rows, ((0, 16 - 2 * depth), (0, width - in_rows)))
    sent = jnp.concatenate([sent, jnp.broadcast_to(norm_pad, (count,) + norm_pad.shape)], 1)
    came = lax.all_to_all(sent, "seq", 0, 0, tiled=True)
    norm_came = came[:, depth * (3 * in_rows + mix_rows) :]
    came = came[:, : depth * (3 * in_rows + mix_rows)].reshape(count, depth, 3 * in_rows + mix_rows, width)

    def gather_dp(block):
        return lax.all_gather(block, "dp", axis=0)

    def early_block(layer):
        block = came[:, layer, : 3 * in_rows].reshape(count, 3, in_rows, width)
        return block.transpose(1, 0, 2, 3).reshape(3 * count * in_rows, width)

    def late_block(layer):
        mix = came[:, layer, 3 * in_rows :].reshape(count * mix_rows, width)
        out = w_out[layer].reshape(mix_rows, model // width, width).transpose(1, 0, 2).reshape(-1, width)
        return jnp.concatenate([mix, out], 0)

    got_norm = None
    weights = []
    for layer in range(depth):
        early = early_block(layer)
        late = late_block(layer)
        n_early = early.shape[0]
        n_mix = count * mix_rows
        if layer == 0:
            early = jnp.concatenate([early, norm_came.reshape(count * 16, width)], 0)
            got = gather_dp(early)
            got_norm = got[:, n_early:].reshape(dp, count, 16, width)[:, :, : 2 * depth, :in_rows]
            got_norm = got_norm.transpose(2, 0, 1, 3).reshape(depth, 2, model).astype(F32)
            got_early = got[:, :n_early]
            got_late = gather_dp(late)
        else:
            got = gather_dp(jnp.concatenate([early, late], 0))
            got_early = got[:, :n_early]
            got_late = got[:, n_early:]
        got_early = got_early.reshape(dp, 3, count * in_rows, width)
        gate = got_early[:, 0].reshape(model, width)
        value = jnp.concatenate(
            [got_early[:, 1].reshape(model, width), got_early[:, 2].reshape(model, width)], 1
        )
        mix = got_late[:, :n_mix].reshape(count, width, width)
        mix = [lax.dynamic_index_in_dim(mix, order[m], 0, keepdims=False) for m in range(count)]
        out = got_late[:, n_mix:].reshape(dp, model // width, mix_rows, width)
        out = out.transpose(0, 2, 1, 3).reshape(dp * mix_rows, model)
        weights.append((gate, value, mix, out, got_norm[layer, 0], got_norm[layer, 1]))

    sign = jnp.concatenate([jnp.ones((width,), F32), -jnp.ones((width,), F32)])
    hats = []
    for layer in range(depth):
        kern = lag_kernels(
            ssm_coef[layer].reshape(2 * width, states), ssm_rate[layer].reshape(2 * width, states), length
        )
        both = dot(waves_flat, kern.astype(BF), 1, 1)
        hats.append((both[:length], both[length:] * sign))
    skips = ssm_skip.reshape(depth, 2 * width)

    stream = tokens.astype(F32)
    kept = []
    for layer in range(depth):
        stream, saved = run_layer(stream, keep, weights[layer], hats[layer], skips[layer], waves, count)
        kept.append(saved)

    grad_stream = cotangent.astype(F32)
    norm_grads = [None] * depth
    ssm_grads = [None] * depth
    shares = [None] * depth
    for layer in reversed(range(depth)):
        grad_stream, terms, norm_terms, kern_hat, grad_skip = back_layer(
            grad_stream, kept[layer], weights[layer], hats[layer], skips[layer], waves, count
        )
        norm_grads[layer] = norm_terms
        both = jnp.concatenate([kern_hat[0], kern_hat[1] * sign], 0).astype(BF)
        kern_grad = dot(both, waves_flat, 0, 0) * (1.0 / length)
        coef_grad, rate_grad = lag_grads(
            ssm_coef[layer].reshape(2 * width, states),
            ssm_rate[layer].reshape(2 * width, states),
            kern_grad,
            length,
        )
        ssm_grads[layer] = (coef_grad, rate_grad, grad_skip)
        grad_gate, grad_value, grad_mix, grad_out = terms
        out_rows = grad_out.astype(BF).reshape(dp, mix_rows, model // width, width).transpose(0, 2, 1, 3)
        mix_blocks = jnp.stack(grad_mix).astype(BF)
        mix_rows_all = jnp.take(mix_blocks, order, axis=0).reshape(dp, count * mix_rows, width)
        late = jnp.concatenate([mix_rows_all, out_rows.reshape(dp, -1, width)], 1)
        early = jnp.concatenate(
            [
                grad_gate.astype(BF).reshape(dp, 1, count * in_rows, width),
                grad_value.astype(BF).reshape(dp, count * in_rows, 2, width).transpose(0, 2, 1, 3),
            ],
            1,
        ).reshape(dp, 3 * count * in_rows, width)
        late = lax.psum_scatter(late, "dp", scatter_dimension=0, tiled=False)
        early = lax.psum_scatter(early, "dp", scatter_dimension=0, tiled=False)
        share_out = late[count * mix_rows :].reshape(model // width, mix_rows, width).transpose(1, 0, 2)
        share_out = share_out.reshape(mix_rows, model).astype(F32)
        back_mix = late[: count * mix_rows].reshape(count, mix_rows, width)
        back_early = early.reshape(3, count, in_rows, width).transpose(1, 0, 2, 3).reshape(count, 3 * in_rows, width)
        back = lax.all_to_all(jnp.concatenate([back_early, back_mix], 1), "seq", 0, 0, tiled=True)

        def columns(block, block_rows):
            cut = block.reshape(count, block_rows, dp, share).transpose(1, 2, 0, 3)
            return cut.reshape(block_rows, gate_width).astype(F32)

        share_gate = columns(back[:, :in_rows], in_rows)
        share_value = back[:, in_rows : 3 * in_rows].reshape(count, 2, in_rows, width).transpose(2, 1, 0, 3)
        share_value = share_value.reshape(in_rows, 2 * count * width).astype(F32)
        share_mix = columns(back[:, 3 * in_rows :], mix_rows)
        shares[layer] = (share_gate, share_value, share_mix, share_out)

    norm_all = jnp.stack(norm_grads).reshape(2 * depth, dp * count, in_rows).transpose(1, 0, 2)
    norm_sum = jnp.sum(
        lax.all_to_all(norm_all.reshape(dp * count, 2 * depth * in_rows), ("dp", "seq"), 0, 0, tiled=True), 0
    ).reshape(depth, 2, in_rows)
    coef_sum = lax.psum(jnp.stack([g[0] for g in ssm_grads]).astype(BF), "dp").astype(F32)
    rate_sum = lax.psum(jnp.stack([g[1] for g in ssm_grads]).astype(BF), "dp").astype(F32)
    skip_sum = lax.psum(jnp.stack([g[2] for g in ssm_grads]).astype(BF), "dp").astype(F32)
    stacked = [jnp.stack([shares[layer][member] for layer in range(depth)]) for member in range(4)]
    return (
        stream,
        grad_stream,
        stacked[0],
        stacked[1],
        stacked[2],
        stacked[3],
        norm_sum[:, 0],
        norm_sum[:, 1],
        coef_sum.reshape(ssm_coef.shape),
        rate_sum.reshape(ssm_rate.shape),
        skip_sum.reshape(ssm_skip.shape),
    )


def solution(mesh):
    in_specs = (
        P(("dp", "seq"), None),
        P("dp"),
        P(("dp", "seq"), None),
        P(None, ("dp", "seq"), None),
        P(None, ("dp", "seq"), None),
        P(None, ("dp", "seq"), None),
        P(None, ("dp", "seq"), None),
        P(None, ("dp", "seq")),
        P(None, ("dp", "seq")),
        P(None, None, "seq", None),
        P(None, None, "seq", None),
        P(None, None, "seq"),
    )
    out_specs = (
        P(("dp", "seq"), None),
        P(("dp", "seq"), None),
        P(None, ("dp", "seq"), None),
        P(None, ("dp", "seq"), None),
        P(None, ("dp", "seq"), None),
        P(None, ("dp", "seq"), None),
        P(None, ("dp", "seq")),
        P(None, ("dp", "seq")),
        P(None, None, "seq", None),
        P(None, None, "seq", None),
        P(None, None, "seq"),
    )
    return jax.shard_map(shards, mesh=mesh, in_specs=in_specs, out_specs=out_specs, check_vma=False)
```

time: 3180 us -> 763 us (0.24)
  matrix products: 857 us -> 206 us
  local copies, waits for them, and re-layouts: 729 us -> 81.4 us
  waiting for transfers between devices: 861 us -> 265 us
  other arithmetic: 531 us -> 118 us
  blocking collectives: 124 us -> 20.3 us
    reduce_scatter x8 -> x4, waiting for transfers between devices: 839 us -> 180 us  [the longest x2 113 us: shards(): late = lax.psum_scatter(late, 'dp', scatter_dimension=0, tiled=False)]
    dot_general x60, matrix products: 857 us -> 206 us  [the longest x56 137 us: dot(): lax.dot_general(left, right, (((left_dim,), (right_dim,)), ((), ())), pre...]
    scatter-add x4 -> x0, other arithmetic: 417 us -> none  [prepare_tables(): toeplitz = jnp.take(lag_kernel, lag_index, axis=1) * lower_mask]
    gather x8 -> x3, local copies, waits for them, and re-layouts: 352 us -> 9.86 us  [the longest x1 5 us: shards(): jnp.take(waves_flat.reshape(2 * length, count, rows), order, axis=1)]
    mul x4, local copies, waits for them, and re-layouts: 99.3 us -> 0.94 us  [the longest x2 0.61 us: run_layer(): mixes = mixes + skip * values.astype(F32)]
    rev x8 -> x0, local copies, waits for them, and re-layouts: 92.8 us -> none  [the longest x4 46.5 us: ssm_local(): jnp.flip(causal_mix(jnp.flip(behind, 0), tables[1]), 0)]
    ppermute x0 -> x36, waiting for transfers between devices: none -> 47 us  [the longest x18 25.5 us: seq_gather(): lax.ppermute(blocks[member], 'seq', seq_pairs(count, bit))]
    reshape x26 -> x18, local copies, waits for them, and re-layouts: 54.6 us -> 9.42 us  [the longest x4 2.26 us: by_column(): cut = weight.reshape(depth, weight.shape[1], dp, count, share)]
  transfers between devices with their start and end apart: 26 -> 48, of which waited for: 10 -> 17; matrix products, arithmetic and copies ran while one was open for 34% -> 49% of each run, Pallas kernels for 0% -> 0%
where the time goes in v1:
time: 763 us; the launch traced here: 753 us
  waiting for transfers between devices  265 us (35%)
  matrix products  206 us (27%)
  other arithmetic  118 us (15%)
  local copies, waits for them, and re-layouts  81.4 us (11%)
  starting transfers between devices  36.9 us (5%)
  between operations  25.6 us (3%)
  blocking collectives  20.3 us (3%)
    dot_general x56, matrix products, dot(): lax.dot_general(left, right, (((left_dim,), (right_dim,)), ((), ())), pre...  137 us
    reduce_scatter x2, waiting for transfers between devices, shards(): late = lax.psum_scatter(late, 'dp', scatter_dimension=0, tiled=False)  113 us
    reduce_scatter x2, waiting for transfers between devices, shards(): early = lax.psum_scatter(early, 'dp', scatter_dimension=0, tiled=False)  66.4 us
    convert_element_type x2, other arithmetic, lag_kernels(): near.astype(BF)  42.3 us
    dot_general x2, matrix products, lag_grads(): lax.dot_general(pieces, pair, (((2,), (1,)), ((0,), (0,))), preferred_ele...  42.2 us
    unnamed x328, local copies, waits for them, and re-layouts  27.9 us
    dot_general x2, matrix products, lag_kernels(): lax.dot_general(left, near.astype(BF), (((2,), (2,)), ((0,), (0,))), pref...  27.5 us
    ppermute x18, waiting for transfers between devices, seq_gather(): lax.ppermute(blocks[member], 'seq', seq_pairs(count, bit))  25.5 us
  transfers between devices with their start and end apart: 48, of which 17 were waited for; matrix products, arithmetic and copies ran while one was open for 49% of the time, Pallas kernels for 0%

profile of v1, /device:TPU:0, one launch (start us, length us, event | category | flops | bytes accessed | tf_op | source)
XLA Modules:
  0.0 753.2 jit_solution(7074565260848594589)
XLA Ops:
  7.7 2.6 collective-permute-start.19
  16.4 3.6 all-to-all-start
  21.9 14.2 %fusion.75 = bf16[768,8,128]{2,1,0:T(8,128)(2,1)} fusion(f32[768,64]{1,0:T(8,128)S(1)} %bitcast.341, f32[8]{0:T(128)S(1)} %iota_multiply_fusion, f32[768,64]{1,0:T(8,128)S(1)} %bitcast.409), kind=kOutput, calls=%fused_computation.131 | convolution fusion | flops 115212288 | bytes 1966112 | tf_op jit(solution)/shard_map/dot_general | solution.py:79
  39.6 5.0 gather_fusion
  44.6 4.8 bitcast_select_fusion
  49.5 5.3 fusion.103
  54.8 21.1 %fusion.1 = (bf16[768,128,64]{2,1,0:T(8,128)(2,1)}, bf16[768,128,64]{2,1,0:T(8,128)(2,1)}) fusion(f32[768,64]{1,0:T(8,128)S(1)} %bitcast.342), kind=kLoop, calls=%fused_computation.8 | loop fusion | flops 25165824 | bytes 25362432 | tf_op jit(solution)/shard_map/convert_element_type | solution.py:80
  75.9 14.3 %all-gather.7.cloned.1.call-done = bf16[2816,384]{1,0:T(8,128)(2,1)} async-done(((bf16[352,384]{1,0:T(8,128)(2,1)}), bf16[2816,384]{1,0:T(8,128)(2,1)}) %all-gather.7.cloned.1.call-update) | async-done | bytes 2162704 | tf_op jit(solution)/shard_map/all_gather | solution.py:231
  94.0 7.6 %collective-permute-done.1 = bf16[256,768]{1,0:T(8,128)(2,1)} collective-permute-done((bf16[256,768]{1,0:T(8,128)(2,1)S(1)}, bf16[256,768]{1,0:T(8,128)(2,1)}, u32[]{:S(2)}, u32[]{:S(2)}) %collective-permute-start.1) | collective-permute-done | bytes 393248 | tf_op jit(solution)/shard_map/ppermute | solution.py:37
  104.4 5.4 multiply_convert_fusion.6
  110.9 3.7 fusion.293
  114.6 2.8 subtract_convert_fusion.3
  117.7 6.5 convert_convert_fusion
  138.1 10.1 %all-gather.9.cloned.1.call-done = bf16[2304,384]{1,0:T(8,128)(2,1)} async-done(((bf16[288,384]{1,0:T(8,128)(2,1)}), bf16[2304,384]{1,0:T(8,128)(2,1)}) %all-gather.9.cloned.1.call-update) | async-done | bytes 1769488 | tf_op jit(solution)/shard_map/all_gather | solution.py:231
  157.2 3.4 multiply_convert_fusion.15
  160.7 2.6 fusion.289
  163.6 21.2 %fusion = (bf16[768,128,64]{2,1,0:T(8,128)(2,1)}, bf16[768,128,64]{2,1,0:T(8,128)(2,1)}) fusion(f32[768,64]{1,0:T(8,128)S(1)} %bitcast.344), kind=kLoop, calls=%fused_computation.6 | loop fusion | flops 25165824 | bytes 25362432 | tf_op jit(solution)/shard_map/convert_element_type | solution.py:80
  188.1 13.3 %fusion.72 = bf16[768,8,128]{2,1,0:T(8,128)(2,1)S(1)} fusion(f32[768,64]{1,0:T(8,128)S(1)} %bitcast.345, f32[768,64]{1,0:T(8,128)S(1)} %bitcast.408, f32[8]{0:T(128)S(1)} %copy-done.127), kind=kOutput, calls=%fused_computation.130 | convolution fusion | flops 115212288 | bytes 1966112 | tf_op jit(solution)/shard_map/dot_general | solution.py:79
  204.8 5.7 fusion.100
  218.7 5.5 multiply_convert_fusion.4
  225.3 3.7 fusion.294
  229.1 2.8 subtract_convert_fusion.2
  232.1 6.4 convert_convert_fusion.1
  245.0 13.6 %collective-permute-done.13 = bf16[1024,384]{1,0:T(8,128)(2,1)S(1)} collective-permute-done((bf16[1024,384]{1,0:T(8,128)(2,1)S(1)}, bf16[1024,384]{1,0:T(8,128)(2,1)S(1)}, u32[]{:S(2)}, u32[]{:S(2)}) %collective-permute-start.13) | collective-permute-done | bytes 786464 | tf_op jit(solution)/shard_map/ppermute | solution.py:37
  261.7 2.6 multiply_convert_fusion.12
  271.4 2.6 fusion.291
  287.1 3.6 convolution_convert_fusion.7
  292.7 7.7 %collective-permute-done.23 = bf16[1024,384]{1,0:T(8,128)(2,1)} collective-permute-done((bf16[1024,384]{1,0:T(8,128)(2,1)}, bf16[1024,384]{1,0:T(8,128)(2,1)}, u32[]{:S(2)}, u32[]{:S(2)}) %collective-permute-start.23) | collective-permute-done | bytes 786464 | tf_op jit(solution)/shard_map/ppermute | solution.py:49
  303.0 3.7 fusion.78
  309.4 6.8 multiply_convert_fusion.3
  317.7 2.6 fusion.290
  321.7 2.6 convolution_convert_fusion
  331.2 7.4 fusion.95
  338.6 2.6 collective-permute-done.26
  341.3 2.2 multiply_reduce_fusion.2
  343.5 3.0 fusion.260
  348.0 5.5 fusion.125
  354.0 3.4 collective-permute-done.28
  357.4 21.5 %fusion.6 = f32[768,8,128]{2,1,0:T(8,128)S(1)} fusion(bf16[768,8,128]{2,1,0:T(8,128)(2,1)S(1)} %bitcast.374, bf16[768,128,64]{2,1,0:T(8,128)(2,1)} %get-tuple-element.171, bf16[768,128,64]{2,1,0:T(8,128)(2,1)} %get-tuple-element.170), kind=kOutput, calls=%fused_computation.13 | convolution fusion | flops 251658240 | bytes 29884416 | tf_op jit(solution)/shard_map/dot_general | solution.py:91
  379.1 3.5 multiply_convert_fusion.10
  393.8 3.1 gather_fusion.1
  399.0 11.0 %collective-permute-done.32 = bf16[1024,384]{1,0:T(8,128)(2,1)} collective-permute-done((bf16[1024,384]{1,0:T(8,128)(2,1)}, bf16[1024,384]{1,0:T(8,128)(2,1)}, u32[]{:S(2)}, u32[]{:S(2)}) %collective-permute-start.32) | collective-permute-done | bytes 786464 | tf_op jit(solution)/shard_map/ppermute | solution.py:49
  409.9 2.4 convert_multiply_fusion.13
  413.9 3.7 fusion.80
  417.7 2.3 fusion.98
  420.9 2.2 fusion.122
  423.6 20.7 %fusion.2 = f32[768,8,128]{2,1,0:T(8,128)S(1)} fusion(bf16[768,8,128]{2,1,0:T(8,128)(2,1)S(1)} %bitcast.375, bf16[768,128,64]{2,1,0:T(8,128)(2,1)} %get-tuple-element.173, bf16[768,128,64]{2,1,0:T(8,128)(2,1)} %get-tuple-element.172), kind=kOutput, calls=%fused_computation.9 | convolution fusion | flops 251658240 | bytes 29884416 | tf_op jit(solution)/shard_map/dot_general | solution.py:91
  444.3 5.3 fusion.43
  464.0 2.5 convolution_convert_fusion.9
  466.7 4.0 add_convert_fusion.1
  472.7 4.4 multiply_convert_fusion.2
  478.3 2.7 convolution_convert_fusion.1
  493.9 20.3 %psum.23 = bf16[2,2,384]{2,1,0:T(2,128)(2,1)} all-reduce(bf16[2,2,384]{2,1,0:T(2,128)(2,1)} %reshape.738), channel_id=1, replica_groups=mesh['dp'=8,'seq'=4] {'dp'}, use_global_device_ids=true, to_apply=%region_25.27 | all-reduce | flops 1536 | bytes 6144 | tf_op jit(solution)/shard_map/psum | solution.py:341
  517.2 6.3 all-reduce.4.cloned.1.call-done
  526.9 3.0 fusion.148
  530.8 3.7 all-to-all-start.3
  535.8 2.6 fusion.147
  538.4 3.2 all-to-all-done.3
  541.7 50.4 %reduce-scatter.11.cloned.1.call-done = bf16[1,288,384]{2,1,0:T(8,128)(2,1)} async-done(((bf16[8,288,384]{2,1,0:T(8,128)(2,1)}), bf16[1,288,384]{2,1,0:T(8,128)(2,1)}) %reduce-scatter.11.cloned.1.call-update) | async-done | bytes 221200 | tf_op jit(solution)/shard_map/reduce_scatter | solution.py:317
  593.8 3.5 all-to-all-start.2
  598.0 63.0 %reduce-scatter.7.cloned.1.call-done = bf16[1,288,384]{2,1,0:T(8,128)(2,1)} async-done(((bf16[8,288,384]{2,1,0:T(8,128)(2,1)}), bf16[1,288,384]{2,1,0:T(8,128)(2,1)}) %reduce-scatter.7.cloned.1.call-update) | async-done | bytes 221200 | tf_op jit(solution)/shard_map/reduce_scatter | solution.py:317
  662.9 66.4 %reduce-scatter.5.cloned.1.call-done = bf16[1,288,384]{2,1,0:T(8,128)(2,1)} async-done(((bf16[8,288,384]{2,1,0:T(8,128)(2,1)}), bf16[1,288,384]{2,1,0:T(8,128)(2,1)}) %reduce-scatter.5.cloned.1.call-update) | async-done | bytes 221200 | tf_op jit(solution)/shard_map/reduce_scatter | solution.py:318
  731.1 3.5 all-to-all-start.1
  737.3 4.4 all-to-all-done.1
  (641 shorter events, 166.8 us)
Async XLA Ops:
  7.2 208.4 %collective-permute-start.18 = (bf16[256,768]{1,0:T(8,128)(2,1)}, bf16[256,768]{1,0:T(8,128)(2,1)}, u32[]{:S(2)}, u32[]{:S(2)}) collective-permute-start(bf16[256,768]{1,0:T(8,128)(2,1)} %param.17), channel_id=1, source_target_pairs={{0,1},{1,0},{2,3},{3,2},{4,5},{5,4},{6,7},{7,6},{8,9},{9,8},{10,11... | collective-permute-start | bytes 1179656 | tf_op jit(solution)/shard_map/ppermute | solution.py:37
  7.7 207.2 %collective-permute-start.19 = (bf16[256,768]{1,0:T(8,128)(2,1)}, bf16[256,768]{1,0:T(8,128)(2,1)}, u32[]{:S(2)}, u32[]{:S(2)}) collective-permute-start(bf16[256,768]{1,0:T(8,128)(2,1)} %param.17), channel_id=1, source_target_pairs={{0,2},{1,3},{2,0},{3,1},{4,6},{5,7},{6,4},{7,5},{8,10},{9,11},{10,... | collective-permute-start | bytes 1179656 | tf_op jit(solution)/shard_map/ppermute | solution.py:37
  16.4 21.0 %all-to-all-start = ((bf16[4,256,384]{2,1,0:T(8,128)(2,1)}), bf16[4,256,384]{2,1,0:T(8,128)(2,1)S(1)}, u32[]{:S(2)}, u32[]{:S(2)}) async-start(bf16[4,256,384]{2,1,0:T(8,128)(2,1)} %pad_maximum_fusion.13), calls=%async_computation | async-start | bytes 1572864 | tf_op jit(solution)/shard_map/all_to_all | solution.py:226
  20.0 70.2 %all-gather.7.cloned.1.call-start = ((), (), s32[]{:S(2)}) async-start(), calls=%async_computation.12 | async-start | bytes 2433024 | tf_op jit(solution)/shard_map/all_gather | solution.py:231
  20.2 71.2 %copy-start.109 = (f32[256]{0:T(256)}, f32[256]{0:T(256)S(1)}, u32[]{:S(2)}) copy-start(f32[256]{0:T(256)S(1)} %broadcast_multiply_fusion.5) | copy-start | bytes 3076
  20.5 70.9 %copy-start.111 = (f32[256]{0:T(256)}, f32[256]{0:T(256)S(1)}, u32[]{:S(2)}) copy-start(f32[256]{0:T(256)S(1)} %add_rsqrt_fusion.1) | copy-start | bytes 3076
  21.9 33.0 %copy-start.25 = (f32[1,2,384,64]{3,2,1,0:T(8,128)}, f32[1,2,384,64]{3,2,1,0:T(8,128)S(1)}, u32[]{:S(2)}) copy-start(f32[1,2,384,64]{3,2,1,0:T(8,128)S(1)} %copy.246) | copy-start | bytes 589828
  38.3 109.8 %all-gather.9.cloned.1.call-start = ((), (), s32[]{:S(2)}) async-start(), calls=%async_computation.13 | async-start | bytes 1990656 | tf_op jit(solution)/shard_map/all_gather | solution.py:231
  91.7 9.9 %collective-permute-start.1 = (bf16[256,768]{1,0:T(8,128)(2,1)S(1)}, bf16[256,768]{1,0:T(8,128)(2,1)}, u32[]{:S(2)}, u32[]{:S(2)}) collective-permute-start(bf16[256,768]{1,0:T(8,128)(2,1)S(1)} %fusion.143), channel_id=1, source_target_pairs={{0,2},{1,3},{2,0},{3,1},{4,6},{5,7},{6,4},{7,5},{8,10},{9,11},{10,... | collective-permute-start | bytes 1179656 | tf_op jit(solution)/shard_map/ppermute | solution.py:37
  93.3 24.4 %copy-start.118 = (f32[768]{0:T(1024)}, f32[768]{0:T(1024)S(1)}, u32[]{:S(2)}) copy-start(f32[768]{0:T(1024)S(1)} %mul.688) | copy-start | bytes 9220
  94.0 10.4 %collective-permute-start = (bf16[256,768]{1,0:T(8,128)(2,1)S(1)}, bf16[256,768]{1,0:T(8,128)(2,1)}, u32[]{:S(2)}, u32[]{:S(2)}) collective-permute-start(bf16[256,768]{1,0:T(8,128)(2,1)S(1)} %fusion.143), channel_id=1, source_target_pairs={{0,1},{1,0},{2,3},{3,2},{4,5},{5,4},{6,7},{7,6},{8,9},{9,8},{10,11... | collective-permute-start | bytes 1179656 | tf_op jit(solution)/shard_map/ppermute | solution.py:37
  101.6 2.7 collective-permute-start.2
  102.3 114.3 %all-gather.11.cloned.1.call-start = ((), (), s32[]{:S(2)}) async-start(), calls=%async_computation.14 | async-start | bytes 3981312 | tf_op jit(solution)/shard_map/all_gather | solution.py:231
  104.3 47.7 %copy-start.38 = (bf16[8,1,96,384]{3,2,1,0:T(8,128)(2,1)}, bf16[8,1,96,384]{3,2,1,0:T(8,128)(2,1)S(1)}, u32[]{:S(2)}) copy-start(bf16[8,1,96,384]{3,2,1,0:T(8,128)(2,1)S(1)} %get-tuple-element.102) | copy-start | bytes 1769476
  124.4 27.0 %copy-start.34 = (bf16[1024,384]{1,0:T(8,128)(2,1)}, bf16[1024,384]{1,0:T(8,128)(2,1)S(1)}, u32[]{:S(2)}) copy-start(bf16[1024,384]{1,0:T(8,128)(2,1)S(1)} %fusion.107) | copy-start | bytes 2359300
  124.4 30.3 %collective-permute-start.4 = (bf16[1024,384]{1,0:T(8,128)(2,1)S(1)}, bf16[1024,384]{1,0:T(8,128)(2,1)S(1)}, u32[]{:S(2)}, u32[]{:S(2)}) collective-permute-start(bf16[1024,384]{1,0:T(8,128)(2,1)S(1)} %fusion.107), channel_id=1, source_target_pairs={{0,2},{1,3},{2,0},{3,1},{4,6},{5,7},{6,4},{7,5},{8,10},{9,11},{10,... | collective-permute-start | bytes 2359304 | tf_op jit(solution)/shard_map/ppermute | solution.py:37
  133.6 54.5 %copy-start.27 = (f32[1,2,384,64]{3,2,1,0:T(8,128)}, f32[1,2,384,64]{3,2,1,0:T(8,128)S(1)}, u32[]{:S(2)}) copy-start(f32[1,2,384,64]{3,2,1,0:T(8,128)S(1)} %copy.249) | copy-start | bytes 589828
  137.9 377.6 %reduce-scatter.9.cloned.1.call-start = ((), (), s32[]{:S(2)}) async-start(), calls=%async_computation.10 | async-start | bytes 1990656 | tf_op jit(solution)/shard_map/reduce_scatter | solution.py:318
  151.3 4.3 collective-permute-start.3
  154.7 2.4 collective-permute-start.5
  163.4 22.0 %collective-permute-start.7 = (bf16[256,768]{1,0:T(8,128)(2,1)S(1)}, bf16[256,768]{1,0:T(8,128)(2,1)S(1)}, u32[]{:S(2)}, u32[]{:S(2)}) collective-permute-start(bf16[256,768]{1,0:T(8,128)(2,1)S(1)} %get-tuple-element.116), channel_id=1, source_target_pairs={{0,1},{1,0},{2,3},{3,2},{4,5},{5,4},{6,7},{7,6},{8,9},{9,8},{10,11... | collective-permute-start | bytes 1179656 | tf_op jit(solution)/shard_map/ppermute | solution.py:49
  184.9 16.4 %collective-permute-start.6 = (bf16[256,768]{1,0:T(8,128)(2,1)S(1)}, bf16[256,768]{1,0:T(8,128)(2,1)S(1)}, u32[]{:S(2)}, u32[]{:S(2)}) collective-permute-start(bf16[256,768]{1,0:T(8,128)(2,1)S(1)} %get-tuple-element.115), channel_id=1, source_target_pairs={{0,1},{1,0},{2,3},{3,2},{4,5},{5,4},{6,7},{7,6},{8,9},{9,8},{10,11... | collective-permute-start | bytes 1179656 | tf_op jit(solution)/shard_map/ppermute | solution.py:49
  186.6 14.8 %collective-permute-start.8 = (bf16[256,768]{1,0:T(8,128)(2,1)S(1)}, bf16[256,768]{1,0:T(8,128)(2,1)S(1)}, u32[]{:S(2)}, u32[]{:S(2)}) collective-permute-start(bf16[256,768]{1,0:T(8,128)(2,1)S(1)} %fusion.157), channel_id=1, source_target_pairs={{0,2},{1,3},{2,0},{3,1},{4,6},{5,7},{6,4},{7,5},{8,10},{9,11},{10,... | collective-permute-start | bytes 1179656 | tf_op jit(solution)/shard_map/ppermute | solution.py:49
  204.1 11.4 %collective-permute-start.10 = (bf16[256,768]{1,0:T(8,128)(2,1)}, bf16[256,768]{1,0:T(8,128)(2,1)}, u32[]{:S(2)}, u32[]{:S(2)}) collective-permute-start(bf16[256,768]{1,0:T(8,128)(2,1)} %add_convert_fusion.8), channel_id=1, source_target_pairs={{0,2},{1,3},{2,0},{3,1},{4,6},{5,7},{6,4},{7,5},{8,10},{9,11},{10,... | collective-permute-start | bytes 1179656 | tf_op jit(solution)/shard_map/ppermute | solution.py:37
  214.9 70.5 %copy-start.116 = (s32[1024]{0:T(1024)}, s32[1024]{0:T(1024)S(1)}, u32[]{:S(2)}) copy-start(s32[1024]{0:T(1024)S(1)} %pad_clamp_fusion) | copy-start | bytes 12292
  214.9 26.3 %collective-permute-start.20 = (bf16[256,768]{1,0:T(8,128)(2,1)}, bf16[256,768]{1,0:T(8,128)(2,1)S(1)}, u32[]{:S(2)}, u32[]{:S(2)}) collective-permute-start(bf16[256,768]{1,0:T(8,128)(2,1)} %collective-permute-done.19), channel_id=1, source_target_pairs={{0,1},{1,0},{2,3},{3,2},{4,5},{5,4},{6,7},{7,6},{8,9},{9,8},{10,11... | collective-permute-start | bytes 1179656 | tf_op jit(solution)/shard_map/ppermute | solution.py:37
  215.0 3.6 collective-permute-start.9
  215.5 3.1 collective-permute-start.11
  218.6 24.3 %copy-start.40 = (bf16[8,1,96,384]{3,2,1,0:T(8,128)(2,1)}, bf16[8,1,96,384]{3,2,1,0:T(8,128)(2,1)S(1)}, u32[]{:S(2)}) copy-start(bf16[8,1,96,384]{3,2,1,0:T(8,128)(2,1)S(1)} %get-tuple-element.99) | copy-start | bytes 1769476
  218.6 24.3 %copy-start.132 = (bf16[256,768]{1,0:T(8,128)(2,1)}, bf16[256,768]{1,0:T(8,128)(2,1)S(1)}, u32[]{:S(2)}) copy-start(bf16[256,768]{1,0:T(8,128)(2,1)S(1)} %collective-permute-done.9) | copy-start | bytes 1179652
  218.6 24.3 %copy-start.134 = (bf16[256,768]{1,0:T(8,128)(2,1)}, bf16[256,768]{1,0:T(8,128)(2,1)S(1)}, u32[]{:S(2)}) copy-start(bf16[256,768]{1,0:T(8,128)(2,1)S(1)} %collective-permute-done.11) | copy-start | bytes 1179652
  238.7 20.0 %collective-permute-start.13 = (bf16[1024,384]{1,0:T(8,128)(2,1)S(1)}, bf16[1024,384]{1,0:T(8,128)(2,1)S(1)}, u32[]{:S(2)}, u32[]{:S(2)}) collective-permute-start(bf16[1024,384]{1,0:T(8,128)(2,1)S(1)} %fusion.106), channel_id=1, source_target_pairs={{0,2},{1,3},{2,0},{3,1},{4,6},{5,7},{6,4},{7,5},{8,10},{9,11},{10,... | collective-permute-start | bytes 2359304 | tf_op jit(solution)/shard_map/ppermute | solution.py:37
  242.1 17.3 %collective-permute-start.12 = (bf16[1024,384]{1,0:T(8,128)(2,1)S(1)}, bf16[1024,384]{1,0:T(8,128)(2,1)S(1)}, u32[]{:S(2)}, u32[]{:S(2)}) collective-permute-start(bf16[1024,384]{1,0:T(8,128)(2,1)S(1)} %fusion.106), channel_id=1, source_target_pairs={{0,1},{1,0},{2,3},{3,2},{4,5},{5,4},{6,7},{7,6},{8,9},{9,8},{10,11... | collective-permute-start | bytes 2359304 | tf_op jit(solution)/shard_map/ppermute | solution.py:37
  258.7 2.3 collective-permute-start.14
  270.8 21.9 %collective-permute-start.21 = (bf16[1024,384]{1,0:T(8,128)(2,1)}, bf16[1024,384]{1,0:T(8,128)(2,1)}, u32[]{:S(2)}, u32[]{:S(2)}) collective-permute-start(bf16[1024,384]{1,0:T(8,128)(2,1)} %pad_maximum_fusion.20), channel_id=1, source_target_pairs={{0,1},{1,0},{2,3},{3,2},{4,5},{5,4},{6,7},{7,6},{8,9},{9,8},{10,11... | collective-permute-start | bytes 2359304 | tf_op jit(solution)/shard_map/ppermute | solution.py:49
  271.0 7.6 %collective-permute-start.22 = (bf16[1024,384]{1,0:T(8,128)(2,1)S(1)}, bf16[1024,384]{1,0:T(8,128)(2,1)S(1)}, u32[]{:S(2)}, u32[]{:S(2)}) collective-permute-start(bf16[1024,384]{1,0:T(8,128)(2,1)S(1)} %pad_maximum_fusion.21), channel_id=1, source_target_pairs={{0,1},{1,0},{2,3},{3,2},{4,5},{5,4},{6,7},{7,6},{8,9},{9,8},{10,11... | collective-permute-start | bytes 2359304 | tf_op jit(solution)/shard_map/ppermute | solution.py:49
  279.6 20.7 %collective-permute-start.23 = (bf16[1024,384]{1,0:T(8,128)(2,1)}, bf16[1024,384]{1,0:T(8,128)(2,1)}, u32[]{:S(2)}, u32[]{:S(2)}) collective-permute-start(bf16[1024,384]{1,0:T(8,128)(2,1)} %fusion.108), channel_id=1, source_target_pairs={{0,2},{1,3},{2,0},{3,1},{4,6},{5,7},{6,4},{7,5},{8,10},{9,11},{10,... | collective-permute-start | bytes 2359304 | tf_op jit(solution)/shard_map/ppermute | solution.py:49
  283.4 60.1 %collective-permute-start.15 = (bf16[256,768]{1,0:T(8,128)(2,1)}, bf16[256,768]{1,0:T(8,128)(2,1)}, u32[]{:S(2)}, u32[]{:S(2)}) collective-permute-start(bf16[256,768]{1,0:T(8,128)(2,1)} %get-tuple-element.113), channel_id=1, source_target_pairs={{0,1},{1,0},{2,3},{3,2},{4,5},{5,4},{6,7},{7,6},{8,9},{9,8},{10,11... | collective-permute-start | bytes 1179656 | tf_op jit(solution)/shard_map/ppermute | solution.py:49
  283.4 7.3 collective-permute-start.16
  292.0 51.5 %collective-permute-start.17 = (bf16[256,768]{1,0:T(8,128)(2,1)S(1)}, bf16[256,768]{1,0:T(8,128)(2,1)}, u32[]{:S(2)}, u32[]{:S(2)}) collective-permute-start(bf16[256,768]{1,0:T(8,128)(2,1)S(1)} %fusion.154), channel_id=1, source_target_pairs={{0,2},{1,3},{2,0},{3,1},{4,6},{5,7},{6,4},{7,5},{8,10},{9,11},{10,... | collective-permute-start | bytes 1179656 | tf_op jit(solution)/shard_map/ppermute | solution.py:49
  321.3 7.0 collective-permute-start.25
  327.2 196.2 %all-reduce.4.cloned.1.call-start = ((), (), s32[]{:S(2)}) async-start(), calls=%async_computation.15 | async-start | bytes 786432 | tf_op jit(solution)/shard_map/psum | solution.py:339
  328.2 10.5 %collective-permute-start.24 = (bf16[256,768]{1,0:T(8,128)(2,1)S(1)}, bf16[256,768]{1,0:T(8,128)(2,1)S(1)}, u32[]{:S(2)}, u32[]{:S(2)}) collective-permute-start(bf16[256,768]{1,0:T(8,128)(2,1)S(1)} %copy-done.92), channel_id=1, source_target_pairs={{0,1},{1,0},{2,3},{3,2},{4,5},{5,4},{6,7},{7,6},{8,9},{9,8},{10,11... | collective-permute-start | bytes 1179656 | tf_op jit(solution)/shard_map/ppermute | solution.py:49
  329.7 11.5 %collective-permute-start.26 = (bf16[256,768]{1,0:T(8,128)(2,1)S(1)}, bf16[256,768]{1,0:T(8,128)(2,1)S(1)}, u32[]{:S(2)}, u32[]{:S(2)}) collective-permute-start(bf16[256,768]{1,0:T(8,128)(2,1)S(1)} %fusion.152), channel_id=1, source_target_pairs={{0,2},{1,3},{2,0},{3,1},{4,6},{5,7},{6,4},{7,5},{8,10},{9,11},{10,... | collective-permute-start | bytes 1179656 | tf_op jit(solution)/shard_map/ppermute | solution.py:49
  346.6 32.4 %copy-start.93 = (bf16[256,768]{1,0:T(8,128)(2,1)}, bf16[256,768]{1,0:T(8,128)(2,1)S(1)}, u32[]{:S(2)}) copy-start(bf16[256,768]{1,0:T(8,128)(2,1)S(1)} %get-tuple-element.79) | copy-start | bytes 1179652
  346.6 10.8 %collective-permute-start.28 = (bf16[256,768]{1,0:T(8,128)(2,1)S(1)}, bf16[256,768]{1,0:T(8,128)(2,1)S(1)}, u32[]{:S(2)}, u32[]{:S(2)}) collective-permute-start(bf16[256,768]{1,0:T(8,128)(2,1)S(1)} %get-tuple-element.79), channel_id=1, source_target_pairs={{0,2},{1,3},{2,0},{3,1},{4,6},{5,7},{6,4},{7,5},{8,10},{9,11},{10,... | collective-permute-start | bytes 1179656 | tf_op jit(solution)/shard_map/ppermute | solution.py:37
  353.9 25.0 %collective-permute-start.27 = (bf16[256,768]{1,0:T(8,128)(2,1)S(1)}, bf16[256,768]{1,0:T(8,128)(2,1)S(1)}, u32[]{:S(2)}, u32[]{:S(2)}) collective-permute-start(bf16[256,768]{1,0:T(8,128)(2,1)S(1)} %get-tuple-element.79), channel_id=1, source_target_pairs={{0,1},{1,0},{2,3},{3,2},{4,5},{5,4},{6,7},{7,6},{8,9},{9,8},{10,11... | collective-permute-start | bytes 1179656 | tf_op jit(solution)/shard_map/ppermute | solution.py:37
  357.4 21.6 %collective-permute-start.29 = (bf16[256,768]{1,0:T(8,128)(2,1)S(1)}, bf16[256,768]{1,0:T(8,128)(2,1)}, u32[]{:S(2)}, u32[]{:S(2)}) collective-permute-start(bf16[256,768]{1,0:T(8,128)(2,1)S(1)} %collective-permute-done.28), channel_id=1, source_target_pairs={{0,1},{1,0},{2,3},{3,2},{4,5},{5,4},{6,7},{7,6},{8,9},{9,8},{10,11... | collective-permute-start | bytes 1179656 | tf_op jit(solution)/shard_map/ppermute | solution.py:37
  385.8 2.9 collective-permute-start.31
  387.1 11.9 %collective-permute-start.30 = (bf16[1024,384]{1,0:T(8,128)(2,1)}, bf16[1024,384]{1,0:T(8,128)(2,1)}, u32[]{:S(2)}, u32[]{:S(2)}) collective-permute-start(bf16[1024,384]{1,0:T(8,128)(2,1)} %pad_maximum_fusion.22), channel_id=1, source_target_pairs={{0,1},{1,0},{2,3},{3,2},{4,5},{5,4},{6,7},{7,6},{8,9},{9,8},{10,11... | collective-permute-start | bytes 2359304 | tf_op jit(solution)/shard_map/ppermute | solution.py:49
  389.8 20.1 %collective-permute-start.32 = (bf16[1024,384]{1,0:T(8,128)(2,1)}, bf16[1024,384]{1,0:T(8,128)(2,1)}, u32[]{:S(2)}, u32[]{:S(2)}) collective-permute-start(bf16[1024,384]{1,0:T(8,128)(2,1)} %fusion.109), channel_id=1, source_target_pairs={{0,2},{1,3},{2,0},{3,1},{4,6},{5,7},{6,4},{7,5},{8,10},{9,11},{10,... | collective-permute-start | bytes 2359304 | tf_op jit(solution)/shard_map/ppermute | solution.py:49
  452.8 139.3 %reduce-scatter.11.cloned.1.call-start = ((), (), s32[]{:S(2)}) async-start(), calls=%async_computation.11 | async-start | bytes 1990656 | tf_op jit(solution)/shard_map/reduce_scatter | solution.py:317
  455.9 205.0 %reduce-scatter.7.cloned.1.call-start = ((), (), s32[]{:S(2)}) async-start(), calls=%async_computation.9 | async-start | bytes 1990656 | tf_op jit(solution)/shard_map/reduce_scatter | solution.py:317
  462.9 266.4 %reduce-scatter.5.cloned.1.call-start = ((), (), s32[]{:S(2)}) async-start(), calls=%async_computation.8 | async-start | bytes 1990656 | tf_op jit(solution)/shard_map/reduce_scatter | solution.py:318
  487.5 1.7 collective-permute-start.34
  489.0 37.9 %collective-permute-start.33 = (bf16[256,768]{1,0:T(8,128)(2,1)}, bf16[256,768]{1,0:T(8,128)(2,1)}, u32[]{:S(2)}, u32[]{:S(2)}) collective-permute-start(bf16[256,768]{1,0:T(8,128)(2,1)} %get-tuple-element.105), channel_id=1, source_target_pairs={{0,1},{1,0},{2,3},{3,2},{4,5},{5,4},{6,7},{7,6},{8,9},{9,8},{10,11... | collective-permute-start | bytes 1179656 | tf_op jit(solution)/shard_map/ppermute | solution.py:49
  490.1 36.8 %collective-permute-start.35 = (bf16[256,768]{1,0:T(8,128)(2,1)}, bf16[256,768]{1,0:T(8,128)(2,1)}, u32[]{:S(2)}, u32[]{:S(2)}) collective-permute-start(bf16[256,768]{1,0:T(8,128)(2,1)} %fusion.150), channel_id=1, source_target_pairs={{0,2},{1,3},{2,0},{3,1},{4,6},{5,7},{6,4},{7,5},{8,10},{9,11},{10,... | collective-permute-start | bytes 1179656 | tf_op jit(solution)/shard_map/ppermute | solution.py:49
  492.0 34.8 %copy-start.1 = (bf16[256,768]{1,0:T(8,128)(2,1)S(1)}, bf16[256,768]{1,0:T(8,128)(2,1)}, u32[]{:S(2)}) copy-start(bf16[256,768]{1,0:T(8,128)(2,1)} %param.15) | copy-start | bytes 1179652
  492.0 34.8 %copy-start.108 = (f32[768]{0:T(1024)S(1)}, f32[768]{0:T(1024)}, u32[]{:S(2)}) copy-start(f32[768]{0:T(1024)} %copy-done.107) | copy-start | bytes 9220
  492.0 34.8 %copy-start.110 = (f32[256]{0:T(256)S(1)}, f32[256]{0:T(256)}, u32[]{:S(2)}) copy-start(f32[256]{0:T(256)} %copy-done.109) | copy-start | bytes 3076
  530.8 62.3 %copy-start.62 = (bf16[3,4,24,384]{3,2,0,1:T(8,128)(2,1)S(1)}, bf16[3,4,24,384]{3,2,0,1:T(8,128)(2,1)}, u32[]{:S(2)}) copy-start(bf16[3,4,24,384]{3,2,0,1:T(8,128)(2,1)} %copy.208) | copy-start | bytes 663556
  530.8 10.8 %all-to-all-start.3 = ((f32[32,1,96]{2,1,0:T(1,128)}), f32[32,1,96]{2,1,0:T(1,128)S(1)}, u32[]{:S(2)}, u32[]{:S(2)}) async-start(f32[32,1,96]{2,1,0:T(1,128)} %bitcast.104), calls=%async_computation.7 | async-start | bytes 32768 | tf_op jit(solution)/shard_map/all_to_all | solution.py:337
  593.8 137.2 %all-to-all-start.2 = ((bf16[4,120,384]{2,1,0:T(8,128)(2,1)}), bf16[4,120,384]{2,1,0:T(8,128)(2,1)S(1)}, u32[]{:S(2)}, u32[]{:S(2)}) async-start(bf16[4,120,384]{2,1,0:T(8,128)(2,1)} %pad_maximum_fusion.37), calls=%async_computation.6 | async-start | bytes 737280 | tf_op jit(solution)/shard_map/all_to_all | solution.py:323
  731.1 10.6 %all-to-all-start.1 = ((bf16[4,120,384]{2,1,0:T(8,128)(2,1)}), bf16[4,120,384]{2,1,0:T(8,128)(2,1)S(1)}, u32[]{:S(2)}, u32[]{:S(2)}) async-start(bf16[4,120,384]{2,1,0:T(8,128)(2,1)} %pad_maximum_fusion.36), calls=%async_computation.3 | async-start | bytes 737280 | tf_op jit(solution)/shard_map/all_to_all | solution.py:323
  (144 other events, 784.3 us)
Sparse Core Ops, SparseCore 0:
  38.5 51.6 all-gather.6
  102.5 45.6 all-gather.8
  151.0 64.0 all-gather.10
  327.3 65.0 reduce-scatter.8
  452.9 70.5 all-reduce.3
  526.8 65.2 reduce-scatter.10
  596.0 64.9 reduce-scatter.6
  664.4 64.8 reduce-scatter.4

commit v2 on v1

--- a/solution.py
+++ b/solution.py
@@ -50,6 +50,52 @@
                 blocks[member ^ bit] = blocks[member ^ bit] + came.astype(F32)
         bit *= 2
     return blocks[0]
+
+
+def dp_pairs(count, bit):
+    return [(i, i ^ bit) for i in range(count)]
+
+
+def bits_of(count):
+    return [1 << j for j in range(count.bit_length() - 1)]
+
+
+def dp_gather(block, count, sequence):
+    me = lax.axis_index("dp")
+    for bit in sequence:
+        other = lax.ppermute(block, "dp", dp_pairs(count, bit))
+        upper = (me & bit) != 0
+        block = jnp.stack([jnp.where(upper, other, block), jnp.where(upper, block, other)])
+    axes = [sequence[::-1].index(bit) for bit in bits_of(count)[::-1]]
+    rest = range(len(axes), block.ndim)
+    block = block.transpose(*axes, *rest)
+    return block.reshape((count,) + block.shape[len(axes) :])
+
+
+def dp_reduce(blocks, count, sequence):
+    me = lax.axis_index("dp")
+    levels = bits_of(count)[::-1]
+    blocks = blocks.reshape((2,) * len(levels) + blocks.shape[1:])
+    for bit in sequence:
+        axis = levels.index(bit)
+        side = (me // bit) % 2
+        sent = lax.dynamic_slice_in_dim(blocks, 1 - side, 1, axis).astype(BF)
+        held = lax.dynamic_slice_in_dim(blocks, side, 1, axis)
+        came = lax.ppermute(sent, "dp", dp_pairs(count, bit))
+        blocks = (held.astype(F32) + came.astype(F32)).astype(BF)
+    return blocks.reshape(blocks.shape[len(levels) :])
+
+
+def dp_reduce_halves(blocks, count):
+    bits = bits_of(count)
+    middle = blocks.shape[1] // 32 * 16
+    return jnp.concatenate(
+        [
+            dp_reduce(blocks[:, :middle], count, bits),
+            dp_reduce(blocks[:, middle:], count, bits[1:] + bits[:1]),
+        ],
+        0,
+    )
 
 
 def gelu_parts(pre):
@@ -248,7 +294,16 @@
         n_mix = count * mix_rows
         if layer == 0:
             early = jnp.concatenate([early, norm_came.reshape(count * 16, width)], 0)
-            got = gather_dp(early)
+            bits = bits_of(dp)
+            middle = early.shape[0] // 32 * 16
+            got = jnp.concatenate(
+                [
+                    dp_gather(early[:middle], dp, bits[:0:-1] + bits[:1]),
+                    dp_gather(early[middle:], dp, bits[:1] + bits[:0:-1]),
+                ],
+                1,
+            )
+            got, late = lax.optimization_barrier((got, late))
             got_norm = got[:, n_early:].reshape(dp, count, 16, width)[:, :, : 2 * depth, :in_rows]
             got_norm = got_norm.transpose(2, 0, 1, 3).reshape(depth, 2, model).astype(F32)
             got_early = got[:, :n_early]
@@ -288,6 +343,7 @@
     norm_grads = [None] * depth
     ssm_grads = [None] * depth
     shares = [None] * depth
+    parts = [None] * depth
     for layer in reversed(range(depth)):
         grad_stream, terms, norm_terms, kern_hat, grad_skip = back_layer(
             grad_stream, kept[layer], weights[layer], hats[layer], skips[layer], waves, count
@@ -314,8 +370,18 @@
             ],
             1,
         ).reshape(dp, 3 * count * in_rows, width)
-        late = lax.psum_scatter(late, "dp", scatter_dimension=0, tiled=False)
-        early = lax.psum_scatter(early, "dp", scatter_dimension=0, tiled=False)
+        if layer:
+            held = lax.psum_scatter(jnp.concatenate([early, late], 1), "dp", scatter_dimension=0, tiled=False)
+            parts[layer] = held
+        else:
+            if depth > 1:
+                early, parts[depth - 1] = lax.optimization_barrier((early, parts[depth - 1]))
+            late = dp_reduce(late, dp, bits_of(dp))
+            early = dp_reduce_halves(early, dp)
+            parts[layer] = jnp.concatenate([early, late], 0)
+    for layer in range(depth):
+        early = parts[layer][: 3 * count * in_rows]
+        late = parts[layer][3 * count * in_rows :]
         share_out = late[count * mix_rows :].reshape(model // width, mix_rows, width).transpose(1, 0, 2)
         share_out = share_out.reshape(mix_rows, model).astype(F32)
         back_mix = late[: count * mix_rows].reshape(count, mix_rows, width)
@@ -336,9 +402,20 @@
     norm_sum = jnp.sum(
         lax.all_to_all(norm_all.reshape(dp * count, 2 * depth * in_rows), ("dp", "seq"), 0, 0, tiled=True), 0
     ).reshape(depth, 2, in_rows)
-    coef_sum = lax.psum(jnp.stack([g[0] for g in ssm_grads]).astype(BF), "dp").astype(F32)
-    rate_sum = lax.psum(jnp.stack([g[1] for g in ssm_grads]).astype(BF), "dp").astype(F32)
-    skip_sum = lax.psum(jnp.stack([g[2] for g in ssm_grads]).astype(BF), "dp").astype(F32)
+    own = 2 * width // dp
+    ssm_rows = []
+    for coef_grad, rate_grad, grad_skip in ssm_grads:
+        ssm_rows.append(jnp.concatenate([coef_grad, rate_grad], 1).reshape(dp, own, 2 * states))
+        skip_row = jnp.pad(grad_skip.reshape(dp, own), ((0, 0), (0, -own % (2 * states))))
+        ssm_rows.append(skip_row.reshape(dp, -1, 2 * states))
+    ssm_rows = jnp.concatenate(ssm_rows, 1)
+    ssm_rows = jnp.pad(ssm_rows, ((0, 0), (0, -ssm_rows.shape[1] % 16), (0, 0))).astype(BF)
+    ssm_sum = dp_gather(dp_reduce(ssm_rows, dp, bits_of(dp)), dp, bits_of(dp)[::-1]).astype(F32)
+    each = own + -(-own // (2 * states))
+    ssm_sum = ssm_sum[:, : depth * each].reshape(dp, depth, each, 2 * states)
+    coef_sum = ssm_sum[:, :, :own, :states].transpose(1, 0, 2, 3)
+    rate_sum = ssm_sum[:, :, :own, states:].transpose(1, 0, 2, 3)
+    skip_sum = ssm_sum[:, :, own:].reshape(dp, depth, -1)[:, :, :own].transpose(1, 0, 2)
     stacked = [jnp.stack([shares[layer][member] for layer in range(depth)]) for member in range(4)]
     return (
         stream,

time: 763 us -> 682 us (0.89)
  waiting for transfers between devices: 265 us -> 146 us
  starting transfers between devices: 36.9 us -> 61.6 us
  blocking collectives: 20.3 us -> 0 us
  matrix products: 206 us -> 225 us
  local copies, waits for them, and re-layouts: 81.4 us -> 93.9 us
    reduce_scatter x4 -> x1, waiting for transfers between devices: 180 us -> 0.01 us  [shards(): lax.psum_scatter(jnp.concatenate([early, late], 1), 'dp', scatter_dimensi...]
    ppermute x0 -> x21, waiting for transfers between devices: none -> 108 us  [the longest x12 72.8 us: dp_reduce(): came = lax.ppermute(sent, 'dp', dp_pairs(count, bit))]
    all_gather x3 -> x2, waiting for transfers between devices: 24.3 us -> 0.04 us  [gather_dp(): return lax.all_gather(block, 'dp', axis=0)]
    ppermute x0 -> x21, starting transfers between devices: none -> 24.3 us  [the longest x12 12.5 us: dp_reduce(): came = lax.ppermute(sent, 'dp', dp_pairs(count, bit))]
    psum x1 -> x0, blocking collectives: 20.3 us -> none  [shards(): lax.psum(jnp.stack([g[2] for g in ssm_grads]).astype(BF), 'dp').astype(F32)]
    dot_general x56, matrix products: 137 us -> 154 us  [dot(): lax.dot_general(left, right, (((left_dim,), (right_dim,)), ((), ())), pre...]
    ppermute x18, waiting for transfers between devices: 21.5 us -> 7.06 us  [seq_reduce(): came = lax.ppermute(sent, 'seq', seq_pairs(count, bit))]
    another operation x9 -> x21, other arithmetic: 12.2 us -> 18.5 us
  transfers between devices with their start and end apart: 48 -> 64, of which waited for: 17 -> 25; matrix products, arithmetic and copies ran while one was open for 49% -> 58% of each run, Pallas kernels for 0% -> 0%
where the time goes in v2:
time: 682 us; the launch traced here: 677 us
  matrix products  225 us (33%)
  waiting for transfers between devices  146 us (21%)
  other arithmetic  125 us (18%)
  local copies, waits for them, and re-layouts  93.9 us (14%)
  starting transfers between devices  61.6 us (9%)
  between operations  25.2 us (4%)
    dot_general x56, matrix products, dot(): lax.dot_general(left, right, (((left_dim,), (right_dim,)), ((), ())), pre...  154 us
    ppermute x12, waiting for transfers between devices, dp_reduce(): came = lax.ppermute(sent, 'dp', dp_pairs(count, bit))  72.8 us
    dot_general x2, matrix products, lag_grads(): lax.dot_general(pieces, pair, (((2,), (1,)), ((0,), (0,))), preferred_ele...  44.5 us
    convert_element_type x2, other arithmetic, lag_kernels(): near.astype(BF)  42.1 us
    ppermute x9, waiting for transfers between devices, dp_gather(): other = lax.ppermute(block, 'dp', dp_pairs(count, bit))  34.7 us
    dot_general x2, matrix products, lag_kernels(): lax.dot_general(left, near.astype(BF), (((2,), (2,)), ((0,), (0,))), pref...  26.9 us
    unnamed x296, local copies, waits for them, and re-layouts  23.9 us
    ppermute x18, waiting for transfers between devices, seq_gather(): lax.ppermute(blocks[member], 'seq', seq_pairs(count, bit))  22.1 us
  transfers between devices with their start and end apart: 64, of which 25 were waited for; matrix products, arithmetic and copies ran while one was open for 58% of the time, Pallas kernels for 0%

profile of v2, /device:TPU:0, one launch (start us, length us, event | category | flops | bytes accessed | tf_op | source)
XLA Modules:
  0.0 676.6 jit_solution(18404048885096892983)
XLA Ops:
  16.4 3.6 all-to-all-start
  22.5 13.6 %fusion.75 = bf16[768,8,128]{2,1,0:T(8,128)(2,1)S(1)} fusion(f32[768,64]{1,0:T(8,128)S(1)} %bitcast.396, f32[8]{0:T(128)S(1)} %iota_multiply_fusion, f32[768,64]{1,0:T(8,128)S(1)} %bitcast.476), kind=kOutput, calls=%fused_computation.136 | convolution fusion | flops 115212288 | bytes 1966112 | tf_op jit(solution)/shard_map/dot_general | solution.py:125
  36.1 5.3 fusion.103
  42.3 2.7 collective-permute-start
  45.0 7.1 %collective-permute-done = bf16[176,384]{1,0:T(8,128)(2,1)S(1)} collective-permute-done((bf16[176,384]{1,0:T(8,128)(2,1)S(1)}, bf16[176,384]{1,0:T(8,128)(2,1)S(1)}, u32[]{:S(2)}, u32[]{:S(2)}) %collective-permute-start) | collective-permute-done | bytes 135200 | tf_op jit(solution)/shard_map/ppermute | solution.py:66
  54.4 5.0 gather_fusion
  60.3 3.4 collective-permute-start.4
  63.8 9.0 %collective-permute-done.1 = bf16[2,176,384]{2,1,0:T(8,128)(2,1)S(1)} collective-permute-done((bf16[2,176,384]{2,1,0:T(8,128)(2,1)S(1)}, bf16[2,176,384]{2,1,0:T(8,128)(2,1)S(1)}, u32[]{:S(2)}, u32[]{:S(2)}) %collective-permute-start.1) | collective-permute-done | bytes 270368 | tf_op jit(solution)/shard_map/ppermute | solution.py:66
  78.3 8.3 %collective-permute-done.2 = bf16[2,2,176,384]{3,2,1,0:T(8,128)(2,1)} collective-permute-done((bf16[2,2,176,384]{3,2,1,0:T(8,128)(2,1)}, bf16[2,2,176,384]{3,2,1,0:T(8,128)(2,1)}, u32[]{:S(2)}, u32[]{:S(2)}) %collective-permute-start.2) | collective-permute-done | bytes 540704 | tf_op jit(solution)/shard_map/ppermute | solution.py:66
  93.3 4.6 bitcast_select_fusion
  105.5 5.1 multiply_convert_fusion.6
  111.7 3.7 fusion.292
  115.5 2.8 subtract_convert_fusion.3
  118.6 6.5 convert_convert_fusion
  127.1 21.0 %fusion.1 = (bf16[768,128,64]{2,1,0:T(8,128)(2,1)}, bf16[768,128,64]{2,1,0:T(8,128)(2,1)}) fusion(f32[768,64]{1,0:T(8,128)S(1)} %bitcast.397), kind=kLoop, calls=%fused_computation.8 | loop fusion | flops 25165824 | bytes 25362432 | tf_op jit(solution)/shard_map/convert_element_type | solution.py:126
  161.9 3.5 fusion.255
  174.6 3.6 multiply_convert_fusion.15
  178.2 2.6 fusion.288
  181.1 21.1 %fusion = (bf16[768,128,64]{2,1,0:T(8,128)(2,1)}, bf16[768,128,64]{2,1,0:T(8,128)(2,1)}) fusion(f32[768,64]{1,0:T(8,128)S(1)} %bitcast.399), kind=kLoop, calls=%fused_computation.6 | loop fusion | flops 25165824 | bytes 25362432 | tf_op jit(solution)/shard_map/convert_element_type | solution.py:126
  204.5 13.3 %fusion.72 = bf16[768,8,128]{2,1,0:T(8,128)(2,1)S(1)} fusion(f32[768,64]{1,0:T(8,128)S(1)} %bitcast.400, f32[768,64]{1,0:T(8,128)S(1)} %bitcast.475, f32[8]{0:T(128)S(1)} %copy-done.119), kind=kOutput, calls=%fused_computation.135 | convolution fusion | flops 115212288 | bytes 1966112 | tf_op jit(solution)/shard_map/dot_general | solution.py:125
  222.2 5.7 fusion.100
  236.6 5.1 multiply_convert_fusion.4
  242.9 3.7 fusion.293
  246.7 2.9 subtract_convert_fusion.2
  249.8 6.4 convert_convert_fusion.1
  262.5 13.8 %collective-permute-done.19 = bf16[1024,384]{1,0:T(8,128)(2,1)S(1)} collective-permute-done((bf16[1024,384]{1,0:T(8,128)(2,1)S(1)}, bf16[1024,384]{1,0:T(8,128)(2,1)S(1)}, u32[]{:S(2)}, u32[]{:S(2)}) %collective-permute-start.19) | collective-permute-done | bytes 786464 | tf_op jit(solution)/shard_map/ppermute | solution.py:37
  290.1 2.6 fusion.290
  303.7 3.6 convolution_convert_fusion.8
  310.8 7.0 %collective-permute-done.29 = bf16[1024,384]{1,0:T(8,128)(2,1)} collective-permute-done((bf16[1024,384]{1,0:T(8,128)(2,1)}, bf16[1024,384]{1,0:T(8,128)(2,1)}, u32[]{:S(2)}, u32[]{:S(2)}) %collective-permute-start.29) | collective-permute-done | bytes 786464 | tf_op jit(solution)/shard_map/ppermute | solution.py:49
  320.5 3.7 fusion.78
  326.8 9.1 %multiply_convert_fusion.3 = bf16[1024,768]{1,0:T(8,128)(2,1)S(1)} fusion(f32[1024,768]{1,0:T(8,128)} %get-tuple-element.230, f32[1024]{0:T(1024)S(1)} %bitcast.490, f32[1024,384]{1,0:T(8,128)S(1)} %convert_multiply_fusion.14, f32[1024,384]{1,0:T(8,128)S(1)} %get-tuple-element.88, f32[768]{0:T(1024)S(1)} %copy-done.114, ...), kind=kOutput, calls=%fused_computation.97 | convolution fusion | flops 3242459136 | bytes 15211520 | tf_op jit(solution)/shard_map/dot_general | solution.py:15
  341.1 3.8 fusion.95
  344.9 4.1 fusion.125
  351.9 23.1 %fusion.6 = f32[768,8,128]{2,1,0:T(8,128)} fusion(bf16[768,8,128]{2,1,0:T(8,128)(2,1)} %bitcast.435, bf16[768,128,64]{2,1,0:T(8,128)(2,1)} %get-tuple-element.193, bf16[768,128,64]{2,1,0:T(8,128)(2,1)} %get-tuple-element.192), kind=kOutput, calls=%fused_computation.13 | convolution fusion | flops 251658240 | bytes 29884416 | tf_op jit(solution)/shard_map/dot_general | solution.py:137
  376.0 3.0 fusion.257
  380.6 2.8 convolution_convert_fusion
  383.5 6.3 collective-permute-done.34
  395.1 3.9 multiply_convert_fusion.10
  420.8 3.1 convolution_convert_fusion.9
  424.5 21.7 %collective-permute-done.48 = bf16[2,2,1,288,384]{4,3,2,1,0:T(8,128)(2,1)S(1)} collective-permute-done((bf16[2,2,1,288,384]{4,3,2,1,0:T(8,128)(2,1)S(1)}, bf16[2,2,1,288,384]{4,3,2,1,0:T(8,128)(2,1)S(1)}, u32[]{:S(2)}, u32[]{:S(2)}) %collective-permute-start.48) | collective-permute-done | bytes 884768 | tf_op jit(solution)/shard_map/ppermute | solution.py:84
  446.5 4.0 collective-permute-start.49
  453.4 16.5 %collective-permute-done.49 = bf16[2,1,1,288,384]{4,3,2,1,0:T(8,128)(2,1)S(1)} collective-permute-done((bf16[2,1,1,288,384]{4,3,2,1,0:T(8,128)(2,1)S(1)}, bf16[2,1,1,288,384]{4,3,2,1,0:T(8,128)(2,1)S(1)}, u32[]{:S(2)}, u32[]{:S(2)}) %collective-permute-start.49) | collective-permute-done | bytes 442400 | tf_op jit(solution)/shard_map/ppermute | solution.py:84
  474.0 8.3 %collective-permute-done.50 = bf16[1,1,1,288,384]{4,3,2,1,0:T(8,128)(2,1)S(1)} collective-permute-done((bf16[1,1,1,288,384]{4,3,2,1,0:T(8,128)(2,1)S(1)}, bf16[1,1,1,288,384]{4,3,2,1,0:T(8,128)(2,1)S(1)}, u32[]{:S(2)}, u32[]{:S(2)}) %collective-permute-start.50) | collective-permute-done | bytes 221216 | tf_op jit(solution)/shard_map/ppermute | solution.py:84
  483.8 2.8 convert_multiply_fusion.13
  489.1 3.7 fusion.80
  492.9 3.3 add_convert_fusion.1
  496.5 5.4 fusion.98
  502.9 8.5 %fusion.122 = bf16[96,8,8,128]{3,1,2,0:T(8,128)(2,1)S(1)} fusion(f32[768,1024]{1,0:T(8,128)} %fusion.98, bf16[1024,1024]{1,0:T(8,128)(2,1)} %constant.205, f32[2048,768]{1,0:T(8,128)} %copy-done.9, f32[768]{0:T(1024)S(1)} %copy-done.98, f32[2048,768]{1,0:T(8,128)} %copy-done.7), kind=kOutput, calls=%fused_computation.194 | convolution fusion | flops 1618477056 | bytes 16256000 | tf_op jit(solution)/shard_map/dot_general | solution.py:15
  513.1 21.4 %fusion.2 = f32[768,8,128]{2,1,0:T(8,128)S(1)} fusion(bf16[768,8,128]{2,1,0:T(8,128)(2,1)} %bitcast.436, bf16[768,128,64]{2,1,0:T(8,128)(2,1)} %get-tuple-element.195, bf16[768,128,64]{2,1,0:T(8,128)(2,1)} %get-tuple-element.194), kind=kOutput, calls=%fused_computation.9 | convolution fusion | flops 251658240 | bytes 29884416 | tf_op jit(solution)/shard_map/dot_general | solution.py:137
  534.5 7.4 %fusion.43 = (f32[768,64]{1,0:T(8,128)}, f32[768,64]{1,0:T(8,128)}, f32[768,64]{1,0:T(8,128)}, f32[768,64]{1,0:T(8,128)}) fusion(f32[768,8,128]{2,1,0:T(8,128)S(1)} %fusion.2, f32[8]{0:T(128)S(1)} %copy-done.120, f32[768,64]{1,0:T(8,128)S(1)} %bitcast.398, f32[768,8,128]{2,1,0:T(8,128)S(1)} %copy-done.2, f32[768,64]{1,0:T(8,128)} %bitcast.401), kind=kLoop, calls=%fused_computation.66 | loop fusion | flops 5308416 | bytes 7471136 | tf_op jit(solution)/shard_map/reduce_sum | solution.py:142
  554.4 9.7 %multiply_convert_fusion.2 = bf16[1024,768]{1,0:T(8,128)(2,1)S(1)} fusion(f32[1024,768]{1,0:T(8,128)} %get-tuple-element.222, f32[1024]{0:T(1024)} %bitcast.487, f32[1024,384]{1,0:T(8,128)S(1)} %convert_multiply_fusion.12, f32[1024,384]{1,0:T(8,128)S(1)} %get-tuple-element.83, f32[768]{0:T(1024)} %mul.652, bf16[2048,1024]{0,1:T(8,128)(2,1)} %bitcast_select_fusion, ...), kind=kOutput, calls=%fused_computation.93 | convolution fusion | flops 3242459136 | bytes 15211520 | tf_op jit(solution)/shard_map/dot_general | solution.py:15
  565.7 2.7 fusion.291
  571.8 2.7 convolution_convert_fusion.1
  578.7 2.8 collective-permute-done.54
  582.0 4.4 collective-permute-done.55
  605.1 4.2 all-to-all-start.3
  611.7 4.7 all-to-all-done.3
  622.0 3.6 all-to-all-start.2
  625.6 5.1 collective-permute-done.42
  634.4 5.9 collective-permute-done.43
  640.5 8.5 %collective-permute-done.46 = bf16[1,1,2,144,384]{4,3,2,1,0:T(8,128)(2,1)S(1)} collective-permute-done((bf16[1,1,2,144,384]{4,3,2,1,0:T(8,128)(2,1)S(1)}, bf16[1,1,2,144,384]{4,3,2,1,0:T(8,128)(2,1)S(1)}, u32[]{:S(2)}, u32[]{:S(2)}) %collective-permute-start.46) | collective-permute-done | bytes 221216 | tf_op jit(solution)/shard_map/ppermute | solution.py:84
  650.7 3.2 collective-permute-done.47
  654.8 3.5 all-to-all-start.1
  661.1 4.4 all-to-all-done.1
  (699 shorter events, 223.7 us)
Async XLA Ops:
  7.2 226.4 %collective-permute-start.24 = (bf16[256,768]{1,0:T(8,128)(2,1)}, bf16[256,768]{1,0:T(8,128)(2,1)}, u32[]{:S(2)}, u32[]{:S(2)}) collective-permute-start(bf16[256,768]{1,0:T(8,128)(2,1)} %param.17), channel_id=1, source_target_pairs={{0,1},{1,0},{2,3},{3,2},{4,5},{5,4},{6,7},{7,6},{8,9},{9,8},{10,11... | collective-permute-start | bytes 1179656 | tf_op jit(solution)/shard_map/ppermute | solution.py:37
  7.7 225.2 %collective-permute-start.25 = (bf16[256,768]{1,0:T(8,128)(2,1)}, bf16[256,768]{1,0:T(8,128)(2,1)}, u32[]{:S(2)}, u32[]{:S(2)}) collective-permute-start(bf16[256,768]{1,0:T(8,128)(2,1)} %param.17), channel_id=1, source_target_pairs={{0,2},{1,3},{2,0},{3,1},{4,6},{5,7},{6,4},{7,5},{8,10},{9,11},{10,... | collective-permute-start | bytes 1179656 | tf_op jit(solution)/shard_map/ppermute | solution.py:37
  16.4 25.1 %all-to-all-start = ((bf16[4,256,384]{2,1,0:T(8,128)(2,1)}), bf16[4,256,384]{2,1,0:T(8,128)(2,1)S(1)}, u32[]{:S(2)}, u32[]{:S(2)}) async-start(bf16[4,256,384]{2,1,0:T(8,128)(2,1)} %pad_maximum_fusion.13), calls=%async_computation | async-start | bytes 1572864 | tf_op jit(solution)/shard_map/all_to_all | solution.py:272
  20.0 147.8 %all-gather.5.cloned.1.call-start = ((), (), s32[]{:S(2)}) async-start(), calls=%async_computation.6 | async-start | bytes 1990656 | tf_op jit(solution)/shard_map/all_gather | solution.py:277
  42.3 9.8 %collective-permute-start = (bf16[176,384]{1,0:T(8,128)(2,1)S(1)}, bf16[176,384]{1,0:T(8,128)(2,1)S(1)}, u32[]{:S(2)}, u32[]{:S(2)}) collective-permute-start(bf16[176,384]{1,0:T(8,128)(2,1)S(1)} %slice.710), channel_id=1, source_target_pairs={{0,16},{4,20},{8,24},{12,28},{16,0},{20,4},{24,8},{28,12},{1,17},{... | collective-permute-start | bytes 405512 | tf_op jit(solution)/shard_map/ppermute | solution.py:66
  52.1 8.1 %collective-permute-start.3 = (bf16[176,384]{1,0:T(8,128)(2,1)S(1)}, bf16[176,384]{1,0:T(8,128)(2,1)S(1)}, u32[]{:S(2)}, u32[]{:S(2)}) collective-permute-start(bf16[176,384]{1,0:T(8,128)(2,1)S(1)} %get-tuple-element.204), channel_id=1, source_target_pairs={{0,4},{4,0},{8,12},{12,8},{16,20},{20,16},{24,28},{28,24},{1,5},{5... | collective-permute-start | bytes 405512 | tf_op jit(solution)/shard_map/ppermute | solution.py:66
  59.5 13.2 %collective-permute-start.1 = (bf16[2,176,384]{2,1,0:T(8,128)(2,1)S(1)}, bf16[2,176,384]{2,1,0:T(8,128)(2,1)S(1)}, u32[]{:S(2)}, u32[]{:S(2)}) collective-permute-start(bf16[2,176,384]{2,1,0:T(8,128)(2,1)S(1)} %pad_maximum_fusion.39), channel_id=1, source_target_pairs={{0,8},{4,12},{8,0},{12,4},{16,24},{20,28},{24,16},{28,20},{1,9},{5... | collective-permute-start | bytes 811016 | tf_op jit(solution)/shard_map/ppermute | solution.py:66
  60.3 15.4 %collective-permute-start.4 = (bf16[2,176,384]{2,1,0:T(8,128)(2,1)S(1)}, bf16[2,176,384]{2,1,0:T(8,128)(2,1)S(1)}, u32[]{:S(2)}, u32[]{:S(2)}) collective-permute-start(bf16[2,176,384]{2,1,0:T(8,128)(2,1)S(1)} %pad_maximum_fusion.40), channel_id=1, source_target_pairs={{0,16},{4,20},{8,24},{12,28},{16,0},{20,4},{24,8},{28,12},{1,17},{... | collective-permute-start | bytes 811016 | tf_op jit(solution)/shard_map/ppermute | solution.py:66
  73.7 12.9 %collective-permute-start.2 = (bf16[2,2,176,384]{3,2,1,0:T(8,128)(2,1)}, bf16[2,2,176,384]{3,2,1,0:T(8,128)(2,1)}, u32[]{:S(2)}, u32[]{:S(2)}) collective-permute-start(bf16[2,2,176,384]{3,2,1,0:T(8,128)(2,1)} %pad_maximum_fusion.29), channel_id=1, source_target_pairs={{0,4},{4,0},{8,12},{12,8},{16,20},{20,16},{24,28},{28,24},{1,5},{5... | collective-permute-start | bytes 1622024 | tf_op jit(solution)/shard_map/ppermute | solution.py:66
  76.7 12.1 %collective-permute-start.5 = (bf16[2,2,176,384]{3,2,1,0:T(8,128)(2,1)}, bf16[2,2,176,384]{3,2,1,0:T(8,128)(2,1)}, u32[]{:S(2)}, u32[]{:S(2)}) collective-permute-start(bf16[2,2,176,384]{3,2,1,0:T(8,128)(2,1)} %pad_maximum_fusion.30), channel_id=1, source_target_pairs={{0,8},{4,12},{8,0},{12,4},{16,24},{20,28},{24,16},{28,20},{1,9},{5... | collective-permute-start | bytes 1622024 | tf_op jit(solution)/shard_map/ppermute | solution.py:66
  91.6 8.7 %collective-permute-start.7 = (bf16[256,768]{1,0:T(8,128)(2,1)S(1)}, bf16[256,768]{1,0:T(8,128)(2,1)}, u32[]{:S(2)}, u32[]{:S(2)}) collective-permute-start(bf16[256,768]{1,0:T(8,128)(2,1)S(1)} %fusion.145), channel_id=1, source_target_pairs={{0,2},{1,3},{2,0},{3,1},{4,6},{5,7},{6,4},{7,5},{8,10},{9,11},{10,... | collective-permute-start | bytes 1179656 | tf_op jit(solution)/shard_map/ppermute | solution.py:37
  99.1 6.3 collective-permute-start.6
  100.3 5.1 collective-permute-start.8
  103.0 131.7 %all-gather.7.cloned.1.call-start = ((), (), s32[]{:S(2)}) async-start(), calls=%async_computation.7 | async-start | bytes 3981312 | tf_op jit(solution)/shard_map/all_gather | solution.py:277
  125.3 36.3 %collective-permute-start.10 = (bf16[1024,384]{1,0:T(8,128)(2,1)S(1)}, bf16[1024,384]{1,0:T(8,128)(2,1)S(1)}, u32[]{:S(2)}, u32[]{:S(2)}) collective-permute-start(bf16[1024,384]{1,0:T(8,128)(2,1)S(1)} %fusion.107), channel_id=1, source_target_pairs={{0,2},{1,3},{2,0},{3,1},{4,6},{5,7},{6,4},{7,5},{8,10},{9,11},{10,... | collective-permute-start | bytes 2359304 | tf_op jit(solution)/shard_map/ppermute | solution.py:37
  126.9 38.5 %collective-permute-start.9 = (bf16[1024,384]{1,0:T(8,128)(2,1)S(1)}, bf16[1024,384]{1,0:T(8,128)(2,1)}, u32[]{:S(2)}, u32[]{:S(2)}) collective-permute-start(bf16[1024,384]{1,0:T(8,128)(2,1)S(1)} %fusion.107), channel_id=1, source_target_pairs={{0,1},{1,0},{2,3},{3,2},{4,5},{5,4},{6,7},{7,6},{8,9},{9,8},{10,11... | collective-permute-start | bytes 2359304 | tf_op jit(solution)/shard_map/ppermute | solution.py:37
  161.5 455.1 %reduce-scatter.2.cloned.1.call-start = ((), (), s32[]{:S(2)}) async-start(), calls=%async_computation.5 | async-start | bytes 3981312 | tf_op jit(solution)/shard_map/reduce_scatter | solution.py:374
  161.6 6.1 collective-permute-start.11
  180.9 22.0 %collective-permute-start.13 = (bf16[256,768]{1,0:T(8,128)(2,1)S(1)}, bf16[256,768]{1,0:T(8,128)(2,1)S(1)}, u32[]{:S(2)}, u32[]{:S(2)}) collective-permute-start(bf16[256,768]{1,0:T(8,128)(2,1)S(1)} %get-tuple-element.124), channel_id=1, source_target_pairs={{0,1},{1,0},{2,3},{3,2},{4,5},{5,4},{6,7},{7,6},{8,9},{9,8},{10,11... | collective-permute-start | bytes 1179656 | tf_op jit(solution)/shard_map/ppermute | solution.py:49
  202.5 15.4 %collective-permute-start.12 = (bf16[256,768]{1,0:T(8,128)(2,1)S(1)}, bf16[256,768]{1,0:T(8,128)(2,1)S(1)}, u32[]{:S(2)}, u32[]{:S(2)}) collective-permute-start(bf16[256,768]{1,0:T(8,128)(2,1)S(1)} %get-tuple-element.123), channel_id=1, source_target_pairs={{0,1},{1,0},{2,3},{3,2},{4,5},{5,4},{6,7},{7,6},{8,9},{9,8},{10,11... | collective-permute-start | bytes 1179656 | tf_op jit(solution)/shard_map/ppermute | solution.py:49
  204.0 13.8 %collective-permute-start.14 = (bf16[256,768]{1,0:T(8,128)(2,1)S(1)}, bf16[256,768]{1,0:T(8,128)(2,1)S(1)}, u32[]{:S(2)}, u32[]{:S(2)}) collective-permute-start(bf16[256,768]{1,0:T(8,128)(2,1)S(1)} %fusion.159), channel_id=1, source_target_pairs={{0,2},{1,3},{2,0},{3,1},{4,6},{5,7},{6,4},{7,5},{8,10},{9,11},{10,... | collective-permute-start | bytes 1179656 | tf_op jit(solution)/shard_map/ppermute | solution.py:49
  220.6 13.0 %collective-permute-start.16 = (bf16[256,768]{1,0:T(8,128)(2,1)}, bf16[256,768]{1,0:T(8,128)(2,1)}, u32[]{:S(2)}, u32[]{:S(2)}) collective-permute-start(bf16[256,768]{1,0:T(8,128)(2,1)} %add_convert_fusion.12), channel_id=1, source_target_pairs={{0,2},{1,3},{2,0},{3,1},{4,6},{5,7},{6,4},{7,5},{8,10},{9,11},{10,... | collective-permute-start | bytes 1179656 | tf_op jit(solution)/shard_map/ppermute | solution.py:37
  233.0 25.3 %collective-permute-start.26 = (bf16[256,768]{1,0:T(8,128)(2,1)}, bf16[256,768]{1,0:T(8,128)(2,1)S(1)}, u32[]{:S(2)}, u32[]{:S(2)}) collective-permute-start(bf16[256,768]{1,0:T(8,128)(2,1)} %collective-permute-done.25), channel_id=1, source_target_pairs={{0,1},{1,0},{2,3},{3,2},{4,5},{5,4},{6,7},{7,6},{8,9},{9,8},{10,11... | collective-permute-start | bytes 1179656 | tf_op jit(solution)/shard_map/ppermute | solution.py:37
  233.0 3.5 collective-permute-start.15
  233.5 3.0 collective-permute-start.17
  256.4 20.0 %collective-permute-start.19 = (bf16[1024,384]{1,0:T(8,128)(2,1)S(1)}, bf16[1024,384]{1,0:T(8,128)(2,1)S(1)}, u32[]{:S(2)}, u32[]{:S(2)}) collective-permute-start(bf16[1024,384]{1,0:T(8,128)(2,1)S(1)} %fusion.106), channel_id=1, source_target_pairs={{0,2},{1,3},{2,0},{3,1},{4,6},{5,7},{6,4},{7,5},{8,10},{9,11},{10,... | collective-permute-start | bytes 2359304 | tf_op jit(solution)/shard_map/ppermute | solution.py:37
  258.5 18.6 %collective-permute-start.18 = (bf16[1024,384]{1,0:T(8,128)(2,1)S(1)}, bf16[1024,384]{1,0:T(8,128)(2,1)S(1)}, u32[]{:S(2)}, u32[]{:S(2)}) collective-permute-start(bf16[1024,384]{1,0:T(8,128)(2,1)S(1)} %fusion.106), channel_id=1, source_target_pairs={{0,1},{1,0},{2,3},{3,2},{4,5},{5,4},{6,7},{7,6},{8,9},{9,8},{10,11... | collective-permute-start | bytes 2359304 | tf_op jit(solution)/shard_map/ppermute | solution.py:37
  276.3 2.3 collective-permute-start.20
  289.5 21.3 %collective-permute-start.27 = (bf16[1024,384]{1,0:T(8,128)(2,1)}, bf16[1024,384]{1,0:T(8,128)(2,1)}, u32[]{:S(2)}, u32[]{:S(2)}) collective-permute-start(bf16[1024,384]{1,0:T(8,128)(2,1)} %pad_maximum_fusion.20), channel_id=1, source_target_pairs={{0,1},{1,0},{2,3},{3,2},{4,5},{5,4},{6,7},{7,6},{8,9},{9,8},{10,11... | collective-permute-start | bytes 2359304 | tf_op jit(solution)/shard_map/ppermute | solution.py:49
  289.7 6.3 collective-permute-start.28
  297.1 20.7 %collective-permute-start.29 = (bf16[1024,384]{1,0:T(8,128)(2,1)}, bf16[1024,384]{1,0:T(8,128)(2,1)}, u32[]{:S(2)}, u32[]{:S(2)}) collective-permute-start(bf16[1024,384]{1,0:T(8,128)(2,1)} %fusion.108), channel_id=1, source_target_pairs={{0,2},{1,3},{2,0},{3,1},{4,6},{5,7},{6,4},{7,5},{8,10},{9,11},{10,... | collective-permute-start | bytes 2359304 | tf_op jit(solution)/shard_map/ppermute | solution.py:49
  299.9 76.1 %collective-permute-start.21 = (bf16[256,768]{1,0:T(8,128)(2,1)}, bf16[256,768]{1,0:T(8,128)(2,1)}, u32[]{:S(2)}, u32[]{:S(2)}) collective-permute-start(bf16[256,768]{1,0:T(8,128)(2,1)} %get-tuple-element.121), channel_id=1, source_target_pairs={{0,1},{1,0},{2,3},{3,2},{4,5},{5,4},{6,7},{7,6},{8,9},{9,8},{10,11... | collective-permute-start | bytes 1179656 | tf_op jit(solution)/shard_map/ppermute | solution.py:49
  299.9 7.4 %collective-permute-start.22 = (bf16[256,768]{1,0:T(8,128)(2,1)S(1)}, bf16[256,768]{1,0:T(8,128)(2,1)S(1)}, u32[]{:S(2)}, u32[]{:S(2)}) collective-permute-start(bf16[256,768]{1,0:T(8,128)(2,1)S(1)} %copy-done.85), channel_id=1, source_target_pairs={{0,1},{1,0},{2,3},{3,2},{4,5},{5,4},{6,7},{7,6},{8,9},{9,8},{10,11... | collective-permute-start | bytes 1179656 | tf_op jit(solution)/shard_map/ppermute | solution.py:49
  309.1 66.9 %collective-permute-start.23 = (bf16[256,768]{1,0:T(8,128)(2,1)S(1)}, bf16[256,768]{1,0:T(8,128)(2,1)}, u32[]{:S(2)}, u32[]{:S(2)}) collective-permute-start(bf16[256,768]{1,0:T(8,128)(2,1)S(1)} %fusion.156), channel_id=1, source_target_pairs={{0,2},{1,3},{2,0},{3,1},{4,6},{5,7},{6,4},{7,5},{8,10},{9,11},{10,... | collective-permute-start | bytes 1179656 | tf_op jit(solution)/shard_map/ppermute | solution.py:49
  340.3 34.6 %collective-permute-start.30 = (bf16[256,768]{1,0:T(8,128)(2,1)}, bf16[256,768]{1,0:T(8,128)(2,1)S(1)}, u32[]{:S(2)}, u32[]{:S(2)}) collective-permute-start(bf16[256,768]{1,0:T(8,128)(2,1)} %get-tuple-element.117), channel_id=1, source_target_pairs={{0,1},{1,0},{2,3},{3,2},{4,5},{5,4},{6,7},{7,6},{8,9},{9,8},{10,11... | collective-permute-start | bytes 1179656 | tf_op jit(solution)/shard_map/ppermute | solution.py:49
  340.3 10.3 %collective-permute-start.31 = (bf16[256,768]{1,0:T(8,128)(2,1)S(1)}, bf16[256,768]{1,0:T(8,128)(2,1)S(1)}, u32[]{:S(2)}, u32[]{:S(2)}) collective-permute-start(bf16[256,768]{1,0:T(8,128)(2,1)S(1)} %get-tuple-element.118), channel_id=1, source_target_pairs={{0,1},{1,0},{2,3},{3,2},{4,5},{5,4},{6,7},{7,6},{8,9},{9,8},{10,11... | collective-permute-start | bytes 1179656 | tf_op jit(solution)/shard_map/ppermute | solution.py:49
  351.4 23.5 %collective-permute-start.32 = (bf16[256,768]{1,0:T(8,128)(2,1)}, bf16[256,768]{1,0:T(8,128)(2,1)S(1)}, u32[]{:S(2)}, u32[]{:S(2)}) collective-permute-start(bf16[256,768]{1,0:T(8,128)(2,1)} %fusion.154), channel_id=1, source_target_pairs={{0,2},{1,3},{2,0},{3,1},{4,6},{5,7},{6,4},{7,5},{8,10},{9,11},{10,... | collective-permute-start | bytes 1179656 | tf_op jit(solution)/shard_map/ppermute | solution.py:49
  379.0 10.8 %collective-permute-start.34 = (bf16[256,768]{1,0:T(8,128)(2,1)}, bf16[256,768]{1,0:T(8,128)(2,1)}, u32[]{:S(2)}, u32[]{:S(2)}) collective-permute-start(bf16[256,768]{1,0:T(8,128)(2,1)} %get-tuple-element.85), channel_id=1, source_target_pairs={{0,2},{1,3},{2,0},{3,1},{4,6},{5,7},{6,4},{7,5},{8,10},{9,11},{10,... | collective-permute-start | bytes 1179656 | tf_op jit(solution)/shard_map/ppermute | solution.py:37
  383.4 11.3 %collective-permute-start.33 = (bf16[256,768]{1,0:T(8,128)(2,1)}, bf16[256,768]{1,0:T(8,128)(2,1)}, u32[]{:S(2)}, u32[]{:S(2)}) collective-permute-start(bf16[256,768]{1,0:T(8,128)(2,1)} %get-tuple-element.85), channel_id=1, source_target_pairs={{0,1},{1,0},{2,3},{3,2},{4,5},{5,4},{6,7},{7,6},{8,9},{9,8},{10,11... | collective-permute-start | bytes 1179656 | tf_op jit(solution)/shard_map/ppermute | solution.py:37
  389.8 4.9 collective-permute-start.35
  418.7 27.5 %collective-permute-start.48 = (bf16[2,2,1,288,384]{4,3,2,1,0:T(8,128)(2,1)S(1)}, bf16[2,2,1,288,384]{4,3,2,1,0:T(8,128)(2,1)S(1)}, u32[]{:S(2)}, u32[]{:S(2)}) collective-permute-start(bf16[2,2,1,288,384]{4,3,2,1,0:T(8,128)(2,1)S(1)} %fusion.142), channel_id=1, source_target_pairs={{0,4},{4,0},{8,12},{12,8},{16,20},{20,16},{24,28},{28,24},{1,5},{5... | collective-permute-start | bytes 2654216 | tf_op jit(solution)/shard_map/ppermute | solution.py:84
  420.1 63.7 %collective-permute-start.36 = (bf16[1024,384]{1,0:T(8,128)(2,1)}, bf16[1024,384]{1,0:T(8,128)(2,1)}, u32[]{:S(2)}, u32[]{:S(2)}) collective-permute-start(bf16[1024,384]{1,0:T(8,128)(2,1)} %pad_maximum_fusion.22), channel_id=1, source_target_pairs={{0,1},{1,0},{2,3},{3,2},{4,5},{5,4},{6,7},{7,6},{8,9},{9,8},{10,11... | collective-permute-start | bytes 2359304 | tf_op jit(solution)/shard_map/ppermute | solution.py:49
  420.4 30.2 %collective-permute-start.37 = (bf16[1024,384]{1,0:T(8,128)(2,1)S(1)}, bf16[1024,384]{1,0:T(8,128)(2,1)S(1)}, u32[]{:S(2)}, u32[]{:S(2)}) collective-permute-start(bf16[1024,384]{1,0:T(8,128)(2,1)S(1)} %pad_maximum_fusion.23), channel_id=1, source_target_pairs={{0,1},{1,0},{2,3},{3,2},{4,5},{5,4},{6,7},{7,6},{8,9},{9,8},{10,11... | collective-permute-start | bytes 2359304 | tf_op jit(solution)/shard_map/ppermute | solution.py:49
  446.5 23.4 %collective-permute-start.49 = (bf16[2,1,1,288,384]{4,3,2,1,0:T(8,128)(2,1)S(1)}, bf16[2,1,1,288,384]{4,3,2,1,0:T(8,128)(2,1)S(1)}, u32[]{:S(2)}, u32[]{:S(2)}) collective-permute-start(bf16[2,1,1,288,384]{4,3,2,1,0:T(8,128)(2,1)S(1)} %constant_dynamic-slice_fusion.4), channel_id=1, source_target_pairs={{0,8},{4,12},{8,0},{12,4},{16,24},{20,28},{24,16},{28,20},{1,9},{5... | collective-permute-start | bytes 1327112 | tf_op jit(solution)/shard_map/ppermute | solution.py:84
  451.7 32.1 %collective-permute-start.38 = (bf16[1024,384]{1,0:T(8,128)(2,1)}, bf16[1024,384]{1,0:T(8,128)(2,1)}, u32[]{:S(2)}, u32[]{:S(2)}) collective-permute-start(bf16[1024,384]{1,0:T(8,128)(2,1)} %fusion.109), channel_id=1, source_target_pairs={{0,2},{1,3},{2,0},{3,1},{4,6},{5,7},{6,4},{7,5},{8,10},{9,11},{10,... | collective-permute-start | bytes 2359304 | tf_op jit(solution)/shard_map/ppermute | solution.py:49
  470.1 12.2 %collective-permute-start.50 = (bf16[1,1,1,288,384]{4,3,2,1,0:T(8,128)(2,1)S(1)}, bf16[1,1,1,288,384]{4,3,2,1,0:T(8,128)(2,1)S(1)}, u32[]{:S(2)}, u32[]{:S(2)}) collective-permute-start(bf16[1,1,1,288,384]{4,3,2,1,0:T(8,128)(2,1)S(1)} %constant_dynamic-slice_fusion.3), channel_id=1, source_target_pairs={{0,16},{4,20},{8,24},{12,28},{16,0},{20,4},{24,8},{28,12},{1,17},{... | collective-permute-start | bytes 663560 | tf_op jit(solution)/shard_map/ppermute | solution.py:84
  553.7 11.8 %collective-permute-start.51 = (bf16[2,2,1,208,128]{4,3,2,1,0:T(8,128)(2,1)S(1)}, bf16[2,2,1,208,128]{4,3,2,1,0:T(8,128)(2,1)S(1)}, u32[]{:S(2)}, u32[]{:S(2)}) collective-permute-start(bf16[2,2,1,208,128]{4,3,2,1,0:T(8,128)(2,1)S(1)} %constant_dynamic-slice_fusion.2), channel_id=1, source_target_pairs={{0,4},{4,0},{8,12},{12,8},{16,20},{20,16},{24,28},{28,24},{1,5},{5... | collective-permute-start | bytes 638984 | tf_op jit(solution)/shard_map/ppermute | solution.py:84
  565.6 4.8 collective-permute-start.52
  570.5 5.4 collective-permute-start.53
  575.9 5.7 collective-permute-start.54
  578.2 24.1 %collective-permute-start.39 = (bf16[256,768]{1,0:T(8,128)(2,1)}, bf16[256,768]{1,0:T(8,128)(2,1)}, u32[]{:S(2)}, u32[]{:S(2)}) collective-permute-start(bf16[256,768]{1,0:T(8,128)(2,1)} %get-tuple-element.113), channel_id=1, source_target_pairs={{0,1},{1,0},{2,3},{3,2},{4,5},{5,4},{6,7},{7,6},{8,9},{9,8},{10,11... | collective-permute-start | bytes 1179656 | tf_op jit(solution)/shard_map/ppermute | solution.py:49
  578.2 9.7 %collective-permute-start.40 = (bf16[256,768]{1,0:T(8,128)(2,1)S(1)}, bf16[256,768]{1,0:T(8,128)(2,1)S(1)}, u32[]{:S(2)}, u32[]{:S(2)}) collective-permute-start(bf16[256,768]{1,0:T(8,128)(2,1)S(1)} %get-tuple-element.114), channel_id=1, source_target_pairs={{0,1},{1,0},{2,3},{3,2},{4,5},{5,4},{6,7},{7,6},{8,9},{9,8},{10,11... | collective-permute-start | bytes 1179656 | tf_op jit(solution)/shard_map/ppermute | solution.py:49
  581.6 4.8 collective-permute-start.55
  586.4 5.9 collective-permute-start.56
  589.8 12.4 %collective-permute-start.41 = (bf16[256,768]{1,0:T(8,128)(2,1)}, bf16[256,768]{1,0:T(8,128)(2,1)}, u32[]{:S(2)}, u32[]{:S(2)}) collective-permute-start(bf16[256,768]{1,0:T(8,128)(2,1)} %fusion.152), channel_id=1, source_target_pairs={{0,2},{1,3},{2,0},{3,1},{4,6},{5,7},{6,4},{7,5},{8,10},{9,11},{10,... | collective-permute-start | bytes 1179656 | tf_op jit(solution)/shard_map/ppermute | solution.py:49
  605.1 11.3 %all-to-all-start.3 = ((f32[32,1,96]{2,1,0:T(1,128)}), f32[32,1,96]{2,1,0:T(1,128)S(1)}, u32[]{:S(2)}, u32[]{:S(2)}) async-start(f32[32,1,96]{2,1,0:T(1,128)} %bitcast.124), calls=%async_computation.4 | async-start | bytes 32768 | tf_op jit(solution)/shard_map/all_to_all | solution.py:403
  618.5 12.3 %collective-permute-start.42 = (bf16[2,2,1,144,384]{4,3,2,1,0:T(8,128)(2,1)}, bf16[2,2,1,144,384]{4,3,2,1,0:T(8,128)(2,1)}, u32[]{:S(2)}, u32[]{:S(2)}) collective-permute-start(bf16[2,2,1,144,384]{4,3,2,1,0:T(8,128)(2,1)} %constant_dynamic-slice_fusion.10), channel_id=1, source_target_pairs={{0,4},{4,0},{8,12},{12,8},{16,20},{20,16},{24,28},{28,24},{1,5},{5... | collective-permute-start | bytes 1327112 | tf_op jit(solution)/shard_map/ppermute | solution.py:84
  620.6 11.9 %collective-permute-start.45 = (bf16[2,1,2,144,384]{4,3,2,1,0:T(8,128)(2,1)}, bf16[2,1,2,144,384]{4,3,2,1,0:T(8,128)(2,1)}, u32[]{:S(2)}, u32[]{:S(2)}) collective-permute-start(bf16[2,1,2,144,384]{4,3,2,1,0:T(8,128)(2,1)} %constant_dynamic-slice_fusion.7), channel_id=1, source_target_pairs={{0,8},{4,12},{8,0},{12,4},{16,24},{20,28},{24,16},{28,20},{1,9},{5... | collective-permute-start | bytes 1327112 | tf_op jit(solution)/shard_map/ppermute | solution.py:84
  622.0 32.8 %all-to-all-start.2 = ((bf16[4,120,384]{2,1,0:T(8,128)(2,1)}), bf16[4,120,384]{2,1,0:T(8,128)(2,1)S(1)}, u32[]{:S(2)}, u32[]{:S(2)}) async-start(bf16[4,120,384]{2,1,0:T(8,128)(2,1)} %pad_maximum_fusion.38), calls=%async_computation.3 | async-start | bytes 737280 | tf_op jit(solution)/shard_map/all_to_all | solution.py:389
  631.9 8.5 %collective-permute-start.43 = (bf16[2,1,1,144,384]{4,3,2,1,0:T(8,128)(2,1)S(1)}, bf16[2,1,1,144,384]{4,3,2,1,0:T(8,128)(2,1)S(1)}, u32[]{:S(2)}, u32[]{:S(2)}) collective-permute-start(bf16[2,1,1,144,384]{4,3,2,1,0:T(8,128)(2,1)S(1)} %constant_dynamic-slice_fusion.9), channel_id=1, source_target_pairs={{0,8},{4,12},{8,0},{12,4},{16,24},{20,28},{24,16},{28,20},{1,9},{5... | collective-permute-start | bytes 663560 | tf_op jit(solution)/shard_map/ppermute | solution.py:84
  633.7 15.3 %collective-permute-start.46 = (bf16[1,1,2,144,384]{4,3,2,1,0:T(8,128)(2,1)S(1)}, bf16[1,1,2,144,384]{4,3,2,1,0:T(8,128)(2,1)S(1)}, u32[]{:S(2)}, u32[]{:S(2)}) collective-permute-start(bf16[1,1,2,144,384]{4,3,2,1,0:T(8,128)(2,1)S(1)} %constant_dynamic-slice_fusion.6), channel_id=1, source_target_pairs={{0,16},{4,20},{8,24},{12,28},{16,0},{20,4},{24,8},{28,12},{1,17},{... | collective-permute-start | bytes 663560 | tf_op jit(solution)/shard_map/ppermute | solution.py:84
  640.4 10.2 %collective-permute-start.44 = (bf16[1,1,1,144,384]{4,3,2,1,0:T(8,128)(2,1)S(1)}, bf16[1,1,1,144,384]{4,3,2,1,0:T(8,128)(2,1)S(1)}, u32[]{:S(2)}, u32[]{:S(2)}) collective-permute-start(bf16[1,1,1,144,384]{4,3,2,1,0:T(8,128)(2,1)S(1)} %constant_dynamic-slice_fusion.8), channel_id=1, source_target_pairs={{0,16},{4,20},{8,24},{12,28},{16,0},{20,4},{24,8},{28,12},{1,17},{... | collective-permute-start | bytes 331784 | tf_op jit(solution)/shard_map/ppermute | solution.py:84
  649.1 4.8 collective-permute-start.47
  654.8 10.6 %all-to-all-start.1 = ((bf16[4,120,384]{2,1,0:T(8,128)(2,1)}), bf16[4,120,384]{2,1,0:T(8,128)(2,1)S(1)}, u32[]{:S(2)}, u32[]{:S(2)}) async-start(bf16[4,120,384]{2,1,0:T(8,128)(2,1)} %pad_maximum_fusion.37), calls=%async_computation.2 | async-start | bytes 737280 | tf_op jit(solution)/shard_map/all_to_all | solution.py:389
  (142 other events, 1216.5 us)
Sparse Core Ops, SparseCore 0:
  103.1 47.0 all-gather.4
  161.6 65.1 all-gather.6
  417.0 91.2 reduce-scatter.1

commit v3 on v1

v3 whole, which is shorter than its diff:
```python
from functools import partial

import numpy as np

import jax
import jax.numpy as jnp
from jax import lax
from jax.experimental import pallas as pl
from jax.experimental.layout import Layout, with_layout_constraint
from jax.experimental.pallas import tpu as pltpu
from jax.sharding import PartitionSpec as P

EPSILON = 1e-05
BF = jnp.bfloat16
F32 = jnp.float32
LANES = 128
VMEM_BYTES = 56 * 2**20


def dot(left, right, left_dim, right_dim):
    return lax.dot_general(
        left, right, (((left_dim,), (right_dim,)), ((), ())), preferred_element_type=F32
    )


def wave_table(length):
    step = np.arange(length, dtype=np.int64)
    phase = ((2 * step[:, None] + 1) * step[None, :]) % (4 * length)
    angle = phase * (np.pi / (2 * length))
    return np.concatenate([np.cos(angle), np.sin(angle)], 0).astype(jnp.bfloat16)


def decay_tiles(rate):
    rows = lax.broadcasted_iota(jnp.int32, (8, LANES), 0).astype(F32)
    tiles = [jnp.exp(-rate * rows)]
    step = jnp.exp(-8.0 * jnp.broadcast_to(rate, (8, LANES)))
    while len(tiles) < LANES // 8:
        tiles = tiles + [tile * step for tile in tiles]
        step = step * step
    return tiles


def block_decays(rate, count):
    starts = lax.broadcasted_iota(jnp.int32, (count, LANES), 0).astype(F32) * float(LANES)
    return starts, jnp.exp(-rate * starts)


def spectra_kernel(unroll, rate_ref, coef_ref, sign_ref, wave_ref, *refs):
    cos_ref, sin_ref, kern_ref, flat_ref = refs[-4:]
    pairs = rate_ref.shape[0]
    length = wave_ref.shape[1]
    count = length // LANES
    lower = lax.broadcasted_iota(jnp.int32, (count, LANES), 1) < LANES // 2

    def pair(step, carry):
        for offset in range(unroll):
            index = step * unroll + offset
            rate = rate_ref[pl.ds(index, 1), :]
            near = jnp.concatenate(decay_tiles(rate), 0).astype(BF)
            far = block_decays(rate, count)[1] * (coef_ref[pl.ds(index, 1), :] * rate)
            left = jnp.concatenate([jnp.where(lower, far, 0.0), jnp.where(lower, 0.0, far)], 0)
            place = pl.ds(pl.multiple_of(index * 2 * count, 2 * count), 2 * count)
            kern_ref[place, :] = dot(left.astype(BF), near, 1, 1)
        return carry

    lax.fori_loop(0, pairs // unroll, pair, 0)
    for part in range(count):
        flat_ref[:, part * LANES : (part + 1) * LANES] = kern_ref[
            pl.ds(part, 2 * pairs, stride=count), :
        ].astype(BF)
    chunk = 256
    for part in range(length // chunk):
        rows = slice(part * chunk, (part + 1) * chunk)
        cos_ref[rows, :] = dot(wave_ref[rows, :], flat_ref[...], 1, 1).astype(BF)
        sines = dot(wave_ref[length + part * chunk : length + (part + 1) * chunk, :], flat_ref[...], 1, 1)
        sin_ref[rows, :] = (sines * sign_ref[...]).astype(BF)


def channel_block(channels):
    return 256 if channels % 256 == 0 else channels


def unroll_of(pairs):
    return 16 if pairs % 16 == 0 else 8


def spectra(coef, rate, sign, wave, part, earlier):
    channels = 2 * coef.shape[0]
    length = wave.shape[1]
    block = channel_block(channels)
    rows = pl.BlockSpec((block // 2, LANES), lambda j: (part, 0))
    lanes = pl.BlockSpec((length, block), lambda j: (0, part))
    shape = jax.ShapeDtypeStruct((length, channels), BF)
    return pl.pallas_call(
        partial(spectra_kernel, unroll_of(block // 2)),
        out_shape=(shape, shape),
        grid=(1,),
        in_specs=[
            rows,
            rows,
            pl.BlockSpec((1, block), lambda j: (0, part)),
            pl.BlockSpec((2 * length, length), lambda j: (0, 0)),
        ]
        + [pl.BlockSpec(memory_space=pl.ANY)] * len(earlier),
        out_specs=(lanes, lanes),
        scratch_shapes=[
            pltpu.VMEM((block * length // LANES, LANES), F32),
            pltpu.VMEM((block, length), BF),
        ],
        input_output_aliases={4 + j: j for j in range(len(earlier))},
        compiler_params=pltpu.CompilerParams(vmem_limit_bytes=VMEM_BYTES),
        cost_estimate=pl.CostEstimate(
            flops=12 * length * length * block,
            bytes_accessed=4 * length * length + 4 * length * block,
            transcendentals=0,
        ),
        name="spectra",
    )(rate, coef, sign, wave, *earlier)


def state_grads_kernel(
    unroll, rate_ref, coef_ref, cos_ref, sin_ref, wave_ref, coef_out, rate_out, turned_ref, kern_ref
):
    pairs = rate_ref.shape[0]
    length = wave_ref.shape[1]
    count = length // LANES
    lower = lax.broadcasted_iota(jnp.int32, (count, LANES), 1) < LANES // 2
    row = lax.broadcasted_iota(jnp.int32, (8, LANES), 0).astype(F32)
    turned_ref[:, :length] = cos_ref[...].T
    turned_ref[:, length:] = sin_ref[...].T
    chunk = 256
    for part in range(length // chunk):
        got = dot(turned_ref[...], wave_ref[:, part * chunk : (part + 1) * chunk], 1, 0)
        for side in range(chunk // LANES):
            place = pl.ds(part * (chunk // LANES) + side, 2 * pairs, stride=count)
            kern_ref[place, :] = got[:, side * LANES : (side + 1) * LANES]

    def pair(step, carry):
        for offset in range(unroll):
            index = step * unroll + offset
            rate = rate_ref[pl.ds(index, 1), :]
            coef = coef_ref[pl.ds(index, 1), :]
            tiles = decay_tiles(rate)
            near = jnp.concatenate(tiles, 0).astype(BF)
            lagged = jnp.concatenate([tile * (row + 8.0 * j) for j, tile in enumerate(tiles)], 0)
            place = pl.ds(pl.multiple_of(index * 2 * count, 2 * count), 2 * count)
            both = jnp.concatenate([near, lagged.astype(BF)], 1)
            got = dot(kern_ref[place, :].astype(BF), both, 1, 0)
            plain = jnp.where(lower, got[:count, :LANES], got[count:, :LANES])
            first = jnp.where(lower, got[:count, LANES:], got[count:, LANES:])
            starts, far = block_decays(rate, count)
            total = jnp.sum(far * plain, axis=0, keepdims=True)
            moment = jnp.sum(far * (starts * plain + first), axis=0, keepdims=True)
            coef_out[pl.ds(index, 1), :] = rate * total * (1.0 / length)
            rate_out[pl.ds(index, 1), :] = coef * (total - rate * moment) * (1.0 / length)
        return carry

    lax.fori_loop(0, pairs // unroll, pair, 0)


def state_grads(coef, rate, cosines, sines, wave):
    channels = 2 * coef.shape[0]
    length = wave.shape[1]
    block = channel_block(channels)
    rows = pl.BlockSpec((block // 2, LANES), lambda j: (j, 0))
    lanes = pl.BlockSpec((length, block), lambda j: (0, j))
    shape = jax.ShapeDtypeStruct(coef.shape, F32)
    return pl.pallas_call(
        partial(state_grads_kernel, unroll_of(block // 2)),
        out_shape=(shape, shape),
        grid=(channels // block,),
        in_specs=[rows, rows, lanes, lanes, pl.BlockSpec((2 * length, length), lambda j: (0, 0))],
        out_specs=(rows, rows),
        scratch_shapes=[
            pltpu.VMEM((block, 2 * length), BF),
            pltpu.VMEM((block * length // LANES, LANES), F32),
        ],
        compiler_params=pltpu.CompilerParams(vmem_limit_bytes=VMEM_BYTES),
        cost_estimate=pl.CostEstimate(
            flops=12 * length * length * channels,
            bytes_accessed=4 * length * length + 4 * length * channels,
            transcendentals=0,
        ),
        name="state_grads",
    )(rate, coef, cosines, sines, wave)


def pairs_of(count, bit):
    return [(i, i ^ bit) for i in range(count)]


def seq_gather(block, count, wait):
    blocks = {0: block}
    bit = count // 2
    while bit:
        for member in list(blocks):
            blocks[member ^ bit] = lax.ppermute(blocks[member], "seq", pairs_of(count, bit))
        if bit == count // 2:
            blocks[bit], wait = together(blocks[bit], wait)
        bit //= 2
    return [blocks[m] for m in range(count)], wait


def seq_rows(block, count, wait):
    whole, wait = gather_bits(block, "seq", count, far_first(count), wait)
    return row_major(whole.reshape(count * block.shape[0], block.shape[1])), wait


def seq_reduce(blocks, count):
    blocks = dict(enumerate(blocks))
    bit = 1
    while bit < count:
        for member in sorted(blocks, reverse=True):
            if member & bit:
                sent = blocks.pop(member).astype(BF)
                came = lax.ppermute(sent, "seq", pairs_of(count, bit))
                blocks[member ^ bit] = blocks[member ^ bit] + came.astype(F32)
        bit *= 2
    return blocks[0]


def seq_reduce_rows(whole, count):
    return reduce_bits(whole.reshape(count, -1, whole.shape[1]), "seq", count, bits_of(count), F32)


def row_major(array):
    return with_layout_constraint(array, Layout(tuple(range(array.ndim))))


def bits_of(count):
    return [1 << j for j in range(count.bit_length() - 1)]


def far_first(count):
    return bits_of(count)[::-1]


def y_first(count):
    return bits_of(count)


def z_first(count):
    return bits_of(count)[1:] + bits_of(count)[:1]


def swap(block, axis, count, bit):
    return lax.ppermute(block, axis, pairs_of(count, bit))


def join(block, other, axis, bit, done):
    upper = (lax.axis_index(axis) & bit) != 0
    pair = [jnp.where(upper, other, block), jnp.where(upper, block, other)]
    return jnp.stack(pair, done.index(bit))


def gather_bits(block, axis, count, sequence, wait=()):
    done = []
    for bit in sequence:
        other = swap(block, axis, count, bit)
        if not done:
            other, wait = together(other, wait)
        done = sorted(done + [bit], reverse=True)
        block = join(block, other, axis, bit, done)
    return block.reshape((count,) + block.shape[len(done) :]), wait


def cut_half(blocks, axis, count, bit):
    level = far_first(count).index(bit)
    side = (lax.axis_index(axis) // bit) % 2
    sent = lax.dynamic_slice_in_dim(blocks, 1 - side, 1, level).astype(BF)
    return lax.dynamic_slice_in_dim(blocks, side, 1, level), sent


def add_half(held, came, kind):
    return (held.astype(F32) + came.astype(F32)).astype(kind)


def bit_blocks(blocks, count):
    return blocks.reshape((2,) * len(bits_of(count)) + blocks.shape[1:])


def reduce_bits(blocks, axis, count, sequence, kind):
    blocks = bit_blocks(blocks, count)
    for bit in sequence:
        held, sent = cut_half(blocks, axis, count, bit)
        blocks = add_half(held, swap(sent, axis, count, bit), kind)
    return blocks.reshape(blocks.shape[len(bits_of(count)) :])


def together(*arrays):
    return lax.optimization_barrier(arrays)


def gelu_parts(pre):
    share = 0.5 * (1.0 + lax.erf(pre * np.float32(np.sqrt(0.5))))
    slope = share + pre * (jnp.exp(-0.5 * pre * pre) * np.float32(1.0 / np.sqrt(2.0 * np.pi)))
    return pre * share, slope


def normalize(stream):
    centre = jnp.mean(stream, axis=-1, keepdims=True)
    centred = stream - centre
    spread = jnp.mean(centred * centred, axis=-1, keepdims=True)
    factor = lax.rsqrt(spread + EPSILON)
    return centred * factor, factor


def turned(spectrum):
    return jnp.stack([-spectrum[1], spectrum[0]])


def run_layer(stream, keep, early, late, hat, skip, tables, count, filler):
    w_value, gain, bias = early
    waves, waves_back = tables
    length = waves.shape[1]
    xhat, factor = normalize(stream)
    own, made = filler[0]((xhat * gain + bias).astype(BF))
    normed, made = seq_rows(own, count, made)
    value_act, value_slope = gelu_parts(dot(normed, w_value, 1, 0))
    values = (value_act * keep).astype(BF)
    value_slope = (value_slope * keep).astype(BF)
    values, value_slope = together(values, value_slope)
    x_hat = dot(waves, values, 1, 0).astype(BF)
    k_cos, k_sin = hat
    x_cos, x_sin = x_hat[:length].astype(F32), x_hat[length:].astype(F32)
    y_hat = jnp.concatenate([k_cos * x_cos - k_sin * x_sin, k_cos * x_sin + k_sin * x_cos], 0).astype(BF)
    mixes = dot(waves_back, y_hat, 1, 0) * (1.0 / length) + skip * values.astype(F32)
    width = mixes.shape[1] // 2
    product = (mixes[:, :width] * mixes[:, width:]).astype(BF)
    product, mixes = together(product, mixes.astype(BF))
    product, made = filler[1](product, made)
    products, made = seq_gather(product, count, made)
    w_gate, w_mix, w_out = late
    gate_act, gate_slope = gelu_parts(dot(normed, w_gate, 1, 0))
    update = dot(products[0], w_mix[0], 1, 0)
    for member in range(1, count):
        update = update + dot(products[member], w_mix[member], 1, 0)
    mixed = (update * gate_act).astype(BF)
    gate_back = (update * gate_slope).astype(BF)
    mixed, gate_act, gate_back = together(mixed, gate_act.astype(BF), gate_back)
    result = stream + seq_reduce_rows(dot(mixed, w_out, 1, 0), count)
    saved = (
        xhat,
        factor,
        normed,
        gate_act,
        gate_back,
        value_slope,
        values,
        x_hat,
        mixes,
        products,
        mixed,
    )
    return result, saved, made


def back_gate(grad_stream, saved, late, count, wait):
    w_gate, w_mix, w_out = late
    xhat, factor, normed, gate_act, gate_back, value_slope, values, x_hat, mixes, products, mixed = saved
    out_low, wait = seq_rows(grad_stream, count, wait)
    grad_mixed = dot(out_low, w_out, 1, 1)
    update_low = (grad_mixed * gate_act.astype(F32)).astype(BF)
    gate_grad = (grad_mixed * gate_back.astype(F32)).astype(BF)
    update_low, gate_grad = together(update_low, gate_grad)
    width = products[0].shape[1]
    model = out_low.shape[1]
    product_low = seq_reduce([dot(update_low, w_mix[m], 1, 1) for m in range(count)], count)
    grad_out = [
        dot(mixed, out_low[:, j * width : (j + 1) * width], 0, 0).astype(BF) for j in range(model // width)
    ]
    grad_mix = [dot(products[m], update_low, 0, 0).astype(BF) for m in range(count)]
    grad_gate = dot(normed, gate_grad, 0, 0).astype(BF)
    gate_part = dot(gate_grad, w_gate, 1, 1)
    return product_low.astype(BF), gate_part, (grad_gate, grad_mix, grad_out), wait


def back_convolution(product_low, saved, hat, skip, tables):
    xhat, factor, normed, gate_act, gate_back, value_slope, values, x_hat, mixes, products, mixed = saved
    waves, waves_back = tables
    length = waves.shape[1]
    width = product_low.shape[1]
    product_low = product_low.astype(F32)
    mixes = mixes.astype(F32)
    back = jnp.concatenate([product_low * mixes[:, width:], product_low * mixes[:, :width]], 1).astype(BF)
    g_hat = dot(waves, back, 1, 0).astype(BF)
    k_cos, k_sin = hat
    g_cos, g_sin = g_hat[:length].astype(F32), g_hat[length:].astype(F32)
    y_hat = jnp.concatenate([k_cos * g_cos + k_sin * g_sin, k_cos * g_sin - k_sin * g_cos], 0).astype(BF)
    grad_values = dot(waves_back, y_hat, 1, 0) * (1.0 / length) + skip * back.astype(F32)
    x_cos, x_sin = x_hat[:length].astype(F32), x_hat[length:].astype(F32)
    sign = jnp.concatenate([jnp.ones((width,), F32), -jnp.ones((width,), F32)])
    kern_hat = (
        (g_cos * x_cos + g_sin * x_sin).astype(BF),
        ((g_sin * x_cos - g_cos * x_sin) * sign).astype(BF),
    )
    grad_skip = jnp.sum(back.astype(F32) * values.astype(F32), axis=0)
    value_grad = (grad_values.astype(BF).astype(F32) * value_slope.astype(F32)).astype(BF)
    return value_grad, kern_hat, grad_skip


def back_norm(grad_stream, grad_normed, saved, gain):
    xhat, factor = saved[:2]
    norm_terms = jnp.stack([jnp.sum(grad_normed * xhat, 0), jnp.sum(grad_normed, 0)])
    inner = grad_normed * gain
    slope = jnp.mean(inner, axis=-1, keepdims=True)
    tilt = jnp.mean(inner * xhat, axis=-1, keepdims=True)
    return grad_stream + (inner - slope - xhat * tilt) * factor, norm_terms


def shards(tokens, lengths, cotangent, w_gate, w_value, w_mix, w_out, ln_gain, ln_bias, ssm_coef, ssm_rate, ssm_skip):
    dp = lax.axis_size("dp")
    count = lax.axis_size("seq")
    rows, model = tokens.shape
    length = rows * count
    depth, in_rows, gate_width = w_gate.shape
    mix_rows = w_mix.shape[1]
    width = ssm_coef.shape[2]
    states = ssm_coef.shape[3]
    share = gate_width // (dp * count)
    out_parts = model // width
    order = [lax.axis_index("seq") ^ m for m in range(count)]
    keep = (jnp.arange(length, dtype=jnp.int32) < lengths[0]).astype(F32)[:, None]
    table = wave_table(length)
    waves = jnp.asarray(table)
    tables = (waves, jnp.asarray(np.ascontiguousarray(table.T)))

    def by_column(weight):
        cut = weight.reshape(weight.shape[0], dp, count, share)
        return cut.transpose(2, 0, 1, 3).reshape(count, weight.shape[0], width)

    def value_columns(layer):
        cut = w_value[layer].reshape(in_rows, 2, count, width).transpose(2, 1, 0, 3)
        return cut.reshape(count, 2 * in_rows, width)

    norm_rows = jnp.stack([ln_gain, ln_bias], 1).reshape(2 * depth, in_rows)
    norm_rows = jnp.pad(norm_rows, ((0, 16 - 2 * depth), (0, width - in_rows)))
    first = jnp.concatenate([value_columns(0), jnp.broadcast_to(norm_rows, (count,) + norm_rows.shape)], 1)
    first = lax.all_to_all(first, "seq", 0, 0, tiled=True)
    pieces = [by_column(w_gate[0]), by_column(w_mix[0])]
    for layer in range(1, depth):
        pieces += [value_columns(layer), by_column(w_gate[layer]), by_column(w_mix[layer])]
    sizes = [piece.shape[1] for piece in pieces]
    rest = lax.all_to_all(jnp.concatenate(pieces, 1), "seq", 0, 0, tiled=True)
    rest = [piece for piece in jnp.split(rest, np.cumsum(sizes)[:-1].tolist(), axis=1)]

    coefs = ssm_coef.reshape(depth, width, 2 * states)
    rates = ssm_rate.reshape(depth, width, 2 * states)
    skips = ssm_skip.reshape(depth, 2 * width)
    sign = jnp.concatenate([jnp.ones((1, width), F32), -jnp.ones((1, width), F32)], 1)
    table_parts = 2 * width // channel_block(2 * width)

    def make_tables(layer, parts_made, hat, tie):
        rate, tie = together(rates[layer], tie)
        for part in parts_made:
            hat = spectra(coefs[layer], rate, sign, waves, part, hat)
        return hat, tie

    def flat(piece):
        return piece.reshape(-1, width)

    def value_sides(piece):
        return [flat(piece[:, side * in_rows : (side + 1) * in_rows]) for side in range(2)]

    def out_sides(layer):
        return [w_out[layer][:, j * width : (j + 1) * width] for j in range(out_parts)]

    norm_piece = first[:, 2 * in_rows :, :in_rows].transpose(1, 0, 2).reshape(16, count * in_rows)
    norm_piece = jnp.pad(norm_piece, ((0, 0), (0, -(count * in_rows) % width)))
    sides = value_sides(first)
    n_in = count * in_rows
    pair = [jnp.concatenate([sides[0], flat(norm_piece)], 0), sides[1]]
    paths = [far_first(dp), y_first(dp)[:1] + far_first(dp)[:-1]]
    late_block = jnp.concatenate([flat(rest[0]), flat(rest[1])] + out_sides(0), 0)
    done = [[], []]
    hat = ()
    for step in range(len(bits_of(dp))):
        others = [swap(block, "dp", dp, path[step]) for block, path in zip(pair, paths)]
        if step < table_parts:
            hat, pair = make_tables(0, [step], hat, pair)
            others, hat = together(others, hat)
        if step == 0:
            others, late_block = together(others, late_block)
        for j in range(2):
            done[j] = sorted(done[j] + [paths[j][step]], reverse=True)
            pair[j] = join(pair[j], others[j], "dp", paths[j][step], done[j])
    hat, pair = make_tables(0, range(len(bits_of(dp)), table_parts), hat, pair)
    hats = [hat]
    side_a, side_b = [block.reshape((dp,) + block.shape[-2:]) for block in pair]
    norms = side_a[:, n_in:].reshape(dp, 16, -1)[:, : 2 * depth, :n_in]
    norms = norms.transpose(1, 0, 2).reshape(depth, 2, model).astype(F32)

    def value_weight(side_a, side_b):
        return jnp.concatenate([side_a.reshape(model, width), side_b.reshape(model, width)], 1)

    def mix_weight(block):
        block = block.reshape(count, width, width)
        return [lax.dynamic_index_in_dim(block, order[m], 0, keepdims=False) for m in range(count)]

    def out_weight(block):
        cut = block.reshape(dp, out_parts, mix_rows, width).transpose(0, 2, 1, 3)
        return cut.reshape(dp * mix_rows, model)

    early = [(value_weight(side_a[:, :n_in], side_b), norms[0, 0], norms[0, 1])]
    got = lax.all_gather(late_block, "dp", axis=0)
    gate, mix, out = jnp.split(got, [n_in, n_in + count * mix_rows], axis=1)
    late = [(gate.reshape(model, width), mix_weight(mix), out_weight(out))]
    for layer in range(1, depth):
        value, gate, mix = rest[3 * layer - 1 : 3 * layer + 2]
        block = jnp.concatenate(value_sides(value) + [flat(gate), flat(mix)] + out_sides(layer), 0)
        got = lax.all_gather(block, "dp", axis=0)
        cuts = np.cumsum([n_in, n_in, n_in, count * mix_rows]).tolist()
        side_a, side_b, gate, mix, out = jnp.split(got, cuts, axis=1)
        early.append((value_weight(side_a, side_b), norms[layer, 0], norms[layer, 1]))
        late.append((gate.reshape(model, width), mix_weight(mix), out_weight(out)))

    stream = tokens.astype(F32)
    kept = []
    for layer in range(depth):
        if layer + 1 < depth:
            cut = min(2, table_parts)
            filler = (
                lambda own: make_tables(layer + 1, range(cut), (), own)[::-1],
                lambda product, made: make_tables(layer + 1, range(cut, table_parts), made, product)[::-1],
            )
        else:
            filler = (lambda own: (own, ()), lambda product, made: (product, made))
        stream, saved, made = run_layer(
            stream, keep, early[layer], late[layer], hats[layer], skips[layer], tables, count, filler
        )
        kept.append(saved)
        hats.append(made)

    def natural(blocks):
        whole = jnp.zeros((count,) + blocks[0].shape, blocks[0].dtype)
        for member, block in enumerate(blocks):
            whole = lax.dynamic_update_index_in_dim(whole, block, order[member], 0)
        return whole

    grad_stream = cotangent.astype(F32)
    norm_grads = [None] * depth
    ssm_grads = [None] * depth
    held = [None] * depth
    whole, kern_hat = None, None
    for layer in reversed(range(depth)):
        low = grad_stream.astype(BF)
        wait = ()
        if kern_hat is not None:
            low, whole, kern_hat = together(low, whole, kern_hat)
            held[layer + 1] = lax.psum_scatter(whole, "dp", scatter_dimension=0, tiled=False)
            wait = state_grads(coefs[layer + 1], rates[layer + 1], *kern_hat, waves)
        product_low, gate_part, terms, wait = back_gate(low, kept[layer], late[layer], count, wait)
        if kern_hat is not None:
            ssm_grads[layer + 1] += wait
        grad_gate, grad_mix, grad_out = terms
        mix = natural(grad_mix).reshape(dp, count * mix_rows, width)
        others = [grad_gate.reshape(dp, n_in, width)] + [g.reshape(dp, mix_rows, width) for g in grad_out]
        others = jnp.concatenate(others, 1)
        if not layer:
            paths = [y_first(dp), z_first(dp)]
            moving = [cut_half(bit_blocks(b, dp), "dp", dp, path[0]) for b, path in zip((mix, others), paths)]
            product_low, moving = together(product_low, moving)
            moving = [(pair[0], swap(pair[1], "dp", dp, path[0])) for pair, path in zip(moving, paths)]
        value_grad, kern_hat, grad_skip = back_convolution(product_low, kept[layer], hats[layer], skips[layer], tables)
        ssm_grads[layer] = (grad_skip,)
        normed = kept[layer][2]
        if not layer:
            value_grad, moving = together(value_grad, moving)
            moving = [cut_half(add_half(*pair, BF), "dp", dp, path[1]) for pair, path in zip(moving, paths)]
        values = [dot(normed, value_grad[:, j * width : (j + 1) * width], 0, 0).astype(BF) for j in range(2)]
        values = [g.reshape(dp, n_in, width) for g in values]
        parts = dot(value_grad, early[layer][0], 1, 1) + gate_part
        if layer:
            grad_normed = reduce_bits(
                parts.reshape(count, rows, model), "seq", count, bits_of(count), F32
            )
            whole = jnp.concatenate([mix, others] + values, 1)
        else:
            moving += [cut_half(bit_blocks(g, dp), "dp", dp, path[0]) for g, path in zip(values, paths)]
            paths = [path[1:] for path in paths] + paths
            sums = bit_blocks(parts.reshape(count, rows, model), count)
            for step, bit in enumerate(bits_of(count)):
                held_rows, sent = cut_half(sums, "seq", count, bit)
                if step == 1:
                    sent, moving, kern_hat = together(sent, moving, kern_hat)
                    moving = [(pair[0], swap(pair[1], "dp", dp, path[0])) for pair, path in zip(moving, paths)]
                    came = swap(sent, "seq", count, bit)
                    last = state_grads(coefs[0], rates[0], *kern_hat, waves)
                    came, moving, last = together(came, moving, last)
                    ssm_grads[0] += last
                else:
                    came = swap(sent, "seq", count, bit)
                sums = add_half(held_rows, came, F32)
            grad_normed = sums.reshape(rows, model)
        grad_stream, norm_grads[layer] = back_norm(grad_stream, grad_normed, kept[layer], early[layer][1])

    own = width // dp
    both = 2 * states
    skip_rows = jnp.stack([g[0].reshape(dp, 2 * own) for g in ssm_grads], 1)
    skip_rows = jnp.pad(skip_rows, ((0, 0), (0, 16 - depth), (0, -2 * own % both))).reshape(dp, -1, both)
    states_all = jnp.stack([g[j].reshape(dp, own, both) for g in ssm_grads for j in (1, 2)], 1).astype(BF)
    ssm_rows = jnp.concatenate([states_all.reshape(dp, 2 * depth * own, both), skip_rows.astype(BF)], 1)

    sums = [add_half(*pair, BF) for pair in moving] + [bit_blocks(ssm_rows, dp)]
    paths = [path[1:] for path in paths] + [y_first(dp)]
    while any(paths):
        active = [j for j, path in enumerate(paths) if path]
        pairs = [cut_half(sums[j], "dp", dp, paths[j][0]) for j in active]
        pairs = lax.optimization_barrier(pairs)
        pairs = [(pair[0], swap(pair[1], "dp", dp, paths[j][0])) for j, pair in zip(active, pairs)]
        pairs = lax.optimization_barrier(pairs)
        for j, pair in zip(active, pairs):
            sums[j] = add_half(*pair, BF)
            paths[j] = paths[j][1:]
    sums = [block.reshape(block.shape[-2:]) for block in sums]
    held[0] = jnp.concatenate(sums[:4], 0)
    ssm_sum = gather_bits(sums[4], "dp", dp, far_first(dp))[0].astype(F32)
    for layer in range(depth):
        cuts = np.cumsum([count * mix_rows, n_in, out_parts * mix_rows, n_in]).tolist()
        mix, gate, outs, side_a, side_b = jnp.split(held[layer], cuts, axis=0)
        held[layer] = ([side_a, side_b], gate, mix, outs)

    pieces = []
    for layer in range(depth):
        values, gate, mix, outs = held[layer]
        pieces += [gate.reshape(count, in_rows, width), mix.reshape(count, mix_rows, width)]
        pieces += [side.reshape(count, in_rows, width) for side in values]
    sizes = [piece.shape[1] for piece in pieces]
    back = lax.all_to_all(jnp.concatenate(pieces, 1), "seq", 0, 0, tiled=True)
    back = jnp.split(back, np.cumsum(sizes)[:-1].tolist(), axis=1)

    def columns(block):
        cut = block.reshape(count, -1, dp, share).transpose(1, 2, 0, 3)
        return cut.reshape(-1, gate_width).astype(F32)

    def value_share(sides):
        sides = jnp.stack(sides, 0)
        return sides.transpose(2, 0, 1, 3).reshape(in_rows, 2 * count * width).astype(F32)

    def out_share(block):
        return block.reshape(out_parts, mix_rows, width).transpose(1, 0, 2).reshape(mix_rows, model).astype(F32)

    gates, mixes, values = [], [], []
    for layer in range(depth):
        gate, mix, side_a, side_b = back[4 * layer : 4 * layer + 4]
        gates.append(columns(gate))
        mixes.append(columns(mix))
        values.append(value_share([side_a, side_b]))
    outs = [out_share(held[layer][3]) for layer in range(depth)]

    norm_all = jnp.stack(norm_grads).reshape(2 * depth, dp * count, in_rows).transpose(1, 0, 2)
    norm_all = norm_all.reshape(dp * count, 2 * depth * in_rows)
    norm_sum = jnp.sum(lax.all_to_all(norm_all, ("dp", "seq"), 0, 0, tiled=True), 0).reshape(depth, 2, in_rows)

    state_sum = ssm_sum[:, : 2 * depth * own].reshape(dp, depth, 2, own, both).transpose(1, 2, 0, 3, 4)
    coef_sum, rate_sum = state_sum[:, 0], state_sum[:, 1]
    skip_sum = ssm_sum[:, 2 * depth * own :].reshape(dp, 16, -1)[:, :depth, : 2 * own].transpose(1, 0, 2)
    return (
        stream,
        grad_stream,
        jnp.stack(gates),
        jnp.stack(values),
        jnp.stack(mixes),
        jnp.stack(outs),
        norm_sum[:, 0],
        norm_sum[:, 1],
        coef_sum.reshape(ssm_coef.shape),
        rate_sum.reshape(ssm_rate.shape),
        skip_sum.reshape(ssm_skip.shape),
    )


def solution(mesh):
    in_specs = (
        P(("dp", "seq"), None),
        P("dp"),
        P(("dp", "seq"), None),
        P(None, ("dp", "seq"), None),
        P(None, ("dp", "seq"), None),
        P(None, ("dp", "seq"), None),
        P(None, ("dp", "seq"), None),
        P(None, ("dp", "seq")),
        P(None, ("dp", "seq")),
        P(None, None, "seq", None),
        P(None, None, "seq", None),
        P(None, None, "seq"),
    )
    out_specs = (
        P(("dp", "seq"), None),
        P(("dp", "seq"), None),
        P(None, ("dp", "seq"), None),
        P(None, ("dp", "seq"), None),
        P(None, ("dp", "seq"), None),
        P(None, ("dp", "seq"), None),
        P(None, ("dp", "seq")),
        P(None, ("dp", "seq")),
        P(None, None, "seq", None),
        P(None, None, "seq", None),
        P(None, None, "seq"),
    )
    return jax.shard_map(shards, mesh=mesh, in_specs=in_specs, out_specs=out_specs, check_vma=False)
```

time: 763 us -> 533 us (0.70)
  waiting for transfers between devices: 265 us -> 149 us
  matrix products: 206 us -> 92.3 us
  Pallas kernels: 0 us -> 76 us
  other arithmetic: 118 us -> 52.5 us
  starting transfers between devices: 36.9 us -> 62.6 us
  blocking collectives: 20.3 us -> 0 us
  between operations: 25.6 us -> 17.4 us
    reduce_scatter x4 -> x1, waiting for transfers between devices: 180 us -> 0.02 us  [shards(): lax.psum_scatter(whole, 'dp', scatter_dimension=0, tiled=False)]
    pallas_call x0 -> x8, Pallas kernels: none -> 76 us  [the longest x6 47.4 us: spectra(): pl.pallas_call(partial(spectra_kernel, unroll_of(block // 2)), out_shape=...]
    dot_general x4 -> x0, matrix products: 69.7 us -> none  [the longest x2 42.2 us: lag_grads(): lax.dot_general(pieces, pair, (((2,), (1,)), ((0,), (0,))), preferred_ele...]
    ppermute x36 -> x52, waiting for transfers between devices: 47 us -> 108 us  [the longest x40 60.6 us: swap(): return lax.ppermute(block, axis, pairs_of(count, bit))]
    dot_general x56 -> x58, matrix products: 137 us -> 92.3 us  [dot(): lax.dot_general(left, right, (((left_dim,), (right_dim,)), ((), ())), pre...]
    convert_element_type x12 -> x27, other arithmetic: 53.4 us -> 22.5 us  [the longest x2 9.82 us: back_convolution(): ((g_sin * x_cos - g_cos * x_sin) * sign).astype(BF)]
    ppermute x36 -> x52, starting transfers between devices: 21.3 us -> 44.8 us  [the longest x40 38.5 us: swap(): return lax.ppermute(block, axis, pairs_of(count, bit))]
    psum x1 -> x0, blocking collectives: 20.3 us -> none  [shards(): lax.psum(jnp.stack([g[2] for g in ssm_grads]).astype(BF), 'dp').astype(F32)]
  transfers between devices with their start and end apart: 48 -> 59, of which waited for: 17 -> 21; matrix products, arithmetic and copies ran while one was open for 49% -> 34% of each run, Pallas kernels for 0% -> 14%
where the time goes in v3:
time: 533 us; the launch traced here: 527 us
  waiting for transfers between devices  149 us (28%)
  matrix products  92.3 us (17%)
  local copies, waits for them, and re-layouts  77.6 us (15%)
  Pallas kernels  76 us (14%)
  starting transfers between devices  62.6 us (12%)
  other arithmetic  52.5 us (10%)
  between operations  17.4 us (3%)
    dot_general x58, matrix products, dot(): lax.dot_general(left, right, (((left_dim,), (right_dim,)), ((), ())), pre...  92.3 us
    ppermute x40, waiting for transfers between devices, swap(): return lax.ppermute(block, axis, pairs_of(count, bit))  60.6 us
    pallas_call x6, Pallas kernels, spectra(): pl.pallas_call(partial(spectra_kernel, unroll_of(block // 2)), out_shape=...  47.4 us
    ppermute x40, starting transfers between devices, swap(): return lax.ppermute(block, axis, pairs_of(count, bit))  38.5 us
    unnamed x242, local copies, waits for them, and re-layouts  38.5 us
    ppermute x6, waiting for transfers between devices, seq_reduce(): came = lax.ppermute(sent, 'seq', pairs_of(count, bit))  29.7 us
    pallas_call x2, Pallas kernels, state_grads(): pl.pallas_call(partial(state_grads_kernel, unroll_of(block // 2)), out_sh...  28.6 us
    ppermute x6, waiting for transfers between devices, seq_gather(): lax.ppermute(blocks[member], 'seq', pairs_of(count, bit))  17.4 us
  transfers between devices with their start and end apart: 59, of which 21 were waited for; matrix products, arithmetic and copies ran while one was open for 34% of the time, Pallas kernels for 14%

profile of v3, /device:TPU:0, one launch (start us, length us, event | category | flops | bytes accessed | tf_op | source)
XLA Modules:
  0.0 527.3 jit_solution(3816240157965918490)
XLA Ops:
  9.8 4.2 all-to-all-start
  25.0 3.5 all-to-all-start.1
  28.8 3.3 collective-permute-start
  33.6 7.9 %spectra.6 = (bf16[1024,768]{1,0:T(8,128)(2,1)}, bf16[1024,768]{1,0:T(8,128)(2,1)}) custom-call(f32[384,128]{1,0:T(8,128)} %squeeze.67.rate_ref, f32[384,128]{1,0:T(8,128)} %squeeze.68.coef_ref, f32[1,768]{1,0:T(1,128)} %constant.227.clone.1.sign_ref, bf16[2048,1024]{1,0:T(8,128)(2,1)} %constant.242.clone.wave_ref), custom_call_target="tpu_custom_call" | custom-call | flops 3221225472 | bytes 5242880 | tf_op jit(solution)/shard_map/spectra/pallas_call | solution.py:94
  45.2 7.9 %spectra.7 = (bf16[1024,768]{1,0:T(8,128)(2,1)}, bf16[1024,768]{1,0:T(8,128)(2,1)}) custom-call(f32[384,128]{1,0:T(8,128)} %squeeze.67.rate_ref, f32[384,128]{1,0:T(8,128)} %squeeze.68.coef_ref, f32[1,768]{1,0:T(1,128)} %constant.227.clone.1.sign_ref, bf16[2048,1024]{1,0:T(8,128)(2,1)} %constant.242.clone.wave_ref, ...), custom_call_target="tpu_custom_call", output_to_operand_aliasing={{0}: (4, {}), {1}: (5, {})} | custom-call | flops 3221225472 | bytes 5242880 | tf_op jit(solution)/shard_map/spectra/pallas_call | solution.py:94
  54.6 8.0 %spectra.8 = (bf16[1024,768]{1,0:T(8,128)(2,1)}, bf16[1024,768]{1,0:T(8,128)(2,1)}) custom-call(f32[384,128]{1,0:T(8,128)} %squeeze.67.rate_ref, f32[384,128]{1,0:T(8,128)} %squeeze.68.coef_ref, f32[1,768]{1,0:T(1,128)} %constant.227.clone.1.sign_ref, bf16[2048,1024]{1,0:T(8,128)(2,1)} %constant.242.clone.wave_ref, ...), custom_call_target="tpu_custom_call", output_to_operand_aliasing={{0}: (4, {}), {1}: (5, {})} | custom-call | flops 3221225472 | bytes 5242880 | tf_op jit(solution)/shard_map/spectra/pallas_call | solution.py:94
  65.0 7.9 %spectra.9 = (bf16[1024,768]{1,0:T(8,128)(2,1)}, bf16[1024,768]{1,0:T(8,128)(2,1)}) custom-call(f32[384,128]{1,0:T(8,128)} %squeeze.66.rate_ref, f32[384,128]{1,0:T(8,128)} %squeeze.70.coef_ref, f32[1,768]{1,0:T(1,128)} %constant.227.clone.1.sign_ref, bf16[2048,1024]{1,0:T(8,128)(2,1)} %constant.242.clone.wave_ref), custom_call_target="tpu_custom_call" | custom-call | flops 3221225472 | bytes 5242880 | tf_op jit(solution)/shard_map/spectra/pallas_call | solution.py:94
  72.8 7.9 %spectra.10 = (bf16[1024,768]{1,0:T(8,128)(2,1)}, bf16[1024,768]{1,0:T(8,128)(2,1)}) custom-call(f32[384,128]{1,0:T(8,128)} %squeeze.66.rate_ref, f32[384,128]{1,0:T(8,128)} %squeeze.70.coef_ref, f32[1,768]{1,0:T(1,128)} %constant.227.clone.1.sign_ref, bf16[2048,1024]{1,0:T(8,128)(2,1)} %constant.242.clone.wave_ref, ...), custom_call_target="tpu_custom_call", output_to_operand_aliasing={{0}: (4, {}), {1}: (5, {})} | custom-call | flops 3221225472 | bytes 5242880 | tf_op jit(solution)/shard_map/spectra/pallas_call | solution.py:94
  86.5 3.5 fusion.13
  90.1 3.6 fusion.46
  93.8 1.9 fusion.75
  96.5 3.4 fusion.249
  103.7 8.0 %spectra.11 = (bf16[1024,768]{1,0:T(8,128)(2,1)}, bf16[1024,768]{1,0:T(8,128)(2,1)}) custom-call(f32[384,128]{1,0:T(8,128)} %squeeze.66.rate_ref, f32[384,128]{1,0:T(8,128)} %squeeze.70.coef_ref, f32[1,768]{1,0:T(1,128)} %constant.227.clone.1.sign_ref, bf16[2048,1024]{1,0:T(8,128)(2,1)} %constant.242.clone.wave_ref, ...), custom_call_target="tpu_custom_call", output_to_operand_aliasing={{0}: (4, {}), {1}: (5, {})} | custom-call | flops 3221225472 | bytes 5242880 | tf_op jit(solution)/shard_map/spectra/pallas_call | solution.py:94
  111.7 8.3 %collective-permute-done.9 = bf16[1024,384]{1,0:T(8,128)(2,1)S(1)} collective-permute-done((bf16[1024,384]{1,0:T(8,128)(2,1)S(1)}, bf16[1024,384]{1,0:T(8,128)(2,1)S(1)}, u32[]{:S(2)}, u32[]{:S(2)}) %collective-permute-start.9) | collective-permute-done | bytes 786464 | tf_op jit(solution)/shard_map/ppermute | solution.py:197
  120.9 14.1 %all-gather.5.cloned.1.call-done = bf16[3072,384]{1,0:T(8,128)(2,1)} async-done(((bf16[384,384]{1,0:T(8,128)(2,1)}), bf16[3072,384]{1,0:T(8,128)(2,1)}) %all-gather.5.cloned.1.call-update) | async-done | bytes 2359312 | tf_op jit(solution)/shard_map/all_gather | solution.py:505
  139.8 2.0 fusion.178
  142.8 2.5 fusion.59
  146.9 2.3 fusion.146
  150.2 2.6 collective-permute-done.11
  156.9 9.7 %collective-permute-done.12 = bf16[1,1,256,768]{3,2,1,0:T(8,128)(2,1)S(1)} collective-permute-done((bf16[1,1,256,768]{3,2,1,0:T(8,128)(2,1)S(1)}, bf16[1,1,256,768]{3,2,1,0:T(8,128)(2,1)S(1)}, u32[]{:S(2)}, u32[]{:S(2)}) %collective-permute-start.12) | collective-permute-done | bytes 393248 | tf_op jit(solution)/shard_map/ppermute | solution.py:247
  170.7 10.0 %collective-permute-done.13 = bf16[256,768]{1,0:T(8,128)(2,1)S(1)} collective-permute-done((bf16[256,768]{1,0:T(8,128)(2,1)S(1)}, bf16[256,768]{1,0:T(8,128)(2,1)S(1)}, u32[]{:S(2)}, u32[]{:S(2)}) %collective-permute-start.13) | collective-permute-done | bytes 393248 | tf_op jit(solution)/shard_map/ppermute | solution.py:247
  182.0 5.2 collective-permute-done.20
  187.4 14.1 %all-gather.7.cloned.1.call-done = bf16[4608,384]{1,0:T(8,128)(2,1)} async-done(((bf16[576,384]{1,0:T(8,128)(2,1)}), bf16[4608,384]{1,0:T(8,128)(2,1)}) %all-gather.7.cloned.1.call-update) | async-done | bytes 3538960 | tf_op jit(solution)/shard_map/all_gather | solution.py:511
  201.5 2.7 fusion.232
  206.7 3.5 fusion.19
  210.2 3.8 fusion.47
  214.1 1.9 fusion.72
  216.8 3.3 fusion.250
  230.7 9.1 %collective-permute-done.16 = bf16[1024,384]{1,0:T(8,128)(2,1)} collective-permute-done((bf16[1024,384]{1,0:T(8,128)(2,1)}, bf16[1024,384]{1,0:T(8,128)(2,1)}, u32[]{:S(2)}, u32[]{:S(2)}) %collective-permute-start.16) | collective-permute-done | bytes 786464 | tf_op jit(solution)/shard_map/ppermute | solution.py:197
  249.8 1.8 fusion.85
  252.2 1.8 fusion.89
  264.9 16.6 %collective-permute-done.24 = bf16[1024,384]{1,0:T(8,128)(2,1)S(1)} collective-permute-done((bf16[1024,384]{1,0:T(8,128)(2,1)S(1)}, bf16[1024,384]{1,0:T(8,128)(2,1)S(1)}, u32[]{:S(2)}, u32[]{:S(2)}) %collective-permute-start.24) | collective-permute-done | bytes 786464 | tf_op jit(solution)/shard_map/ppermute | solution.py:216
  282.1 2.1 copy-done.87
  284.3 3.6 fusion.48
  288.0 2.0 fusion.69
  291.1 3.9 multiply_convert_fusion.1
  301.9 1.9 convert_add_fusion.1
  305.5 4.8 fusion.36
  310.3 4.8 collective-permute-done.26
  316.1 2.5 fusion.230
  320.1 14.3 %state_grads.2 = (f32[384,128]{1,0:T(8,128)}, f32[384,128]{1,0:T(8,128)}) custom-call(f32[384,128]{1,0:T(8,128)} %squeeze.66.rate_ref, f32[384,128]{1,0:T(8,128)} %squeeze.70.coef_ref, bf16[1024,768]{1,0:T(8,128)(2,1)} %get-tuple-element.217.cos_ref, bf16[1024,768]{1,0:T(8,128)(2,1)} %get-tuple-element.218.sin_ref, bf16[2048,1024]{1,0:T(8,128)(2,1)} %constant.242.clone.wave_ref), custom_call_target="tpu_custom_call" | custom-call | flops 9663676416 | bytes 7340032 | tf_op jit(solution)/shard_map/state_grads/pallas_call | solution.py:168
  336.1 1.8 convert_element_type.773
  353.8 1.9 fusion.95
  362.4 2.7 fusion.253
  365.1 13.0 %collective-permute-done.31 = bf16[1024,384]{1,0:T(8,128)(2,1)S(1)} collective-permute-done((bf16[1024,384]{1,0:T(8,128)(2,1)S(1)}, bf16[1024,384]{1,0:T(8,128)(2,1)S(1)}, u32[]{:S(2)}, u32[]{:S(2)}) %collective-permute-start.31) | collective-permute-done | bytes 786464 | tf_op jit(solution)/shard_map/ppermute | solution.py:216
  378.8 1.9 copy-done.88
  380.7 3.8 fusion.49
  384.6 2.0 fusion.66
  388.4 4.5 multiply_convert_fusion
  394.8 5.0 fusion.45
  399.8 3.8 collective-permute-done.32
  416.4 2.2 collective-permute-start.38
  419.8 14.4 %state_grads.3 = (f32[384,128]{1,0:T(8,128)}, f32[384,128]{1,0:T(8,128)}) custom-call(f32[384,128]{1,0:T(8,128)} %squeeze.67.rate_ref, f32[384,128]{1,0:T(8,128)} %squeeze.68.coef_ref, bf16[1024,768]{1,0:T(8,128)(2,1)} %get-tuple-element.247.cos_ref, bf16[1024,768]{1,0:T(8,128)(2,1)} %get-tuple-element.248.sin_ref, bf16[2048,1024]{1,0:T(8,128)(2,1)} %constant.242.clone.wave_ref), custom_call_target="tpu_custom_call" | custom-call | flops 9663676416 | bytes 7340032 | tf_op jit(solution)/shard_map/state_grads/pallas_call | solution.py:168
  434.4 5.9 %collective-permute-done.39 = bf16[2,1,2,96,384]{4,3,2,1,0:T(8,128)(2,1)S(1)} collective-permute-done((bf16[2,1,2,96,384]{4,3,2,1,0:T(8,128)(2,1)S(1)}, bf16[2,1,2,96,384]{4,3,2,1,0:T(8,128)(2,1)S(1)}, u32[]{:S(2)}, u32[]{:S(2)}) %collective-permute-start.39) | collective-permute-done | bytes 294944 | tf_op jit(solution)/shard_map/ppermute | solution.py:247
  445.1 2.3 collective-permute-start.40
  450.3 5.7 %all-to-all-start.3 = ((f32[32,1,96]{2,1,0:T(1,128)}), f32[32,1,96]{2,1,0:T(1,128)S(1)}, u32[]{:S(2)}, u32[]{:S(2)}) async-start(f32[32,1,96]{2,1,0:T(1,128)} %bitcast.154), calls=%async_computation.4 | async-start | bytes 32768 | tf_op jit(solution)/shard_map/all_to_all | solution.py:653
  457.3 5.9 %all-to-all-done.3 = f32[32,1,96]{2,1,0:T(1,128)S(1)} async-done(((f32[32,1,96]{2,1,0:T(1,128)}), f32[32,1,96]{2,1,0:T(1,128)S(1)}, u32[]{:S(2)}, u32[]{:S(2)}) %all-to-all-start.3) | async-done | bytes 12320 | tf_op jit(solution)/shard_map/all_to_all | solution.py:653
  471.1 2.0 collective-permute-done.45
  474.8 3.9 collective-permute-done.48
  479.2 4.6 collective-permute-done.49
  484.0 4.7 collective-permute-done.50
  491.3 3.3 collective-permute-done.51
  499.4 3.5 all-to-all-start.2
  506.9 7.0 %all-to-all-done.2 = bf16[4,240,384]{2,1,0:T(8,128)(2,1)S(1)} async-done(((bf16[4,240,384]{2,1,0:T(8,128)(2,1)}), bf16[4,240,384]{2,1,0:T(8,128)(2,1)S(1)}, u32[]{:S(2)}, u32[]{:S(2)}) %all-to-all-start.2) | async-done | bytes 737312 | tf_op jit(solution)/shard_map/all_to_all | solution.py:629
  (608 shorter events, 178.4 us)
Async XLA Ops:
  9.8 15.2 %all-to-all-start = ((bf16[4,64,384]{2,1,0:T(8,128)(2,1)}), bf16[4,64,384]{2,1,0:T(8,128)(2,1)S(1)}, u32[]{:S(2)}, u32[]{:S(2)}) async-start(bf16[4,64,384]{2,1,0:T(8,128)(2,1)} %pad_maximum_fusion.26), calls=%async_computation | async-start | bytes 393216 | tf_op jit(solution)/shard_map/all_to_all | solution.py:439
  17.4 45.7 %copy-start.71 = (f32[256]{0:T(256)}, f32[256]{0:T(256)S(1)}, u32[]{:S(2)}) copy-start(f32[256]{0:T(256)S(1)} %broadcast_multiply_fusion.5) | copy-start | bytes 3076
  17.7 45.4 %copy-start.75 = (f32[256]{0:T(256)}, f32[256]{0:T(256)S(1)}, u32[]{:S(2)}) copy-start(f32[256]{0:T(256)S(1)} %add_rsqrt_fusion.1) | copy-start | bytes 3076
  25.0 16.5 %all-to-all-start.1 = ((bf16[4,192,384]{2,1,0:T(8,128)(2,1)}), bf16[4,192,384]{2,1,0:T(8,128)(2,1)S(1)}, u32[]{:S(2)}, u32[]{:S(2)}) async-start(bf16[4,192,384]{2,1,0:T(8,128)(2,1)} %constant_dynamic-update-slice_fusion), calls=%async_computation.1 | async-start | bytes 1179648 | tf_op jit(solution)/shard_map/all_to_all | solution.py:444
  28.5 106.5 %all-gather.5.cloned.1.call-start = ((), (), s32[]{:S(2)}) async-start(), calls=%async_computation.6 | async-start | bytes 2654208 | tf_op jit(solution)/shard_map/all_gather | solution.py:505
  28.8 12.7 %collective-permute-start = (bf16[112,384]{1,0:T(8,128)(2,1)S(1)}, bf16[112,384]{1,0:T(8,128)(2,1)S(1)}, u32[]{:S(2)}, u32[]{:S(2)}) collective-permute-start(bf16[112,384]{1,0:T(8,128)(2,1)S(1)} %fusion.203), channel_id=1, source_target_pairs={{0,16},{4,20},{8,24},{12,28},{16,0},{20,4},{24,8},{28,12},{1,17},{... | collective-permute-start | bytes 258056 | tf_op jit(solution)/shard_map/ppermute | solution.py:247
  32.1 9.4 %collective-permute-start.1 = (bf16[96,384]{1,0:T(8,128)(2,1)S(1)}, bf16[96,384]{1,0:T(8,128)(2,1)S(1)}, u32[]{:S(2)}, u32[]{:S(2)}) collective-permute-start(bf16[96,384]{1,0:T(8,128)(2,1)S(1)} %bitcast.561), channel_id=1, source_target_pairs={{0,4},{4,0},{8,12},{12,8},{16,20},{20,16},{24,28},{28,24},{1,5},{5... | collective-permute-start | bytes 221192 | tf_op jit(solution)/shard_map/ppermute | solution.py:247
  43.1 10.0 %collective-permute-start.3 = (bf16[2,96,384]{2,1,0:T(8,128)(2,1)S(1)}, bf16[2,96,384]{2,1,0:T(8,128)(2,1)S(1)}, u32[]{:S(2)}, u32[]{:S(2)}) collective-permute-start(bf16[2,96,384]{2,1,0:T(8,128)(2,1)S(1)} %pad_maximum_fusion.28), channel_id=1, source_target_pairs={{0,16},{4,20},{8,24},{12,28},{16,0},{20,4},{24,8},{28,12},{1,17},{... | collective-permute-start | bytes 442376 | tf_op jit(solution)/shard_map/ppermute | solution.py:247
  43.5 9.5 %collective-permute-start.2 = (bf16[2,112,384]{2,1,0:T(8,128)(2,1)S(1)}, bf16[2,112,384]{2,1,0:T(8,128)(2,1)S(1)}, u32[]{:S(2)}, u32[]{:S(2)}) collective-permute-start(bf16[2,112,384]{2,1,0:T(8,128)(2,1)S(1)} %pad_maximum_fusion.27), channel_id=1, source_target_pairs={{0,8},{4,12},{8,0},{12,4},{16,24},{20,28},{24,16},{28,20},{1,9},{5... | collective-permute-start | bytes 516104 | tf_op jit(solution)/shard_map/ppermute | solution.py:247
  53.1 9.5 %collective-permute-start.4 = (bf16[2,2,112,384]{3,2,1,0:T(8,128)(2,1)S(1)}, bf16[2,2,112,384]{3,2,1,0:T(8,128)(2,1)S(1)}, u32[]{:S(2)}, u32[]{:S(2)}) collective-permute-start(bf16[2,2,112,384]{3,2,1,0:T(8,128)(2,1)S(1)} %pad_maximum_fusion.22), channel_id=1, source_target_pairs={{0,4},{4,0},{8,12},{12,8},{16,20},{20,16},{24,28},{28,24},{1,5},{5... | collective-permute-start | bytes 1032200 | tf_op jit(solution)/shard_map/ppermute | solution.py:247
  54.1 8.5 %collective-permute-start.5 = (bf16[2,2,96,384]{3,2,1,0:T(8,128)(2,1)S(1)}, bf16[2,2,96,384]{3,2,1,0:T(8,128)(2,1)S(1)}, u32[]{:S(2)}, u32[]{:S(2)}) collective-permute-start(bf16[2,2,96,384]{3,2,1,0:T(8,128)(2,1)S(1)} %pad_maximum_fusion.24), channel_id=1, source_target_pairs={{0,8},{4,12},{8,0},{12,4},{16,24},{20,28},{24,16},{28,20},{1,9},{5... | collective-permute-start | bytes 884744 | tf_op jit(solution)/shard_map/ppermute | solution.py:247
  63.4 17.3 %collective-permute-start.6 = (bf16[256,768]{1,0:T(8,128)(2,1)S(1)}, bf16[256,768]{1,0:T(8,128)(2,1)S(1)}, u32[]{:S(2)}, u32[]{:S(2)}) collective-permute-start(bf16[256,768]{1,0:T(8,128)(2,1)S(1)} %fusion.123), channel_id=1, source_target_pairs={{0,2},{1,3},{2,0},{3,1},{4,6},{5,7},{6,4},{7,5},{8,10},{9,11},{10,... | collective-permute-start | bytes 1179656 | tf_op jit(solution)/shard_map/ppermute | solution.py:247
  80.9 3.7 collective-permute-start.7
  82.2 13.5 %copy-start.81 = (f32[768]{0:T(1024)}, f32[768]{0:T(1024)S(1)}, u32[]{:S(2)}) copy-start(f32[768]{0:T(1024)S(1)} %mul.424) | copy-start | bytes 9220
  82.3 119.3 %all-gather.7.cloned.1.call-start = ((), (), s32[]{:S(2)}) async-start(), calls=%async_computation.7 | async-start | bytes 3981312 | tf_op jit(solution)/shard_map/all_gather | solution.py:511
  86.5 55.3 %copy-start.34 = (bf16[2,2,256,768]{3,2,1,0:T(8,128)(2,1)}, bf16[2,2,256,768]{3,2,1,0:T(8,128)(2,1)S(1)}, u32[]{:S(2)}) copy-start(bf16[2,2,256,768]{3,2,1,0:T(8,128)(2,1)S(1)} %copy.240) | copy-start | bytes 4718596
  100.0 36.4 %copy-start.24 = (bf16[1024,384]{1,0:T(8,128)(2,1)}, bf16[1024,384]{1,0:T(8,128)(2,1)S(1)}, u32[]{:S(2)}) copy-start(bf16[1024,384]{1,0:T(8,128)(2,1)S(1)} %fusion.79) | copy-start | bytes 2359300
  100.0 20.0 %collective-permute-start.9 = (bf16[1024,384]{1,0:T(8,128)(2,1)S(1)}, bf16[1024,384]{1,0:T(8,128)(2,1)S(1)}, u32[]{:S(2)}, u32[]{:S(2)}) collective-permute-start(bf16[1024,384]{1,0:T(8,128)(2,1)S(1)} %fusion.79), channel_id=1, source_target_pairs={{0,2},{1,3},{2,0},{3,1},{4,6},{5,7},{6,4},{7,5},{8,10},{9,11},{10,... | collective-permute-start | bytes 2359304 | tf_op jit(solution)/shard_map/ppermute | solution.py:197
  102.7 392.1 %reduce-scatter.2.cloned.1.call-start = ((), (), s32[]{:S(2)}) async-start(), calls=%async_computation.5 | async-start | bytes 3981312 | tf_op jit(solution)/shard_map/reduce_scatter | solution.py:550
  103.2 36.6 %collective-permute-start.8 = (bf16[1024,384]{1,0:T(8,128)(2,1)S(1)}, bf16[1024,384]{1,0:T(8,128)(2,1)}, u32[]{:S(2)}, u32[]{:S(2)}) collective-permute-start(bf16[1024,384]{1,0:T(8,128)(2,1)S(1)} %fusion.79), channel_id=1, source_target_pairs={{0,1},{1,0},{2,3},{3,2},{4,5},{5,4},{6,7},{7,6},{8,9},{9,8},{10,11... | collective-permute-start | bytes 2359304 | tf_op jit(solution)/shard_map/ppermute | solution.py:197
  120.9 21.9 %collective-permute-start.10 = (bf16[1024,384]{1,0:T(8,128)(2,1)}, bf16[1024,384]{1,0:T(8,128)(2,1)S(1)}, u32[]{:S(2)}, u32[]{:S(2)}) collective-permute-start(bf16[1024,384]{1,0:T(8,128)(2,1)} %copy-done.47), channel_id=1, source_target_pairs={{0,1},{1,0},{2,3},{3,2},{4,5},{5,4},{6,7},{7,6},{8,9},{9,8},{10,11... | collective-permute-start | bytes 2359304 | tf_op jit(solution)/shard_map/ppermute | solution.py:197
  150.2 2.6 collective-permute-start.11
  155.3 11.2 %collective-permute-start.12 = (bf16[1,1,256,768]{3,2,1,0:T(8,128)(2,1)S(1)}, bf16[1,1,256,768]{3,2,1,0:T(8,128)(2,1)S(1)}, u32[]{:S(2)}, u32[]{:S(2)}) collective-permute-start(bf16[1,1,256,768]{3,2,1,0:T(8,128)(2,1)S(1)} %dynamic-slice_convert_fusion.7), channel_id=1, source_target_pairs={{0,2},{1,3},{2,0},{3,1},{4,6},{5,7},{6,4},{7,5},{8,10},{9,11},{10,... | collective-permute-start | bytes 1179656 | tf_op jit(solution)/shard_map/ppermute | solution.py:247
  168.6 12.1 %collective-permute-start.13 = (bf16[256,768]{1,0:T(8,128)(2,1)S(1)}, bf16[256,768]{1,0:T(8,128)(2,1)S(1)}, u32[]{:S(2)}, u32[]{:S(2)}) collective-permute-start(bf16[256,768]{1,0:T(8,128)(2,1)S(1)} %add_convert_fusion.6), channel_id=1, source_target_pairs={{0,2},{1,3},{2,0},{3,1},{4,6},{5,7},{6,4},{7,5},{8,10},{9,11},{10,... | collective-permute-start | bytes 1179656 | tf_op jit(solution)/shard_map/ppermute | solution.py:247
  169.9 17.3 %collective-permute-start.20 = (bf16[256,768]{1,0:T(8,128)(2,1)S(1)}, bf16[256,768]{1,0:T(8,128)(2,1)S(1)}, u32[]{:S(2)}, u32[]{:S(2)}) collective-permute-start(bf16[256,768]{1,0:T(8,128)(2,1)S(1)} %copy-done.43), channel_id=1, source_target_pairs={{0,2},{1,3},{2,0},{3,1},{4,6},{5,7},{6,4},{7,5},{8,10},{9,11},{10,... | collective-permute-start | bytes 1179656 | tf_op jit(solution)/shard_map/ppermute | solution.py:247
  182.0 22.2 %collective-permute-start.14 = (bf16[2,256,768]{2,1,0:T(8,128)(2,1)}, bf16[2,256,768]{2,1,0:T(8,128)(2,1)}, u32[]{:S(2)}, u32[]{:S(2)}) collective-permute-start(bf16[2,256,768]{2,1,0:T(8,128)(2,1)} %pad_maximum_fusion.10), channel_id=1, source_target_pairs={{0,1},{1,0},{2,3},{3,2},{4,5},{5,4},{6,7},{7,6},{8,9},{9,8},{10,11... | collective-permute-start | bytes 2359304 | tf_op jit(solution)/shard_map/ppermute | solution.py:247
  187.4 35.2 %collective-permute-start.21 = (bf16[2,256,768]{2,1,0:T(8,128)(2,1)S(1)}, bf16[2,256,768]{2,1,0:T(8,128)(2,1)}, u32[]{:S(2)}, u32[]{:S(2)}) collective-permute-start(bf16[2,256,768]{2,1,0:T(8,128)(2,1)S(1)} %pad_maximum_fusion.11), channel_id=1, source_target_pairs={{0,1},{1,0},{2,3},{3,2},{4,5},{5,4},{6,7},{7,6},{8,9},{9,8},{10,11... | collective-permute-start | bytes 2359304 | tf_op jit(solution)/shard_map/ppermute | solution.py:247
  221.1 18.6 %collective-permute-start.16 = (bf16[1024,384]{1,0:T(8,128)(2,1)}, bf16[1024,384]{1,0:T(8,128)(2,1)}, u32[]{:S(2)}, u32[]{:S(2)}) collective-permute-start(bf16[1024,384]{1,0:T(8,128)(2,1)} %fusion.78), channel_id=1, source_target_pairs={{0,2},{1,3},{2,0},{3,1},{4,6},{5,7},{6,4},{7,5},{8,10},{9,11},{10,... | collective-permute-start | bytes 2359304 | tf_op jit(solution)/shard_map/ppermute | solution.py:197
  227.6 15.7 %collective-permute-start.15 = (bf16[1024,384]{1,0:T(8,128)(2,1)}, bf16[1024,384]{1,0:T(8,128)(2,1)S(1)}, u32[]{:S(2)}, u32[]{:S(2)}) collective-permute-start(bf16[1024,384]{1,0:T(8,128)(2,1)} %fusion.78), channel_id=1, source_target_pairs={{0,1},{1,0},{2,3},{3,2},{4,5},{5,4},{6,7},{7,6},{8,9},{9,8},{10,11... | collective-permute-start | bytes 2359304 | tf_op jit(solution)/shard_map/ppermute | solution.py:197
  239.8 4.2 collective-permute-start.17
  248.0 16.9 %collective-permute-start.22 = (bf16[1024,384]{1,0:T(8,128)(2,1)S(1)}, bf16[1024,384]{1,0:T(8,128)(2,1)S(1)}, u32[]{:S(2)}, u32[]{:S(2)}) collective-permute-start(bf16[1024,384]{1,0:T(8,128)(2,1)S(1)} %convolution_convert_fusion.7), channel_id=1, source_target_pairs={{0,1},{1,0},{2,3},{3,2},{4,5},{5,4},{6,7},{7,6},{8,9},{9,8},{10,11... | collective-permute-start | bytes 2359304 | tf_op jit(solution)/shard_map/ppermute | solution.py:216
  248.6 11.8 %collective-permute-start.23 = (bf16[1024,384]{1,0:T(8,128)(2,1)S(1)}, bf16[1024,384]{1,0:T(8,128)(2,1)S(1)}, u32[]{:S(2)}, u32[]{:S(2)}) collective-permute-start(bf16[1024,384]{1,0:T(8,128)(2,1)S(1)} %convolution_convert_fusion.6), channel_id=1, source_target_pairs={{0,1},{1,0},{2,3},{3,2},{4,5},{5,4},{6,7},{7,6},{8,9},{9,8},{10,11... | collective-permute-start | bytes 2359304 | tf_op jit(solution)/shard_map/ppermute | solution.py:216
  256.9 7.0 %collective-permute-start.18 = (bf16[2,1,256,768]{3,2,1,0:T(8,128)(2,1)S(1)}, bf16[2,1,256,768]{3,2,1,0:T(8,128)(2,1)S(1)}, u32[]{:S(2)}, u32[]{:S(2)}) collective-permute-start(bf16[2,1,256,768]{3,2,1,0:T(8,128)(2,1)S(1)} %dynamic-slice_convert_fusion.2), channel_id=1, source_target_pairs={{0,1},{1,0},{2,3},{3,2},{4,5},{5,4},{6,7},{7,6},{8,9},{9,8},{10,11... | collective-permute-start | bytes 2359304 | tf_op jit(solution)/shard_map/ppermute | solution.py:247
  261.0 20.5 %collective-permute-start.24 = (bf16[1024,384]{1,0:T(8,128)(2,1)S(1)}, bf16[1024,384]{1,0:T(8,128)(2,1)S(1)}, u32[]{:S(2)}, u32[]{:S(2)}) collective-permute-start(bf16[1024,384]{1,0:T(8,128)(2,1)S(1)} %add_convert_fusion.3), channel_id=1, source_target_pairs={{0,2},{1,3},{2,0},{3,1},{4,6},{5,7},{6,4},{7,5},{8,10},{9,11},{10,... | collective-permute-start | bytes 2359304 | tf_op jit(solution)/shard_map/ppermute | solution.py:216
  264.2 51.9 %collective-permute-start.19 = (bf16[1,1,256,768]{3,2,1,0:T(8,128)(2,1)S(1)}, bf16[1,1,256,768]{3,2,1,0:T(8,128)(2,1)}, u32[]{:S(2)}, u32[]{:S(2)}) collective-permute-start(bf16[1,1,256,768]{3,2,1,0:T(8,128)(2,1)S(1)} %dynamic-slice_convert_fusion.6), channel_id=1, source_target_pairs={{0,2},{1,3},{2,0},{3,1},{4,6},{5,7},{6,4},{7,5},{8,10},{9,11},{10,... | collective-permute-start | bytes 1179656 | tf_op jit(solution)/shard_map/ppermute | solution.py:247
  297.6 4.4 collective-permute-start.25
  303.9 11.1 %collective-permute-start.26 = (bf16[1,1,256,768]{3,2,1,0:T(8,128)(2,1)S(1)}, bf16[1,1,256,768]{3,2,1,0:T(8,128)(2,1)S(1)}, u32[]{:S(2)}, u32[]{:S(2)}) collective-permute-start(bf16[1,1,256,768]{3,2,1,0:T(8,128)(2,1)S(1)} %dynamic-slice_convert_fusion.5), channel_id=1, source_target_pairs={{0,2},{1,3},{2,0},{3,1},{4,6},{5,7},{6,4},{7,5},{8,10},{9,11},{10,... | collective-permute-start | bytes 1179656 | tf_op jit(solution)/shard_map/ppermute | solution.py:247
  318.6 15.7 %collective-permute-start.27 = (bf16[256,768]{1,0:T(8,128)(2,1)S(1)}, bf16[256,768]{1,0:T(8,128)(2,1)S(1)}, u32[]{:S(2)}, u32[]{:S(2)}) collective-permute-start(bf16[256,768]{1,0:T(8,128)(2,1)S(1)} %get-tuple-element.216), channel_id=1, source_target_pairs={{0,2},{1,3},{2,0},{3,1},{4,6},{5,7},{6,4},{7,5},{8,10},{9,11},{10,... | collective-permute-start | bytes 1179656 | tf_op jit(solution)/shard_map/ppermute | solution.py:247
  336.1 7.7 %collective-permute-start.28 = (bf16[2,256,768]{2,1,0:T(8,128)(2,1)}, bf16[2,256,768]{2,1,0:T(8,128)(2,1)}, u32[]{:S(2)}, u32[]{:S(2)}) collective-permute-start(bf16[2,256,768]{2,1,0:T(8,128)(2,1)} %pad_maximum_fusion.12), channel_id=1, source_target_pairs={{0,1},{1,0},{2,3},{3,2},{4,5},{5,4},{6,7},{7,6},{8,9},{9,8},{10,11... | collective-permute-start | bytes 2359304 | tf_op jit(solution)/shard_map/ppermute | solution.py:247
  353.0 12.1 %collective-permute-start.29 = (bf16[1024,384]{1,0:T(8,128)(2,1)S(1)}, bf16[1024,384]{1,0:T(8,128)(2,1)S(1)}, u32[]{:S(2)}, u32[]{:S(2)}) collective-permute-start(bf16[1024,384]{1,0:T(8,128)(2,1)S(1)} %convolution_convert_fusion.5), channel_id=1, source_target_pairs={{0,1},{1,0},{2,3},{3,2},{4,5},{5,4},{6,7},{7,6},{8,9},{9,8},{10,11... | collective-permute-start | bytes 2359304 | tf_op jit(solution)/shard_map/ppermute | solution.py:216
  353.6 3.9 collective-permute-start.30
  358.2 20.0 %collective-permute-start.31 = (bf16[1024,384]{1,0:T(8,128)(2,1)S(1)}, bf16[1024,384]{1,0:T(8,128)(2,1)S(1)}, u32[]{:S(2)}, u32[]{:S(2)}) collective-permute-start(bf16[1024,384]{1,0:T(8,128)(2,1)S(1)} %add_convert_fusion.1), channel_id=1, source_target_pairs={{0,2},{1,3},{2,0},{3,1},{4,6},{5,7},{6,4},{7,5},{8,10},{9,11},{10,... | collective-permute-start | bytes 2359304 | tf_op jit(solution)/shard_map/ppermute | solution.py:216
  386.6 17.0 %collective-permute-start.32 = (bf16[2,2,1,192,384]{4,3,2,1,0:T(8,128)(2,1)}, bf16[2,2,1,192,384]{4,3,2,1,0:T(8,128)(2,1)}, u32[]{:S(2)}, u32[]{:S(2)}) collective-permute-start(bf16[2,2,1,192,384]{4,3,2,1,0:T(8,128)(2,1)} %get-tuple-element.230), channel_id=1, source_target_pairs={{0,4},{4,0},{8,12},{12,8},{16,20},{20,16},{24,28},{28,24},{1,5},{5... | collective-permute-start | bytes 1769480 | tf_op jit(solution)/shard_map/ppermute | solution.py:247
  387.5 16.2 %collective-permute-start.33 = (bf16[2,1,2,192,384]{4,3,2,1,0:T(8,128)(2,1)}, bf16[2,1,2,192,384]{4,3,2,1,0:T(8,128)(2,1)}, u32[]{:S(2)}, u32[]{:S(2)}) collective-permute-start(bf16[2,1,2,192,384]{4,3,2,1,0:T(8,128)(2,1)} %get-tuple-element.232), channel_id=1, source_target_pairs={{0,8},{4,12},{8,0},{12,4},{16,24},{20,28},{24,16},{28,20},{1,9},{5... | collective-permute-start | bytes 1769480 | tf_op jit(solution)/shard_map/ppermute | solution.py:247
  408.7 3.6 collective-permute-start.34
  412.6 27.7 %collective-permute-start.35 = (bf16[1,1,256,768]{3,2,1,0:T(8,128)(2,1)S(1)}, bf16[1,1,256,768]{3,2,1,0:T(8,128)(2,1)S(1)}, u32[]{:S(2)}, u32[]{:S(2)}) collective-permute-start(bf16[1,1,256,768]{3,2,1,0:T(8,128)(2,1)S(1)} %dynamic-slice_convert_fusion.4), channel_id=1, source_target_pairs={{0,2},{1,3},{2,0},{3,1},{4,6},{5,7},{6,4},{7,5},{8,10},{9,11},{10,... | collective-permute-start | bytes 1179656 | tf_op jit(solution)/shard_map/ppermute | solution.py:247
  414.1 20.2 %collective-permute-start.36 = (bf16[2,1,1,192,384]{4,3,2,1,0:T(8,128)(2,1)S(1)}, bf16[2,1,1,192,384]{4,3,2,1,0:T(8,128)(2,1)S(1)}, u32[]{:S(2)}, u32[]{:S(2)}) collective-permute-start(bf16[2,1,1,192,384]{4,3,2,1,0:T(8,128)(2,1)S(1)} %get-tuple-element.240), channel_id=1, source_target_pairs={{0,8},{4,12},{8,0},{12,4},{16,24},{20,28},{24,16},{28,20},{1,9},{5... | collective-permute-start | bytes 884744 | tf_op jit(solution)/shard_map/ppermute | solution.py:247
  415.7 18.7 %collective-permute-start.37 = (bf16[1,1,2,192,384]{4,3,2,1,0:T(8,128)(2,1)S(1)}, bf16[1,1,2,192,384]{4,3,2,1,0:T(8,128)(2,1)S(1)}, u32[]{:S(2)}, u32[]{:S(2)}) collective-permute-start(bf16[1,1,2,192,384]{4,3,2,1,0:T(8,128)(2,1)S(1)} %get-tuple-element.242), channel_id=1, source_target_pairs={{0,16},{4,20},{8,24},{12,28},{16,0},{20,4},{24,8},{28,12},{1,17},{... | collective-permute-start | bytes 884744 | tf_op jit(solution)/shard_map/ppermute | solution.py:247
  416.4 17.9 %collective-permute-start.38 = (bf16[2,2,1,96,384]{4,3,2,1,0:T(8,128)(2,1)S(1)}, bf16[2,2,1,96,384]{4,3,2,1,0:T(8,128)(2,1)S(1)}, u32[]{:S(2)}, u32[]{:S(2)}) collective-permute-start(bf16[2,2,1,96,384]{4,3,2,1,0:T(8,128)(2,1)S(1)} %get-tuple-element.244), channel_id=1, source_target_pairs={{0,4},{4,0},{8,12},{12,8},{16,20},{20,16},{24,28},{28,24},{1,5},{5... | collective-permute-start | bytes 884744 | tf_op jit(solution)/shard_map/ppermute | solution.py:247
  418.6 21.7 %collective-permute-start.39 = (bf16[2,1,2,96,384]{4,3,2,1,0:T(8,128)(2,1)S(1)}, bf16[2,1,2,96,384]{4,3,2,1,0:T(8,128)(2,1)S(1)}, u32[]{:S(2)}, u32[]{:S(2)}) collective-permute-start(bf16[2,1,2,96,384]{4,3,2,1,0:T(8,128)(2,1)S(1)} %get-tuple-element.246), channel_id=1, source_target_pairs={{0,8},{4,12},{8,0},{12,4},{16,24},{20,28},{24,16},{28,20},{1,9},{5... | collective-permute-start | bytes 884744 | tf_op jit(solution)/shard_map/ppermute | solution.py:247
  443.6 20.2 %collective-permute-start.44 = (bf16[2,2,1,208,128]{4,3,2,1,0:T(8,128)(2,1)S(1)}, bf16[2,2,1,208,128]{4,3,2,1,0:T(8,128)(2,1)S(1)}, u32[]{:S(2)}, u32[]{:S(2)}) collective-permute-start(bf16[2,2,1,208,128]{4,3,2,1,0:T(8,128)(2,1)S(1)} %get-tuple-element.273), channel_id=1, source_target_pairs={{0,4},{4,0},{8,12},{12,8},{16,20},{20,16},{24,28},{28,24},{1,5},{5... | collective-permute-start | bytes 638984 | tf_op jit(solution)/shard_map/ppermute | solution.py:247
  445.1 18.7 %collective-permute-start.40 = (bf16[1,1,1,192,384]{4,3,2,1,0:T(8,128)(2,1)}, bf16[1,1,1,192,384]{4,3,2,1,0:T(8,128)(2,1)S(1)}, u32[]{:S(2)}, u32[]{:S(2)}) collective-permute-start(bf16[1,1,1,192,384]{4,3,2,1,0:T(8,128)(2,1)} %get-tuple-element.265), channel_id=1, source_target_pairs={{0,16},{4,20},{8,24},{12,28},{16,0},{20,4},{24,8},{28,12},{1,17},{... | collective-permute-start | bytes 442376 | tf_op jit(solution)/shard_map/ppermute | solution.py:247
  447.5 16.4 %collective-permute-start.41 = (bf16[1,1,1,192,384]{4,3,2,1,0:T(8,128)(2,1)}, bf16[1,1,1,192,384]{4,3,2,1,0:T(8,128)(2,1)}, u32[]{:S(2)}, u32[]{:S(2)}) collective-permute-start(bf16[1,1,1,192,384]{4,3,2,1,0:T(8,128)(2,1)} %get-tuple-element.267), channel_id=1, source_target_pairs={{0,4},{4,0},{8,12},{12,8},{16,20},{20,16},{24,28},{28,24},{1,5},{5... | collective-permute-start | bytes 442376 | tf_op jit(solution)/shard_map/ppermute | solution.py:247
  448.0 15.8 %collective-permute-start.42 = (bf16[2,1,1,96,384]{4,3,2,1,0:T(8,128)(2,1)}, bf16[2,1,1,96,384]{4,3,2,1,0:T(8,128)(2,1)}, u32[]{:S(2)}, u32[]{:S(2)}) collective-permute-start(bf16[2,1,1,96,384]{4,3,2,1,0:T(8,128)(2,1)} %get-tuple-element.269), channel_id=1, source_target_pairs={{0,8},{4,12},{8,0},{12,4},{16,24},{20,28},{24,16},{28,20},{1,9},{5... | collective-permute-start | bytes 442376 | tf_op jit(solution)/shard_map/ppermute | solution.py:247
  448.5 15.3 %collective-permute-start.43 = (bf16[1,1,2,96,384]{4,3,2,1,0:T(8,128)(2,1)}, bf16[1,1,2,96,384]{4,3,2,1,0:T(8,128)(2,1)}, u32[]{:S(2)}, u32[]{:S(2)}) collective-permute-start(bf16[1,1,2,96,384]{4,3,2,1,0:T(8,128)(2,1)} %get-tuple-element.271), channel_id=1, source_target_pairs={{0,16},{4,20},{8,24},{12,28},{16,0},{20,4},{24,8},{28,12},{1,17},{... | collective-permute-start | bytes 442376 | tf_op jit(solution)/shard_map/ppermute | solution.py:247
  450.3 12.8 %all-to-all-start.3 = ((f32[32,1,96]{2,1,0:T(1,128)}), f32[32,1,96]{2,1,0:T(1,128)S(1)}, u32[]{:S(2)}, u32[]{:S(2)}) async-start(f32[32,1,96]{2,1,0:T(1,128)} %bitcast.154), calls=%async_computation.4 | async-start | bytes 32768 | tf_op jit(solution)/shard_map/all_to_all | solution.py:653
  465.9 7.2 %collective-permute-start.47 = (bf16[2,1,1,208,128]{4,3,2,1,0:T(8,128)(2,1)S(1)}, bf16[2,1,1,208,128]{4,3,2,1,0:T(8,128)(2,1)S(1)}, u32[]{:S(2)}, u32[]{:S(2)}) collective-permute-start(bf16[2,1,1,208,128]{4,3,2,1,0:T(8,128)(2,1)S(1)} %get-tuple-element.289), channel_id=1, source_target_pairs={{0,8},{4,12},{8,0},{12,4},{16,24},{20,28},{24,16},{28,20},{1,9},{5... | collective-permute-start | bytes 319496 | tf_op jit(solution)/shard_map/ppermute | solution.py:247
  466.6 6.5 %collective-permute-start.45 = (bf16[1,1,1,96,384]{4,3,2,1,0:T(8,128)(2,1)S(1)}, bf16[1,1,1,96,384]{4,3,2,1,0:T(8,128)(2,1)S(1)}, u32[]{:S(2)}, u32[]{:S(2)}) collective-permute-start(bf16[1,1,1,96,384]{4,3,2,1,0:T(8,128)(2,1)S(1)} %get-tuple-element.285), channel_id=1, source_target_pairs={{0,16},{4,20},{8,24},{12,28},{16,0},{20,4},{24,8},{28,12},{1,17},{... | collective-permute-start | bytes 221192 | tf_op jit(solution)/shard_map/ppermute | solution.py:247
  468.0 5.1 collective-permute-start.46
  473.2 5.5 %collective-permute-start.48 = (bf16[1,1,1,208,128]{4,3,2,1,0:T(8,128)(2,1)S(1)}, bf16[1,1,1,208,128]{4,3,2,1,0:T(8,128)(2,1)S(1)}, u32[]{:S(2)}, u32[]{:S(2)}) collective-permute-start(bf16[1,1,1,208,128]{4,3,2,1,0:T(8,128)(2,1)S(1)} %get-tuple-element.298), channel_id=1, source_target_pairs={{0,16},{4,20},{8,24},{12,28},{16,0},{20,4},{24,8},{28,12},{1,17},{... | collective-permute-start | bytes 159752 | tf_op jit(solution)/shard_map/ppermute | solution.py:247
  478.7 5.1 collective-permute-start.49
  483.8 4.8 collective-permute-start.50
  488.7 5.9 %collective-permute-start.51 = (bf16[2,2,208,128]{3,2,0,1:T(8,128)(2,1)S(1)}, bf16[2,2,208,128]{3,2,0,1:T(8,128)(2,1)S(1)}, u32[]{:S(2)}, u32[]{:S(2)}) collective-permute-start(bf16[2,2,208,128]{3,2,0,1:T(8,128)(2,1)S(1)} %pad_maximum_fusion.25), channel_id=1, source_target_pairs={{0,4},{4,0},{8,12},{12,8},{16,20},{20,16},{24,28},{28,24},{1,5},{5... | collective-permute-start | bytes 638984 | tf_op jit(solution)/shard_map/ppermute | solution.py:247
  499.4 14.6 %all-to-all-start.2 = ((bf16[4,240,384]{2,1,0:T(8,128)(2,1)}), bf16[4,240,384]{2,1,0:T(8,128)(2,1)S(1)}, u32[]{:S(2)}, u32[]{:S(2)}) async-start(bf16[4,240,384]{2,1,0:T(8,128)(2,1)} %constant_dynamic-update-slice_fusion.17), calls=%async_computation.3 | async-start | bytes 1474560 | tf_op jit(solution)/shard_map/all_to_all | solution.py:629
  (103 other events, 344.2 us)
Sparse Core Ops, SparseCore 0:
  82.4 52.5 all-gather.4
  137.8 63.7 all-gather.6
  340.7 90.4 reduce-scatter.1

commit v4 on v3

--- a/solution.py
+++ b/solution.py
@@ -14,7 +14,6 @@
 BF = jnp.bfloat16
 F32 = jnp.float32
 LANES = 128
-VMEM_BYTES = 56 * 2**20
 
 
 def dot(left, right, left_dim, right_dim):
@@ -45,10 +44,12 @@
     return starts, jnp.exp(-rate * starts)
 
 
-def spectra_kernel(unroll, rate_ref, coef_ref, sign_ref, wave_ref, *refs):
-    cos_ref, sin_ref, kern_ref, flat_ref = refs[-4:]
+def spectra_kernel(unroll, rate_ref, coef_ref, sign_ref, wave_home, *refs):
+    cos_ref, sin_ref, kern_ref, flat_ref, wave_ref, sem = refs[-6:]
     pairs = rate_ref.shape[0]
     length = wave_ref.shape[1]
+    load = pltpu.make_async_copy(wave_home, wave_ref, sem)
+    load.start()
     count = length // LANES
     lower = lax.broadcasted_iota(jnp.int32, (count, LANES), 1) < LANES // 2
 
@@ -68,6 +69,7 @@
         flat_ref[:, part * LANES : (part + 1) * LANES] = kern_ref[
             pl.ds(part, 2 * pairs, stride=count), :
         ].astype(BF)
+    load.wait()
     chunk = 256
     for part in range(length // chunk):
         rows = slice(part * chunk, (part + 1) * chunk)
@@ -84,11 +86,19 @@
     return 16 if pairs % 16 == 0 else 8
 
 
-def spectra(coef, rate, sign, wave, part, earlier):
-    channels = 2 * coef.shape[0]
+def table_bytes(wave):
+    return 2 * wave.shape[0] * wave.shape[1] + 12 * 2**20
+
+
+def whole_table(wave):
+    return pl.BlockSpec(wave.shape, lambda j: (0, 0), pipeline_mode=pl.Buffered(1))
+
+
+def spectra(coef, rate, sign, wave, layer, part, earlier):
+    channels = 2 * coef.shape[1]
     length = wave.shape[1]
     block = channel_block(channels)
-    rows = pl.BlockSpec((block // 2, LANES), lambda j: (part, 0))
+    rows = pl.BlockSpec((None, block // 2, LANES), lambda j: (layer, part, 0))
     lanes = pl.BlockSpec((length, block), lambda j: (0, part))
     shape = jax.ShapeDtypeStruct((length, channels), BF)
     return pl.pallas_call(
@@ -99,16 +109,18 @@
             rows,
             rows,
             pl.BlockSpec((1, block), lambda j: (0, part)),
-            pl.BlockSpec((2 * length, length), lambda j: (0, 0)),
+            pl.BlockSpec(memory_space=pltpu.HBM),
         ]
         + [pl.BlockSpec(memory_space=pl.ANY)] * len(earlier),
         out_specs=(lanes, lanes),
         scratch_shapes=[
             pltpu.VMEM((block * length // LANES, LANES), F32),
             pltpu.VMEM((block, length), BF),
+            pltpu.VMEM(wave.shape, BF),
+            pltpu.SemaphoreType.DMA,
         ],
         input_output_aliases={4 + j: j for j in range(len(earlier))},
-        compiler_params=pltpu.CompilerParams(vmem_limit_bytes=VMEM_BYTES),
+        compiler_params=pltpu.CompilerParams(vmem_limit_bytes=table_bytes(wave)),
         cost_estimate=pl.CostEstimate(
             flops=12 * length * length * block,
             bytes_accessed=4 * length * length + 4 * length * block,
@@ -158,24 +170,25 @@
     lax.fori_loop(0, pairs // unroll, pair, 0)
 
 
-def state_grads(coef, rate, cosines, sines, wave):
-    channels = 2 * coef.shape[0]
+def state_grads(coef, rate, cosines, sines, wave, layer):
+    channels = 2 * coef.shape[1]
     length = wave.shape[1]
     block = channel_block(channels)
-    rows = pl.BlockSpec((block // 2, LANES), lambda j: (j, 0))
+    rows = pl.BlockSpec((None, block // 2, LANES), lambda j: (layer, j, 0))
+    made = pl.BlockSpec((block // 2, LANES), lambda j: (j, 0))
     lanes = pl.BlockSpec((length, block), lambda j: (0, j))
-    shape = jax.ShapeDtypeStruct(coef.shape, F32)
+    shape = jax.ShapeDtypeStruct(coef.shape[1:], F32)
     return pl.pallas_call(
         partial(state_grads_kernel, unroll_of(block // 2)),
         out_shape=(shape, shape),
         grid=(channels // block,),
-        in_specs=[rows, rows, lanes, lanes, pl.BlockSpec((2 * length, length), lambda j: (0, 0))],
-        out_specs=(rows, rows),
+        in_specs=[rows, rows, lanes, lanes, whole_table(wave)],
+        out_specs=(made, made),
         scratch_shapes=[
             pltpu.VMEM((block, 2 * length), BF),
             pltpu.VMEM((block * length // LANES, LANES), F32),
         ],
-        compiler_params=pltpu.CompilerParams(vmem_limit_bytes=VMEM_BYTES),
+        compiler_params=pltpu.CompilerParams(vmem_limit_bytes=table_bytes(wave)),
         cost_estimate=pl.CostEstimate(
             flops=12 * length * length * channels,
             bytes_accessed=4 * length * length + 4 * length * channels,
@@ -206,21 +219,9 @@
     return row_major(whole.reshape(count * block.shape[0], block.shape[1])), wait
 
 
-def seq_reduce(blocks, count):
-    blocks = dict(enumerate(blocks))
-    bit = 1
-    while bit < count:
-        for member in sorted(blocks, reverse=True):
-            if member & bit:
-                sent = blocks.pop(member).astype(BF)
-                came = lax.ppermute(sent, "seq", pairs_of(count, bit))
-                blocks[member ^ bit] = blocks[member ^ bit] + came.astype(F32)
-        bit *= 2
-    return blocks[0]
-
-
 def seq_reduce_rows(whole, count):
-    return reduce_bits(whole.reshape(count, -1, whole.shape[1]), "seq", count, bits_of(count), F32)
+    blocks = whole.reshape(count, -1, whole.shape[1])
+    return reduce_bits(blocks, "seq", count, bits_of(count), F32)
 
 
 def row_major(array):
@@ -264,9 +265,9 @@
     return block.reshape((count,) + block.shape[len(done) :]), wait
 
 
-def cut_half(blocks, axis, count, bit):
+def cut_half(blocks, axis, count, bit, turn=0):
     level = far_first(count).index(bit)
-    side = (lax.axis_index(axis) // bit) % 2
+    side = ((lax.axis_index(axis) ^ turn) // bit) % 2
     sent = lax.dynamic_slice_in_dim(blocks, 1 - side, 1, level).astype(BF)
     return lax.dynamic_slice_in_dim(blocks, side, 1, level), sent
 
@@ -309,28 +310,32 @@
     return jnp.stack([-spectrum[1], spectrum[0]])
 
 
-def run_layer(stream, keep, early, late, hat, skip, tables, count, filler):
-    w_value, gain, bias = early
+def run_layer(stream, rows_all, keep, norm, early, late, hat, skip, tables, count, beside_rows, beside_product):
+    gain, bias = norm
     waves, waves_back = tables
     length = waves.shape[1]
     xhat, factor = normalize(stream)
-    own, made = filler[0]((xhat * gain + bias).astype(BF))
-    normed, made = seq_rows(own, count, made)
+    if rows_all is None:
+        own, wait = beside_rows((xhat * gain + bias).astype(BF))
+        normed, wait = seq_rows(own, count, wait)
+    else:
+        normed, wait = (normalize(rows_all.astype(F32))[0] * gain + bias).astype(BF), ()
+    w_value = early(wait)
     value_act, value_slope = gelu_parts(dot(normed, w_value, 1, 0))
     values = (value_act * keep).astype(BF)
     value_slope = (value_slope * keep).astype(BF)
     values, value_slope = together(values, value_slope)
     x_hat = dot(waves, values, 1, 0).astype(BF)
-    k_cos, k_sin = hat
+    k_cos, k_sin = hat()
     x_cos, x_sin = x_hat[:length].astype(F32), x_hat[length:].astype(F32)
     y_hat = jnp.concatenate([k_cos * x_cos - k_sin * x_sin, k_cos * x_sin + k_sin * x_cos], 0).astype(BF)
     mixes = dot(waves_back, y_hat, 1, 0) * (1.0 / length) + skip * values.astype(F32)
     width = mixes.shape[1] // 2
     product = (mixes[:, :width] * mixes[:, width:]).astype(BF)
     product, mixes = together(product, mixes.astype(BF))
-    product, made = filler[1](product, made)
-    products, made = seq_gather(product, count, made)
-    w_gate, w_mix, w_out = late
+    product, wait = beside_product(product)
+    products, wait = seq_gather(product, count, wait)
+    w_gate, w_mix, w_out = late(wait)
     gate_act, gate_slope = gelu_parts(dot(normed, w_gate, 1, 0))
     update = dot(products[0], w_mix[0], 1, 0)
     for member in range(1, count):
@@ -352,7 +357,7 @@
         products,
         mixed,
     )
-    return result, saved, made
+    return result, saved
 
 
 def back_gate(grad_stream, saved, late, count, wait):
@@ -365,7 +370,15 @@
     update_low, gate_grad = together(update_low, gate_grad)
     width = products[0].shape[1]
     model = out_low.shape[1]
-    product_low = seq_reduce([dot(update_low, w_mix[m], 1, 1) for m in range(count)], count)
+    blocks = dict(enumerate(dot(update_low, w_mix[m], 1, 1) for m in range(count)))
+    for bit in bits_of(count):
+        for member in sorted(blocks, reverse=True):
+            if member & bit:
+                sent = blocks.pop(member).astype(BF)
+                if member == count // 2:
+                    sent, update_low, gate_grad, out_low = together(sent, update_low, gate_grad, out_low)
+                blocks[member ^ bit] = add_half(blocks[member ^ bit], swap(sent, "seq", count, bit), F32)
+    product_low = blocks[0]
     grad_out = [
         dot(mixed, out_low[:, j * width : (j + 1) * width], 0, 0).astype(BF) for j in range(model // width)
     ]
@@ -436,13 +449,14 @@
     norm_rows = jnp.stack([ln_gain, ln_bias], 1).reshape(2 * depth, in_rows)
     norm_rows = jnp.pad(norm_rows, ((0, 16 - 2 * depth), (0, width - in_rows)))
     first = jnp.concatenate([value_columns(0), jnp.broadcast_to(norm_rows, (count,) + norm_rows.shape)], 1)
+    first, tokens = together(first, tokens)
     first = lax.all_to_all(first, "seq", 0, 0, tiled=True)
+    rows_all, _ = seq_rows(tokens, count, ())
     pieces = [by_column(w_gate[0]), by_column(w_mix[0])]
     for layer in range(1, depth):
         pieces += [value_columns(layer), by_column(w_gate[layer]), by_column(w_mix[layer])]
     sizes = [piece.shape[1] for piece in pieces]
-    rest = lax.all_to_all(jnp.concatenate(pieces, 1), "seq", 0, 0, tiled=True)
-    rest = [piece for piece in jnp.split(rest, np.cumsum(sizes)[:-1].tolist(), axis=1)]
+    first, rest = together(first, jnp.concatenate(pieces, 1))
 
     coefs = ssm_coef.reshape(depth, width, 2 * states)
     rates = ssm_rate.reshape(depth, width, 2 * states)
@@ -451,9 +465,9 @@
     table_parts = 2 * width // channel_block(2 * width)
 
     def make_tables(layer, parts_made, hat, tie):
-        rate, tie = together(rates[layer], tie)
+        rate, tie = together(rates, tie)
         for part in parts_made:
-            hat = spectra(coefs[layer], rate, sign, waves, part, hat)
+            hat = spectra(coefs, rate, sign, waves, layer, part, hat)
         return hat, tie
 
     def flat(piece):
@@ -471,6 +485,9 @@
     n_in = count * in_rows
     pair = [jnp.concatenate([sides[0], flat(norm_piece)], 0), sides[1]]
     paths = [far_first(dp), y_first(dp)[:1] + far_first(dp)[:-1]]
+    pair, rest = together(pair, rest)
+    rest = lax.all_to_all(rest, "seq", 0, 0, tiled=True)
+    rest = jnp.split(rest, np.cumsum(sizes)[:-1].tolist(), axis=1)
     late_block = jnp.concatenate([flat(rest[0]), flat(rest[1])] + out_sides(0), 0)
     done = [[], []]
     hat = ()
@@ -479,13 +496,14 @@
         if step < table_parts:
             hat, pair = make_tables(0, [step], hat, pair)
             others, hat = together(others, hat)
-        if step == 0:
+        if step == 1:
             others, late_block = together(others, late_block)
         for j in range(2):
             done[j] = sorted(done[j] + [paths[j][step]], reverse=True)
             pair[j] = join(pair[j], others[j], "dp", paths[j][step], done[j])
     hat, pair = make_tables(0, range(len(bits_of(dp)), table_parts), hat, pair)
     hats = [hat]
+    pair, rows_all = together(pair, rows_all)
     side_a, side_b = [block.reshape((dp,) + block.shape[-2:]) for block in pair]
     norms = side_a[:, n_in:].reshape(dp, 16, -1)[:, : 2 * depth, :n_in]
     norms = norms.transpose(1, 0, 2).reshape(depth, 2, model).astype(F32)
@@ -502,34 +520,54 @@
         return cut.reshape(dp * mix_rows, model)
 
     early = [(value_weight(side_a[:, :n_in], side_b), norms[0, 0], norms[0, 1])]
-    got = lax.all_gather(late_block, "dp", axis=0)
-    gate, mix, out = jnp.split(got, [n_in, n_in + count * mix_rows], axis=1)
-    late = [(gate.reshape(model, width), mix_weight(mix), out_weight(out))]
-    for layer in range(1, depth):
+    got_late = lax.all_gather(late_block, "dp", axis=0)
+
+    def late_weights(got):
+        gate, mix, out = jnp.split(got, [n_in, n_in + count * mix_rows], axis=1)
+        return gate.reshape(model, width), mix_weight(mix), out_weight(out)
+
+    def layer_block(layer):
         value, gate, mix = rest[3 * layer - 1 : 3 * layer + 2]
-        block = jnp.concatenate(value_sides(value) + [flat(gate), flat(mix)] + out_sides(layer), 0)
-        got = lax.all_gather(block, "dp", axis=0)
-        cuts = np.cumsum([n_in, n_in, n_in, count * mix_rows]).tolist()
-        side_a, side_b, gate, mix, out = jnp.split(got, cuts, axis=1)
-        early.append((value_weight(side_a, side_b), norms[layer, 0], norms[layer, 1]))
-        late.append((gate.reshape(model, width), mix_weight(mix), out_weight(out)))
-
+        return jnp.concatenate(value_sides(value) + [flat(gate), flat(mix)] + out_sides(layer), 0)
+
+    got_layers = [None] + [lax.all_gather(layer_block(layer), "dp", axis=0) for layer in range(1, depth)]
+
+    late = []
     stream = tokens.astype(F32)
     kept = []
     for layer in range(depth):
-        if layer + 1 < depth:
-            cut = min(2, table_parts)
-            filler = (
-                lambda own: make_tables(layer + 1, range(cut), (), own)[::-1],
-                lambda product, made: make_tables(layer + 1, range(cut, table_parts), made, product)[::-1],
-            )
-        else:
-            filler = (lambda own: (own, ()), lambda product, made: (product, made))
-        stream, saved, made = run_layer(
-            stream, keep, early[layer], late[layer], hats[layer], skips[layer], tables, count, filler
+
+        def beside_rows(own):
+            return own, got_layers[layer]
+
+        def early_weights(got):
+            if layer:
+                side_a, side_b, got = jnp.split(got, [n_in, 2 * n_in], axis=1)
+                early.append((value_weight(side_a, side_b), norms[layer, 0], norms[layer, 1]))
+                late.append(late_weights(got))
+            return early[layer][0]
+
+        def beside_product(product):
+            hat = ()
+            if layer + 1 < depth:
+                hat, product = make_tables(layer + 1, range(table_parts), (), product)
+            return product, (() if layer else got_late, hat)
+
+        def later_weights(wait):
+            if not layer:
+                late.append(late_weights(wait[0]))
+            hats.append(wait[1])
+            return late[layer]
+
+        stream, saved = run_layer(
+            stream, None if layer else rows_all, keep, norms[layer], early_weights, later_weights,
+            lambda: hats[layer], skips[layer], tables, count, beside_rows, beside_product,
         )
         kept.append(saved)
-        hats.append(made)
+
+    def owner_pieces(rows_list):
+        pieces = [piece.reshape(count, -1, width) for piece in rows_list]
+        return jnp.concatenate(pieces, 1), np.cumsum([piece.shape[1] for piece in pieces])[:-1].tolist()
 
     def natural(blocks):
         whole = jnp.zeros((count,) + blocks[0].shape, blocks[0].dtype)
@@ -541,93 +579,128 @@
     norm_grads = [None] * depth
     ssm_grads = [None] * depth
     held = [None] * depth
-    whole, kern_hat = None, None
+    kern_hat = None
+    turn = lax.axis_index("seq") * (dp // count)
+    paths = [y_first(dp), z_first(dp), y_first(dp)]
+    turns = [turn, 0, 0]
+
+    def sent_dp(pairs, at):
+        return [
+            (pair[0], swap(pair[1], "dp", dp, path[step])) for pair, path, step in zip(pairs, paths, at)
+        ]
+
+    def next_dp(pairs, at):
+        return [
+            cut_half(add_half(*pair, BF), "dp", dp, path[step], side)
+            for pair, path, side, step in zip(pairs, paths, turns, at)
+        ]
+
     for layer in reversed(range(depth)):
         low = grad_stream.astype(BF)
         wait = ()
         if kern_hat is not None:
-            low, whole, kern_hat = together(low, whole, kern_hat)
-            held[layer + 1] = lax.psum_scatter(whole, "dp", scatter_dimension=0, tiled=False)
-            wait = state_grads(coefs[layer + 1], rates[layer + 1], *kern_hat, waves)
+            low, kern_hat = together(low, kern_hat)
+            wait = state_grads(coefs, rates, *kern_hat, waves, layer + 1)
         product_low, gate_part, terms, wait = back_gate(low, kept[layer], late[layer], count, wait)
         if kern_hat is not None:
             ssm_grads[layer + 1] += wait
         grad_gate, grad_mix, grad_out = terms
-        mix = natural(grad_mix).reshape(dp, count * mix_rows, width)
         others = [grad_gate.reshape(dp, n_in, width)] + [g.reshape(dp, mix_rows, width) for g in grad_out]
-        others = jnp.concatenate(others, 1)
         if not layer:
-            paths = [y_first(dp), z_first(dp)]
-            moving = [cut_half(bit_blocks(b, dp), "dp", dp, path[0]) for b, path in zip((mix, others), paths)]
+            blocks = [jnp.stack(grad_mix).reshape(dp, count * mix_rows, width), jnp.concatenate(others, 1)]
+            moving = [
+                cut_half(bit_blocks(block, dp), "dp", dp, path[0], side)
+                for block, path, side in zip(blocks, paths, turns)
+            ]
             product_low, moving = together(product_low, moving)
-            moving = [(pair[0], swap(pair[1], "dp", dp, path[0])) for pair, path in zip(moving, paths)]
+            moving = sent_dp(moving, (0, 0))
         value_grad, kern_hat, grad_skip = back_convolution(product_low, kept[layer], hats[layer], skips[layer], tables)
         ssm_grads[layer] = (grad_skip,)
-        normed = kept[layer][2]
         if not layer:
             value_grad, moving = together(value_grad, moving)
-            moving = [cut_half(add_half(*pair, BF), "dp", dp, path[1]) for pair, path in zip(moving, paths)]
-        values = [dot(normed, value_grad[:, j * width : (j + 1) * width], 0, 0).astype(BF) for j in range(2)]
-        values = [g.reshape(dp, n_in, width) for g in values]
+            moving = next_dp(moving, (1, 1))
+        normed = kept[layer][2]
+        values = dot(normed, value_grad, 0, 0).astype(BF).reshape(dp, n_in, 2 * width)
         parts = dot(value_grad, early[layer][0], 1, 1) + gate_part
+        sums = bit_blocks(parts.reshape(count, rows, model), count)
         if layer:
-            grad_normed = reduce_bits(
-                parts.reshape(count, rows, model), "seq", count, bits_of(count), F32
-            )
-            whole = jnp.concatenate([mix, others] + values, 1)
+            block = [natural(grad_mix).reshape(dp, count * mix_rows, width)] + others
+            block = jnp.concatenate(block + [values[:, :, :width], values[:, :, width:]], 1)
+            held[layer] = lax.psum_scatter(block, "dp", scatter_dimension=0, tiled=False)
         else:
-            moving += [cut_half(bit_blocks(g, dp), "dp", dp, path[0]) for g, path in zip(values, paths)]
-            paths = [path[1:] for path in paths] + paths
-            sums = bit_blocks(parts.reshape(count, rows, model), count)
-            for step, bit in enumerate(bits_of(count)):
-                held_rows, sent = cut_half(sums, "seq", count, bit)
-                if step == 1:
-                    sent, moving, kern_hat = together(sent, moving, kern_hat)
-                    moving = [(pair[0], swap(pair[1], "dp", dp, path[0])) for pair, path in zip(moving, paths)]
-                    came = swap(sent, "seq", count, bit)
-                    last = state_grads(coefs[0], rates[0], *kern_hat, waves)
-                    came, moving, last = together(came, moving, last)
-                    ssm_grads[0] += last
-                else:
-                    came = swap(sent, "seq", count, bit)
-                sums = add_half(held_rows, came, F32)
-            grad_normed = sums.reshape(rows, model)
+            moving.append(cut_half(bit_blocks(values, dp), "dp", dp, paths[2][0]))
+        for step, bit in enumerate(bits_of(count)):
+            held_rows, sent = cut_half(sums, "seq", count, bit)
+            if step == 1 and not layer:
+                sent, moving, kern_hat = together(sent, moving, kern_hat)
+                came = swap(sent, "seq", count, bit)
+                moving = sent_dp(moving, (1, 1, 0))
+                last = state_grads(coefs, rates, *kern_hat, waves, 0)
+                came, moving, last = together(came, moving, last)
+                ssm_grads[0] += last
+            else:
+                came = swap(sent, "seq", count, bit)
+            sums = add_half(held_rows, came, F32)
+        grad_normed = sums.reshape(rows, model)
         grad_stream, norm_grads[layer] = back_norm(grad_stream, grad_normed, kept[layer], early[layer][1])
 
     own = width // dp
     both = 2 * states
+    norm_all = jnp.stack(norm_grads).reshape(2 * depth, dp, n_in).transpose(1, 0, 2)
+    lanes = -(-max(2 * own, n_in) // both) * both
     skip_rows = jnp.stack([g[0].reshape(dp, 2 * own) for g in ssm_grads], 1)
-    skip_rows = jnp.pad(skip_rows, ((0, 0), (0, 16 - depth), (0, -2 * own % both))).reshape(dp, -1, both)
+    skip_rows = jnp.concatenate(
+        [
+            jnp.pad(skip_rows, ((0, 0), (0, 0), (0, lanes - 2 * own))),
+            jnp.pad(norm_all, ((0, 0), (0, 16 - 3 * depth), (0, lanes - n_in))),
+        ],
+        1,
+    ).reshape(dp, -1, both)
     states_all = jnp.stack([g[j].reshape(dp, own, both) for g in ssm_grads for j in (1, 2)], 1).astype(BF)
     ssm_rows = jnp.concatenate([states_all.reshape(dp, 2 * depth * own, both), skip_rows.astype(BF)], 1)
 
     sums = [add_half(*pair, BF) for pair in moving] + [bit_blocks(ssm_rows, dp)]
-    paths = [path[1:] for path in paths] + [y_first(dp)]
+    paths = [paths[0][2:], paths[1][2:], paths[2][1:], y_first(dp)]
+    turns = turns + [0]
+
+    def flat_sum(j):
+        return sums[j].reshape(sums[j].shape[-2:])
+
+    first_round = True
     while any(paths):
         active = [j for j, path in enumerate(paths) if path]
-        pairs = [cut_half(sums[j], "dp", dp, paths[j][0]) for j in active]
+        pairs = [cut_half(sums[j], "dp", dp, paths[j][0], turns[j]) for j in active]
         pairs = lax.optimization_barrier(pairs)
         pairs = [(pair[0], swap(pair[1], "dp", dp, paths[j][0])) for j, pair in zip(active, pairs)]
-        pairs = lax.optimization_barrier(pairs)
+        if first_round:
+            pairs, held = together(pairs, held)
+            first_round = False
+        else:
+            pairs = lax.optimization_barrier(pairs)
         for j, pair in zip(active, pairs):
             sums[j] = add_half(*pair, BF)
             paths[j] = paths[j][1:]
-    sums = [block.reshape(block.shape[-2:]) for block in sums]
-    held[0] = jnp.concatenate(sums[:4], 0)
-    ssm_sum = gather_bits(sums[4], "dp", dp, far_first(dp))[0].astype(F32)
-    for layer in range(depth):
-        cuts = np.cumsum([count * mix_rows, n_in, out_parts * mix_rows, n_in]).tolist()
-        mix, gate, outs, side_a, side_b = jnp.split(held[layer], cuts, axis=0)
-        held[layer] = ([side_a, side_b], gate, mix, outs)
-
-    pieces = []
-    for layer in range(depth):
-        values, gate, mix, outs = held[layer]
-        pieces += [gate.reshape(count, in_rows, width), mix.reshape(count, mix_rows, width)]
-        pieces += [side.reshape(count, in_rows, width) for side in values]
-    sizes = [piece.shape[1] for piece in pieces]
-    back = lax.all_to_all(jnp.concatenate(pieces, 1), "seq", 0, 0, tiled=True)
-    back = jnp.split(back, np.cumsum(sizes)[:-1].tolist(), axis=1)
+    own_sum = flat_sum(3)
+    norm_own = own_sum[2 * depth * own :].reshape(16, lanes)[depth : 3 * depth, :n_in]
+    norm_own = norm_own.reshape(2 * depth, count, in_rows).transpose(1, 0, 2)
+    norm_own = jnp.pad(norm_own, ((0, 0), (0, 16 - 2 * depth), (0, width - in_rows)))
+    cuts = np.cumsum([count * mix_rows, n_in, out_parts * mix_rows, n_in]).tolist()
+    value_sums = flat_sum(2)
+    rows_list = [flat_sum(1)[:n_in], flat_sum(0), value_sums[:, :width], value_sums[:, width:]]
+    outs = [flat_sum(1)[n_in:]]
+    for layer in range(1, depth):
+        mix, gate, out, side_a, side_b = jnp.split(held[layer], cuts, axis=0)
+        outs.append(out)
+        rows_list += [gate, mix, side_a, side_b]
+    last, last_cuts = owner_pieces(rows_list + [norm_own.reshape(count * 16, width)])
+    own_sum, last = together(own_sum, last)
+    last = lax.all_to_all(last, "seq", 0, 0, tiled=True)
+    ssm_sum, last = gather_bits(own_sum, "dp", dp, far_first(dp), last)
+    ssm_sum = ssm_sum.astype(F32)
+    back_parts = jnp.split(last, last_cuts, axis=1)
+    norm_came = back_parts.pop()
+    back = back_parts
+    norm_sum = jnp.sum(norm_came[:, : 2 * depth, :in_rows].astype(F32), 0).reshape(depth, 2, in_rows)
 
     def columns(block):
         cut = block.reshape(count, -1, dp, share).transpose(1, 2, 0, 3)
@@ -646,15 +719,11 @@
         gates.append(columns(gate))
         mixes.append(columns(mix))
         values.append(value_share([side_a, side_b]))
-    outs = [out_share(held[layer][3]) for layer in range(depth)]
-
-    norm_all = jnp.stack(norm_grads).reshape(2 * depth, dp * count, in_rows).transpose(1, 0, 2)
-    norm_all = norm_all.reshape(dp * count, 2 * depth * in_rows)
-    norm_sum = jnp.sum(lax.all_to_all(norm_all, ("dp", "seq"), 0, 0, tiled=True), 0).reshape(depth, 2, in_rows)
+    outs = [out_share(out) for out in outs]
 
     state_sum = ssm_sum[:, : 2 * depth * own].reshape(dp, depth, 2, own, both).transpose(1, 2, 0, 3, 4)
     coef_sum, rate_sum = state_sum[:, 0], state_sum[:, 1]
-    skip_sum = ssm_sum[:, 2 * depth * own :].reshape(dp, 16, -1)[:, :depth, : 2 * own].transpose(1, 0, 2)
+    skip_sum = ssm_sum[:, 2 * depth * own :].reshape(dp, 16, lanes)[:, :depth, : 2 * own].transpose(1, 0, 2)
     return (
         stream,
         grad_stream,

time: 533 us -> 490 us (0.919)
  waiting for transfers between devices: 149 us -> 122 us
  Pallas kernels: 76 us -> 52.8 us
  starting transfers between devices: 62.6 us -> 51.9 us
  matrix products: 92.3 us -> 101 us
    ppermute x40 -> x43, waiting for transfers between devices: 60.6 us -> 105 us  [swap(): return lax.ppermute(block, axis, pairs_of(count, bit))]
    ppermute x6 -> x0, waiting for transfers between devices: 29.7 us -> none  [seq_reduce(): came = lax.ppermute(sent, 'seq', pairs_of(count, bit))]
    all_gather x2, waiting for transfers between devices: 28.2 us -> 9.06 us  [the longest x1 9.06 us: shards(): lax.all_gather(layer_block(layer), 'dp', axis=0)]
    pallas_call x6, Pallas kernels: 47.4 us -> 30.4 us  [spectra(): pl.pallas_call(partial(spectra_kernel, unroll_of(block // 2)), out_shape=...]
    ppermute x6, waiting for transfers between devices: 17.4 us -> 4.34 us  [seq_gather(): lax.ppermute(blocks[member], 'seq', pairs_of(count, bit))]
    dot_general x58 -> x56, matrix products: 92.3 us -> 101 us  [dot(): lax.dot_general(left, right, (((left_dim,), (right_dim,)), ((), ())), pre...]
    all_to_all x3 -> x2, waiting for transfers between devices: 12.9 us -> 4.36 us  [the longest x1 4.36 us: shards(): last = lax.all_to_all(last, 'seq', 0, 0, tiled=True)]
    pallas_call x2, Pallas kernels: 28.6 us -> 22.3 us  [state_grads(): pl.pallas_call(partial(state_grads_kernel, unroll_of(block // 2)), out_sh...]
  transfers between devices with their start and end apart: 59 -> 55, of which waited for: 21 -> 21; matrix products, arithmetic and copies ran while one was open for 34% -> 40% of each run, Pallas kernels for 14% -> 11%
where the time goes in v4:
time: 490 us; the launch traced here: 482 us
  waiting for transfers between devices  122 us (25%)
  matrix products  101 us (21%)
  local copies, waits for them, and re-layouts  79.5 us (16%)
  other arithmetic  56.7 us (12%)
  Pallas kernels  52.8 us (11%)
  starting transfers between devices  51.9 us (11%)
  between operations  17.6 us (4%)
    ppermute x43, waiting for transfers between devices, swap(): return lax.ppermute(block, axis, pairs_of(count, bit))  105 us
    dot_general x56, matrix products, dot(): lax.dot_general(left, right, (((left_dim,), (right_dim,)), ((), ())), pre...  101 us
    unnamed x284, local copies, waits for them, and re-layouts  39.1 us
    ppermute x43, starting transfers between devices, swap(): return lax.ppermute(block, axis, pairs_of(count, bit))  37.4 us
    pallas_call x6, Pallas kernels, spectra(): pl.pallas_call(partial(spectra_kernel, unroll_of(block // 2)), out_shape=...  30.4 us
    pallas_call x2, Pallas kernels, state_grads(): pl.pallas_call(partial(state_grads_kernel, unroll_of(block // 2)), out_sh...  22.3 us
    another operation x33, other arithmetic, join(): return jnp.stack(pair, done.index(bit))  13.7 us
  transfers between devices with their start and end apart: 55, of which 21 were waited for; matrix products, arithmetic and copies ran while one was open for 40% of the time, Pallas kernels for 11%

profile of v4, /device:TPU:0, one launch (start us, length us, event | category | flops | bytes accessed | tf_op | source)
XLA Modules:
  0.0 481.9 jit_solution(10057340416192710338)
XLA Ops:
  9.8 4.2 all-to-all-start
  21.8 3.3 collective-permute-start
  26.6 3.5 all-to-all-start.1
  30.2 2.2 copy-done
  32.4 5.0 %spectra.6 = (bf16[1024,768]{1,0:T(8,128)(2,1)S(1)}, bf16[1024,768]{1,0:T(8,128)(2,1)S(1)}) custom-call(f32[2,384,128]{2,1,0:T(8,128)S(1)} %reshape.414.rate_ref, f32[2,384,128]{2,1,0:T(8,128)S(1)} %reshape.423.coef_ref, f32[1,768]{1,0:T(1,128)S(1)} %copy-done.7, bf16[2048,1024]{1,0:T(8,128)(2,1)S(1)} %copy-done), custom_call_target="tpu_custom_call" | custom-call | flops 3221225472 | bytes 5242880 | tf_op jit(solution)/shard_map/spectra/pallas_call | solution.py:104
  39.6 5.0 %spectra.7 = (bf16[1024,768]{1,0:T(8,128)(2,1)S(1)}, bf16[1024,768]{1,0:T(8,128)(2,1)S(1)}) custom-call(f32[2,384,128]{2,1,0:T(8,128)S(1)} %reshape.414.rate_ref, f32[2,384,128]{2,1,0:T(8,128)S(1)} %reshape.423.coef_ref, f32[1,768]{1,0:T(1,128)S(1)} %copy-done.7, bf16[2048,1024]{1,0:T(8,128)(2,1)S(1)} %copy-done, ...), custom_call_target="tpu_custom_call", output_to_operand_aliasing={{0}: (4, {}), {1}: (5, {})} | custom-call | flops 3221225472 | bytes 5242880 | tf_op jit(solution)/shard_map/spectra/pallas_call | solution.py:104
  45.8 2.0 collective-permute-done.3
  53.8 7.8 %collective-permute-done.6 = bf16[256,768]{1,0:T(8,128)(2,1)} collective-permute-done((bf16[256,768]{1,0:T(8,128)(2,1)S(1)}, bf16[256,768]{1,0:T(8,128)(2,1)}, u32[]{:S(2)}, u32[]{:S(2)}) %collective-permute-start.6) | collective-permute-done | bytes 393248 | tf_op jit(solution)/shard_map/ppermute | solution.py:248
  69.4 2.2 copy-done.1
  73.0 5.0 %spectra.8 = (bf16[1024,768]{1,0:T(8,128)(2,1)S(1)}, bf16[1024,768]{1,0:T(8,128)(2,1)S(1)}) custom-call(f32[2,384,128]{2,1,0:T(8,128)S(1)} %reshape.414.rate_ref, f32[2,384,128]{2,1,0:T(8,128)S(1)} %reshape.423.coef_ref, f32[1,768]{1,0:T(1,128)S(1)} %copy-done.7, bf16[2048,1024]{1,0:T(8,128)(2,1)S(1)} %copy-done.1, ...), custom_call_target="tpu_custom_call", output_to_operand_aliasing={{0}: (4, {}), {1}: (5, {})} | custom-call | flops 3221225472 | bytes 5242880 | tf_op jit(solution)/shard_map/spectra/pallas_call | solution.py:104
  85.1 2.1 fusion.5
  87.2 3.5 fusion.19
  90.8 3.6 fusion.52
  94.5 1.9 fusion.81
  97.2 3.3 fusion.241
  102.9 5.0 %spectra.9 = (bf16[1024,768]{1,0:T(8,128)(2,1)S(1)}, bf16[1024,768]{1,0:T(8,128)(2,1)S(1)}) custom-call(f32[2,384,128]{2,1,0:T(8,128)S(1)} %reshape.414.rate_ref, f32[2,384,128]{2,1,0:T(8,128)S(1)} %reshape.423.coef_ref, f32[1,768]{1,0:T(1,128)S(1)} %copy-done.7, bf16[2048,1024]{1,0:T(8,128)(2,1)S(1)} %copy-done.2), custom_call_target="tpu_custom_call" | custom-call | flops 3221225472 | bytes 5242880 | tf_op jit(solution)/shard_map/spectra/pallas_call | solution.py:104
  107.9 5.4 %spectra.10 = (bf16[1024,768]{1,0:T(8,128)(2,1)S(1)}, bf16[1024,768]{1,0:T(8,128)(2,1)S(1)}) custom-call(f32[2,384,128]{2,1,0:T(8,128)S(1)} %reshape.414.rate_ref, f32[2,384,128]{2,1,0:T(8,128)S(1)} %reshape.423.coef_ref, f32[1,768]{1,0:T(1,128)S(1)} %copy-done.7, bf16[2048,1024]{1,0:T(8,128)(2,1)S(1)} %copy-done.2, ...), custom_call_target="tpu_custom_call", output_to_operand_aliasing={{0}: (4, {}), {1}: (5, {})} | custom-call | flops 3221225472 | bytes 5242880 | tf_op jit(solution)/shard_map/spectra/pallas_call | solution.py:104
  113.4 5.0 %spectra.11 = (bf16[1024,768]{1,0:T(8,128)(2,1)S(1)}, bf16[1024,768]{1,0:T(8,128)(2,1)S(1)}) custom-call(f32[2,384,128]{2,1,0:T(8,128)S(1)} %reshape.414.rate_ref, f32[2,384,128]{2,1,0:T(8,128)S(1)} %reshape.423.coef_ref, f32[1,768]{1,0:T(1,128)S(1)} %copy-done.7, bf16[2048,1024]{1,0:T(8,128)(2,1)S(1)} %copy-done.2, ...), custom_call_target="tpu_custom_call", output_to_operand_aliasing={{0}: (4, {}), {1}: (5, {})} | custom-call | flops 3221225472 | bytes 5242880 | tf_op jit(solution)/shard_map/spectra/pallas_call | solution.py:104
  125.7 2.8 reshape.469
  132.0 1.9 fusion.173
  135.0 3.7 fusion.65
  141.5 2.3 collective-permute-done.11
  148.5 9.7 %collective-permute-done.12 = bf16[1,1,256,768]{3,2,1,0:T(8,128)(2,1)} collective-permute-done((bf16[1,1,256,768]{3,2,1,0:T(8,128)(2,1)S(1)}, bf16[1,1,256,768]{3,2,1,0:T(8,128)(2,1)}, u32[]{:S(2)}, u32[]{:S(2)}) %collective-permute-start.12) | collective-permute-done | bytes 393248 | tf_op jit(solution)/shard_map/ppermute | solution.py:248
  158.2 2.2 fusion.224
  163.6 9.1 %all-gather.7.cloned.1.call-done = bf16[4608,384]{1,0:T(8,128)(2,1)} async-done(((bf16[576,384]{1,0:T(8,128)(2,1)}), bf16[4608,384]{1,0:T(8,128)(2,1)}) %all-gather.7.cloned.1.call-update) | async-done | bytes 3538960 | tf_op jit(solution)/shard_map/all_gather | solution.py:533
  178.2 2.4 collective-permute-done.20
  182.0 2.8 fusion.225
  187.3 3.6 fusion.25
  190.9 3.8 fusion.53
  194.8 1.9 fusion.78
  197.5 3.1 fusion.242
  205.3 1.9 convert_element_type.743
  208.7 2.4 split.87
  212.4 2.8 reshape.470
  219.4 2.5 collective-permute-done.16
  243.6 10.8 %collective-permute-done.24 = bf16[1024,384]{1,0:T(8,128)(2,1)S(1)} collective-permute-done((bf16[1024,384]{1,0:T(8,128)(2,1)S(1)}, bf16[1024,384]{1,0:T(8,128)(2,1)S(1)}, u32[]{:S(2)}, u32[]{:S(2)}) %collective-permute-start.24) | collective-permute-done | bytes 786464 | tf_op jit(solution)/shard_map/ppermute | solution.py:248
  256.6 3.6 fusion.54
  260.2 1.9 fusion.75
  262.2 4.9 %multiply_convert_fusion.1 = bf16[1024,768]{1,0:T(8,128)(2,1)S(1)} fusion(bf16[1024,768]{1,0:T(8,128)(2,1)} %get-tuple-element.232, f32[768]{0:T(1024)S(1)} %copy-done.114, f32[768,1024]{0,1:T(8,128)S(1)} %fusion.75, bf16[1024,1024]{1,0:T(8,128)(2,1)S(1)} %copy-done.119, bf16[1024,768]{1,0:T(8,128)(2,1)S(1)} %get-tuple-element.219, ...), kind=kOutput, calls=%fused_computation.95 | convolution fusion | flops 1627127808 | bytes 16256000 | tf_op jit(solution)/shard_map/dot_general | solution.py:20
  276.7 8.5 %collective-permute-done.26 = bf16[1,1,256,768]{3,2,1,0:T(8,128)(2,1)S(1)} collective-permute-done((bf16[1,1,256,768]{3,2,1,0:T(8,128)(2,1)S(1)}, bf16[1,1,256,768]{3,2,1,0:T(8,128)(2,1)S(1)}, u32[]{:S(2)}, u32[]{:S(2)}) %collective-permute-start.26) | collective-permute-done | bytes 393248 | tf_op jit(solution)/shard_map/ppermute | solution.py:248
  285.7 2.5 fusion.223
  289.6 11.1 %state_grads.2 = (f32[384,128]{1,0:T(8,128)S(1)}, f32[384,128]{1,0:T(8,128)S(1)}) custom-call(f32[2,384,128]{2,1,0:T(8,128)S(1)} %reshape.414.rate_ref, f32[2,384,128]{2,1,0:T(8,128)S(1)} %reshape.423.coef_ref, bf16[1024,768]{1,0:T(8,128)(2,1)S(1)} %get-tuple-element.235.cos_ref, bf16[1024,768]{1,0:T(8,128)(2,1)S(1)} %get-tuple-element.236.sin_ref, ...), custom_call_target="tpu_custom_call" | custom-call | flops 9663676416 | bytes 7340032 | tf_op jit(solution)/shard_map/state_grads/pallas_call | solution.py:181
  306.2 1.9 multiply_convert_fusion.4
  313.9 1.9 add_convert_fusion.1
  317.1 2.0 fusion.90
  328.4 2.6 fusion.245
  331.1 10.8 %collective-permute-done.31 = bf16[1024,384]{1,0:T(8,128)(2,1)S(1)} collective-permute-done((bf16[1024,384]{1,0:T(8,128)(2,1)S(1)}, bf16[1024,384]{1,0:T(8,128)(2,1)S(1)}, u32[]{:S(2)}, u32[]{:S(2)}) %collective-permute-start.31) | collective-permute-done | bytes 786464 | tf_op jit(solution)/shard_map/ppermute | solution.py:248
  342.5 1.9 copy-done.5
  344.5 4.0 fusion.55
  348.6 1.9 fusion.72
  353.4 4.4 multiply_convert_fusion
  359.7 4.3 fusion.51
  364.0 6.8 %collective-permute-done.32 = bf16[2,2,1,192,384]{4,3,2,1,0:T(8,128)(2,1)} collective-permute-done((bf16[2,2,1,192,384]{4,3,2,1,0:T(8,128)(2,1)}, bf16[2,2,1,192,384]{4,3,2,1,0:T(8,128)(2,1)}, u32[]{:S(2)}, u32[]{:S(2)}) %collective-permute-start.32) | collective-permute-done | bytes 589856 | tf_op jit(solution)/shard_map/ppermute | solution.py:248
  383.4 11.2 %state_grads.3 = (f32[384,128]{1,0:T(8,128)S(1)}, f32[384,128]{1,0:T(8,128)S(1)}) custom-call(f32[2,384,128]{2,1,0:T(8,128)S(1)} %reshape.414.rate_ref, f32[2,384,128]{2,1,0:T(8,128)S(1)} %reshape.423.coef_ref, bf16[1024,768]{1,0:T(8,128)(2,1)S(1)} %get-tuple-element.267.cos_ref, bf16[1024,768]{1,0:T(8,128)(2,1)S(1)} %get-tuple-element.268.sin_ref, ...), custom_call_target="tpu_custom_call" | custom-call | flops 9663676416 | bytes 7340032 | tf_op jit(solution)/shard_map/state_grads/pallas_call | solution.py:181
  394.7 12.1 %collective-permute-done.36 = bf16[2,1,1,192,384]{4,3,2,1,0:T(8,128)(2,1)S(1)} collective-permute-done((bf16[2,1,1,192,384]{4,3,2,1,0:T(8,128)(2,1)S(1)}, bf16[2,1,1,192,384]{4,3,2,1,0:T(8,128)(2,1)S(1)}, u32[]{:S(2)}, u32[]{:S(2)}) %collective-permute-start.36) | collective-permute-done | bytes 294944 | tf_op jit(solution)/shard_map/ppermute | solution.py:248
  412.2 2.5 collective-permute-start.41
  417.3 7.8 %collective-permute-done.39 = bf16[1,1,1,192,384]{4,3,2,1,0:T(8,128)(2,1)S(1)} collective-permute-done((bf16[1,1,1,192,384]{4,3,2,1,0:T(8,128)(2,1)S(1)}, bf16[1,1,1,192,384]{4,3,2,1,0:T(8,128)(2,1)S(1)}, u32[]{:S(2)}, u32[]{:S(2)}) %collective-permute-start.39) | collective-permute-done | bytes 147488 | tf_op jit(solution)/shard_map/ppermute | solution.py:248
  427.4 2.3 collective-permute-start.43
  429.8 6.4 %collective-permute-done.44 = bf16[2,1,1,208,128]{4,3,2,1,0:T(8,128)(2,1)S(1)} collective-permute-done((bf16[2,1,1,208,128]{4,3,2,1,0:T(8,128)(2,1)S(1)}, bf16[2,1,1,208,128]{4,3,2,1,0:T(8,128)(2,1)S(1)}, u32[]{:S(2)}, u32[]{:S(2)}) %collective-permute-start.44) | collective-permute-done | bytes 106528 | tf_op jit(solution)/shard_map/ppermute | solution.py:248
  436.9 5.0 %collective-permute-done.45 = bf16[1,1,1,208,128]{4,3,2,1,0:T(8,128)(2,1)S(1)} collective-permute-done((bf16[1,1,1,208,128]{4,3,2,1,0:T(8,128)(2,1)S(1)}, bf16[1,1,1,208,128]{4,3,2,1,0:T(8,128)(2,1)S(1)}, u32[]{:S(2)}, u32[]{:S(2)}) %collective-permute-start.45) | collective-permute-done | bytes 53280 | tf_op jit(solution)/shard_map/ppermute | solution.py:248
  443.0 3.5 all-to-all-start.2
  448.8 4.9 %collective-permute-done.46 = bf16[208,128]{1,0:T(8,128)(2,1)S(1)} collective-permute-done((bf16[208,128]{1,0:T(8,128)(2,1)S(1)}, bf16[208,128]{1,0:T(8,128)(2,1)S(1)}, u32[]{:S(2)}, u32[]{:S(2)}) %collective-permute-start.46) | collective-permute-done | bytes 53280 | tf_op jit(solution)/shard_map/ppermute | solution.py:248
  453.7 4.4 all-to-all-done.2
  467.0 4.7 collective-permute-done.48
  (632 shorter events, 184.3 us)
Async XLA Ops:
  9.8 11.9 %all-to-all-start = ((bf16[4,64,384]{2,1,0:T(8,128)(2,1)}), bf16[4,64,384]{2,1,0:T(8,128)(2,1)S(1)}, u32[]{:S(2)}, u32[]{:S(2)}) async-start(bf16[4,64,384]{2,1,0:T(8,128)(2,1)} %pad_maximum_fusion.28), calls=%async_computation | async-start | bytes 393216 | tf_op jit(solution)/shard_map/all_to_all | solution.py:453
  21.8 15.6 %collective-permute-start = (bf16[112,384]{1,0:T(8,128)(2,1)S(1)}, bf16[112,384]{1,0:T(8,128)(2,1)S(1)}, u32[]{:S(2)}, u32[]{:S(2)}) collective-permute-start(bf16[112,384]{1,0:T(8,128)(2,1)S(1)} %fusion.197), channel_id=1, source_target_pairs={{0,16},{4,20},{8,24},{12,28},{16,0},{20,4},{24,8},{28,12},{1,17},{... | collective-permute-start | bytes 258056 | tf_op jit(solution)/shard_map/ppermute | solution.py:248
  25.1 12.3 %collective-permute-start.1 = (bf16[96,384]{1,0:T(8,128)(2,1)S(1)}, bf16[96,384]{1,0:T(8,128)(2,1)S(1)}, u32[]{:S(2)}, u32[]{:S(2)}) collective-permute-start(bf16[96,384]{1,0:T(8,128)(2,1)S(1)} %bitcast.555), channel_id=1, source_target_pairs={{0,4},{4,0},{8,12},{12,8},{16,20},{20,16},{24,28},{28,24},{1,5},{5... | collective-permute-start | bytes 221192 | tf_op jit(solution)/shard_map/ppermute | solution.py:248
  26.6 21.9 %all-to-all-start.1 = ((bf16[4,192,384]{2,1,0:T(8,128)(2,1)}), bf16[4,192,384]{2,1,0:T(8,128)(2,1)S(1)}, u32[]{:S(2)}, u32[]{:S(2)}) async-start(bf16[4,192,384]{2,1,0:T(8,128)(2,1)} %constant_dynamic-update-slice_fusion), calls=%async_computation.1 | async-start | bytes 1179648 | tf_op jit(solution)/shard_map/all_to_all | solution.py:489
  30.1 91.3 %all-gather.5.cloned.1.call-start = ((), (), s32[]{:S(2)}) async-start(), calls=%async_computation.5 | async-start | bytes 2654208 | tf_op jit(solution)/shard_map/all_gather | solution.py:523
  37.5 10.3 %collective-permute-start.3 = (bf16[2,96,384]{2,1,0:T(8,128)(2,1)S(1)}, bf16[2,96,384]{2,1,0:T(8,128)(2,1)S(1)}, u32[]{:S(2)}, u32[]{:S(2)}) collective-permute-start(bf16[2,96,384]{2,1,0:T(8,128)(2,1)S(1)} %pad_maximum_fusion.30), channel_id=1, source_target_pairs={{0,16},{4,20},{8,24},{12,28},{16,0},{20,4},{24,8},{28,12},{1,17},{... | collective-permute-start | bytes 442376 | tf_op jit(solution)/shard_map/ppermute | solution.py:248
  37.9 9.9 %collective-permute-start.2 = (bf16[2,112,384]{2,1,0:T(8,128)(2,1)S(1)}, bf16[2,112,384]{2,1,0:T(8,128)(2,1)S(1)}, u32[]{:S(2)}, u32[]{:S(2)}) collective-permute-start(bf16[2,112,384]{2,1,0:T(8,128)(2,1)S(1)} %pad_maximum_fusion.29), channel_id=1, source_target_pairs={{0,8},{4,12},{8,0},{12,4},{16,24},{20,28},{24,16},{28,20},{1,9},{5... | collective-permute-start | bytes 516104 | tf_op jit(solution)/shard_map/ppermute | solution.py:248
  50.7 122.0 %all-gather.7.cloned.1.call-start = ((), (), s32[]{:S(2)}) async-start(), calls=%async_computation.6 | async-start | bytes 3981312 | tf_op jit(solution)/shard_map/all_gather | solution.py:533
  50.8 10.8 %collective-permute-start.6 = (bf16[256,768]{1,0:T(8,128)(2,1)S(1)}, bf16[256,768]{1,0:T(8,128)(2,1)}, u32[]{:S(2)}, u32[]{:S(2)}) collective-permute-start(bf16[256,768]{1,0:T(8,128)(2,1)S(1)} %copy-done.23), channel_id=1, source_target_pairs={{0,2},{1,3},{2,0},{3,1},{4,6},{5,7},{6,4},{7,5},{8,10},{9,11},{10,... | collective-permute-start | bytes 1179656 | tf_op jit(solution)/shard_map/ppermute | solution.py:248
  53.7 42.7 %copy-start.112 = (f32[768]{0:T(1024)}, f32[768]{0:T(1024)S(1)}, u32[]{:S(2)}) copy-start(f32[768]{0:T(1024)S(1)} %mul.440) | copy-start | bytes 9220
  53.7 33.5 %copy-start.115 = (f32[1024]{0:T(1024)}, f32[1024]{0:T(1024)S(1)}, u32[]{:S(2)}) copy-start(f32[1024]{0:T(1024)S(1)} %fusion.214) | copy-start | bytes 12292
  63.7 18.6 %collective-permute-start.7 = (bf16[2,256,768]{2,1,0:T(8,128)(2,1)}, bf16[2,256,768]{2,1,0:T(8,128)(2,1)}, u32[]{:S(2)}, u32[]{:S(2)}) collective-permute-start(bf16[2,256,768]{2,1,0:T(8,128)(2,1)} %pad_maximum_fusion.10), channel_id=1, source_target_pairs={{0,1},{1,0},{2,3},{3,2},{4,5},{5,4},{6,7},{7,6},{8,9},{9,8},{10,11... | collective-permute-start | bytes 2359304 | tf_op jit(solution)/shard_map/ppermute | solution.py:248
  64.6 14.4 %collective-permute-start.5 = (bf16[2,2,96,384]{3,2,1,0:T(8,128)(2,1)}, bf16[2,2,96,384]{3,2,1,0:T(8,128)(2,1)}, u32[]{:S(2)}, u32[]{:S(2)}) collective-permute-start(bf16[2,2,96,384]{3,2,1,0:T(8,128)(2,1)} %pad_maximum_fusion.26), channel_id=1, source_target_pairs={{0,8},{4,12},{8,0},{12,4},{16,24},{20,28},{24,16},{28,20},{1,9},{5... | collective-permute-start | bytes 884744 | tf_op jit(solution)/shard_map/ppermute | solution.py:248
  64.7 14.3 %collective-permute-start.4 = (bf16[2,2,112,384]{3,2,1,0:T(8,128)(2,1)S(1)}, bf16[2,2,112,384]{3,2,1,0:T(8,128)(2,1)}, u32[]{:S(2)}, u32[]{:S(2)}) collective-permute-start(bf16[2,2,112,384]{3,2,1,0:T(8,128)(2,1)S(1)} %pad_maximum_fusion.24), channel_id=1, source_target_pairs={{0,4},{4,0},{8,12},{12,8},{16,20},{20,16},{24,28},{28,24},{1,5},{5... | collective-permute-start | bytes 1032200 | tf_op jit(solution)/shard_map/ppermute | solution.py:248
  69.2 356.0 %reduce-scatter.2.cloned.1.call-start = ((), (), s32[]{:S(2)}) async-start(), calls=%async_computation.4 | async-start | bytes 3981312 | tf_op jit(solution)/shard_map/reduce_scatter | solution.py:629
  78.0 18.4 %copy-start.8 = (bf16[1024,768]{1,0:T(8,128)(2,1)}, bf16[1024,768]{1,0:T(8,128)(2,1)S(1)}, u32[]{:S(2)}) copy-start(bf16[1024,768]{1,0:T(8,128)(2,1)S(1)} %get-tuple-element.194) | copy-start | bytes 4718596
  101.5 19.9 %collective-permute-start.8 = (bf16[1024,384]{1,0:T(8,128)(2,1)}, bf16[1024,384]{1,0:T(8,128)(2,1)}, u32[]{:S(2)}, u32[]{:S(2)}) collective-permute-start(bf16[1024,384]{1,0:T(8,128)(2,1)} %fusion.85), channel_id=1, source_target_pairs={{0,2},{1,3},{2,0},{3,1},{4,6},{5,7},{6,4},{7,5},{8,10},{9,11},{10,... | collective-permute-start | bytes 2359304 | tf_op jit(solution)/shard_map/ppermute | solution.py:210
  102.9 29.1 %collective-permute-start.9 = (bf16[1024,384]{1,0:T(8,128)(2,1)}, bf16[1024,384]{1,0:T(8,128)(2,1)}, u32[]{:S(2)}, u32[]{:S(2)}) collective-permute-start(bf16[1024,384]{1,0:T(8,128)(2,1)} %fusion.85), channel_id=1, source_target_pairs={{0,1},{1,0},{2,3},{3,2},{4,5},{5,4},{6,7},{7,6},{8,9},{9,8},{10,11... | collective-permute-start | bytes 2359304 | tf_op jit(solution)/shard_map/ppermute | solution.py:210
  123.0 12.0 %copy-start.20 = (bf16[8,192,384]{2,1,0:T(8,128)(2,1)}, bf16[8,192,384]{2,1,0:T(8,128)(2,1)S(1)}, u32[]{:S(2)}) copy-start(bf16[8,192,384]{2,1,0:T(8,128)(2,1)S(1)} %split.80) | copy-start | bytes 3538948
  123.0 12.0 %collective-permute-start.10 = (bf16[1024,384]{1,0:T(8,128)(2,1)}, bf16[1024,384]{1,0:T(8,128)(2,1)}, u32[]{:S(2)}, u32[]{:S(2)}) collective-permute-start(bf16[1024,384]{1,0:T(8,128)(2,1)} %collective-permute-done.8), channel_id=1, source_target_pairs={{0,1},{1,0},{2,3},{3,2},{4,5},{5,4},{6,7},{7,6},{8,9},{9,8},{10,11... | collective-permute-start | bytes 2359304 | tf_op jit(solution)/shard_map/ppermute | solution.py:210
  141.4 2.5 collective-permute-start.11
  146.9 11.3 %collective-permute-start.12 = (bf16[1,1,256,768]{3,2,1,0:T(8,128)(2,1)S(1)}, bf16[1,1,256,768]{3,2,1,0:T(8,128)(2,1)}, u32[]{:S(2)}, u32[]{:S(2)}) collective-permute-start(bf16[1,1,256,768]{3,2,1,0:T(8,128)(2,1)S(1)} %dynamic-slice_convert_fusion.7), channel_id=1, source_target_pairs={{0,2},{1,3},{2,0},{3,1},{4,6},{5,7},{6,4},{7,5},{8,10},{9,11},{10,... | collective-permute-start | bytes 1179656 | tf_op jit(solution)/shard_map/ppermute | solution.py:248
  148.5 12.1 %copy-start.101 = (f32[256]{0:T(256)}, f32[256]{0:T(256)S(1)}, u32[]{:S(2)}) copy-start(f32[256]{0:T(256)S(1)} %broadcast_multiply_fusion.2) | copy-start | bytes 3076
  161.6 12.3 %collective-permute-start.13 = (bf16[256,768]{1,0:T(8,128)(2,1)}, bf16[256,768]{1,0:T(8,128)(2,1)S(1)}, u32[]{:S(2)}, u32[]{:S(2)}) collective-permute-start(bf16[256,768]{1,0:T(8,128)(2,1)} %add_convert_fusion.7), channel_id=1, source_target_pairs={{0,2},{1,3},{2,0},{3,1},{4,6},{5,7},{6,4},{7,5},{8,10},{9,11},{10,... | collective-permute-start | bytes 1179656 | tf_op jit(solution)/shard_map/ppermute | solution.py:248
  162.9 17.7 %collective-permute-start.20 = (bf16[256,768]{1,0:T(8,128)(2,1)}, bf16[256,768]{1,0:T(8,128)(2,1)}, u32[]{:S(2)}, u32[]{:S(2)}) collective-permute-start(bf16[256,768]{1,0:T(8,128)(2,1)} %param.16), channel_id=1, source_target_pairs={{0,2},{1,3},{2,0},{3,1},{4,6},{5,7},{6,4},{7,5},{8,10},{9,11},{10,... | collective-permute-start | bytes 1179656 | tf_op jit(solution)/shard_map/ppermute | solution.py:248
  177.6 7.2 %collective-permute-start.14 = (bf16[2,256,768]{2,1,0:T(8,128)(2,1)}, bf16[2,256,768]{2,1,0:T(8,128)(2,1)}, u32[]{:S(2)}, u32[]{:S(2)}) collective-permute-start(bf16[2,256,768]{2,1,0:T(8,128)(2,1)} %pad_maximum_fusion.11), channel_id=1, source_target_pairs={{0,1},{1,0},{2,3},{3,2},{4,5},{5,4},{6,7},{7,6},{8,9},{9,8},{10,11... | collective-permute-start | bytes 2359304 | tf_op jit(solution)/shard_map/ppermute | solution.py:248
  181.9 21.1 %collective-permute-start.21 = (bf16[2,256,768]{2,1,0:T(8,128)(2,1)S(1)}, bf16[2,256,768]{2,1,0:T(8,128)(2,1)S(1)}, u32[]{:S(2)}, u32[]{:S(2)}) collective-permute-start(bf16[2,256,768]{2,1,0:T(8,128)(2,1)S(1)} %pad_maximum_fusion.12), channel_id=1, source_target_pairs={{0,1},{1,0},{2,3},{3,2},{4,5},{5,4},{6,7},{7,6},{8,9},{9,8},{10,11... | collective-permute-start | bytes 2359304 | tf_op jit(solution)/shard_map/ppermute | solution.py:248
  201.7 20.2 %collective-permute-start.16 = (bf16[1024,384]{1,0:T(8,128)(2,1)}, bf16[1024,384]{1,0:T(8,128)(2,1)}, u32[]{:S(2)}, u32[]{:S(2)}) collective-permute-start(bf16[1024,384]{1,0:T(8,128)(2,1)} %fusion.84), channel_id=1, source_target_pairs={{0,2},{1,3},{2,0},{3,1},{4,6},{5,7},{6,4},{7,5},{8,10},{9,11},{10,... | collective-permute-start | bytes 2359304 | tf_op jit(solution)/shard_map/ppermute | solution.py:210
  216.3 9.1 %collective-permute-start.15 = (bf16[1024,384]{1,0:T(8,128)(2,1)}, bf16[1024,384]{1,0:T(8,128)(2,1)S(1)}, u32[]{:S(2)}, u32[]{:S(2)}) collective-permute-start(bf16[1024,384]{1,0:T(8,128)(2,1)} %fusion.84), channel_id=1, source_target_pairs={{0,1},{1,0},{2,3},{3,2},{4,5},{5,4},{6,7},{7,6},{8,9},{9,8},{10,11... | collective-permute-start | bytes 2359304 | tf_op jit(solution)/shard_map/ppermute | solution.py:210
  221.9 4.2 collective-permute-start.17
  229.7 3.6 collective-permute-start.23
  230.9 12.7 %collective-permute-start.22 = (bf16[1024,384]{1,0:T(8,128)(2,1)S(1)}, bf16[1024,384]{1,0:T(8,128)(2,1)S(1)}, u32[]{:S(2)}, u32[]{:S(2)}) collective-permute-start(bf16[1024,384]{1,0:T(8,128)(2,1)S(1)} %convolution_convert_fusion.9), channel_id=1, source_target_pairs={{0,1},{1,0},{2,3},{3,2},{4,5},{5,4},{6,7},{7,6},{8,9},{9,8},{10,11... | collective-permute-start | bytes 2359304 | tf_op jit(solution)/shard_map/ppermute | solution.py:248
  232.0 7.7 %collective-permute-start.18 = (bf16[2,1,256,768]{3,2,1,0:T(8,128)(2,1)S(1)}, bf16[2,1,256,768]{3,2,1,0:T(8,128)(2,1)S(1)}, u32[]{:S(2)}, u32[]{:S(2)}) collective-permute-start(bf16[2,1,256,768]{3,2,1,0:T(8,128)(2,1)S(1)} %dynamic-slice_convert_fusion.2), channel_id=1, source_target_pairs={{0,1},{1,0},{2,3},{3,2},{4,5},{5,4},{6,7},{7,6},{8,9},{9,8},{10,11... | collective-permute-start | bytes 2359304 | tf_op jit(solution)/shard_map/ppermute | solution.py:248
  233.9 20.5 %collective-permute-start.24 = (bf16[1024,384]{1,0:T(8,128)(2,1)S(1)}, bf16[1024,384]{1,0:T(8,128)(2,1)S(1)}, u32[]{:S(2)}, u32[]{:S(2)}) collective-permute-start(bf16[1024,384]{1,0:T(8,128)(2,1)S(1)} %add_convert_fusion.3), channel_id=1, source_target_pairs={{0,2},{1,3},{2,0},{3,1},{4,6},{5,7},{6,4},{7,5},{8,10},{9,11},{10,... | collective-permute-start | bytes 2359304 | tf_op jit(solution)/shard_map/ppermute | solution.py:248
  239.9 45.8 %collective-permute-start.19 = (bf16[1,1,256,768]{3,2,1,0:T(8,128)(2,1)S(1)}, bf16[1,1,256,768]{3,2,1,0:T(8,128)(2,1)S(1)}, u32[]{:S(2)}, u32[]{:S(2)}) collective-permute-start(bf16[1,1,256,768]{3,2,1,0:T(8,128)(2,1)S(1)} %dynamic-slice_convert_fusion.6), channel_id=1, source_target_pairs={{0,2},{1,3},{2,0},{3,1},{4,6},{5,7},{6,4},{7,5},{8,10},{9,11},{10,... | collective-permute-start | bytes 1179656 | tf_op jit(solution)/shard_map/ppermute | solution.py:248
  269.7 3.7 collective-permute-start.25
  273.6 11.6 %collective-permute-start.26 = (bf16[1,1,256,768]{3,2,1,0:T(8,128)(2,1)S(1)}, bf16[1,1,256,768]{3,2,1,0:T(8,128)(2,1)S(1)}, u32[]{:S(2)}, u32[]{:S(2)}) collective-permute-start(bf16[1,1,256,768]{3,2,1,0:T(8,128)(2,1)S(1)} %dynamic-slice_convert_fusion.5), channel_id=1, source_target_pairs={{0,2},{1,3},{2,0},{3,1},{4,6},{5,7},{6,4},{7,5},{8,10},{9,11},{10,... | collective-permute-start | bytes 1179656 | tf_op jit(solution)/shard_map/ppermute | solution.py:248
  288.2 12.5 %collective-permute-start.27 = (bf16[256,768]{1,0:T(8,128)(2,1)S(1)}, bf16[256,768]{1,0:T(8,128)(2,1)S(1)}, u32[]{:S(2)}, u32[]{:S(2)}) collective-permute-start(bf16[256,768]{1,0:T(8,128)(2,1)S(1)} %get-tuple-element.234), channel_id=1, source_target_pairs={{0,2},{1,3},{2,0},{3,1},{4,6},{5,7},{6,4},{7,5},{8,10},{9,11},{10,... | collective-permute-start | bytes 1179656 | tf_op jit(solution)/shard_map/ppermute | solution.py:248
  300.8 3.0 collective-permute-start.28
  309.6 4.3 collective-permute-start.30
  313.1 17.9 %collective-permute-start.29 = (bf16[1024,384]{1,0:T(8,128)(2,1)S(1)}, bf16[1024,384]{1,0:T(8,128)(2,1)S(1)}, u32[]{:S(2)}, u32[]{:S(2)}) collective-permute-start(bf16[1024,384]{1,0:T(8,128)(2,1)S(1)} %convolution_convert_fusion.7), channel_id=1, source_target_pairs={{0,1},{1,0},{2,3},{3,2},{4,5},{5,4},{6,7},{7,6},{8,9},{9,8},{10,11... | collective-permute-start | bytes 2359304 | tf_op jit(solution)/shard_map/ppermute | solution.py:248
  322.0 19.9 %collective-permute-start.31 = (bf16[1024,384]{1,0:T(8,128)(2,1)S(1)}, bf16[1024,384]{1,0:T(8,128)(2,1)S(1)}, u32[]{:S(2)}, u32[]{:S(2)}) collective-permute-start(bf16[1024,384]{1,0:T(8,128)(2,1)S(1)} %add_convert_fusion.1), channel_id=1, source_target_pairs={{0,2},{1,3},{2,0},{3,1},{4,6},{5,7},{6,4},{7,5},{8,10},{9,11},{10,... | collective-permute-start | bytes 2359304 | tf_op jit(solution)/shard_map/ppermute | solution.py:248
  350.5 20.3 %collective-permute-start.32 = (bf16[2,2,1,192,384]{4,3,2,1,0:T(8,128)(2,1)}, bf16[2,2,1,192,384]{4,3,2,1,0:T(8,128)(2,1)}, u32[]{:S(2)}, u32[]{:S(2)}) collective-permute-start(bf16[2,2,1,192,384]{4,3,2,1,0:T(8,128)(2,1)} %get-tuple-element.252), channel_id=1, source_target_pairs={{0,4},{4,0},{8,12},{12,8},{16,20},{20,16},{24,28},{28,24},{1,5},{5... | collective-permute-start | bytes 1769480 | tf_op jit(solution)/shard_map/ppermute | solution.py:248
  352.2 18.6 %collective-permute-start.33 = (bf16[2,1,2,192,384]{4,3,2,1,0:T(8,128)(2,1)}, bf16[2,1,2,192,384]{4,3,2,1,0:T(8,128)(2,1)}, u32[]{:S(2)}, u32[]{:S(2)}) collective-permute-start(bf16[2,1,2,192,384]{4,3,2,1,0:T(8,128)(2,1)} %get-tuple-element.254), channel_id=1, source_target_pairs={{0,8},{4,12},{8,0},{12,4},{16,24},{20,28},{24,16},{28,20},{1,9},{5... | collective-permute-start | bytes 1769480 | tf_op jit(solution)/shard_map/ppermute | solution.py:248
  372.4 5.6 %collective-permute-start.34 = (bf16[2,1,256,768]{3,2,1,0:T(8,128)(2,1)S(1)}, bf16[2,1,256,768]{3,2,1,0:T(8,128)(2,1)S(1)}, u32[]{:S(2)}, u32[]{:S(2)}) collective-permute-start(bf16[2,1,256,768]{3,2,1,0:T(8,128)(2,1)S(1)} %dynamic-slice_convert_fusion), channel_id=1, source_target_pairs={{0,1},{1,0},{2,3},{3,2},{4,5},{5,4},{6,7},{7,6},{8,9},{9,8},{10,11... | collective-permute-start | bytes 2359304 | tf_op jit(solution)/shard_map/ppermute | solution.py:248
  378.2 28.6 %collective-permute-start.38 = (bf16[2,2,1,96,768]{4,3,2,1,0:T(8,128)(2,1)S(1)}, bf16[2,2,1,96,768]{4,3,2,1,0:T(8,128)(2,1)S(1)}, u32[]{:S(2)}, u32[]{:S(2)}) collective-permute-start(bf16[2,2,1,96,768]{4,3,2,1,0:T(8,128)(2,1)S(1)} %get-tuple-element.266), channel_id=1, source_target_pairs={{0,4},{4,0},{8,12},{12,8},{16,20},{20,16},{24,28},{28,24},{1,5},{5... | collective-permute-start | bytes 1769480 | tf_op jit(solution)/shard_map/ppermute | solution.py:248
  379.9 26.9 %collective-permute-start.35 = (bf16[1,1,256,768]{3,2,1,0:T(8,128)(2,1)S(1)}, bf16[1,1,256,768]{3,2,1,0:T(8,128)(2,1)S(1)}, u32[]{:S(2)}, u32[]{:S(2)}) collective-permute-start(bf16[1,1,256,768]{3,2,1,0:T(8,128)(2,1)S(1)} %dynamic-slice_convert_fusion.4), channel_id=1, source_target_pairs={{0,2},{1,3},{2,0},{3,1},{4,6},{5,7},{6,4},{7,5},{8,10},{9,11},{10,... | collective-permute-start | bytes 1179656 | tf_op jit(solution)/shard_map/ppermute | solution.py:248
  380.3 26.5 %collective-permute-start.36 = (bf16[2,1,1,192,384]{4,3,2,1,0:T(8,128)(2,1)S(1)}, bf16[2,1,1,192,384]{4,3,2,1,0:T(8,128)(2,1)S(1)}, u32[]{:S(2)}, u32[]{:S(2)}) collective-permute-start(bf16[2,1,1,192,384]{4,3,2,1,0:T(8,128)(2,1)S(1)} %get-tuple-element.262), channel_id=1, source_target_pairs={{0,8},{4,12},{8,0},{12,4},{16,24},{20,28},{24,16},{28,20},{1,9},{5... | collective-permute-start | bytes 884744 | tf_op jit(solution)/shard_map/ppermute | solution.py:248
  381.7 25.2 %collective-permute-start.37 = (bf16[1,1,2,192,384]{4,3,2,1,0:T(8,128)(2,1)S(1)}, bf16[1,1,2,192,384]{4,3,2,1,0:T(8,128)(2,1)S(1)}, u32[]{:S(2)}, u32[]{:S(2)}) collective-permute-start(bf16[1,1,2,192,384]{4,3,2,1,0:T(8,128)(2,1)S(1)} %get-tuple-element.264), channel_id=1, source_target_pairs={{0,16},{4,20},{8,24},{12,28},{16,0},{20,4},{24,8},{28,12},{1,17},{... | collective-permute-start | bytes 884744 | tf_op jit(solution)/shard_map/ppermute | solution.py:248
  394.7 13.7 %copy-start.25 = (bf16[256,768]{1,0:T(8,128)(2,1)S(1)}, bf16[256,768]{1,0:T(8,128)(2,1)}, u32[]{:S(2)}) copy-start(bf16[256,768]{1,0:T(8,128)(2,1)} %param.14) | copy-start | bytes 1179652
  394.7 13.7 %copy-start.98 = (f32[768]{0:T(1024)S(1)}, f32[768]{0:T(1024)}, u32[]{:S(2)}) copy-start(f32[768]{0:T(1024)} %copy-done.97) | copy-start | bytes 9220
  394.7 13.7 %copy-start.102 = (f32[256]{0:T(256)S(1)}, f32[256]{0:T(256)}, u32[]{:S(2)}) copy-start(f32[256]{0:T(256)} %copy-done.101) | copy-start | bytes 3076
  394.7 13.7 %copy-start.105 = (f32[256]{0:T(256)S(1)}, f32[256]{0:T(256)}, u32[]{:S(2)}) copy-start(f32[256]{0:T(256)} %add_rsqrt_fusion.1) | copy-start | bytes 3076
  412.2 13.0 %collective-permute-start.41 = (bf16[2,1,1,96,768]{4,3,2,1,0:T(8,128)(2,1)S(1)}, bf16[2,1,1,96,768]{4,3,2,1,0:T(8,128)(2,1)S(1)}, u32[]{:S(2)}, u32[]{:S(2)}) collective-permute-start(bf16[2,1,1,96,768]{4,3,2,1,0:T(8,128)(2,1)S(1)} %get-tuple-element.287), channel_id=1, source_target_pairs={{0,8},{4,12},{8,0},{12,4},{16,24},{20,28},{24,16},{28,20},{1,9},{5... | collective-permute-start | bytes 884744 | tf_op jit(solution)/shard_map/ppermute | solution.py:248
  414.6 10.5 %collective-permute-start.42 = (bf16[2,2,1,208,128]{4,3,2,1,0:T(8,128)(2,1)S(1)}, bf16[2,2,1,208,128]{4,3,2,1,0:T(8,128)(2,1)S(1)}, u32[]{:S(2)}, u32[]{:S(2)}) collective-permute-start(bf16[2,2,1,208,128]{4,3,2,1,0:T(8,128)(2,1)S(1)} %get-tuple-element.289), channel_id=1, source_target_pairs={{0,4},{4,0},{8,12},{12,8},{16,20},{20,16},{24,28},{28,24},{1,5},{5... | collective-permute-start | bytes 638984 | tf_op jit(solution)/shard_map/ppermute | solution.py:248
  416.1 9.1 %collective-permute-start.39 = (bf16[1,1,1,192,384]{4,3,2,1,0:T(8,128)(2,1)S(1)}, bf16[1,1,1,192,384]{4,3,2,1,0:T(8,128)(2,1)S(1)}, u32[]{:S(2)}, u32[]{:S(2)}) collective-permute-start(bf16[1,1,1,192,384]{4,3,2,1,0:T(8,128)(2,1)S(1)} %get-tuple-element.283), channel_id=1, source_target_pairs={{0,16},{4,20},{8,24},{12,28},{16,0},{20,4},{24,8},{28,12},{1,17},{... | collective-permute-start | bytes 442376 | tf_op jit(solution)/shard_map/ppermute | solution.py:248
  416.7 8.5 %collective-permute-start.40 = (bf16[1,1,1,192,384]{4,3,2,1,0:T(8,128)(2,1)S(1)}, bf16[1,1,1,192,384]{4,3,2,1,0:T(8,128)(2,1)S(1)}, u32[]{:S(2)}, u32[]{:S(2)}) collective-permute-start(bf16[1,1,1,192,384]{4,3,2,1,0:T(8,128)(2,1)S(1)} %get-tuple-element.285), channel_id=1, source_target_pairs={{0,4},{4,0},{8,12},{12,8},{16,20},{20,16},{24,28},{28,24},{1,5},{5... | collective-permute-start | bytes 442376 | tf_op jit(solution)/shard_map/ppermute | solution.py:248
  427.4 8.8 %collective-permute-start.43 = (bf16[1,1,1,96,768]{4,3,2,1,0:T(8,128)(2,1)S(1)}, bf16[1,1,1,96,768]{4,3,2,1,0:T(8,128)(2,1)S(1)}, u32[]{:S(2)}, u32[]{:S(2)}) collective-permute-start(bf16[1,1,1,96,768]{4,3,2,1,0:T(8,128)(2,1)S(1)} %get-tuple-element.297), channel_id=1, source_target_pairs={{0,16},{4,20},{8,24},{12,28},{16,0},{20,4},{24,8},{28,12},{1,17},{... | collective-permute-start | bytes 442376 | tf_op jit(solution)/shard_map/ppermute | solution.py:248
  429.6 6.5 %collective-permute-start.44 = (bf16[2,1,1,208,128]{4,3,2,1,0:T(8,128)(2,1)S(1)}, bf16[2,1,1,208,128]{4,3,2,1,0:T(8,128)(2,1)S(1)}, u32[]{:S(2)}, u32[]{:S(2)}) collective-permute-start(bf16[2,1,1,208,128]{4,3,2,1,0:T(8,128)(2,1)S(1)} %get-tuple-element.299), channel_id=1, source_target_pairs={{0,8},{4,12},{8,0},{12,4},{16,24},{20,28},{24,16},{28,20},{1,9},{5... | collective-permute-start | bytes 319496 | tf_op jit(solution)/shard_map/ppermute | solution.py:248
  436.4 5.5 %collective-permute-start.45 = (bf16[1,1,1,208,128]{4,3,2,1,0:T(8,128)(2,1)S(1)}, bf16[1,1,1,208,128]{4,3,2,1,0:T(8,128)(2,1)S(1)}, u32[]{:S(2)}, u32[]{:S(2)}) collective-permute-start(bf16[1,1,1,208,128]{4,3,2,1,0:T(8,128)(2,1)S(1)} %get-tuple-element.303), channel_id=1, source_target_pairs={{0,16},{4,20},{8,24},{12,28},{16,0},{20,4},{24,8},{28,12},{1,17},{... | collective-permute-start | bytes 159752 | tf_op jit(solution)/shard_map/ppermute | solution.py:248
  443.0 15.1 %all-to-all-start.2 = ((bf16[4,256,384]{2,1,0:T(8,128)(2,1)}), bf16[4,256,384]{2,1,0:T(8,128)(2,1)S(1)}, u32[]{:S(2)}, u32[]{:S(2)}) async-start(bf16[4,256,384]{2,1,0:T(8,128)(2,1)} %copy-done.64), calls=%async_computation.3 | async-start | bytes 1572864 | tf_op jit(solution)/shard_map/all_to_all | solution.py:697
  448.0 5.8 %collective-permute-start.46 = (bf16[208,128]{1,0:T(8,128)(2,1)S(1)}, bf16[208,128]{1,0:T(8,128)(2,1)S(1)}, u32[]{:S(2)}, u32[]{:S(2)}) collective-permute-start(bf16[208,128]{1,0:T(8,128)(2,1)S(1)} %bitcast.557), channel_id=1, source_target_pairs={{0,16},{4,20},{8,24},{12,28},{16,0},{20,4},{24,8},{28,12},{1,17},{... | collective-permute-start | bytes 159752 | tf_op jit(solution)/shard_map/ppermute | solution.py:248
  458.2 6.6 %collective-permute-start.47 = (bf16[2,208,128]{2,1,0:T(8,128)(2,1)S(1)}, bf16[2,208,128]{2,1,0:T(8,128)(2,1)S(1)}, u32[]{:S(2)}, u32[]{:S(2)}) collective-permute-start(bf16[2,208,128]{2,1,0:T(8,128)(2,1)S(1)} %pad_maximum_fusion.31), channel_id=1, source_target_pairs={{0,8},{4,12},{8,0},{12,4},{16,24},{20,28},{24,16},{28,20},{1,9},{5... | collective-permute-start | bytes 319496 | tf_op jit(solution)/shard_map/ppermute | solution.py:248
  464.9 6.8 %collective-permute-start.48 = (bf16[2,2,208,128]{3,2,0,1:T(8,128)(2,1)S(1)}, bf16[2,2,208,128]{3,2,0,1:T(8,128)(2,1)S(1)}, u32[]{:S(2)}, u32[]{:S(2)}) collective-permute-start(bf16[2,2,208,128]{3,2,0,1:T(8,128)(2,1)S(1)} %pad_maximum_fusion.27), channel_id=1, source_target_pairs={{0,4},{4,0},{8,12},{12,8},{16,20},{20,16},{24,28},{28,24},{1,5},{5... | collective-permute-start | bytes 638984 | tf_op jit(solution)/shard_map/ppermute | solution.py:248
  (118 other events, 448.0 us)
Sparse Core Ops, SparseCore 0:
  50.8 55.8 all-gather.4
  108.9 63.7 all-gather.6
  311.2 95.9 reduce-scatter.1

commit v5 on v4

--- a/solution.py
+++ b/solution.py
@@ -351,7 +351,7 @@
         gate_act,
         gate_back,
         value_slope,
-        values,
+        together(values)[0],
         x_hat,
         mixes,
         products,
@@ -393,9 +393,7 @@
     waves, waves_back = tables
     length = waves.shape[1]
     width = product_low.shape[1]
-    product_low = product_low.astype(F32)
-    mixes = mixes.astype(F32)
-    back = jnp.concatenate([product_low * mixes[:, width:], product_low * mixes[:, :width]], 1).astype(BF)
+    back = jnp.concatenate([product_low * mixes[:, width:], product_low * mixes[:, :width]], 1)
     g_hat = dot(waves, back, 1, 0).astype(BF)
     k_cos, k_sin = hat
     g_cos, g_sin = g_hat[:length].astype(F32), g_hat[length:].astype(F32)
@@ -451,7 +449,7 @@
     first = jnp.concatenate([value_columns(0), jnp.broadcast_to(norm_rows, (count,) + norm_rows.shape)], 1)
     first, tokens = together(first, tokens)
     first = lax.all_to_all(first, "seq", 0, 0, tiled=True)
-    rows_all, _ = seq_rows(tokens, count, ())
+    rows_all, first = seq_rows(tokens, count, first)
     pieces = [by_column(w_gate[0]), by_column(w_mix[0])]
     for layer in range(1, depth):
         pieces += [value_columns(layer), by_column(w_gate[layer]), by_column(w_mix[layer])]

time: 490 us -> 481 us (0.982)
  waiting for transfers between devices: 122 us -> 108 us
    ppermute x43, waiting for transfers between devices: 105 us -> 80.1 us  [swap(): return lax.ppermute(block, axis, pairs_of(count, bit))]
    all_gather x1, waiting for transfers between devices: 9.06 us -> 16.9 us  [shards(): lax.all_gather(layer_block(layer), 'dp', axis=0)]
    unnamed x284 -> x302, local copies, waits for them, and re-layouts: 39.1 us -> 37.7 us
  transfers between devices with their start and end apart: 55 -> 55, of which waited for: 21 -> 20; matrix products, arithmetic and copies ran while one was open for 40% -> 42% of each run, Pallas kernels for 11% -> 11%
where the time goes in v5:
time: 481 us; the launch traced here: 472 us
  waiting for transfers between devices  108 us (22%)
  matrix products  103 us (21%)
  local copies, waits for them, and re-layouts  80.8 us (17%)
  other arithmetic  56.7 us (12%)
  starting transfers between devices  53.5 us (11%)
  Pallas kernels  52.5 us (11%)
  between operations  17.6 us (4%)
    dot_general x56, matrix products, dot(): lax.dot_general(left, right, (((left_dim,), (right_dim,)), ((), ())), pre...  103 us
    ppermute x43, waiting for transfers between devices, swap(): return lax.ppermute(block, axis, pairs_of(count, bit))  80.1 us
    ppermute x43, starting transfers between devices, swap(): return lax.ppermute(block, axis, pairs_of(count, bit))  39.3 us
    unnamed x302, local copies, waits for them, and re-layouts  37.7 us
    pallas_call x6, Pallas kernels, spectra(): pl.pallas_call(partial(spectra_kernel, unroll_of(block // 2)), out_shape=...  30.2 us
    pallas_call x2, Pallas kernels, state_grads(): pl.pallas_call(partial(state_grads_kernel, unroll_of(block // 2)), out_sh...  22.3 us
    all_gather x1, waiting for transfers between devices, shards(): lax.all_gather(layer_block(layer), 'dp', axis=0)  16.9 us
    another operation x33, other arithmetic, join(): return jnp.stack(pair, done.index(bit))  15.9 us
  transfers between devices with their start and end apart: 55, of which 20 were waited for; matrix products, arithmetic and copies ran while one was open for 42% of the time, Pallas kernels for 11%

profile of v5, /device:TPU:0, one launch (start us, length us, event | category | flops | bytes accessed | tf_op | source)
XLA Modules:
  0.0 472.4 jit_solution(1048749327148222292)
XLA Ops:
  9.8 2.9 collective-permute-start
  12.8 3.4 all-to-all-start
  25.9 2.6 collective-permute-start.1
  30.0 3.5 all-to-all-start.1
  33.6 2.2 copy-done
  35.7 5.0 %spectra.6 = (bf16[1024,768]{1,0:T(8,128)(2,1)S(1)}, bf16[1024,768]{1,0:T(8,128)(2,1)S(1)}) custom-call(f32[2,384,128]{2,1,0:T(8,128)S(1)} %reshape.414.rate_ref, f32[2,384,128]{2,1,0:T(8,128)S(1)} %reshape.423.coef_ref, f32[1,768]{1,0:T(1,128)S(1)} %copy-done.7, bf16[2048,1024]{1,0:T(8,128)(2,1)S(1)} %copy-done), custom_call_target="tpu_custom_call" | custom-call | flops 3221225472 | bytes 5242880 | tf_op jit(solution)/shard_map/spectra/pallas_call | solution.py:104
  44.8 5.0 %spectra.7 = (bf16[1024,768]{1,0:T(8,128)(2,1)S(1)}, bf16[1024,768]{1,0:T(8,128)(2,1)S(1)}) custom-call(f32[2,384,128]{2,1,0:T(8,128)S(1)} %reshape.414.rate_ref, f32[2,384,128]{2,1,0:T(8,128)S(1)} %reshape.423.coef_ref, f32[1,768]{1,0:T(1,128)S(1)} %copy-done.7, bf16[2048,1024]{1,0:T(8,128)(2,1)S(1)} %copy-done, ...), custom_call_target="tpu_custom_call", output_to_operand_aliasing={{0}: (4, {}), {1}: (5, {})} | custom-call | flops 3221225472 | bytes 5242880 | tf_op jit(solution)/shard_map/spectra/pallas_call | solution.py:104
  64.9 2.2 copy-done.1
  68.5 5.0 %spectra.8 = (bf16[1024,768]{1,0:T(8,128)(2,1)S(1)}, bf16[1024,768]{1,0:T(8,128)(2,1)S(1)}) custom-call(f32[2,384,128]{2,1,0:T(8,128)S(1)} %reshape.414.rate_ref, f32[2,384,128]{2,1,0:T(8,128)S(1)} %reshape.423.coef_ref, f32[1,768]{1,0:T(1,128)S(1)} %copy-done.7, bf16[2048,1024]{1,0:T(8,128)(2,1)S(1)} %copy-done.1, ...), custom_call_target="tpu_custom_call", output_to_operand_aliasing={{0}: (4, {}), {1}: (5, {})} | custom-call | flops 3221225472 | bytes 5242880 | tf_op jit(solution)/shard_map/spectra/pallas_call | solution.py:104
  80.2 2.1 fusion.5
  82.4 3.5 fusion.17
  85.9 3.6 fusion.50
  89.6 1.9 fusion.75
  92.3 3.3 fusion.235
  98.3 5.0 %spectra.9 = (bf16[1024,768]{1,0:T(8,128)(2,1)S(1)}, bf16[1024,768]{1,0:T(8,128)(2,1)S(1)}) custom-call(f32[2,384,128]{2,1,0:T(8,128)S(1)} %reshape.414.rate_ref, f32[2,384,128]{2,1,0:T(8,128)S(1)} %reshape.423.coef_ref, f32[1,768]{1,0:T(1,128)S(1)} %copy-done.7, bf16[2048,1024]{1,0:T(8,128)(2,1)S(1)} %copy-done.2), custom_call_target="tpu_custom_call" | custom-call | flops 3221225472 | bytes 5242880 | tf_op jit(solution)/shard_map/spectra/pallas_call | solution.py:104
  103.3 5.2 %spectra.10 = (bf16[1024,768]{1,0:T(8,128)(2,1)S(1)}, bf16[1024,768]{1,0:T(8,128)(2,1)S(1)}) custom-call(f32[2,384,128]{2,1,0:T(8,128)S(1)} %reshape.414.rate_ref, f32[2,384,128]{2,1,0:T(8,128)S(1)} %reshape.423.coef_ref, f32[1,768]{1,0:T(1,128)S(1)} %copy-done.7, bf16[2048,1024]{1,0:T(8,128)(2,1)S(1)} %copy-done.2, ...), custom_call_target="tpu_custom_call", output_to_operand_aliasing={{0}: (4, {}), {1}: (5, {})} | custom-call | flops 3221225472 | bytes 5242880 | tf_op jit(solution)/shard_map/spectra/pallas_call | solution.py:104
  108.5 5.0 %spectra.11 = (bf16[1024,768]{1,0:T(8,128)(2,1)S(1)}, bf16[1024,768]{1,0:T(8,128)(2,1)S(1)}) custom-call(f32[2,384,128]{2,1,0:T(8,128)S(1)} %reshape.414.rate_ref, f32[2,384,128]{2,1,0:T(8,128)S(1)} %reshape.423.coef_ref, f32[1,768]{1,0:T(1,128)S(1)} %copy-done.7, bf16[2048,1024]{1,0:T(8,128)(2,1)S(1)} %copy-done.2, ...), custom_call_target="tpu_custom_call", output_to_operand_aliasing={{0}: (4, {}), {1}: (5, {})} | custom-call | flops 3221225472 | bytes 5242880 | tf_op jit(solution)/shard_map/spectra/pallas_call | solution.py:104
  120.7 2.8 reshape.469
  127.0 1.9 fusion.167
  129.9 3.7 fusion.59
  133.6 2.7 fusion.135
  138.0 2.3 collective-permute-done.11
  145.1 9.5 %collective-permute-done.12 = bf16[1,1,256,768]{3,2,1,0:T(8,128)(2,1)} collective-permute-done((bf16[1,1,256,768]{3,2,1,0:T(8,128)(2,1)S(1)}, bf16[1,1,256,768]{3,2,1,0:T(8,128)(2,1)}, u32[]{:S(2)}, u32[]{:S(2)}) %collective-permute-start.12) | collective-permute-done | bytes 393248 | tf_op jit(solution)/shard_map/ppermute | solution.py:248
  154.6 2.2 fusion.218
  160.0 16.9 %all-gather.7.cloned.1.call-done = bf16[4608,384]{1,0:T(8,128)(2,1)} async-done(((bf16[576,384]{1,0:T(8,128)(2,1)}), bf16[4608,384]{1,0:T(8,128)(2,1)}) %all-gather.7.cloned.1.call-update) | async-done | bytes 3538960 | tf_op jit(solution)/shard_map/all_gather | solution.py:531
  183.0 2.7 fusion.219
  188.3 3.5 fusion.23
  191.8 3.8 fusion.51
  195.7 1.9 fusion.72
  198.4 3.2 fusion.236
  207.2 2.4 split.87
  210.9 2.8 reshape.470
  214.9 2.6 fusion.238
  217.5 5.0 %collective-permute-done.16 = bf16[1024,384]{1,0:T(8,128)(2,1)} collective-permute-done((bf16[1024,384]{1,0:T(8,128)(2,1)}, bf16[1024,384]{1,0:T(8,128)(2,1)}, u32[]{:S(2)}, u32[]{:S(2)}) %collective-permute-start.16) | collective-permute-done | bytes 786464 | tf_op jit(solution)/shard_map/ppermute | solution.py:210
  226.7 1.9 fusion.65
  244.9 10.2 %collective-permute-done.24 = bf16[1024,384]{1,0:T(8,128)(2,1)S(1)} collective-permute-done((bf16[1024,384]{1,0:T(8,128)(2,1)S(1)}, bf16[1024,384]{1,0:T(8,128)(2,1)S(1)}, u32[]{:S(2)}, u32[]{:S(2)}) %collective-permute-start.24) | collective-permute-done | bytes 786464 | tf_op jit(solution)/shard_map/ppermute | solution.py:248
  255.6 2.2 copy-done.4
  257.8 3.6 fusion.52
  261.5 1.9 fusion.69
  263.5 3.7 multiply_convert_fusion.1
  276.9 8.5 %collective-permute-done.26 = bf16[1,1,256,768]{3,2,1,0:T(8,128)(2,1)S(1)} collective-permute-done((bf16[1,1,256,768]{3,2,1,0:T(8,128)(2,1)S(1)}, bf16[1,1,256,768]{3,2,1,0:T(8,128)(2,1)S(1)}, u32[]{:S(2)}, u32[]{:S(2)}) %collective-permute-start.26) | collective-permute-done | bytes 393248 | tf_op jit(solution)/shard_map/ppermute | solution.py:248
  287.0 2.5 fusion.217
  291.0 11.1 %state_grads.2 = (f32[384,128]{1,0:T(8,128)S(1)}, f32[384,128]{1,0:T(8,128)S(1)}) custom-call(f32[2,384,128]{2,1,0:T(8,128)S(1)} %reshape.414.rate_ref, f32[2,384,128]{2,1,0:T(8,128)S(1)} %reshape.423.coef_ref, bf16[1024,768]{1,0:T(8,128)(2,1)S(1)} %get-tuple-element.239.cos_ref, bf16[1024,768]{1,0:T(8,128)(2,1)S(1)} %get-tuple-element.240.sin_ref, ...), custom_call_target="tpu_custom_call" | custom-call | flops 9663676416 | bytes 7340032 | tf_op jit(solution)/shard_map/state_grads/pallas_call | solution.py:181
  308.1 1.9 multiply_convert_fusion.4
  315.5 1.9 add_convert_fusion.1
  318.7 1.9 fusion.84
  329.9 2.7 fusion.239
  332.6 10.7 %collective-permute-done.31 = bf16[1024,384]{1,0:T(8,128)(2,1)S(1)} collective-permute-done((bf16[1024,384]{1,0:T(8,128)(2,1)S(1)}, bf16[1024,384]{1,0:T(8,128)(2,1)S(1)}, u32[]{:S(2)}, u32[]{:S(2)}) %collective-permute-start.31) | collective-permute-done | bytes 786464 | tf_op jit(solution)/shard_map/ppermute | solution.py:248
  345.5 4.0 fusion.53
  349.7 1.9 fusion.66
  353.6 4.4 multiply_convert_fusion
  359.9 4.3 fusion.49
  364.2 3.2 collective-permute-done.32
  380.9 11.2 %state_grads.3 = (f32[384,128]{1,0:T(8,128)S(1)}, f32[384,128]{1,0:T(8,128)S(1)}) custom-call(f32[2,384,128]{2,1,0:T(8,128)S(1)} %reshape.414.rate_ref, f32[2,384,128]{2,1,0:T(8,128)S(1)} %reshape.423.coef_ref, bf16[1024,768]{1,0:T(8,128)(2,1)S(1)} %get-tuple-element.271.cos_ref, bf16[1024,768]{1,0:T(8,128)(2,1)S(1)} %get-tuple-element.272.sin_ref, ...), custom_call_target="tpu_custom_call" | custom-call | flops 9663676416 | bytes 7340032 | tf_op jit(solution)/shard_map/state_grads/pallas_call | solution.py:181
  392.2 5.2 %collective-permute-done.36 = bf16[2,1,1,192,384]{4,3,2,1,0:T(8,128)(2,1)S(1)} collective-permute-done((bf16[2,1,1,192,384]{4,3,2,1,0:T(8,128)(2,1)S(1)}, bf16[2,1,1,192,384]{4,3,2,1,0:T(8,128)(2,1)S(1)}, u32[]{:S(2)}, u32[]{:S(2)}) %collective-permute-start.36) | collective-permute-done | bytes 294944 | tf_op jit(solution)/shard_map/ppermute | solution.py:248
  402.7 2.3 collective-permute-start.41
  408.2 7.5 %collective-permute-done.39 = bf16[1,1,1,192,384]{4,3,2,1,0:T(8,128)(2,1)S(1)} collective-permute-done((bf16[1,1,1,192,384]{4,3,2,1,0:T(8,128)(2,1)S(1)}, bf16[1,1,1,192,384]{4,3,2,1,0:T(8,128)(2,1)S(1)}, u32[]{:S(2)}, u32[]{:S(2)}) %collective-permute-start.39) | collective-permute-done | bytes 147488 | tf_op jit(solution)/shard_map/ppermute | solution.py:248
  417.9 2.2 collective-permute-start.43
  420.3 6.3 %collective-permute-done.44 = bf16[2,1,1,208,128]{4,3,2,1,0:T(8,128)(2,1)S(1)} collective-permute-done((bf16[2,1,1,208,128]{4,3,2,1,0:T(8,128)(2,1)S(1)}, bf16[2,1,1,208,128]{4,3,2,1,0:T(8,128)(2,1)S(1)}, u32[]{:S(2)}, u32[]{:S(2)}) %collective-permute-start.44) | collective-permute-done | bytes 106528 | tf_op jit(solution)/shard_map/ppermute | solution.py:248
  427.3 5.1 %collective-permute-done.45 = bf16[1,1,1,208,128]{4,3,2,1,0:T(8,128)(2,1)S(1)} collective-permute-done((bf16[1,1,1,208,128]{4,3,2,1,0:T(8,128)(2,1)S(1)}, bf16[1,1,1,208,128]{4,3,2,1,0:T(8,128)(2,1)S(1)}, u32[]{:S(2)}, u32[]{:S(2)}) %collective-permute-start.45) | collective-permute-done | bytes 53280 | tf_op jit(solution)/shard_map/ppermute | solution.py:248
  433.5 3.5 all-to-all-start.2
  439.3 5.1 %collective-permute-done.46 = bf16[208,128]{1,0:T(8,128)(2,1)S(1)} collective-permute-done((bf16[208,128]{1,0:T(8,128)(2,1)S(1)}, bf16[208,128]{1,0:T(8,128)(2,1)S(1)}, u32[]{:S(2)}, u32[]{:S(2)}) %collective-permute-start.46) | collective-permute-done | bytes 53280 | tf_op jit(solution)/shard_map/ppermute | solution.py:248
  444.3 4.3 all-to-all-done.2
  457.5 4.7 %collective-permute-done.48 = bf16[2,2,208,128]{3,2,0,1:T(8,128)(2,1)S(1)} collective-permute-done((bf16[2,2,208,128]{3,2,0,1:T(8,128)(2,1)S(1)}, bf16[2,2,208,128]{3,2,0,1:T(8,128)(2,1)S(1)}, u32[]{:S(2)}, u32[]{:S(2)}) %collective-permute-start.48) | collective-permute-done | bytes 213024 | tf_op jit(solution)/shard_map/ppermute | solution.py:248
  (648 shorter events, 183.5 us)
Async XLA Ops:
  9.8 14.6 %collective-permute-start = (bf16[256,768]{1,0:T(8,128)(2,1)S(1)}, bf16[256,768]{1,0:T(8,128)(2,1)S(1)}, u32[]{:S(2)}, u32[]{:S(2)}) collective-permute-start(bf16[256,768]{1,0:T(8,128)(2,1)S(1)} %copy-done.22), channel_id=1, source_target_pairs={{0,2},{1,3},{2,0},{3,1},{4,6},{5,7},{6,4},{7,5},{8,10},{9,11},{10,... | collective-permute-start | bytes 1179656 | tf_op jit(solution)/shard_map/ppermute | solution.py:248
  12.8 11.7 %all-to-all-start = ((bf16[4,64,384]{2,1,0:T(8,128)(2,1)}), bf16[4,64,384]{2,1,0:T(8,128)(2,1)S(1)}, u32[]{:S(2)}, u32[]{:S(2)}) async-start(bf16[4,64,384]{2,1,0:T(8,128)(2,1)} %pad_maximum_fusion.28), calls=%async_computation | async-start | bytes 393216 | tf_op jit(solution)/shard_map/all_to_all | solution.py:451
  25.9 14.9 %collective-permute-start.1 = (bf16[112,384]{1,0:T(8,128)(2,1)}, bf16[112,384]{1,0:T(8,128)(2,1)}, u32[]{:S(2)}, u32[]{:S(2)}) collective-permute-start(bf16[112,384]{1,0:T(8,128)(2,1)} %fusion.191), channel_id=1, source_target_pairs={{0,16},{4,20},{8,24},{12,28},{16,0},{20,4},{24,8},{28,12},{1,17},{... | collective-permute-start | bytes 258056 | tf_op jit(solution)/shard_map/ppermute | solution.py:248
  28.5 12.3 %collective-permute-start.2 = (bf16[96,384]{1,0:T(8,128)(2,1)}, bf16[96,384]{1,0:T(8,128)(2,1)}, u32[]{:S(2)}, u32[]{:S(2)}) collective-permute-start(bf16[96,384]{1,0:T(8,128)(2,1)} %bitcast.13), channel_id=1, source_target_pairs={{0,4},{4,0},{8,12},{12,8},{16,20},{20,16},{24,28},{28,24},{1,5},{5... | collective-permute-start | bytes 221192 | tf_op jit(solution)/shard_map/ppermute | solution.py:248
  30.0 23.3 %all-to-all-start.1 = ((bf16[4,192,384]{2,1,0:T(8,128)(2,1)}), bf16[4,192,384]{2,1,0:T(8,128)(2,1)S(1)}, u32[]{:S(2)}, u32[]{:S(2)}) async-start(bf16[4,192,384]{2,1,0:T(8,128)(2,1)} %constant_dynamic-update-slice_fusion), calls=%async_computation.1 | async-start | bytes 1179648 | tf_op jit(solution)/shard_map/all_to_all | solution.py:487
  33.5 82.9 %all-gather.5.cloned.1.call-start = ((), (), s32[]{:S(2)}) async-start(), calls=%async_computation.5 | async-start | bytes 2654208 | tf_op jit(solution)/shard_map/all_gather | solution.py:521
  41.8 10.4 %collective-permute-start.4 = (bf16[2,96,384]{2,1,0:T(8,128)(2,1)S(1)}, bf16[2,96,384]{2,1,0:T(8,128)(2,1)S(1)}, u32[]{:S(2)}, u32[]{:S(2)}) collective-permute-start(bf16[2,96,384]{2,1,0:T(8,128)(2,1)S(1)} %pad_maximum_fusion.30), channel_id=1, source_target_pairs={{0,16},{4,20},{8,24},{12,28},{16,0},{20,4},{24,8},{28,12},{1,17},{... | collective-permute-start | bytes 442376 | tf_op jit(solution)/shard_map/ppermute | solution.py:248
  43.2 11.5 %copy-start.97 = (bf16[48,384]{1,0:T(8,128)(2,1)S(1)}, bf16[48,384]{1,0:T(8,128)(2,1)}, u32[]{:S(2)}) copy-start(bf16[48,384]{1,0:T(8,128)(2,1)} %get-tuple-element.494) | copy-start | bytes 110596
  43.2 11.5 %copy-start.98 = (bf16[48,384]{1,0:T(8,128)(2,1)S(1)}, bf16[48,384]{1,0:T(8,128)(2,1)}, u32[]{:S(2)}) copy-start(bf16[48,384]{1,0:T(8,128)(2,1)} %get-tuple-element.495) | copy-start | bytes 110596
  43.2 9.4 %collective-permute-start.3 = (bf16[2,112,384]{2,1,0:T(8,128)(2,1)S(1)}, bf16[2,112,384]{2,1,0:T(8,128)(2,1)S(1)}, u32[]{:S(2)}, u32[]{:S(2)}) collective-permute-start(bf16[2,112,384]{2,1,0:T(8,128)(2,1)S(1)} %pad_maximum_fusion.29), channel_id=1, source_target_pairs={{0,8},{4,12},{8,0},{12,4},{16,24},{20,28},{24,16},{28,20},{1,9},{5... | collective-permute-start | bytes 516104 | tf_op jit(solution)/shard_map/ppermute | solution.py:248
  55.5 121.4 %all-gather.7.cloned.1.call-start = ((), (), s32[]{:S(2)}) async-start(), calls=%async_computation.6 | async-start | bytes 3981312 | tf_op jit(solution)/shard_map/all_gather | solution.py:531
  56.8 34.7 %copy-start.120 = (f32[768]{0:T(1024)}, f32[768]{0:T(1024)S(1)}, u32[]{:S(2)}) copy-start(f32[768]{0:T(1024)S(1)} %mul.440) | copy-start | bytes 9220
  56.8 25.5 %copy-start.123 = (f32[1024]{0:T(1024)}, f32[1024]{0:T(1024)S(1)}, u32[]{:S(2)}) copy-start(f32[1024]{0:T(1024)S(1)} %fusion.208) | copy-start | bytes 12292
  59.0 18.4 %collective-permute-start.7 = (bf16[2,256,768]{2,1,0:T(8,128)(2,1)}, bf16[2,256,768]{2,1,0:T(8,128)(2,1)}, u32[]{:S(2)}, u32[]{:S(2)}) collective-permute-start(bf16[2,256,768]{2,1,0:T(8,128)(2,1)} %pad_maximum_fusion.10), channel_id=1, source_target_pairs={{0,1},{1,0},{2,3},{3,2},{4,5},{5,4},{6,7},{7,6},{8,9},{9,8},{10,11... | collective-permute-start | bytes 2359304 | tf_op jit(solution)/shard_map/ppermute | solution.py:248
  59.9 13.8 %collective-permute-start.6 = (bf16[2,2,96,384]{3,2,1,0:T(8,128)(2,1)}, bf16[2,2,96,384]{3,2,1,0:T(8,128)(2,1)}, u32[]{:S(2)}, u32[]{:S(2)}) collective-permute-start(bf16[2,2,96,384]{3,2,1,0:T(8,128)(2,1)} %pad_maximum_fusion.26), channel_id=1, source_target_pairs={{0,8},{4,12},{8,0},{12,4},{16,24},{20,28},{24,16},{28,20},{1,9},{5... | collective-permute-start | bytes 884744 | tf_op jit(solution)/shard_map/ppermute | solution.py:248
  60.0 13.8 %collective-permute-start.5 = (bf16[2,2,112,384]{3,2,1,0:T(8,128)(2,1)S(1)}, bf16[2,2,112,384]{3,2,1,0:T(8,128)(2,1)}, u32[]{:S(2)}, u32[]{:S(2)}) collective-permute-start(bf16[2,2,112,384]{3,2,1,0:T(8,128)(2,1)S(1)} %pad_maximum_fusion.24), channel_id=1, source_target_pairs={{0,4},{4,0},{8,12},{12,8},{16,20},{20,16},{24,28},{28,24},{1,5},{5... | collective-permute-start | bytes 1032200 | tf_op jit(solution)/shard_map/ppermute | solution.py:248
  64.4 351.3 %reduce-scatter.2.cloned.1.call-start = ((), (), s32[]{:S(2)}) async-start(), calls=%async_computation.4 | async-start | bytes 3981312 | tf_op jit(solution)/shard_map/reduce_scatter | solution.py:627
  73.5 18.0 %copy-start.8 = (bf16[1024,768]{1,0:T(8,128)(2,1)}, bf16[1024,768]{1,0:T(8,128)(2,1)S(1)}, u32[]{:S(2)}) copy-start(bf16[1024,768]{1,0:T(8,128)(2,1)S(1)} %get-tuple-element.197) | copy-start | bytes 4718596
  96.7 19.8 %collective-permute-start.8 = (bf16[1024,384]{1,0:T(8,128)(2,1)}, bf16[1024,384]{1,0:T(8,128)(2,1)}, u32[]{:S(2)}, u32[]{:S(2)}) collective-permute-start(bf16[1024,384]{1,0:T(8,128)(2,1)} %fusion.79), channel_id=1, source_target_pairs={{0,2},{1,3},{2,0},{3,1},{4,6},{5,7},{6,4},{7,5},{8,10},{9,11},{10,... | collective-permute-start | bytes 2359304 | tf_op jit(solution)/shard_map/ppermute | solution.py:210
  98.3 28.7 %collective-permute-start.9 = (bf16[1024,384]{1,0:T(8,128)(2,1)}, bf16[1024,384]{1,0:T(8,128)(2,1)}, u32[]{:S(2)}, u32[]{:S(2)}) collective-permute-start(bf16[1024,384]{1,0:T(8,128)(2,1)} %fusion.79), channel_id=1, source_target_pairs={{0,1},{1,0},{2,3},{3,2},{4,5},{5,4},{6,7},{7,6},{8,9},{9,8},{10,11... | collective-permute-start | bytes 2359304 | tf_op jit(solution)/shard_map/ppermute | solution.py:210
  118.0 12.0 %copy-start.19 = (bf16[8,192,384]{2,1,0:T(8,128)(2,1)}, bf16[8,192,384]{2,1,0:T(8,128)(2,1)S(1)}, u32[]{:S(2)}) copy-start(bf16[8,192,384]{2,1,0:T(8,128)(2,1)S(1)} %split.80) | copy-start | bytes 3538948
  118.0 11.9 %collective-permute-start.10 = (bf16[1024,384]{1,0:T(8,128)(2,1)}, bf16[1024,384]{1,0:T(8,128)(2,1)}, u32[]{:S(2)}, u32[]{:S(2)}) collective-permute-start(bf16[1024,384]{1,0:T(8,128)(2,1)} %collective-permute-done.8), channel_id=1, source_target_pairs={{0,1},{1,0},{2,3},{3,2},{4,5},{5,4},{6,7},{7,6},{8,9},{9,8},{10,11... | collective-permute-start | bytes 2359304 | tf_op jit(solution)/shard_map/ppermute | solution.py:210
  137.8 2.5 collective-permute-start.11
  143.3 11.3 %collective-permute-start.12 = (bf16[1,1,256,768]{3,2,1,0:T(8,128)(2,1)S(1)}, bf16[1,1,256,768]{3,2,1,0:T(8,128)(2,1)}, u32[]{:S(2)}, u32[]{:S(2)}) collective-permute-start(bf16[1,1,256,768]{3,2,1,0:T(8,128)(2,1)S(1)} %dynamic-slice_convert_fusion.7), channel_id=1, source_target_pairs={{0,2},{1,3},{2,0},{3,1},{4,6},{5,7},{6,4},{7,5},{8,10},{9,11},{10,... | collective-permute-start | bytes 1179656 | tf_op jit(solution)/shard_map/ppermute | solution.py:248
  145.1 11.9 %copy-start.107 = (f32[256]{0:T(256)}, f32[256]{0:T(256)S(1)}, u32[]{:S(2)}) copy-start(f32[256]{0:T(256)S(1)} %broadcast_multiply_fusion.2) | copy-start | bytes 3076
  157.9 18.9 %collective-permute-start.13 = (bf16[256,768]{1,0:T(8,128)(2,1)}, bf16[256,768]{1,0:T(8,128)(2,1)S(1)}, u32[]{:S(2)}, u32[]{:S(2)}) collective-permute-start(bf16[256,768]{1,0:T(8,128)(2,1)} %add_convert_fusion.7), channel_id=1, source_target_pairs={{0,2},{1,3},{2,0},{3,1},{4,6},{5,7},{6,4},{7,5},{8,10},{9,11},{10,... | collective-permute-start | bytes 1179656 | tf_op jit(solution)/shard_map/ppermute | solution.py:248
  159.6 21.6 %collective-permute-start.20 = (bf16[256,768]{1,0:T(8,128)(2,1)}, bf16[256,768]{1,0:T(8,128)(2,1)}, u32[]{:S(2)}, u32[]{:S(2)}) collective-permute-start(bf16[256,768]{1,0:T(8,128)(2,1)} %param.16), channel_id=1, source_target_pairs={{0,2},{1,3},{2,0},{3,1},{4,6},{5,7},{6,4},{7,5},{8,10},{9,11},{10,... | collective-permute-start | bytes 1179656 | tf_op jit(solution)/shard_map/ppermute | solution.py:248
  180.6 5.2 %collective-permute-start.14 = (bf16[2,256,768]{2,1,0:T(8,128)(2,1)}, bf16[2,256,768]{2,1,0:T(8,128)(2,1)}, u32[]{:S(2)}, u32[]{:S(2)}) collective-permute-start(bf16[2,256,768]{2,1,0:T(8,128)(2,1)} %pad_maximum_fusion.11), channel_id=1, source_target_pairs={{0,1},{1,0},{2,3},{3,2},{4,5},{5,4},{6,7},{7,6},{8,9},{9,8},{10,11... | collective-permute-start | bytes 2359304 | tf_op jit(solution)/shard_map/ppermute | solution.py:248
  182.5 21.7 %collective-permute-start.21 = (bf16[2,256,768]{2,1,0:T(8,128)(2,1)S(1)}, bf16[2,256,768]{2,1,0:T(8,128)(2,1)S(1)}, u32[]{:S(2)}, u32[]{:S(2)}) collective-permute-start(bf16[2,256,768]{2,1,0:T(8,128)(2,1)S(1)} %pad_maximum_fusion.12), channel_id=1, source_target_pairs={{0,1},{1,0},{2,3},{3,2},{4,5},{5,4},{6,7},{7,6},{8,9},{9,8},{10,11... | collective-permute-start | bytes 2359304 | tf_op jit(solution)/shard_map/ppermute | solution.py:248
  202.7 19.8 %collective-permute-start.16 = (bf16[1024,384]{1,0:T(8,128)(2,1)}, bf16[1024,384]{1,0:T(8,128)(2,1)}, u32[]{:S(2)}, u32[]{:S(2)}) collective-permute-start(bf16[1024,384]{1,0:T(8,128)(2,1)} %fusion.78), channel_id=1, source_target_pairs={{0,2},{1,3},{2,0},{3,1},{4,6},{5,7},{6,4},{7,5},{8,10},{9,11},{10,... | collective-permute-start | bytes 2359304 | tf_op jit(solution)/shard_map/ppermute | solution.py:210
  214.8 11.3 %collective-permute-start.15 = (bf16[1024,384]{1,0:T(8,128)(2,1)}, bf16[1024,384]{1,0:T(8,128)(2,1)S(1)}, u32[]{:S(2)}, u32[]{:S(2)}) collective-permute-start(bf16[1024,384]{1,0:T(8,128)(2,1)} %fusion.78), channel_id=1, source_target_pairs={{0,1},{1,0},{2,3},{3,2},{4,5},{5,4},{6,7},{7,6},{8,9},{9,8},{10,11... | collective-permute-start | bytes 2359304 | tf_op jit(solution)/shard_map/ppermute | solution.py:210
  222.5 4.2 collective-permute-start.17
  230.3 3.6 collective-permute-start.23
  231.6 13.3 %collective-permute-start.22 = (bf16[1024,384]{1,0:T(8,128)(2,1)S(1)}, bf16[1024,384]{1,0:T(8,128)(2,1)S(1)}, u32[]{:S(2)}, u32[]{:S(2)}) collective-permute-start(bf16[1024,384]{1,0:T(8,128)(2,1)S(1)} %convolution_convert_fusion.9), channel_id=1, source_target_pairs={{0,1},{1,0},{2,3},{3,2},{4,5},{5,4},{6,7},{7,6},{8,9},{9,8},{10,11... | collective-permute-start | bytes 2359304 | tf_op jit(solution)/shard_map/ppermute | solution.py:248
  232.7 7.8 %collective-permute-start.18 = (bf16[2,1,256,768]{3,2,1,0:T(8,128)(2,1)S(1)}, bf16[2,1,256,768]{3,2,1,0:T(8,128)(2,1)S(1)}, u32[]{:S(2)}, u32[]{:S(2)}) collective-permute-start(bf16[2,1,256,768]{3,2,1,0:T(8,128)(2,1)S(1)} %dynamic-slice_convert_fusion.2), channel_id=1, source_target_pairs={{0,1},{1,0},{2,3},{3,2},{4,5},{5,4},{6,7},{7,6},{8,9},{9,8},{10,11... | collective-permute-start | bytes 2359304 | tf_op jit(solution)/shard_map/ppermute | solution.py:248
  234.6 20.5 %collective-permute-start.24 = (bf16[1024,384]{1,0:T(8,128)(2,1)S(1)}, bf16[1024,384]{1,0:T(8,128)(2,1)S(1)}, u32[]{:S(2)}, u32[]{:S(2)}) collective-permute-start(bf16[1024,384]{1,0:T(8,128)(2,1)S(1)} %add_convert_fusion.3), channel_id=1, source_target_pairs={{0,2},{1,3},{2,0},{3,1},{4,6},{5,7},{6,4},{7,5},{8,10},{9,11},{10,... | collective-permute-start | bytes 2359304 | tf_op jit(solution)/shard_map/ppermute | solution.py:248
  240.7 46.3 %collective-permute-start.19 = (bf16[1,1,256,768]{3,2,1,0:T(8,128)(2,1)S(1)}, bf16[1,1,256,768]{3,2,1,0:T(8,128)(2,1)S(1)}, u32[]{:S(2)}, u32[]{:S(2)}) collective-permute-start(bf16[1,1,256,768]{3,2,1,0:T(8,128)(2,1)S(1)} %dynamic-slice_convert_fusion.6), channel_id=1, source_target_pairs={{0,2},{1,3},{2,0},{3,1},{4,6},{5,7},{6,4},{7,5},{8,10},{9,11},{10,... | collective-permute-start | bytes 1179656 | tf_op jit(solution)/shard_map/ppermute | solution.py:248
  243.9 11.2 %copy-start.64 = (bf16[1024,768]{1,0:T(8,128)(2,1)S(1)}, bf16[1024,768]{1,0:T(8,128)(2,1)}, u32[]{:S(2)}) copy-start(bf16[1024,768]{1,0:T(8,128)(2,1)} %get-tuple-element.235) | copy-start | bytes 4718596
  269.8 3.8 collective-permute-start.25
  273.8 11.6 %collective-permute-start.26 = (bf16[1,1,256,768]{3,2,1,0:T(8,128)(2,1)S(1)}, bf16[1,1,256,768]{3,2,1,0:T(8,128)(2,1)S(1)}, u32[]{:S(2)}, u32[]{:S(2)}) collective-permute-start(bf16[1,1,256,768]{3,2,1,0:T(8,128)(2,1)S(1)} %dynamic-slice_convert_fusion.5), channel_id=1, source_target_pairs={{0,2},{1,3},{2,0},{3,1},{4,6},{5,7},{6,4},{7,5},{8,10},{9,11},{10,... | collective-permute-start | bytes 1179656 | tf_op jit(solution)/shard_map/ppermute | solution.py:248
  289.5 12.6 %collective-permute-start.27 = (bf16[256,768]{1,0:T(8,128)(2,1)S(1)}, bf16[256,768]{1,0:T(8,128)(2,1)S(1)}, u32[]{:S(2)}, u32[]{:S(2)}) collective-permute-start(bf16[256,768]{1,0:T(8,128)(2,1)S(1)} %get-tuple-element.238), channel_id=1, source_target_pairs={{0,2},{1,3},{2,0},{3,1},{4,6},{5,7},{6,4},{7,5},{8,10},{9,11},{10,... | collective-permute-start | bytes 1179656 | tf_op jit(solution)/shard_map/ppermute | solution.py:248
  302.2 3.4 collective-permute-start.28
  311.6 3.9 collective-permute-start.30
  314.7 18.0 %collective-permute-start.29 = (bf16[1024,384]{1,0:T(8,128)(2,1)S(1)}, bf16[1024,384]{1,0:T(8,128)(2,1)S(1)}, u32[]{:S(2)}, u32[]{:S(2)}) collective-permute-start(bf16[1024,384]{1,0:T(8,128)(2,1)S(1)} %convolution_convert_fusion.7), channel_id=1, source_target_pairs={{0,1},{1,0},{2,3},{3,2},{4,5},{5,4},{6,7},{7,6},{8,9},{9,8},{10,11... | collective-permute-start | bytes 2359304 | tf_op jit(solution)/shard_map/ppermute | solution.py:248
  323.4 20.0 %collective-permute-start.31 = (bf16[1024,384]{1,0:T(8,128)(2,1)S(1)}, bf16[1024,384]{1,0:T(8,128)(2,1)S(1)}, u32[]{:S(2)}, u32[]{:S(2)}) collective-permute-start(bf16[1024,384]{1,0:T(8,128)(2,1)S(1)} %add_convert_fusion.1), channel_id=1, source_target_pairs={{0,2},{1,3},{2,0},{3,1},{4,6},{5,7},{6,4},{7,5},{8,10},{9,11},{10,... | collective-permute-start | bytes 2359304 | tf_op jit(solution)/shard_map/ppermute | solution.py:248
  332.6 11.0 %copy-start.61 = (bf16[1024,768]{1,0:T(8,128)(2,1)S(1)}, bf16[1024,768]{1,0:T(8,128)(2,1)}, u32[]{:S(2)}) copy-start(bf16[1024,768]{1,0:T(8,128)(2,1)} %get-tuple-element.253) | copy-start | bytes 4718596
  351.6 15.8 %collective-permute-start.32 = (bf16[2,2,1,192,384]{4,3,2,1,0:T(8,128)(2,1)}, bf16[2,2,1,192,384]{4,3,2,1,0:T(8,128)(2,1)}, u32[]{:S(2)}, u32[]{:S(2)}) collective-permute-start(bf16[2,2,1,192,384]{4,3,2,1,0:T(8,128)(2,1)} %get-tuple-element.256), channel_id=1, source_target_pairs={{0,4},{4,0},{8,12},{12,8},{16,20},{20,16},{24,28},{28,24},{1,5},{5... | collective-permute-start | bytes 1769480 | tf_op jit(solution)/shard_map/ppermute | solution.py:248
  352.3 15.1 %collective-permute-start.33 = (bf16[2,1,2,192,384]{4,3,2,1,0:T(8,128)(2,1)}, bf16[2,1,2,192,384]{4,3,2,1,0:T(8,128)(2,1)}, u32[]{:S(2)}, u32[]{:S(2)}) collective-permute-start(bf16[2,1,2,192,384]{4,3,2,1,0:T(8,128)(2,1)} %get-tuple-element.258), channel_id=1, source_target_pairs={{0,8},{4,12},{8,0},{12,4},{16,24},{20,28},{24,16},{28,20},{1,9},{5... | collective-permute-start | bytes 1769480 | tf_op jit(solution)/shard_map/ppermute | solution.py:248
  369.0 5.6 %collective-permute-start.34 = (bf16[2,1,256,768]{3,2,1,0:T(8,128)(2,1)S(1)}, bf16[2,1,256,768]{3,2,1,0:T(8,128)(2,1)S(1)}, u32[]{:S(2)}, u32[]{:S(2)}) collective-permute-start(bf16[2,1,256,768]{3,2,1,0:T(8,128)(2,1)S(1)} %dynamic-slice_convert_fusion), channel_id=1, source_target_pairs={{0,1},{1,0},{2,3},{3,2},{4,5},{5,4},{6,7},{7,6},{8,9},{9,8},{10,11... | collective-permute-start | bytes 2359304 | tf_op jit(solution)/shard_map/ppermute | solution.py:248
  374.8 22.5 %collective-permute-start.38 = (bf16[2,2,1,96,768]{4,3,2,1,0:T(8,128)(2,1)S(1)}, bf16[2,2,1,96,768]{4,3,2,1,0:T(8,128)(2,1)S(1)}, u32[]{:S(2)}, u32[]{:S(2)}) collective-permute-start(bf16[2,2,1,96,768]{4,3,2,1,0:T(8,128)(2,1)S(1)} %get-tuple-element.270), channel_id=1, source_target_pairs={{0,4},{4,0},{8,12},{12,8},{16,20},{20,16},{24,28},{28,24},{1,5},{5... | collective-permute-start | bytes 1769480 | tf_op jit(solution)/shard_map/ppermute | solution.py:248
  376.7 20.7 %collective-permute-start.35 = (bf16[1,1,256,768]{3,2,1,0:T(8,128)(2,1)S(1)}, bf16[1,1,256,768]{3,2,1,0:T(8,128)(2,1)S(1)}, u32[]{:S(2)}, u32[]{:S(2)}) collective-permute-start(bf16[1,1,256,768]{3,2,1,0:T(8,128)(2,1)S(1)} %dynamic-slice_convert_fusion.4), channel_id=1, source_target_pairs={{0,2},{1,3},{2,0},{3,1},{4,6},{5,7},{6,4},{7,5},{8,10},{9,11},{10,... | collective-permute-start | bytes 1179656 | tf_op jit(solution)/shard_map/ppermute | solution.py:248
  377.8 19.6 %collective-permute-start.36 = (bf16[2,1,1,192,384]{4,3,2,1,0:T(8,128)(2,1)S(1)}, bf16[2,1,1,192,384]{4,3,2,1,0:T(8,128)(2,1)S(1)}, u32[]{:S(2)}, u32[]{:S(2)}) collective-permute-start(bf16[2,1,1,192,384]{4,3,2,1,0:T(8,128)(2,1)S(1)} %get-tuple-element.266), channel_id=1, source_target_pairs={{0,8},{4,12},{8,0},{12,4},{16,24},{20,28},{24,16},{28,20},{1,9},{5... | collective-permute-start | bytes 884744 | tf_op jit(solution)/shard_map/ppermute | solution.py:248
  379.4 17.9 %collective-permute-start.37 = (bf16[1,1,2,192,384]{4,3,2,1,0:T(8,128)(2,1)S(1)}, bf16[1,1,2,192,384]{4,3,2,1,0:T(8,128)(2,1)S(1)}, u32[]{:S(2)}, u32[]{:S(2)}) collective-permute-start(bf16[1,1,2,192,384]{4,3,2,1,0:T(8,128)(2,1)S(1)} %get-tuple-element.268), channel_id=1, source_target_pairs={{0,16},{4,20},{8,24},{12,28},{16,0},{20,4},{24,8},{28,12},{1,17},{... | collective-permute-start | bytes 884744 | tf_op jit(solution)/shard_map/ppermute | solution.py:248
  402.7 13.0 %collective-permute-start.41 = (bf16[2,1,1,96,768]{4,3,2,1,0:T(8,128)(2,1)S(1)}, bf16[2,1,1,96,768]{4,3,2,1,0:T(8,128)(2,1)S(1)}, u32[]{:S(2)}, u32[]{:S(2)}) collective-permute-start(bf16[2,1,1,96,768]{4,3,2,1,0:T(8,128)(2,1)S(1)} %get-tuple-element.291), channel_id=1, source_target_pairs={{0,8},{4,12},{8,0},{12,4},{16,24},{20,28},{24,16},{28,20},{1,9},{5... | collective-permute-start | bytes 884744 | tf_op jit(solution)/shard_map/ppermute | solution.py:248
  405.0 10.7 %collective-permute-start.42 = (bf16[2,2,1,208,128]{4,3,2,1,0:T(8,128)(2,1)S(1)}, bf16[2,2,1,208,128]{4,3,2,1,0:T(8,128)(2,1)S(1)}, u32[]{:S(2)}, u32[]{:S(2)}) collective-permute-start(bf16[2,2,1,208,128]{4,3,2,1,0:T(8,128)(2,1)S(1)} %get-tuple-element.293), channel_id=1, source_target_pairs={{0,4},{4,0},{8,12},{12,8},{16,20},{20,16},{24,28},{28,24},{1,5},{5... | collective-permute-start | bytes 638984 | tf_op jit(solution)/shard_map/ppermute | solution.py:248
  406.5 9.2 %collective-permute-start.39 = (bf16[1,1,1,192,384]{4,3,2,1,0:T(8,128)(2,1)S(1)}, bf16[1,1,1,192,384]{4,3,2,1,0:T(8,128)(2,1)S(1)}, u32[]{:S(2)}, u32[]{:S(2)}) collective-permute-start(bf16[1,1,1,192,384]{4,3,2,1,0:T(8,128)(2,1)S(1)} %get-tuple-element.287), channel_id=1, source_target_pairs={{0,16},{4,20},{8,24},{12,28},{16,0},{20,4},{24,8},{28,12},{1,17},{... | collective-permute-start | bytes 442376 | tf_op jit(solution)/shard_map/ppermute | solution.py:248
  407.1 8.6 %collective-permute-start.40 = (bf16[1,1,1,192,384]{4,3,2,1,0:T(8,128)(2,1)S(1)}, bf16[1,1,1,192,384]{4,3,2,1,0:T(8,128)(2,1)S(1)}, u32[]{:S(2)}, u32[]{:S(2)}) collective-permute-start(bf16[1,1,1,192,384]{4,3,2,1,0:T(8,128)(2,1)S(1)} %get-tuple-element.289), channel_id=1, source_target_pairs={{0,4},{4,0},{8,12},{12,8},{16,20},{20,16},{24,28},{28,24},{1,5},{5... | collective-permute-start | bytes 442376 | tf_op jit(solution)/shard_map/ppermute | solution.py:248
  417.9 8.6 %collective-permute-start.43 = (bf16[1,1,1,96,768]{4,3,2,1,0:T(8,128)(2,1)S(1)}, bf16[1,1,1,96,768]{4,3,2,1,0:T(8,128)(2,1)S(1)}, u32[]{:S(2)}, u32[]{:S(2)}) collective-permute-start(bf16[1,1,1,96,768]{4,3,2,1,0:T(8,128)(2,1)S(1)} %get-tuple-element.301), channel_id=1, source_target_pairs={{0,16},{4,20},{8,24},{12,28},{16,0},{20,4},{24,8},{28,12},{1,17},{... | collective-permute-start | bytes 442376 | tf_op jit(solution)/shard_map/ppermute | solution.py:248
  420.1 6.4 %collective-permute-start.44 = (bf16[2,1,1,208,128]{4,3,2,1,0:T(8,128)(2,1)S(1)}, bf16[2,1,1,208,128]{4,3,2,1,0:T(8,128)(2,1)S(1)}, u32[]{:S(2)}, u32[]{:S(2)}) collective-permute-start(bf16[2,1,1,208,128]{4,3,2,1,0:T(8,128)(2,1)S(1)} %get-tuple-element.303), channel_id=1, source_target_pairs={{0,8},{4,12},{8,0},{12,4},{16,24},{20,28},{24,16},{28,20},{1,9},{5... | collective-permute-start | bytes 319496 | tf_op jit(solution)/shard_map/ppermute | solution.py:248
  426.7 5.7 %collective-permute-start.45 = (bf16[1,1,1,208,128]{4,3,2,1,0:T(8,128)(2,1)S(1)}, bf16[1,1,1,208,128]{4,3,2,1,0:T(8,128)(2,1)S(1)}, u32[]{:S(2)}, u32[]{:S(2)}) collective-permute-start(bf16[1,1,1,208,128]{4,3,2,1,0:T(8,128)(2,1)S(1)} %get-tuple-element.307), channel_id=1, source_target_pairs={{0,16},{4,20},{8,24},{12,28},{16,0},{20,4},{24,8},{28,12},{1,17},{... | collective-permute-start | bytes 159752 | tf_op jit(solution)/shard_map/ppermute | solution.py:248
  433.5 15.1 %all-to-all-start.2 = ((bf16[4,256,384]{2,1,0:T(8,128)(2,1)}), bf16[4,256,384]{2,1,0:T(8,128)(2,1)S(1)}, u32[]{:S(2)}, u32[]{:S(2)}) async-start(bf16[4,256,384]{2,1,0:T(8,128)(2,1)} %copy-done.67), calls=%async_computation.3 | async-start | bytes 1572864 | tf_op jit(solution)/shard_map/all_to_all | solution.py:695
  438.5 5.9 %collective-permute-start.46 = (bf16[208,128]{1,0:T(8,128)(2,1)S(1)}, bf16[208,128]{1,0:T(8,128)(2,1)S(1)}, u32[]{:S(2)}, u32[]{:S(2)}) collective-permute-start(bf16[208,128]{1,0:T(8,128)(2,1)S(1)} %bitcast.555), channel_id=1, source_target_pairs={{0,16},{4,20},{8,24},{12,28},{16,0},{20,4},{24,8},{28,12},{1,17},{... | collective-permute-start | bytes 159752 | tf_op jit(solution)/shard_map/ppermute | solution.py:248
  448.7 6.7 %collective-permute-start.47 = (bf16[2,208,128]{2,1,0:T(8,128)(2,1)S(1)}, bf16[2,208,128]{2,1,0:T(8,128)(2,1)S(1)}, u32[]{:S(2)}, u32[]{:S(2)}) collective-permute-start(bf16[2,208,128]{2,1,0:T(8,128)(2,1)S(1)} %pad_maximum_fusion.31), channel_id=1, source_target_pairs={{0,8},{4,12},{8,0},{12,4},{16,24},{20,28},{24,16},{28,20},{1,9},{5... | collective-permute-start | bytes 319496 | tf_op jit(solution)/shard_map/ppermute | solution.py:248
  455.5 6.7 %collective-permute-start.48 = (bf16[2,2,208,128]{3,2,0,1:T(8,128)(2,1)S(1)}, bf16[2,2,208,128]{3,2,0,1:T(8,128)(2,1)S(1)}, u32[]{:S(2)}, u32[]{:S(2)}) collective-permute-start(bf16[2,2,208,128]{3,2,0,1:T(8,128)(2,1)S(1)} %pad_maximum_fusion.27), channel_id=1, source_target_pairs={{0,4},{4,0},{8,12},{12,8},{16,20},{20,16},{24,28},{28,24},{1,5},{5... | collective-permute-start | bytes 638984 | tf_op jit(solution)/shard_map/ppermute | solution.py:248
  (127 other events, 461.6 us)
Sparse Core Ops, SparseCore 0:
  55.6 55.2 all-gather.4
  113.1 63.7 all-gather.6
  305.8 88.3 reduce-scatter.1

commit v6 on v5

--- a/solution.py
+++ b/solution.py
@@ -533,13 +533,16 @@
     late = []
     stream = tokens.astype(F32)
     kept = []
+    cut = min(2, table_parts)
     for layer in range(depth):
 
         def beside_rows(own):
-            return own, got_layers[layer]
-
-        def early_weights(got):
+            hat, own = make_tables(layer, range(cut, table_parts), hats[layer], own)
+            return own, (got_layers[layer], hat)
+
+        def early_weights(wait):
             if layer:
+                got, hats[layer] = wait
                 side_a, side_b, got = jnp.split(got, [n_in, 2 * n_in], axis=1)
                 early.append((value_weight(side_a, side_b), norms[layer, 0], norms[layer, 1]))
                 late.append(late_weights(got))
@@ -548,12 +551,12 @@
         def beside_product(product):
             hat = ()
             if layer + 1 < depth:
-                hat, product = make_tables(layer + 1, range(table_parts), (), product)
-            return product, (() if layer else got_late, hat)
+                hat, product = make_tables(layer + 1, range(cut), (), product)
+            return product, (() if layer else late_weights(got_late), hat)
 
         def later_weights(wait):
             if not layer:
-                late.append(late_weights(wait[0]))
+                late.append(wait[0])
             hats.append(wait[1])
             return late[layer]
 
@@ -615,7 +618,6 @@
         value_grad, kern_hat, grad_skip = back_convolution(product_low, kept[layer], hats[layer], skips[layer], tables)
         ssm_grads[layer] = (grad_skip,)
         if not layer:
-            value_grad, moving = together(value_grad, moving)
             moving = next_dp(moving, (1, 1))
         normed = kept[layer][2]
         values = dot(normed, value_grad, 0, 0).astype(BF).reshape(dp, n_in, 2 * width)

time: 481 us -> 477 us (level)
  matrix products: 103 us -> 97.2 us
  waiting for transfers between devices: 108 us -> 113 us
    unnamed x302 -> x314, local copies, waits for them, and re-layouts: 37.7 us -> 43.7 us
    dot_general x56, matrix products: 103 us -> 97.2 us  [dot(): lax.dot_general(left, right, (((left_dim,), (right_dim,)), ((), ())), pre...]
  transfers between devices with their start and end apart: 55 -> 55, of which waited for: 20 -> 22; matrix products, arithmetic and copies ran while one was open for 42% -> 40% of each run, Pallas kernels for 11% -> 11%
where the time goes in v6:
time: 477 us; the launch traced here: 468 us
  waiting for transfers between devices  113 us (24%)
  matrix products  97.2 us (20%)
  local copies, waits for them, and re-layouts  81.2 us (17%)
  other arithmetic  56.9 us (12%)
  Pallas kernels  53 us (11%)
  starting transfers between devices  48.8 us (10%)
  between operations  18.1 us (4%)
    dot_general x56, matrix products, dot(): lax.dot_general(left, right, (((left_dim,), (right_dim,)), ((), ())), pre...  97.2 us
    ppermute x43, waiting for transfers between devices, swap(): return lax.ppermute(block, axis, pairs_of(count, bit))  82.6 us
    unnamed x314, local copies, waits for them, and re-layouts  43.7 us
    ppermute x43, starting transfers between devices, swap(): return lax.ppermute(block, axis, pairs_of(count, bit))  35 us
    pallas_call x6, Pallas kernels, spectra(): pl.pallas_call(partial(spectra_kernel, unroll_of(block // 2)), out_shape=...  30.5 us
    pallas_call x2, Pallas kernels, state_grads(): pl.pallas_call(partial(state_grads_kernel, unroll_of(block // 2)), out_sh...  22.6 us
    all_gather x1, waiting for transfers between devices, shards(): lax.all_gather(layer_block(layer), 'dp', axis=0)  16.7 us
    another operation x33, other arithmetic, join(): return jnp.stack(pair, done.index(bit))  16.5 us
  transfers between devices with their start and end apart: 55, of which 22 were waited for; matrix products, arithmetic and copies ran while one was open for 40% of the time, Pallas kernels for 11%

profile of v6, /device:TPU:0, one launch (start us, length us, event | category | flops | bytes accessed | tf_op | source)
XLA Modules:
  0.0 468.4 jit_solution(13879477597940388403)
XLA Ops:
  9.8 2.9 collective-permute-start
  12.8 3.4 all-to-all-start
  25.2 2.7 collective-permute-start.1
  29.4 3.5 all-to-all-start.1
  32.9 2.2 copy-done
  35.1 5.0 %spectra.6 = (bf16[1024,768]{1,0:T(8,128)(2,1)S(1)}, bf16[1024,768]{1,0:T(8,128)(2,1)S(1)}) custom-call(f32[2,384,128]{2,1,0:T(8,128)S(1)} %reshape.413.rate_ref, f32[2,384,128]{2,1,0:T(8,128)S(1)} %reshape.422.coef_ref, f32[1,768]{1,0:T(1,128)S(1)} %copy-done.8, bf16[2048,1024]{1,0:T(8,128)(2,1)S(1)} %copy-done), custom_call_target="tpu_custom_call" | custom-call | flops 3221225472 | bytes 5242880 | tf_op jit(solution)/shard_map/spectra/pallas_call | solution.py:104
  44.8 5.0 %spectra.7 = (bf16[1024,768]{1,0:T(8,128)(2,1)S(1)}, bf16[1024,768]{1,0:T(8,128)(2,1)S(1)}) custom-call(f32[2,384,128]{2,1,0:T(8,128)S(1)} %reshape.413.rate_ref, f32[2,384,128]{2,1,0:T(8,128)S(1)} %reshape.422.coef_ref, f32[1,768]{1,0:T(1,128)S(1)} %copy-done.8, bf16[2048,1024]{1,0:T(8,128)(2,1)S(1)} %copy-done, ...), custom_call_target="tpu_custom_call", output_to_operand_aliasing={{0}: (4, {}), {1}: (5, {})} | custom-call | flops 3221225472 | bytes 5242880 | tf_op jit(solution)/shard_map/spectra/pallas_call | solution.py:104
  67.2 2.2 copy-done.1
  70.8 5.0 %spectra.8 = (bf16[1024,768]{1,0:T(8,128)(2,1)S(1)}, bf16[1024,768]{1,0:T(8,128)(2,1)S(1)}) custom-call(f32[2,384,128]{2,1,0:T(8,128)S(1)} %reshape.413.rate_ref, f32[2,384,128]{2,1,0:T(8,128)S(1)} %reshape.422.coef_ref, f32[1,768]{1,0:T(1,128)S(1)} %copy-done.8, bf16[2048,1024]{1,0:T(8,128)(2,1)S(1)} %copy-done.1, ...), custom_call_target="tpu_custom_call", output_to_operand_aliasing={{0}: (4, {}), {1}: (5, {})} | custom-call | flops 3221225472 | bytes 5242880 | tf_op jit(solution)/shard_map/spectra/pallas_call | solution.py:104
  83.8 2.1 fusion.5
  86.0 3.5 fusion.17
  89.6 3.6 fusion.50
  93.3 1.9 fusion.75
  96.0 3.3 fusion.200
  102.0 5.0 %spectra.9 = (bf16[1024,768]{1,0:T(8,128)(2,1)S(1)}, bf16[1024,768]{1,0:T(8,128)(2,1)S(1)}) custom-call(f32[2,384,128]{2,1,0:T(8,128)S(1)} %reshape.413.rate_ref, f32[2,384,128]{2,1,0:T(8,128)S(1)} %reshape.422.coef_ref, f32[1,768]{1,0:T(1,128)S(1)} %copy-done.8, bf16[2048,1024]{1,0:T(8,128)(2,1)S(1)} %copy-done.2), custom_call_target="tpu_custom_call" | custom-call | flops 3221225472 | bytes 5242880 | tf_op jit(solution)/shard_map/spectra/pallas_call | solution.py:104
  107.0 5.4 %spectra.10 = (bf16[1024,768]{1,0:T(8,128)(2,1)S(1)}, bf16[1024,768]{1,0:T(8,128)(2,1)S(1)}) custom-call(f32[2,384,128]{2,1,0:T(8,128)S(1)} %reshape.413.rate_ref, f32[2,384,128]{2,1,0:T(8,128)S(1)} %reshape.422.coef_ref, f32[1,768]{1,0:T(1,128)S(1)} %copy-done.8, bf16[2048,1024]{1,0:T(8,128)(2,1)S(1)} %copy-done.2, ...), custom_call_target="tpu_custom_call", output_to_operand_aliasing={{0}: (4, {}), {1}: (5, {})} | custom-call | flops 3221225472 | bytes 5242880 | tf_op jit(solution)/shard_map/spectra/pallas_call | solution.py:104
  116.4 3.3 collective-permute-done.8
  121.6 1.8 fusion.204
  123.5 1.9 fusion.203
  126.4 2.2 fusion.59
  132.4 2.0 collective-permute-done.11
  134.4 1.8 convert_add_fusion.3
  139.3 9.7 %collective-permute-done.12 = bf16[1,1,256,768]{3,2,1,0:T(8,128)(2,1)} collective-permute-done((bf16[1,1,256,768]{3,2,1,0:T(8,128)(2,1)S(1)}, bf16[1,1,256,768]{3,2,1,0:T(8,128)(2,1)}, u32[]{:S(2)}, u32[]{:S(2)}) %collective-permute-start.12) | collective-permute-done | bytes 393248 | tf_op jit(solution)/shard_map/ppermute | solution.py:248
  149.0 2.3 fusion.183
  155.3 5.0 %spectra.11 = (bf16[1024,768]{1,0:T(8,128)(2,1)S(1)}, bf16[1024,768]{1,0:T(8,128)(2,1)S(1)}) custom-call(f32[2,384,128]{2,1,0:T(8,128)S(1)} %reshape.413.rate_ref, f32[2,384,128]{2,1,0:T(8,128)S(1)} %reshape.422.coef_ref, f32[1,768]{1,0:T(1,128)S(1)} %copy-done.8, bf16[2048,1024]{1,0:T(8,128)(2,1)S(1)} %copy-done.3, ...), custom_call_target="tpu_custom_call", output_to_operand_aliasing={{0}: (4, {}), {1}: (5, {})} | custom-call | flops 3221225472 | bytes 5242880 | tf_op jit(solution)/shard_map/spectra/pallas_call | solution.py:104
  161.6 16.7 %all-gather.7.cloned.1.call-done = bf16[4608,384]{1,0:T(8,128)(2,1)} async-done(((bf16[576,384]{1,0:T(8,128)(2,1)}), bf16[4608,384]{1,0:T(8,128)(2,1)}) %all-gather.7.cloned.1.call-update) | async-done | bytes 3538960 | tf_op jit(solution)/shard_map/all_gather | solution.py:531
  183.1 2.8 fusion.184
  188.4 3.7 fusion.23
  192.1 3.6 fusion.51
  195.8 1.9 fusion.72
  198.5 3.2 fusion.201
  205.8 2.4 split.87
  209.5 2.8 reshape.468
  213.5 2.6 fusion.207
  216.1 6.5 %collective-permute-done.16 = bf16[1024,384]{1,0:T(8,128)(2,1)} collective-permute-done((bf16[1024,384]{1,0:T(8,128)(2,1)}, bf16[1024,384]{1,0:T(8,128)(2,1)}, u32[]{:S(2)}, u32[]{:S(2)}) %collective-permute-start.16) | collective-permute-done | bytes 786464 | tf_op jit(solution)/shard_map/ppermute | solution.py:210
  244.8 10.1 %collective-permute-done.24 = bf16[1024,384]{1,0:T(8,128)(2,1)S(1)} collective-permute-done((bf16[1024,384]{1,0:T(8,128)(2,1)S(1)}, bf16[1024,384]{1,0:T(8,128)(2,1)S(1)}, u32[]{:S(2)}, u32[]{:S(2)}) %collective-permute-start.24) | collective-permute-done | bytes 786464 | tf_op jit(solution)/shard_map/ppermute | solution.py:248
  255.5 2.2 copy-done.5
  257.7 3.6 fusion.52
  261.4 1.9 fusion.69
  263.4 3.9 multiply_convert_fusion.1
  276.9 8.5 %collective-permute-done.26 = bf16[1,1,256,768]{3,2,1,0:T(8,128)(2,1)S(1)} collective-permute-done((bf16[1,1,256,768]{3,2,1,0:T(8,128)(2,1)S(1)}, bf16[1,1,256,768]{3,2,1,0:T(8,128)(2,1)S(1)}, u32[]{:S(2)}, u32[]{:S(2)}) %collective-permute-start.26) | collective-permute-done | bytes 393248 | tf_op jit(solution)/shard_map/ppermute | solution.py:248
  290.0 11.3 %state_grads.2 = (f32[384,128]{1,0:T(8,128)S(1)}, f32[384,128]{1,0:T(8,128)S(1)}) custom-call(f32[2,384,128]{2,1,0:T(8,128)S(1)} %reshape.413.rate_ref, f32[2,384,128]{2,1,0:T(8,128)S(1)} %reshape.422.coef_ref, bf16[1024,768]{1,0:T(8,128)(2,1)S(1)} %get-tuple-element.252.cos_ref, bf16[1024,768]{1,0:T(8,128)(2,1)S(1)} %get-tuple-element.253.sin_ref, ...), custom_call_target="tpu_custom_call" | custom-call | flops 9663676416 | bytes 7340032 | tf_op jit(solution)/shard_map/state_grads/pallas_call | solution.py:181
  306.7 1.9 multiply_convert_fusion.4
  317.2 1.8 add_convert_fusion.1
  320.2 1.9 fusion.84
  322.1 1.8 fusion.86
  326.7 1.8 fusion.85
  330.3 14.5 %collective-permute-done.31 = bf16[1024,384]{1,0:T(8,128)(2,1)S(1)} collective-permute-done((bf16[1024,384]{1,0:T(8,128)(2,1)S(1)}, bf16[1024,384]{1,0:T(8,128)(2,1)S(1)}, u32[]{:S(2)}, u32[]{:S(2)}) %collective-permute-start.31) | collective-permute-done | bytes 786464 | tf_op jit(solution)/shard_map/ppermute | solution.py:248
  347.0 3.8 fusion.53
  350.9 1.9 fusion.66
  354.8 3.5 multiply_convert_fusion
  364.0 4.3 fusion.49
  369.9 4.3 collective-permute-done.34
  380.5 11.3 %state_grads.3 = (f32[384,128]{1,0:T(8,128)S(1)}, f32[384,128]{1,0:T(8,128)S(1)}) custom-call(f32[2,384,128]{2,1,0:T(8,128)S(1)} %reshape.413.rate_ref, f32[2,384,128]{2,1,0:T(8,128)S(1)} %reshape.422.coef_ref, bf16[1024,768]{1,0:T(8,128)(2,1)S(1)} %get-tuple-element.279.cos_ref, bf16[1024,768]{1,0:T(8,128)(2,1)S(1)} %get-tuple-element.280.sin_ref, ...), custom_call_target="tpu_custom_call" | custom-call | flops 9663676416 | bytes 7340032 | tf_op jit(solution)/shard_map/state_grads/pallas_call | solution.py:181
  391.9 2.9 collective-permute-done.36
  399.6 1.9 collective-permute-start.41
  404.1 6.4 %collective-permute-done.39 = bf16[1,1,1,192,384]{4,3,2,1,0:T(8,128)(2,1)S(1)} collective-permute-done((bf16[1,1,1,192,384]{4,3,2,1,0:T(8,128)(2,1)S(1)}, bf16[1,1,1,192,384]{4,3,2,1,0:T(8,128)(2,1)S(1)}, u32[]{:S(2)}, u32[]{:S(2)}) %collective-permute-start.39) | collective-permute-done | bytes 147488 | tf_op jit(solution)/shard_map/ppermute | solution.py:248
  413.8 3.0 collective-permute-start.43
  417.1 4.5 collective-permute-done.44
  423.6 4.7 collective-permute-done.45
  429.3 3.5 all-to-all-start.2
  435.2 5.0 %collective-permute-done.46 = bf16[208,128]{1,0:T(8,128)(2,1)S(1)} collective-permute-done((bf16[208,128]{1,0:T(8,128)(2,1)S(1)}, bf16[208,128]{1,0:T(8,128)(2,1)S(1)}, u32[]{:S(2)}, u32[]{:S(2)}) %collective-permute-start.46) | collective-permute-done | bytes 53280 | tf_op jit(solution)/shard_map/ppermute | solution.py:248
  440.3 4.1 all-to-all-done.2
  452.1 5.9 %collective-permute-done.48 = bf16[2,2,208,128]{3,2,0,1:T(8,128)(2,1)S(1)} collective-permute-done((bf16[2,2,208,128]{3,2,0,1:T(8,128)(2,1)S(1)}, bf16[2,2,208,128]{3,2,0,1:T(8,128)(2,1)S(1)}, u32[]{:S(2)}, u32[]{:S(2)}) %collective-permute-start.48) | collective-permute-done | bytes 213024 | tf_op jit(solution)/shard_map/ppermute | solution.py:248
  (661 shorter events, 180.8 us)
Async XLA Ops:
  9.8 14.6 %collective-permute-start = (bf16[256,768]{1,0:T(8,128)(2,1)S(1)}, bf16[256,768]{1,0:T(8,128)(2,1)}, u32[]{:S(2)}, u32[]{:S(2)}) collective-permute-start(bf16[256,768]{1,0:T(8,128)(2,1)S(1)} %copy-done.23), channel_id=1, source_target_pairs={{0,2},{1,3},{2,0},{3,1},{4,6},{5,7},{6,4},{7,5},{8,10},{9,11},{10,... | collective-permute-start | bytes 1179656 | tf_op jit(solution)/shard_map/ppermute | solution.py:248
  12.8 11.7 %all-to-all-start = ((bf16[4,64,384]{2,1,0:T(8,128)(2,1)}), bf16[4,64,384]{2,1,0:T(8,128)(2,1)S(1)}, u32[]{:S(2)}, u32[]{:S(2)}) async-start(bf16[4,64,384]{2,1,0:T(8,128)(2,1)} %pad_maximum_fusion.28), calls=%async_computation | async-start | bytes 393216 | tf_op jit(solution)/shard_map/all_to_all | solution.py:451
  25.2 14.9 %collective-permute-start.1 = (bf16[112,384]{1,0:T(8,128)(2,1)S(1)}, bf16[112,384]{1,0:T(8,128)(2,1)S(1)}, u32[]{:S(2)}, u32[]{:S(2)}) collective-permute-start(bf16[112,384]{1,0:T(8,128)(2,1)S(1)} %fusion.164), channel_id=1, source_target_pairs={{0,16},{4,20},{8,24},{12,28},{16,0},{20,4},{24,8},{28,12},{1,17},{... | collective-permute-start | bytes 258056 | tf_op jit(solution)/shard_map/ppermute | solution.py:248
  27.9 12.3 %collective-permute-start.2 = (bf16[96,384]{1,0:T(8,128)(2,1)}, bf16[96,384]{1,0:T(8,128)(2,1)}, u32[]{:S(2)}, u32[]{:S(2)}) collective-permute-start(bf16[96,384]{1,0:T(8,128)(2,1)} %bitcast.13), channel_id=1, source_target_pairs={{0,4},{4,0},{8,12},{12,8},{16,20},{20,16},{24,28},{28,24},{1,5},{5... | collective-permute-start | bytes 221192 | tf_op jit(solution)/shard_map/ppermute | solution.py:248
  29.4 23.9 %all-to-all-start.1 = ((bf16[4,192,384]{2,1,0:T(8,128)(2,1)}), bf16[4,192,384]{2,1,0:T(8,128)(2,1)S(1)}, u32[]{:S(2)}, u32[]{:S(2)}) async-start(bf16[4,192,384]{2,1,0:T(8,128)(2,1)} %constant_dynamic-update-slice_fusion), calls=%async_computation.1 | async-start | bytes 1179648 | tf_op jit(solution)/shard_map/all_to_all | solution.py:487
  32.9 80.7 %all-gather.5.cloned.1.call-start = ((), (), s32[]{:S(2)}) async-start(), calls=%async_computation.5 | async-start | bytes 2654208 | tf_op jit(solution)/shard_map/all_gather | solution.py:521
  41.8 10.4 %collective-permute-start.4 = (bf16[2,96,384]{2,1,0:T(8,128)(2,1)S(1)}, bf16[2,96,384]{2,1,0:T(8,128)(2,1)S(1)}, u32[]{:S(2)}, u32[]{:S(2)}) collective-permute-start(bf16[2,96,384]{2,1,0:T(8,128)(2,1)S(1)} %pad_maximum_fusion.30), channel_id=1, source_target_pairs={{0,16},{4,20},{8,24},{12,28},{16,0},{20,4},{24,8},{28,12},{1,17},{... | collective-permute-start | bytes 442376 | tf_op jit(solution)/shard_map/ppermute | solution.py:248
  43.1 9.5 %collective-permute-start.3 = (bf16[2,112,384]{2,1,0:T(8,128)(2,1)S(1)}, bf16[2,112,384]{2,1,0:T(8,128)(2,1)S(1)}, u32[]{:S(2)}, u32[]{:S(2)}) collective-permute-start(bf16[2,112,384]{2,1,0:T(8,128)(2,1)S(1)} %pad_maximum_fusion.29), channel_id=1, source_target_pairs={{0,8},{4,12},{8,0},{12,4},{16,24},{20,28},{24,16},{28,20},{1,9},{5... | collective-permute-start | bytes 516104 | tf_op jit(solution)/shard_map/ppermute | solution.py:248
  56.2 122.1 %all-gather.7.cloned.1.call-start = ((), (), s32[]{:S(2)}) async-start(), calls=%async_computation.6 | async-start | bytes 3981312 | tf_op jit(solution)/shard_map/all_gather | solution.py:531
  60.8 19.4 %collective-permute-start.7 = (bf16[2,256,768]{2,1,0:T(8,128)(2,1)}, bf16[2,256,768]{2,1,0:T(8,128)(2,1)}, u32[]{:S(2)}, u32[]{:S(2)}) collective-permute-start(bf16[2,256,768]{2,1,0:T(8,128)(2,1)} %pad_maximum_fusion.10), channel_id=1, source_target_pairs={{0,1},{1,0},{2,3},{3,2},{4,5},{5,4},{6,7},{7,6},{8,9},{9,8},{10,11... | collective-permute-start | bytes 2359304 | tf_op jit(solution)/shard_map/ppermute | solution.py:248
  61.7 14.8 %collective-permute-start.6 = (bf16[2,2,96,384]{3,2,1,0:T(8,128)(2,1)}, bf16[2,2,96,384]{3,2,1,0:T(8,128)(2,1)}, u32[]{:S(2)}, u32[]{:S(2)}) collective-permute-start(bf16[2,2,96,384]{3,2,1,0:T(8,128)(2,1)} %pad_maximum_fusion.26), channel_id=1, source_target_pairs={{0,8},{4,12},{8,0},{12,4},{16,24},{20,28},{24,16},{28,20},{1,9},{5... | collective-permute-start | bytes 884744 | tf_op jit(solution)/shard_map/ppermute | solution.py:248
  62.6 13.9 %collective-permute-start.5 = (bf16[2,2,112,384]{3,2,1,0:T(8,128)(2,1)}, bf16[2,2,112,384]{3,2,1,0:T(8,128)(2,1)}, u32[]{:S(2)}, u32[]{:S(2)}) collective-permute-start(bf16[2,2,112,384]{3,2,1,0:T(8,128)(2,1)} %pad_maximum_fusion.24), channel_id=1, source_target_pairs={{0,4},{4,0},{8,12},{12,8},{16,20},{20,16},{24,28},{28,24},{1,5},{5... | collective-permute-start | bytes 1032200 | tf_op jit(solution)/shard_map/ppermute | solution.py:248
  67.0 344.5 %reduce-scatter.2.cloned.1.call-start = ((), (), s32[]{:S(2)}) async-start(), calls=%async_computation.4 | async-start | bytes 3981312 | tf_op jit(solution)/shard_map/reduce_scatter | solution.py:629
  75.9 19.3 %copy-start.9 = (bf16[1024,768]{1,0:T(8,128)(2,1)}, bf16[1024,768]{1,0:T(8,128)(2,1)S(1)}, u32[]{:S(2)}) copy-start(bf16[1024,768]{1,0:T(8,128)(2,1)S(1)} %get-tuple-element.201) | copy-start | bytes 4718596
  100.3 19.4 %collective-permute-start.8 = (bf16[1024,384]{1,0:T(8,128)(2,1)}, bf16[1024,384]{1,0:T(8,128)(2,1)}, u32[]{:S(2)}, u32[]{:S(2)}) collective-permute-start(bf16[1024,384]{1,0:T(8,128)(2,1)} %fusion.79), channel_id=1, source_target_pairs={{0,2},{1,3},{2,0},{3,1},{4,6},{5,7},{6,4},{7,5},{8,10},{9,11},{10,... | collective-permute-start | bytes 2359304 | tf_op jit(solution)/shard_map/ppermute | solution.py:210
  102.0 21.5 %collective-permute-start.9 = (bf16[1024,384]{1,0:T(8,128)(2,1)}, bf16[1024,384]{1,0:T(8,128)(2,1)}, u32[]{:S(2)}, u32[]{:S(2)}) collective-permute-start(bf16[1024,384]{1,0:T(8,128)(2,1)} %fusion.79), channel_id=1, source_target_pairs={{0,1},{1,0},{2,3},{3,2},{4,5},{5,4},{6,7},{7,6},{8,9},{9,8},{10,11... | collective-permute-start | bytes 2359304 | tf_op jit(solution)/shard_map/ppermute | solution.py:210
  116.3 12.8 %copy-start.29 = (bf16[48,8,2,384]{3,1,2,0:T(8,128)(2,1)}, bf16[48,8,2,384]{3,1,2,0:T(8,128)(2,1)S(1)}, u32[]{:S(2)}) copy-start(bf16[48,8,2,384]{3,1,2,0:T(8,128)(2,1)S(1)} %copy.237) | copy-start | bytes 1769476
  116.4 9.9 %copy-start.48 = (bf16[384,384]{1,0:T(8,128)(2,1)}, bf16[384,384]{1,0:T(8,128)(2,1)S(1)}, u32[]{:S(2)}) copy-start(bf16[384,384]{1,0:T(8,128)(2,1)S(1)} %get-tuple-element.226) | copy-start | bytes 884740
  119.8 6.6 %collective-permute-start.10 = (bf16[1024,384]{1,0:T(8,128)(2,1)}, bf16[1024,384]{1,0:T(8,128)(2,1)S(1)}, u32[]{:S(2)}, u32[]{:S(2)}) collective-permute-start(bf16[1024,384]{1,0:T(8,128)(2,1)} %collective-permute-done.8), channel_id=1, source_target_pairs={{0,1},{1,0},{2,3},{3,2},{4,5},{5,4},{6,7},{7,6},{8,9},{9,8},{10,11... | collective-permute-start | bytes 2359304 | tf_op jit(solution)/shard_map/ppermute | solution.py:210
  131.9 2.6 collective-permute-start.11
  137.5 11.6 %collective-permute-start.12 = (bf16[1,1,256,768]{3,2,1,0:T(8,128)(2,1)S(1)}, bf16[1,1,256,768]{3,2,1,0:T(8,128)(2,1)}, u32[]{:S(2)}, u32[]{:S(2)}) collective-permute-start(bf16[1,1,256,768]{3,2,1,0:T(8,128)(2,1)S(1)} %dynamic-slice_convert_fusion.7), channel_id=1, source_target_pairs={{0,2},{1,3},{2,0},{3,1},{4,6},{5,7},{6,4},{7,5},{8,10},{9,11},{10,... | collective-permute-start | bytes 1179656 | tf_op jit(solution)/shard_map/ppermute | solution.py:248
  139.3 12.2 %copy-start.114 = (f32[256]{0:T(256)}, f32[256]{0:T(256)S(1)}, u32[]{:S(2)}) copy-start(f32[256]{0:T(256)S(1)} %broadcast_multiply_fusion.2) | copy-start | bytes 3076
  151.8 26.5 %collective-permute-start.13 = (bf16[256,768]{1,0:T(8,128)(2,1)S(1)}, bf16[256,768]{1,0:T(8,128)(2,1)}, u32[]{:S(2)}, u32[]{:S(2)}) collective-permute-start(bf16[256,768]{1,0:T(8,128)(2,1)S(1)} %add_convert_fusion.7), channel_id=1, source_target_pairs={{0,2},{1,3},{2,0},{3,1},{4,6},{5,7},{6,4},{7,5},{8,10},{9,11},{10,... | collective-permute-start | bytes 1179656 | tf_op jit(solution)/shard_map/ppermute | solution.py:248
  153.5 27.7 %collective-permute-start.20 = (bf16[256,768]{1,0:T(8,128)(2,1)}, bf16[256,768]{1,0:T(8,128)(2,1)}, u32[]{:S(2)}, u32[]{:S(2)}) collective-permute-start(bf16[256,768]{1,0:T(8,128)(2,1)} %param.16), channel_id=1, source_target_pairs={{0,2},{1,3},{2,0},{3,1},{4,6},{5,7},{6,4},{7,5},{8,10},{9,11},{10,... | collective-permute-start | bytes 1179656 | tf_op jit(solution)/shard_map/ppermute | solution.py:248
  181.2 4.7 %collective-permute-start.14 = (bf16[2,256,768]{2,1,0:T(8,128)(2,1)}, bf16[2,256,768]{2,1,0:T(8,128)(2,1)}, u32[]{:S(2)}, u32[]{:S(2)}) collective-permute-start(bf16[2,256,768]{2,1,0:T(8,128)(2,1)} %pad_maximum_fusion.11), channel_id=1, source_target_pairs={{0,1},{1,0},{2,3},{3,2},{4,5},{5,4},{6,7},{7,6},{8,9},{9,8},{10,11... | collective-permute-start | bytes 2359304 | tf_op jit(solution)/shard_map/ppermute | solution.py:248
  181.2 16.5 %copy-start.126 = (f32[768]{0:T(1024)}, f32[768]{0:T(1024)S(1)}, u32[]{:S(2)}) copy-start(f32[768]{0:T(1024)S(1)} %mul.474) | copy-start | bytes 9220
  182.5 21.7 %collective-permute-start.21 = (bf16[2,256,768]{2,1,0:T(8,128)(2,1)S(1)}, bf16[2,256,768]{2,1,0:T(8,128)(2,1)S(1)}, u32[]{:S(2)}, u32[]{:S(2)}) collective-permute-start(bf16[2,256,768]{2,1,0:T(8,128)(2,1)S(1)} %pad_maximum_fusion.12), channel_id=1, source_target_pairs={{0,1},{1,0},{2,3},{3,2},{4,5},{5,4},{6,7},{7,6},{8,9},{9,8},{10,11... | collective-permute-start | bytes 2359304 | tf_op jit(solution)/shard_map/ppermute | solution.py:248
  202.8 19.8 %collective-permute-start.16 = (bf16[1024,384]{1,0:T(8,128)(2,1)}, bf16[1024,384]{1,0:T(8,128)(2,1)}, u32[]{:S(2)}, u32[]{:S(2)}) collective-permute-start(bf16[1024,384]{1,0:T(8,128)(2,1)} %fusion.78), channel_id=1, source_target_pairs={{0,2},{1,3},{2,0},{3,1},{4,6},{5,7},{6,4},{7,5},{8,10},{9,11},{10,... | collective-permute-start | bytes 2359304 | tf_op jit(solution)/shard_map/ppermute | solution.py:210
  213.4 12.7 %collective-permute-start.15 = (bf16[1024,384]{1,0:T(8,128)(2,1)}, bf16[1024,384]{1,0:T(8,128)(2,1)S(1)}, u32[]{:S(2)}, u32[]{:S(2)}) collective-permute-start(bf16[1024,384]{1,0:T(8,128)(2,1)} %fusion.78), channel_id=1, source_target_pairs={{0,1},{1,0},{2,3},{3,2},{4,5},{5,4},{6,7},{7,6},{8,9},{9,8},{10,11... | collective-permute-start | bytes 2359304 | tf_op jit(solution)/shard_map/ppermute | solution.py:210
  222.6 4.2 collective-permute-start.17
  230.2 3.6 collective-permute-start.23
  231.4 13.4 %collective-permute-start.22 = (bf16[1024,384]{1,0:T(8,128)(2,1)S(1)}, bf16[1024,384]{1,0:T(8,128)(2,1)S(1)}, u32[]{:S(2)}, u32[]{:S(2)}) collective-permute-start(bf16[1024,384]{1,0:T(8,128)(2,1)S(1)} %convolution_convert_fusion.9), channel_id=1, source_target_pairs={{0,1},{1,0},{2,3},{3,2},{4,5},{5,4},{6,7},{7,6},{8,9},{9,8},{10,11... | collective-permute-start | bytes 2359304 | tf_op jit(solution)/shard_map/ppermute | solution.py:248
  232.6 7.8 %collective-permute-start.18 = (bf16[2,1,256,768]{3,2,1,0:T(8,128)(2,1)S(1)}, bf16[2,1,256,768]{3,2,1,0:T(8,128)(2,1)S(1)}, u32[]{:S(2)}, u32[]{:S(2)}) collective-permute-start(bf16[2,1,256,768]{3,2,1,0:T(8,128)(2,1)S(1)} %dynamic-slice_convert_fusion.2), channel_id=1, source_target_pairs={{0,1},{1,0},{2,3},{3,2},{4,5},{5,4},{6,7},{7,6},{8,9},{9,8},{10,11... | collective-permute-start | bytes 2359304 | tf_op jit(solution)/shard_map/ppermute | solution.py:248
  234.4 20.5 %collective-permute-start.24 = (bf16[1024,384]{1,0:T(8,128)(2,1)S(1)}, bf16[1024,384]{1,0:T(8,128)(2,1)S(1)}, u32[]{:S(2)}, u32[]{:S(2)}) collective-permute-start(bf16[1024,384]{1,0:T(8,128)(2,1)S(1)} %add_convert_fusion.3), channel_id=1, source_target_pairs={{0,2},{1,3},{2,0},{3,1},{4,6},{5,7},{6,4},{7,5},{8,10},{9,11},{10,... | collective-permute-start | bytes 2359304 | tf_op jit(solution)/shard_map/ppermute | solution.py:248
  240.6 46.4 %collective-permute-start.19 = (bf16[1,1,256,768]{3,2,1,0:T(8,128)(2,1)S(1)}, bf16[1,1,256,768]{3,2,1,0:T(8,128)(2,1)S(1)}, u32[]{:S(2)}, u32[]{:S(2)}) collective-permute-start(bf16[1,1,256,768]{3,2,1,0:T(8,128)(2,1)S(1)} %dynamic-slice_convert_fusion.6), channel_id=1, source_target_pairs={{0,2},{1,3},{2,0},{3,1},{4,6},{5,7},{6,4},{7,5},{8,10},{9,11},{10,... | collective-permute-start | bytes 1179656 | tf_op jit(solution)/shard_map/ppermute | solution.py:248
  243.7 11.2 %copy-start.72 = (bf16[1024,768]{1,0:T(8,128)(2,1)S(1)}, bf16[1024,768]{1,0:T(8,128)(2,1)}, u32[]{:S(2)}) copy-start(bf16[1024,768]{1,0:T(8,128)(2,1)} %get-tuple-element.248) | copy-start | bytes 4718596
  269.9 3.7 collective-permute-start.25
  273.8 11.6 %collective-permute-start.26 = (bf16[1,1,256,768]{3,2,1,0:T(8,128)(2,1)S(1)}, bf16[1,1,256,768]{3,2,1,0:T(8,128)(2,1)S(1)}, u32[]{:S(2)}, u32[]{:S(2)}) collective-permute-start(bf16[1,1,256,768]{3,2,1,0:T(8,128)(2,1)S(1)} %dynamic-slice_convert_fusion.5), channel_id=1, source_target_pairs={{0,2},{1,3},{2,0},{3,1},{4,6},{5,7},{6,4},{7,5},{8,10},{9,11},{10,... | collective-permute-start | bytes 1179656 | tf_op jit(solution)/shard_map/ppermute | solution.py:248
  276.9 10.1 %copy-start.73 = (bf16[256,768]{1,0:T(8,128)(2,1)S(1)}, bf16[256,768]{1,0:T(8,128)(2,1)}, u32[]{:S(2)}) copy-start(bf16[256,768]{1,0:T(8,128)(2,1)} %param.16) | copy-start | bytes 1179652
  288.6 12.7 %collective-permute-start.27 = (bf16[256,768]{1,0:T(8,128)(2,1)S(1)}, bf16[256,768]{1,0:T(8,128)(2,1)S(1)}, u32[]{:S(2)}, u32[]{:S(2)}) collective-permute-start(bf16[256,768]{1,0:T(8,128)(2,1)S(1)} %get-tuple-element.251), channel_id=1, source_target_pairs={{0,2},{1,3},{2,0},{3,1},{4,6},{5,7},{6,4},{7,5},{8,10},{9,11},{10,... | collective-permute-start | bytes 1179656 | tf_op jit(solution)/shard_map/ppermute | solution.py:248
  301.4 3.5 collective-permute-start.28
  310.2 6.8 %collective-permute-start.30 = (bf16[1024,384]{1,0:T(8,128)(2,1)}, bf16[1024,384]{1,0:T(8,128)(2,1)}, u32[]{:S(2)}, u32[]{:S(2)}) collective-permute-start(bf16[1024,384]{1,0:T(8,128)(2,1)} %convolution_convert_fusion.6), channel_id=1, source_target_pairs={{0,1},{1,0},{2,3},{3,2},{4,5},{5,4},{6,7},{7,6},{8,9},{9,8},{10,11... | collective-permute-start | bytes 2359304 | tf_op jit(solution)/shard_map/ppermute | solution.py:248
  316.2 14.1 %collective-permute-start.29 = (bf16[1024,384]{1,0:T(8,128)(2,1)S(1)}, bf16[1024,384]{1,0:T(8,128)(2,1)S(1)}, u32[]{:S(2)}, u32[]{:S(2)}) collective-permute-start(bf16[1024,384]{1,0:T(8,128)(2,1)S(1)} %convolution_convert_fusion.7), channel_id=1, source_target_pairs={{0,1},{1,0},{2,3},{3,2},{4,5},{5,4},{6,7},{7,6},{8,9},{9,8},{10,11... | collective-permute-start | bytes 2359304 | tf_op jit(solution)/shard_map/ppermute | solution.py:248
  325.0 19.8 %collective-permute-start.31 = (bf16[1024,384]{1,0:T(8,128)(2,1)S(1)}, bf16[1024,384]{1,0:T(8,128)(2,1)S(1)}, u32[]{:S(2)}, u32[]{:S(2)}) collective-permute-start(bf16[1024,384]{1,0:T(8,128)(2,1)S(1)} %add_convert_fusion.1), channel_id=1, source_target_pairs={{0,2},{1,3},{2,0},{3,1},{4,6},{5,7},{6,4},{7,5},{8,10},{9,11},{10,... | collective-permute-start | bytes 2359304 | tf_op jit(solution)/shard_map/ppermute | solution.py:248
  330.3 14.8 %copy-start.68 = (bf16[1024,768]{1,0:T(8,128)(2,1)S(1)}, bf16[1024,768]{1,0:T(8,128)(2,1)}, u32[]{:S(2)}) copy-start(bf16[1024,768]{1,0:T(8,128)(2,1)} %get-tuple-element.266) | copy-start | bytes 4718596
  352.9 21.3 %collective-permute-start.34 = (bf16[2,1,2,192,384]{4,3,2,1,0:T(8,128)(2,1)}, bf16[2,1,2,192,384]{4,3,2,1,0:T(8,128)(2,1)}, u32[]{:S(2)}, u32[]{:S(2)}) collective-permute-start(bf16[2,1,2,192,384]{4,3,2,1,0:T(8,128)(2,1)} %get-tuple-element.271), channel_id=1, source_target_pairs={{0,8},{4,12},{8,0},{12,4},{16,24},{20,28},{24,16},{28,20},{1,9},{5... | collective-permute-start | bytes 1769480 | tf_op jit(solution)/shard_map/ppermute | solution.py:248
  354.2 21.3 %collective-permute-start.33 = (bf16[2,2,1,192,384]{4,3,2,1,0:T(8,128)(2,1)}, bf16[2,2,1,192,384]{4,3,2,1,0:T(8,128)(2,1)}, u32[]{:S(2)}, u32[]{:S(2)}) collective-permute-start(bf16[2,2,1,192,384]{4,3,2,1,0:T(8,128)(2,1)} %get-tuple-element.269), channel_id=1, source_target_pairs={{0,4},{4,0},{8,12},{12,8},{16,20},{20,16},{24,28},{28,24},{1,5},{5... | collective-permute-start | bytes 1769480 | tf_op jit(solution)/shard_map/ppermute | solution.py:248
  362.6 14.3 %collective-permute-start.32 = (bf16[2,1,256,768]{3,2,1,0:T(8,128)(2,1)S(1)}, bf16[2,1,256,768]{3,2,1,0:T(8,128)(2,1)}, u32[]{:S(2)}, u32[]{:S(2)}) collective-permute-start(bf16[2,1,256,768]{3,2,1,0:T(8,128)(2,1)S(1)} %dynamic-slice_convert_fusion), channel_id=1, source_target_pairs={{0,1},{1,0},{2,3},{3,2},{4,5},{5,4},{6,7},{7,6},{8,9},{9,8},{10,11... | collective-permute-start | bytes 2359304 | tf_op jit(solution)/shard_map/ppermute | solution.py:248
  379.2 15.7 %collective-permute-start.38 = (bf16[2,2,1,96,768]{4,3,2,1,0:T(8,128)(2,1)S(1)}, bf16[2,2,1,96,768]{4,3,2,1,0:T(8,128)(2,1)S(1)}, u32[]{:S(2)}, u32[]{:S(2)}) collective-permute-start(bf16[2,2,1,96,768]{4,3,2,1,0:T(8,128)(2,1)S(1)} %get-tuple-element.278), channel_id=1, source_target_pairs={{0,4},{4,0},{8,12},{12,8},{16,20},{20,16},{24,28},{28,24},{1,5},{5... | collective-permute-start | bytes 1769480 | tf_op jit(solution)/shard_map/ppermute | solution.py:248
  379.3 15.6 %collective-permute-start.35 = (bf16[1,1,256,768]{3,2,1,0:T(8,128)(2,1)S(1)}, bf16[1,1,256,768]{3,2,1,0:T(8,128)(2,1)S(1)}, u32[]{:S(2)}, u32[]{:S(2)}) collective-permute-start(bf16[1,1,256,768]{3,2,1,0:T(8,128)(2,1)S(1)} %dynamic-slice_convert_fusion.4), channel_id=1, source_target_pairs={{0,2},{1,3},{2,0},{3,1},{4,6},{5,7},{6,4},{7,5},{8,10},{9,11},{10,... | collective-permute-start | bytes 1179656 | tf_op jit(solution)/shard_map/ppermute | solution.py:248
  379.3 15.5 %collective-permute-start.36 = (bf16[2,1,1,192,384]{4,3,2,1,0:T(8,128)(2,1)S(1)}, bf16[2,1,1,192,384]{4,3,2,1,0:T(8,128)(2,1)S(1)}, u32[]{:S(2)}, u32[]{:S(2)}) collective-permute-start(bf16[2,1,1,192,384]{4,3,2,1,0:T(8,128)(2,1)S(1)} %get-tuple-element.274), channel_id=1, source_target_pairs={{0,8},{4,12},{8,0},{12,4},{16,24},{20,28},{24,16},{28,20},{1,9},{5... | collective-permute-start | bytes 884744 | tf_op jit(solution)/shard_map/ppermute | solution.py:248
  379.4 15.4 %collective-permute-start.37 = (bf16[1,1,2,192,384]{4,3,2,1,0:T(8,128)(2,1)S(1)}, bf16[1,1,2,192,384]{4,3,2,1,0:T(8,128)(2,1)S(1)}, u32[]{:S(2)}, u32[]{:S(2)}) collective-permute-start(bf16[1,1,2,192,384]{4,3,2,1,0:T(8,128)(2,1)S(1)} %get-tuple-element.276), channel_id=1, source_target_pairs={{0,16},{4,20},{8,24},{12,28},{16,0},{20,4},{24,8},{28,12},{1,17},{... | collective-permute-start | bytes 884744 | tf_op jit(solution)/shard_map/ppermute | solution.py:248
  399.6 11.8 %collective-permute-start.41 = (bf16[2,1,1,96,768]{4,3,2,1,0:T(8,128)(2,1)S(1)}, bf16[2,1,1,96,768]{4,3,2,1,0:T(8,128)(2,1)S(1)}, u32[]{:S(2)}, u32[]{:S(2)}) collective-permute-start(bf16[2,1,1,96,768]{4,3,2,1,0:T(8,128)(2,1)S(1)} %get-tuple-element.299), channel_id=1, source_target_pairs={{0,8},{4,12},{8,0},{12,4},{16,24},{20,28},{24,16},{28,20},{1,9},{5... | collective-permute-start | bytes 884744 | tf_op jit(solution)/shard_map/ppermute | solution.py:248
  401.5 9.4 %collective-permute-start.42 = (bf16[2,2,1,208,128]{4,3,2,1,0:T(8,128)(2,1)S(1)}, bf16[2,2,1,208,128]{4,3,2,1,0:T(8,128)(2,1)S(1)}, u32[]{:S(2)}, u32[]{:S(2)}) collective-permute-start(bf16[2,2,1,208,128]{4,3,2,1,0:T(8,128)(2,1)S(1)} %get-tuple-element.301), channel_id=1, source_target_pairs={{0,4},{4,0},{8,12},{12,8},{16,20},{20,16},{24,28},{28,24},{1,5},{5... | collective-permute-start | bytes 638984 | tf_op jit(solution)/shard_map/ppermute | solution.py:248
  402.1 8.4 %collective-permute-start.39 = (bf16[1,1,1,192,384]{4,3,2,1,0:T(8,128)(2,1)S(1)}, bf16[1,1,1,192,384]{4,3,2,1,0:T(8,128)(2,1)S(1)}, u32[]{:S(2)}, u32[]{:S(2)}) collective-permute-start(bf16[1,1,1,192,384]{4,3,2,1,0:T(8,128)(2,1)S(1)} %get-tuple-element.295), channel_id=1, source_target_pairs={{0,16},{4,20},{8,24},{12,28},{16,0},{20,4},{24,8},{28,12},{1,17},{... | collective-permute-start | bytes 442376 | tf_op jit(solution)/shard_map/ppermute | solution.py:248
  402.7 8.2 %collective-permute-start.40 = (bf16[1,1,1,192,384]{4,3,2,1,0:T(8,128)(2,1)S(1)}, bf16[1,1,1,192,384]{4,3,2,1,0:T(8,128)(2,1)S(1)}, u32[]{:S(2)}, u32[]{:S(2)}) collective-permute-start(bf16[1,1,1,192,384]{4,3,2,1,0:T(8,128)(2,1)S(1)} %get-tuple-element.297), channel_id=1, source_target_pairs={{0,4},{4,0},{8,12},{12,8},{16,20},{20,16},{24,28},{28,24},{1,5},{5... | collective-permute-start | bytes 442376 | tf_op jit(solution)/shard_map/ppermute | solution.py:248
  413.8 8.6 %collective-permute-start.43 = (bf16[1,1,1,96,768]{4,3,2,1,0:T(8,128)(2,1)S(1)}, bf16[1,1,1,96,768]{4,3,2,1,0:T(8,128)(2,1)S(1)}, u32[]{:S(2)}, u32[]{:S(2)}) collective-permute-start(bf16[1,1,1,96,768]{4,3,2,1,0:T(8,128)(2,1)S(1)} %get-tuple-element.309), channel_id=1, source_target_pairs={{0,16},{4,20},{8,24},{12,28},{16,0},{20,4},{24,8},{28,12},{1,17},{... | collective-permute-start | bytes 442376 | tf_op jit(solution)/shard_map/ppermute | solution.py:248
  416.9 4.7 %collective-permute-start.44 = (bf16[2,1,1,208,128]{4,3,2,1,0:T(8,128)(2,1)S(1)}, bf16[2,1,1,208,128]{4,3,2,1,0:T(8,128)(2,1)S(1)}, u32[]{:S(2)}, u32[]{:S(2)}) collective-permute-start(bf16[2,1,1,208,128]{4,3,2,1,0:T(8,128)(2,1)S(1)} %get-tuple-element.311), channel_id=1, source_target_pairs={{0,8},{4,12},{8,0},{12,4},{16,24},{20,28},{24,16},{28,20},{1,9},{5... | collective-permute-start | bytes 319496 | tf_op jit(solution)/shard_map/ppermute | solution.py:248
  422.5 10.3 %copy-start.43 = (f32[256,768]{1,0:T(8,128)S(1)}, f32[256,768]{1,0:T(8,128)}, u32[]{:S(2)}) copy-start(f32[256,768]{1,0:T(8,128)} %get-tuple-element.377) | copy-start | bytes 2359300
  422.6 5.7 %collective-permute-start.45 = (bf16[1,1,1,208,128]{4,3,2,1,0:T(8,128)(2,1)S(1)}, bf16[1,1,1,208,128]{4,3,2,1,0:T(8,128)(2,1)S(1)}, u32[]{:S(2)}, u32[]{:S(2)}) collective-permute-start(bf16[1,1,1,208,128]{4,3,2,1,0:T(8,128)(2,1)S(1)} %get-tuple-element.315), channel_id=1, source_target_pairs={{0,16},{4,20},{8,24},{12,28},{16,0},{20,4},{24,8},{28,12},{1,17},{... | collective-permute-start | bytes 159752 | tf_op jit(solution)/shard_map/ppermute | solution.py:248
  429.3 15.1 %all-to-all-start.2 = ((bf16[4,256,384]{2,1,0:T(8,128)(2,1)}), bf16[4,256,384]{2,1,0:T(8,128)(2,1)S(1)}, u32[]{:S(2)}, u32[]{:S(2)}) async-start(bf16[4,256,384]{2,1,0:T(8,128)(2,1)} %copy-done.74), calls=%async_computation.3 | async-start | bytes 1572864 | tf_op jit(solution)/shard_map/all_to_all | solution.py:697
  434.2 6.0 %collective-permute-start.46 = (bf16[208,128]{1,0:T(8,128)(2,1)S(1)}, bf16[208,128]{1,0:T(8,128)(2,1)S(1)}, u32[]{:S(2)}, u32[]{:S(2)}) collective-permute-start(bf16[208,128]{1,0:T(8,128)(2,1)S(1)} %bitcast.538), channel_id=1, source_target_pairs={{0,16},{4,20},{8,24},{12,28},{16,0},{20,4},{24,8},{28,12},{1,17},{... | collective-permute-start | bytes 159752 | tf_op jit(solution)/shard_map/ppermute | solution.py:248
  444.5 6.9 %collective-permute-start.47 = (bf16[2,208,128]{2,1,0:T(8,128)(2,1)S(1)}, bf16[2,208,128]{2,1,0:T(8,128)(2,1)S(1)}, u32[]{:S(2)}, u32[]{:S(2)}) collective-permute-start(bf16[2,208,128]{2,1,0:T(8,128)(2,1)S(1)} %pad_maximum_fusion.31), channel_id=1, source_target_pairs={{0,8},{4,12},{8,0},{12,4},{16,24},{20,28},{24,16},{28,20},{1,9},{5... | collective-permute-start | bytes 319496 | tf_op jit(solution)/shard_map/ppermute | solution.py:248
  451.4 6.6 %collective-permute-start.48 = (bf16[2,2,208,128]{3,2,0,1:T(8,128)(2,1)S(1)}, bf16[2,2,208,128]{3,2,0,1:T(8,128)(2,1)S(1)}, u32[]{:S(2)}, u32[]{:S(2)}) collective-permute-start(bf16[2,2,208,128]{3,2,0,1:T(8,128)(2,1)S(1)} %pad_maximum_fusion.27), channel_id=1, source_target_pairs={{0,4},{4,0},{8,12},{12,8},{16,20},{20,16},{24,28},{28,24},{1,5},{5... | collective-permute-start | bytes 638984 | tf_op jit(solution)/shard_map/ppermute | solution.py:248
  (133 other events, 424.0 us)
Sparse Core Ops, SparseCore 0:
  56.3 55.4 all-gather.4
  114.5 63.7 all-gather.6
  305.0 85.4 reduce-scatter.1
